TPU v7x, 32 devices: a whole 2x2x4 slice. The times are simulated.
32 devices in a mesh: dp: 8 (over z, x), seq: 4 (over y, core).
Axes of the slice: x: 2, y: 2, z: 4, core: 2. Of those that a mesh axis runs over, the one named last changes fastest.
Arguments:
- text_input: bfloat16 [16, 512, 768], P('dp', 'seq'), may hold values from -6 to 6
- layout_input: bfloat16 [16, 512, 192], P('dp', 'seq'), may hold values from -6 to 6
- segments: int32 [16, 512], P('dp', 'seq'), may hold values from 0 to 4, as said below
- text_cotangent: bfloat16 [16, 512, 768], P('dp', 'seq'), may hold values from -6 to 6
- layout_cotangent: bfloat16 [16, 512, 192], P('dp', 'seq'), may hold values from -6 to 6
- text_project: bfloat16 [768, 2304], replicated, may hold values from -0.21875 to 0.21875
- text_biases: bfloat16 [6, 768], replicated, may hold values from -3 to 3
- text_gains: bfloat16 [2, 768], replicated, may hold values from 0.5 to 1.5
- text_merge: bfloat16 [768, 768], replicated, may hold values from -1.5 to 1.5
- text_expand: bfloat16 [768, 3072], replicated, may hold values from -0.21875 to 0.21875
- text_offsets: bfloat16 [3072], replicated, may hold values from -3 to 3
- text_shrink: bfloat16 [3072, 768], replicated, may hold values from -0.109375 to 0.109375
- layout_project: bfloat16 [192, 576], replicated, may hold values from -0.4375 to 0.4375
- layout_biases: bfloat16 [6, 192], replicated, may hold values from -3 to 3
- layout_gains: bfloat16 [2, 192], replicated, may hold values from 0.5 to 1.5
- layout_merge: bfloat16 [192, 192], replicated, may hold values from -3 to 3
- layout_expand: bfloat16 [192, 768], replicated, may hold values from -0.4375 to 0.4375
- layout_offsets: bfloat16 [768], replicated, may hold values from -3 to 3
- layout_shrink: bfloat16 [768, 192], replicated, may hold values from -0.21875 to 0.21875
Outputs:
- text_result: bfloat16 [16, 512, 768], P('dp', 'seq')
- layout_result: bfloat16 [16, 512, 192], P('dp', 'seq')
- text_sensitivity: float32 [16, 512, 768], P('dp', 'seq')
- layout_sensitivity: float32 [16, 512, 192], P('dp', 'seq')
- text_project_delta: float32 [768, 2304], P(None, 'seq')
- text_biases_delta: float32 [6, 768], P(None, 'seq')
- text_gains_delta: float32 [2, 768], P(None, 'seq')
- text_merge_delta: float32 [768, 768], P(None, 'seq')
- text_expand_delta: float32 [768, 3072], P(None, 'seq')
- text_offsets_delta: float32 [3072], P('seq')
- text_shrink_delta: float32 [3072, 768], P(None, 'seq')
- layout_project_delta: float32 [192, 576], P(None, 'seq')
- layout_biases_delta: float32 [6, 192], P(None, 'seq')
- layout_gains_delta: float32 [2, 192], P(None, 'seq')
- layout_merge_delta: float32 [192, 192], P(None, 'seq')
- layout_expand_delta: float32 [192, 768], P(None, 'seq')
- layout_offsets_delta: float32 [768], P('seq')
- layout_shrink_delta: float32 [768, 192], P(None, 'seq')
Inputs may be any that keep to these rules, and one draw needn't show every extreme that they name: `segments`: along the 512 rows of a pack the segment ids never fall; rows with equal ids form one document. Each pack holds one long document through its middle and up to four short ones at its ends.
All inputs are finite; a program needn't handle non-finite values.
Results may differ from a plain program's by a relative error of at most 0.014.
Values may be sent and summed in bfloat16 or wider, within the bound.
No kernel may reach another device: no remote copies, remote signals or barrier semaphores. Data moves between devices by JAX's collectives and lax.ppermute only.
A program may use at most 192 MiB of HBM per device.

v0:
```python
import math

import jax
import jax.numpy as jnp
from jax import lax
from jax.sharding import PartitionSpec as P

HEADS = 12
ET = 64
EL = 16


EPSILON = 1e-05
MASKED = -1000000000.0


def layer_norm(values, gains, shifts):
    centre = values - jnp.mean(values, axis=-1, keepdims=True)
    spread = jnp.mean(centre * centre, axis=-1, keepdims=True)
    return centre * lax.rsqrt(spread + EPSILON) * gains + shifts


def gelu_exact(values):
    return jax.nn.gelu(values, approximate=False)


def matmul(left, right):
    return jnp.dot(left, right, preferred_element_type=jnp.float32)


def outer_sum(left, right):
    return lax.dot_general(
        left, right, (((0,), (0,)), ((), ())), preferred_element_type=jnp.float32
    )


def back_product(left, right):
    return lax.dot_general(
        left, right, (((1,), (1,)), ((), ())), preferred_element_type=jnp.float32
    )


def head_split(array, heads):
    return array.reshape(array.shape[0], array.shape[1], heads, array.shape[2] // heads)


def grouped(array, group_size):
    return array.reshape((array.shape[0] // group_size, group_size) + array.shape[1:])


def ungrouped(array):
    return array.reshape((array.shape[0] * array.shape[1],) + array.shape[2:])


def project(flat_rows, weight, biases, pack_count):
    model_width = flat_rows.shape[1]
    bias_rows = biases.astype(jnp.float32)
    joined = matmul(flat_rows, weight)
    queries = (joined[:, :model_width] + bias_rows[0]).astype(jnp.bfloat16)
    key_rows = joined[:, model_width : 2 * model_width].astype(jnp.bfloat16)
    value_rows = (joined[:, 2 * model_width :] + bias_rows[1]).astype(jnp.bfloat16)
    return (
        queries.reshape(pack_count, -1, model_width),
        key_rows.reshape(pack_count, -1, model_width),
        value_rows.reshape(pack_count, -1, model_width),
    )


def head_scores(queries, key_rows, head_size):
    raw = jnp.einsum(
        "gihe,gjhe->ghij",
        head_split(queries, HEADS),
        head_split(key_rows, HEADS),
        preferred_element_type=jnp.float32,
    )
    return raw * head_size ** (-0.5)


def coupled_probs(text_query, text_key, layout_query, layout_key, query_segment, key_segment):
    text_score = head_scores(text_query, text_key, ET)
    layout_score = head_scores(layout_query, layout_key, EL)
    allowed = query_segment[:, None, :, None] == key_segment[:, None, None, :]
    text_prob = jax.nn.softmax(jnp.where(allowed, text_score + layout_score, MASKED), axis=-1)
    layout_prob = jax.nn.softmax(jnp.where(allowed, layout_score + text_score, MASKED), axis=-1)
    return (text_prob, layout_prob)


def mixing(probs, value_rows):
    mixed = jnp.einsum(
        "ghij,gjhe->gihe",
        probs.astype(jnp.bfloat16),
        head_split(value_rows, HEADS),
        preferred_element_type=jnp.float32,
    )
    return mixed.reshape(mixed.shape[0], mixed.shape[1], -1).astype(jnp.bfloat16)


def attend_forward(block_inputs):
    (
        text_query,
        text_key,
        text_value,
        layout_query,
        layout_key,
        layout_value,
        query_segment,
        key_segment,
    ) = block_inputs
    text_prob, layout_prob = coupled_probs(
        text_query, text_key, layout_query, layout_key, query_segment, key_segment
    )
    return (mixing(text_prob, text_value), mixing(layout_prob, layout_value))


def logit_change(probs, context_delta, value_rows):
    prob_delta = jnp.einsum(
        "gihe,gjhe->ghij",
        head_split(context_delta, HEADS),
        head_split(value_rows, HEADS),
        preferred_element_type=jnp.float32,
    )
    return probs * (prob_delta - jnp.sum(probs * prob_delta, axis=-1, keepdims=True))


def input_change(probs, score_delta, context_delta, queries, key_rows, head_size):
    group_count, key_count = (key_rows.shape[0], key_rows.shape[1])
    value_delta = jnp.einsum(
        "ghij,gihe->gjhe",
        probs.astype(jnp.bfloat16),
        head_split(context_delta, HEADS),
        preferred_element_type=jnp.float32,
    )
    query_delta = jnp.einsum(
        "ghij,gjhe->gihe",
        score_delta,
        head_split(key_rows, HEADS),
        preferred_element_type=jnp.float32,
    ) * head_size ** (-0.5)
    key_delta = jnp.einsum(
        "ghij,gihe->gjhe",
        score_delta,
        head_split(queries, HEADS),
        preferred_element_type=jnp.float32,
    ) * head_size ** (-0.5)
    return (
        query_delta.reshape(queries.shape),
        key_delta.reshape(group_count, key_count, -1),
        value_delta.reshape(group_count, key_count, -1),
    )


def attend_backward(block_inputs):
    (
        text_query,
        text_key,
        text_value,
        layout_query,
        layout_key,
        layout_value,
        query_segment,
        key_segment,
        text_delta,
        layout_delta,
    ) = block_inputs
    text_prob, layout_prob = coupled_probs(
        text_query, text_key, layout_query, layout_key, query_segment, key_segment
    )
    text_logit = logit_change(text_prob, text_delta, text_value)
    layout_logit = logit_change(layout_prob, layout_delta, layout_value)
    text_score = (text_logit + layout_logit).astype(jnp.bfloat16)
    layout_score = layout_logit.astype(jnp.bfloat16)
    text_parts = input_change(text_prob, text_score, text_delta, text_query, text_key, ET)
    layout_parts = input_change(
        layout_prob, layout_score, layout_delta, layout_query, layout_key, EL
    )
    return (
        text_parts[0],
        layout_parts[0],
        text_parts[1],
        text_parts[2],
        layout_parts[1],
        layout_parts[2],
    )


def stream_tail(flat_rows, context, biases, gains, merge, expand, offsets, shrink, cotangent):
    bias_rows = biases.astype(jnp.float32)
    gain_rows = gains.astype(jnp.float32)
    attention_rows = matmul(context, merge) + bias_rows[2]
    middle = flat_rows.astype(jnp.float32) + attention_rows
    hidden, norm_first = jax.vjp(layer_norm, middle, gain_rows[0], bias_rows[3])
    hidden_low = hidden.astype(jnp.bfloat16)
    before = matmul(hidden_low, expand) + offsets.astype(jnp.float32)
    active, gelu_back = jax.vjp(gelu_exact, before)
    active_low = active.astype(jnp.bfloat16)
    branch = matmul(active_low, shrink) + bias_rows[4]
    result, norm_second = jax.vjp(layer_norm, hidden + branch, gain_rows[1], bias_rows[5])
    sum_delta, second_gain, second_shift = norm_second(cotangent)
    branch_delta = sum_delta.astype(jnp.bfloat16)
    shrink_delta = outer_sum(active_low, branch_delta)
    branch_bias = jnp.sum(branch_delta.astype(jnp.float32), axis=0)
    before_delta = gelu_back(back_product(branch_delta, shrink))[0].astype(jnp.bfloat16)
    expand_delta = outer_sum(hidden_low, before_delta)
    offsets_delta = jnp.sum(before_delta.astype(jnp.float32), axis=0)
    hidden_delta = sum_delta + back_product(before_delta, expand)
    middle_delta, first_gain, first_shift = norm_first(hidden_delta)
    attention_delta = middle_delta.astype(jnp.bfloat16)
    merge_delta = outer_sum(context, attention_delta)
    merge_bias = jnp.sum(attention_delta.astype(jnp.float32), axis=0)
    context_delta = back_product(attention_delta, merge).astype(jnp.bfloat16)
    tail_biases = jnp.stack([merge_bias, first_shift, branch_bias, second_shift])
    gains_delta = jnp.stack([first_gain, second_gain])
    return (
        result.astype(jnp.bfloat16),
        (expand_delta, offsets_delta, shrink_delta),
        context_delta,
        middle_delta,
        merge_delta,
        tail_biases,
        gains_delta,
    )


def project_back(flat_rows, weight, query_delta, key_delta, value_delta):
    joined = jnp.concatenate([query_delta, key_delta, value_delta], axis=-1).reshape(
        flat_rows.shape[0], -1
    )
    return (
        outer_sum(flat_rows, joined),
        back_product(joined, weight),
        jnp.sum(query_delta.astype(jnp.float32), axis=(0, 1)),
        jnp.sum(value_delta.astype(jnp.float32), axis=(0, 1)),
    )


def own_share(total):
    share = total.shape[-1] // lax.axis_size("seq")
    return lax.dynamic_slice_in_dim(total, lax.axis_index("seq") * share, share, total.ndim - 1)


def local(
    text_input,
    layout_input,
    segments,
    text_cotangent,
    layout_cotangent,
    text_project,
    text_biases,
    text_gains,
    text_merge,
    text_expand,
    text_offsets,
    text_shrink,
    layout_project,
    layout_biases,
    layout_gains,
    layout_merge,
    layout_expand,
    layout_offsets,
    layout_shrink,
):
    pack_count, row_count, text_width = text_input.shape
    layout_width = layout_input.shape[2]
    token_count = pack_count * row_count
    group_size = math.gcd(pack_count, max(1, 512 // row_count))
    text_flat = text_input.reshape(token_count, text_width)
    layout_flat = layout_input.reshape(token_count, layout_width)
    text_query, text_key, text_value = project(text_flat, text_project, text_biases, pack_count)
    layout_query, layout_key, layout_value = project(
        layout_flat, layout_project, layout_biases, pack_count
    )
    gathered = (
        lax.all_gather(text_key, "seq", axis=1, tiled=True),
        lax.all_gather(text_value, "seq", axis=1, tiled=True),
        lax.all_gather(layout_key, "seq", axis=1, tiled=True),
        lax.all_gather(layout_value, "seq", axis=1, tiled=True),
        lax.all_gather(segments, "seq", axis=1, tiled=True),
    )
    forward_inputs = (
        text_query,
        gathered[0],
        gathered[1],
        layout_query,
        gathered[2],
        gathered[3],
        segments,
        gathered[4],
    )
    contexts = lax.map(
        attend_forward, tuple((grouped(member, group_size) for member in forward_inputs))
    )
    text_context = ungrouped(contexts[0]).reshape(token_count, text_width)
    layout_context = ungrouped(contexts[1]).reshape(token_count, layout_width)
    text_tail = stream_tail(
        text_flat,
        text_context,
        text_biases,
        text_gains,
        text_merge,
        text_expand,
        text_offsets,
        text_shrink,
        text_cotangent.reshape(token_count, text_width).astype(jnp.float32),
    )
    layout_tail = stream_tail(
        layout_flat,
        layout_context,
        layout_biases,
        layout_gains,
        layout_merge,
        layout_expand,
        layout_offsets,
        layout_shrink,
        layout_cotangent.reshape(token_count, layout_width).astype(jnp.float32),
    )
    text_feed = text_tail[1]
    layout_feed = layout_tail[1]
    backward_inputs = (
        text_query,
        gathered[0],
        gathered[1],
        layout_query,
        gathered[2],
        gathered[3],
        segments,
        gathered[4],
        text_tail[2].reshape(pack_count, row_count, text_width),
        layout_tail[2].reshape(pack_count, row_count, layout_width),
    )
    attention_parts = lax.map(
        attend_backward, tuple((grouped(member, group_size) for member in backward_inputs))
    )
    (
        text_query_delta,
        layout_query_delta,
        text_key_delta,
        text_value_delta,
        layout_key_delta,
        layout_value_delta,
    ) = tuple((ungrouped(member) for member in attention_parts))
    key_sums = (
        lax.psum_scatter(
            text_key_delta.astype(jnp.bfloat16), "seq", scatter_dimension=1, tiled=True
        ).astype(jnp.float32),
        lax.psum_scatter(
            text_value_delta.astype(jnp.bfloat16), "seq", scatter_dimension=1, tiled=True
        ).astype(jnp.float32),
        lax.psum_scatter(
            layout_key_delta.astype(jnp.bfloat16), "seq", scatter_dimension=1, tiled=True
        ).astype(jnp.float32),
        lax.psum_scatter(
            layout_value_delta.astype(jnp.bfloat16), "seq", scatter_dimension=1, tiled=True
        ).astype(jnp.float32),
    )
    text_back = project_back(
        text_flat,
        text_project,
        text_query_delta.astype(jnp.bfloat16),
        key_sums[0].astype(jnp.bfloat16),
        key_sums[1].astype(jnp.bfloat16),
    )
    layout_back = project_back(
        layout_flat,
        layout_project,
        layout_query_delta.astype(jnp.bfloat16),
        key_sums[2].astype(jnp.bfloat16),
        key_sums[3].astype(jnp.bfloat16),
    )
    text_sensitivity = (text_tail[3] + text_back[1]).reshape(pack_count, row_count, text_width)
    layout_sensitivity = (layout_tail[3] + layout_back[1]).reshape(
        pack_count, row_count, layout_width
    )
    text_bias_total = jnp.concatenate(
        [jnp.stack([text_back[2], text_back[3]]), text_tail[5]], axis=0
    )
    layout_bias_total = jnp.concatenate(
        [jnp.stack([layout_back[2], layout_back[3]]), layout_tail[5]], axis=0
    )
    totals = lax.psum(
        (
            text_back[0],
            text_bias_total,
            text_tail[6],
            text_tail[4],
            layout_back[0],
            layout_bias_total,
            layout_tail[6],
            layout_tail[4],
            text_feed[0],
            text_feed[1],
            text_feed[2],
            layout_feed[0],
            layout_feed[1],
            layout_feed[2],
        ),
        ("dp", "seq"),
    )
    finals = tuple((own_share(member) for member in totals))
    return (
        text_tail[0].reshape(pack_count, row_count, text_width),
        layout_tail[0].reshape(pack_count, row_count, layout_width),
        text_sensitivity,
        layout_sensitivity,
        finals[0],
        finals[1],
        finals[2],
        finals[3],
        finals[8],
        finals[9],
        finals[10],
        finals[4],
        finals[5],
        finals[6],
        finals[7],
        finals[11],
        finals[12],
        finals[13],
    )


def solution(mesh):
    in_specs = (
        P("dp", "seq", None),
        P("dp", "seq", None),
        P("dp", "seq"),
        P("dp", "seq", None),
        P("dp", "seq", None),
        P(),
        P(),
        P(),
        P(),
        P(),
        P(),
        P(),
        P(),
        P(),
        P(),
        P(),
        P(),
        P(),
        P(),
    )
    out_specs = (
        P("dp", "seq", None),
        P("dp", "seq", None),
        P("dp", "seq", None),
        P("dp", "seq", None),
        P(None, "seq"),
        P(None, "seq"),
        P(None, "seq"),
        P(None, "seq"),
        P(None, "seq"),
        P("seq"),
        P(None, "seq"),
        P(None, "seq"),
        P(None, "seq"),
        P(None, "seq"),
        P(None, "seq"),
        P(None, "seq"),
        P("seq"),
        P(None, "seq"),
    )
    return jax.shard_map(local, mesh=mesh, in_specs=in_specs, out_specs=out_specs, check_vma=False)
```

profile of v0, /device:TPU:0, one launch (start us, length us, event | category | flops | bytes accessed | tf_op | source)
XLA Modules:
  0.0 774.1 jit_solution(8657553088719163877)
XLA Ops:
  7.3 1.9 copy-done
  9.2 2.1 fusion.113
  14.9 2.4 fusion.38
  20.0 6.3 all_gather.16
  37.0 7.2 all_gather.18
  45.0 9.1 %all_gather.19 = bf16[2,512,192]{1,0,2:T(2,128)(2,1)S(1)} all-gather(bf16[2,128,192]{1,0,2:T(2,128)(2,1)} %reshape.377), channel_id=1, replica_groups=mesh['dp'=8,'seq'=4] {'seq'}, dimensions={1}, use_global_device_ids=true | all-gather | bytes 491520 | tf_op jit(solution)/shard_map/all_gather | solution.py:276
  54.9 1.9 copy.78
  56.8 1.9 reshape.369
  58.7 4.7 fusion.80
  63.5 2.7 copy.79
  66.2 9.4 %fusion.104 = (f32[2,12,128]{2,1,0:T(8,128)}, f32[2,12,128,512]{3,2,1,0:T(8,128)}) fusion(f32[2,12,128,512]{3,2,1,0:T(8,128)} %fusion.80, pred[2,128,512]{2,1,0:T(8,128)(4,1)} %broadcast_compare_fusion, bf16[2,512,12,64]{1,3,2,0:T(8,128)(2,1)} %bitcast.221, bf16[2,128,12,64]{1,0,3,2:T(2,128)(2,1)} %reshape.369), kind=kOutput, calls=%fused_computation.223 | convolution fusion | flops 210764288 | bytes 14692352 | tf_op jit(solution)/shard_map/while/body/eval_jaxpr/sub | solution.py:83
  75.6 3.2 fusion.95
  80.7 2.0 multiply_convert_fusion.2
  92.0 3.3 convolution_convert_fusion.1
  95.3 5.8 multiply_reduce_fusion
  101.1 2.6 copy.77
  103.7 3.7 fusion.31
  110.1 2.0 copy.106
  112.1 2.1 reshape.404
  114.3 12.0 %multiply_convert_fusion.1 = (bf16[256,3072]{1,0:T(8,128)(2,1)S(1)}, f32[256,3072]{1,0:T(8,128)S(1)}, f32[256,3072]{1,0:T(8,128)}) fusion(f32[3072]{0:T(1024)} %convert_element_type.250, bf16[768,3072]{1,0:T(8,128)(2,1)} %param.28, f32[256,768]{1,0:T(8,128)} %copy-done.6, f32[768]{0:T(1024)S(1)} %get-tuple-element.168, f32[768]{0:T(1024)S(1)} %get-tuple-element.246, ...), kind=kOutput, calls=%fused_computation.21 | convolution fusion | flops 1260847104 | bytes 13389824 | tf_op jit(solution)/shard_map/dot_general | solution.py:28
  126.4 4.5 fusion.106
  134.0 4.9 convert_reduce_fusion
  138.9 6.0 multiply_reduce_fusion.2
  149.1 2.0 copy.104
  151.0 2.1 reshape.402
  153.8 2.5 fusion.98
  156.6 1.9 convert_reduce_fusion.4
  159.3 2.5 convolution_convert_fusion.2
  161.8 1.9 copy.87
  163.7 1.8 reshape.380
  165.5 3.8 convolution_convert_fusion
  169.3 5.0 copy.102
  174.3 2.8 copy.116
  177.2 5.2 fusion.56
  182.4 23.9 %multiply_convert_fusion = bf16[2,12,64,512]{3,2,1,0:T(8,128)(2,1)} fusion(f32[2,12,128,512]{3,2,1,0:T(8,128)} %fusion.56, f32[2,12,128,512]{3,2,1,0:T(8,128)} %get-tuple-element.239, f32[2,12,128]{2,1,0:T(8,128)} %get-tuple-element.238, bf16[2,128,12,64]{1,0,3,2:T(2,128)(2,1)} %reshape.369, f32[2,12,128,512]{3,2,1,0:T(8,128)} %get-tuple-element.225, ...), kind=kOutput, calls=%fused_computation.17 | convolution fusion | flops 217058816 | bytes 20865024 | tf_op jit(solution)/shard_map/while/body/eval_jaxpr/ghij,gihe->gjhe/dot_general | solution.py:139
  206.3 5.0 copy.100
  211.4 2.8 copy.115
  214.2 1.8 fusion.68
  216.0 2.1 fusion.115
  218.2 2.2 fusion.89
  220.4 24.8 %convert_reduce_fusion.6 = (f32[12,64]{1,0:T(8,128)}, bf16[2,12,64,128]{3,2,1,0:T(8,128)(2,1)}) fusion(bf16[2,512,12,64]{1,3,2,0:T(8,128)(2,1)} %bitcast.222, f32[2,12,128,512]{3,2,1,0:T(8,128)} %fusion.56, f32[2,12,128,512]{3,2,1,0:T(8,128)} %get-tuple-element.239, f32[2,12,128]{2,1,0:T(8,128)} %get-tuple-element.238, ...), kind=kOutput, calls=%fused_computation.87 | convolution fusion | flops 216271616 | bytes 20868096 | tf_op jit(solution)/shard_map/while/body/eval_jaxpr/ghij,gjhe->gihe/dot_general | solution.py:133
  245.2 3.2 fusion.50
  248.4 2.6 convert_reduce_fusion.11
  251.0 5.1 fusion.114
  256.1 5.2 fusion.92
  261.4 1.7 reshape.405
  268.0 2.1 convolution_bitcast_fusion.1
  270.2 1.8 reshape.401
  272.0 1.9 copy.103
  273.9 1.8 reshape.399
  275.8 1.9 copy.101
  277.7 5.4 convolution_bitcast_fusion
  302.5 2.3 pad_maximum_fusion
  304.8 2.4 copy.93
  308.6 44.0 %all-reduce = (f32[6,768]{1,0:T(8,128)}, f32[2,768]{1,0:T(2,128)}, f32[3072]{0:T(1024)}, f32[6,192]{1,0:T(8,128)}, f32[2,192]{1,0:T(2,128)}, /*index=5*/f32[768]{0:T(1024)}) all-reduce(f32[6,768]{1,0:T(8,128)} %concatenate.14, f32[2,768]{1,0:T(2,128)S(1)} %pad_maximum_fusion.3, ...), channel_id=1, replica_groups=mesh['dp'=8,'seq'=4] {'dp','seq'}, use_global_device_ids=true, to_apply=%region_31.32 | all-reduce | flops 11520 | bytes 92160 | tf_op jit(solution)/shard_map/psum | solution.py:379
  360.6 3.5 convolution_add_fusion.3
  364.2 383.4 %all-reduce.4.cloned.1.call-done = (f32[768,2304]{0,1:T(8,128)}, f32[768,768]{0,1:T(8,128)}, f32[768,3072]{1,0:T(8,128)}, f32[3072,768]{0,1:T(8,128)}, f32[192,5...) async-done(((f32[768,2304]{0,1:T(8,128)}, f32[768,768]{0,1:T(8,128)}, f32[768,3072]{1,0:T(8,128)}, f32[3072,768]{0,1:T(8,128)}, ...) | async-done | bytes 30081040 | tf_op jit(solution)/shard_map/psum | solution.py:379
  750.6 1.8 constant_dynamic-slice_fusion.5
  752.4 1.7 copy.99
  754.1 1.8 constant_dynamic-slice_fusion.1
  755.8 1.9 constant_dynamic-slice_fusion.8
  757.7 3.3 constant_dynamic-slice_fusion.6
  761.0 3.2 constant_dynamic-slice_fusion.7
  764.2 2.8 constant_dynamic-slice_fusion.11
  (248 shorter events, 78.3 us)
Async XLA Ops:
  7.2 2.0 copy-start
  7.2 56.3 %all-gather.5.cloned.1.call-start = ((), (), s32[]{:S(2)}) async-start(), calls=%async_computation.5 | async-start | bytes 1966080 | tf_op jit(solution)/shard_map/all_gather | solution.py:273
  9.2 5.1 copy-start.50
  12.7 13.5 %copy-start.53 = (bf16[6,192]{1,0:T(8,128)(2,1)S(1)}, bf16[6,192]{1,0:T(8,128)(2,1)}, u32[]{:S(2)}) copy-start(bf16[6,192]{1,0:T(8,128)(2,1)} %param.32) | copy-start | bytes 6916
  13.5 87.6 %all-gather.3.cloned.1.call-start = ((), (), s32[]{:S(2)}) async-start(), calls=%async_computation.4 | async-start | bytes 1966080 | tf_op jit(solution)/shard_map/all_gather | solution.py:274
  17.3 244.1 %reduce-scatter.19.cloned.1.call-start = ((), (), s32[]{:S(2)}) async-start(), calls=%async_computation.9 | async-start | bytes 491520
  75.6 3.3 copy-start.18
  78.8 3.8 copy-start.1
  78.9 1.7 copy-start.34
  78.9 1.7 copy-start.39
  78.9 1.7 copy-start.54
  78.9 1.7 copy-start.60
  80.3 7.2 copy-start.5
  80.4 7.1 copy-start.37
  80.6 2.1 copy-start.33
  80.6 2.1 copy-start.61
  80.6 2.5 copy-start.24
  80.7 2.5 copy-start.51
  80.7 3.2 copy-start.55
  82.7 1.9 copy-start.16
  85.3 3.7 copy-start.29
  92.0 3.3 copy-start.19
  92.0 3.3 copy-start.32
  92.0 3.3 copy-start.35
  103.7 4.1 copy-start.13
  103.7 4.1 copy-start.23
  103.7 4.1 copy-start.59
  107.8 1.7 copy-start.17
  108.4 1.7 copy-start.40
  114.2 150.4 %reduce-scatter.17.cloned.1.call-start = ((), (), s32[]{:S(2)}) async-start(), calls=%async_computation.8 | async-start | bytes 491520
  114.3 12.0 %copy-start.7 = (f32[256,768]{1,0:T(8,128)S(1)}, f32[256,768]{1,0:T(8,128)}, u32[]{:S(2)}) copy-start(f32[256,768]{1,0:T(8,128)} %copy-done.6) | copy-start | bytes 2359300
  114.3 12.0 %copy-start.41 = (f32[256]{0:T(256)S(1)}, f32[256]{0:T(256)}, u32[]{:S(2)}) copy-start(f32[256]{0:T(256)} %copy-done.40) | copy-start | bytes 3076
  114.3 12.0 %copy-start.48 = (f32[256]{0:T(256)S(1)}, f32[256]{0:T(256)}, u32[]{:S(2)}) copy-start(f32[256]{0:T(256)} %fusion.82) | copy-start | bytes 3076
  114.3 12.0 %copy-start.58 = (f32[768]{0:T(1024)S(1)}, f32[768]{0:T(1024)}, u32[]{:S(2)}) copy-start(f32[768]{0:T(1024)} %get-tuple-element.167) | copy-start | bytes 9220
  126.3 4.5 copy-start.11
  126.3 7.7 slice-start.4
  126.4 4.7 copy-start.9
  126.4 5.7 copy-start.44
  126.4 7.6 slice-start.5
  134.0 4.9 copy-start.14
  134.0 10.9 %slice-start = ((s8[6291456]{0:T(1024)(128)(4,1)}), s8[4194304]{0:T(1024)(128)(4,1)S(1)}, s32[]{:S(2)}) async-start(s8[6291456]{0:T(1024)(128)(4,1)} %bitcast.210), calls=%async_computation.11 | async-start | bytes 8388608
  134.0 10.9 %slice-start.2 = ((s8[6291456]{0:T(1024)(128)(4,1)}), s8[4194304]{0:T(1024)(128)(4,1)S(1)}, s32[]{:S(2)}) async-start(s8[6291456]{0:T(1024)(128)(4,1)} %bitcast.219), calls=%async_computation.13 | async-start | bytes 8388608
  134.0 10.9 %slice-start.1 = ((s8[6291456]{0:T(1024)(128)(4,1)}), s8[2097152]{0:T(1024)(128)(4,1)S(1)}, s32[]{:S(2)}) async-start(s8[6291456]{0:T(1024)(128)(4,1)} %bitcast.210), calls=%async_computation.12 | async-start | bytes 4194304
  134.0 10.9 %slice-start.3 = ((s8[6291456]{0:T(1024)(128)(4,1)}), s8[2097152]{0:T(1024)(128)(4,1)S(1)}, s32[]{:S(2)}) async-start(s8[6291456]{0:T(1024)(128)(4,1)} %bitcast.219), calls=%async_computation.14 | async-start | bytes 4194304
  138.9 6.0 copy-start.21
  138.9 6.1 copy-start.36
  138.9 6.1 copy-start.47
  145.0 2.8 copy-start.27
  146.1 1.7 copy-start.2
  147.7 6.1 copy-start.42
  156.4 13.0 %copy-start.62 = (f32[256]{0:T(256)}, f32[256]{0:T(256)S(1)}, u32[]{:S(2)}) copy-start(f32[256]{0:T(256)S(1)} %negate_multiply_fusion.4) | copy-start | bytes 3076
  156.4 113.8 %reduce-scatter.15.cloned.1.call-start = ((), (), s32[]{:S(2)}) async-start(), calls=%async_computation.7 | async-start | bytes 1966080
  177.1 96.8 %reduce-scatter.13.cloned.1.call-start = ((), (), s32[]{:S(2)}) async-start(), calls=%async_computation.6 | async-start | bytes 1966080
  211.3 6.8 copy-start.38
  214.2 533.4 %all-reduce.4.cloned.1.call-start = ((), (), s32[]{:S(2)}) async-start(), calls=%async_computation.10 | async-start | bytes 60358656 | tf_op jit(solution)/shard_map/psum | solution.py:379
  245.2 3.2 copy-start.3
  245.2 5.8 copy-start.12
  245.2 5.8 copy-start.15
  251.0 5.1 copy-start.8
  251.0 5.1 copy-start.22
  251.0 5.1 copy-start.43
  251.0 5.1 copy-start.49
  283.0 5.5 copy-start.45
  283.0 6.0 copy-start.46
  (12 other events, 11.6 us)
Sparse Core Ops, SparseCore 0:
  13.6 22.3 all-gather.4
  38.2 21.7 all-gather.2
  114.4 22.3 reduce-scatter.18
  156.5 22.4 reduce-scatter.16
  182.0 28.2 reduce-scatter.14
  214.3 29.8 reduce-scatter.12
  283.2 464.3 all-reduce.3
where the time goes:
time: 780 us; the launch traced here: 774 us
  waiting for transfers between devices  384 us (49%)
  matrix products  161 us (21%)
  local copies, waits for them, and re-layouts  113 us (14%)
  blocking collectives  66.6 us (9%)
  other arithmetic  34 us (4%)
  between operations  15.1 us (2%)
    psum x1, waiting for transfers between devices, local(): lax.psum((text_back[0], text_bias_total, text_tail[6], text_tail[4], layo...  383 us
    unnamed x155, local copies, waits for them, and re-layouts  48.2 us
    psum x1, blocking collectives, local(): lax.psum((text_back[0], text_bias_total, text_tail[6], text_tail[4], layo...  44 us
    dot_general x2, matrix products, input_change(): jnp.einsum('ghij,gjhe->gihe', score_delta, head_split(key_rows, HEADS), p...  27.4 us
    dot_general x8, matrix products, outer_sum(): lax.dot_general(left, right, (((0,), (0,)), ((), ())), preferred_element_...  27.1 us
    dynamic_slice x14, local copies, waits for them, and re-layouts, own_share(): lax.dynamic_slice_in_dim(total, lax.axis_index('seq') * share, share, tot...  25.8 us
    dot_general x2, matrix products, input_change(): jnp.einsum('ghij,gihe->gjhe', score_delta, head_split(queries, HEADS), pr...  25.2 us
    dot_general x8, matrix products, matmul(): return jnp.dot(left, right, preferred_element_type=jnp.float32)  23 us
  transfers between devices with their start and end apart: 7, of which 1 were waited for; matrix products, arithmetic and copies ran while one was open for 33% of the time, Pallas kernels for 0%

commit v1 on v0

v1 whole, which is shorter than its diff:
```python
import functools

import jax
import jax.numpy as jnp
from jax import lax
from jax.experimental import pallas as pl
from jax.experimental.pallas import tpu as pltpu
from jax.sharding import PartitionSpec as P

HEADS = 12
EPSILON = 1e-05
MASKED = -1000000000.0
F32 = jnp.float32
BF16 = jnp.bfloat16
DT = 768
DL = 192
FT = 3072
FL = 768
LANES = 128
SLAB = 256
MIB = 1024 * 1024

VMEM = pl.BlockSpec(memory_space=pltpu.VMEM)
ANY = pl.BlockSpec(memory_space=pl.ANY)
SMEM = pl.BlockSpec(memory_space=pltpu.SMEM)


def dot(left, right):
    return jnp.dot(left, right, preferred_element_type=F32)


def dot_nt(left, right):
    return lax.dot_general(left, right, (((1,), (1,)), ((), ())), preferred_element_type=F32)


def shape_of(shape, dtype):
    return jax.ShapeDtypeStruct(shape, dtype)


def copies_of(pairs, sems, base):
    made = []
    for at, (source, target) in enumerate(pairs):
        copy = pltpu.make_async_copy(source, target, sems.at[base + at])
        copy.start()
        made.append(copy)
    return made


def wait_all(made):
    for copy in made:
        copy.wait()


def gather_pairs(blocks, rows, packs, target):
    span = rows * len(blocks)
    pairs = []
    for at, block in enumerate(blocks):
        for pack in range(packs):
            pairs.append(
                (
                    block.at[pl.ds(pack * rows, rows), :],
                    target.at[pl.ds(pack * span + at * rows, rows), :],
                )
            )
    return pairs


def lane_masks(pair_at):
    lanes = lax.broadcasted_iota(jnp.int32, (1, LANES), 1)
    low_half = lanes < 64
    group_of_16 = lax.shift_right_logical(lanes, 4)
    first = group_of_16 == 2 * lax.rem(pair_at, 4)
    second = group_of_16 == 2 * lax.rem(pair_at, 4) + 1
    return (low_half, first, second)


def stacked_heads(text_rows, layout_rows, masks):
    low_half, first, second = masks
    zero_text = jnp.zeros_like(text_rows)
    zero_layout = jnp.zeros_like(layout_rows)
    top = jnp.concatenate(
        [jnp.where(low_half, text_rows, zero_text), jnp.where(first, layout_rows, zero_layout)],
        axis=1,
    )
    bottom = jnp.concatenate(
        [jnp.where(low_half, zero_text, text_rows), jnp.where(second, layout_rows, zero_layout)],
        axis=1,
    )
    return jnp.concatenate([top, bottom], axis=0)


def normalized(values):
    centre = values - jnp.mean(values, axis=-1, keepdims=True)
    spread = jnp.mean(centre * centre, axis=-1, keepdims=True)
    inverse = lax.rsqrt(spread + EPSILON)
    return (centre * inverse, inverse)


def norm_back(delta, unit, inverse):
    return inverse * (
        delta
        - jnp.mean(delta, axis=-1, keepdims=True)
        - unit * jnp.mean(delta * unit, axis=-1, keepdims=True)
    )


def column_sum(values):
    return jnp.sum(values, axis=0, keepdims=True)


def feed_forward(hidden_low, expand, offsets, shrink, active, slope, chunk, branch_ref):
    width = expand.shape[1]
    for at in range(width // chunk):
        part = pl.ds(at * chunk, chunk)
        before = dot(hidden_low, expand[:, part]) + offsets[:, part].astype(F32)
        share = 0.5 + 0.5 * lax.erf(before * (0.5**0.5))
        density = jnp.exp(-0.5 * (before * before)) * 0.3989422804014327
        active_part = (before * share).astype(BF16)
        active[:, part] = active_part
        slope[:, part] = (share + before * density).astype(BF16)
        product = dot(active_part, shrink[part, :])
        if at == 0:
            branch_ref[...] = product
        else:
            branch_ref[...] += product


def forward_kernel(
    packs,
    rows,
    place,
    x0,
    x1,
    x2,
    x3,
    wt_in,
    wl_in,
    mt_in,
    et_in,
    st_in,
    ml,
    el,
    sl,
    cot_t,
    cot_l,
    bt,
    gt,
    ot,
    bl,
    gl,
    ol,
    res_t,
    res_l,
    q_t,
    q_l,
    kt_out,
    kl_out,
    vt_out,
    vl_out,
    p_out,
    ctx_t,
    ctx_l,
    hid_t,
    unit_t,
    inv_t,
    sum_t,
    slope_t,
    hid_l,
    unit_l,
    inv_l,
    sum_l,
    slope_l,
    act_l,
    sv_t,
    sv_l,
    g0,
    g1,
    g2,
    g3,
    xs,
    wt,
    wl,
    mt,
    et,
    st,
    k_t,
    k_l,
    v_t,
    v_l,
    prob,
    bias,
    act_t,
    turned,
    branch_t,
    branch_l,
    grads,
    sems,
):
    blocks = (x0, x1, x2, x3)
    keys = rows * len(blocks)
    tokens = packs * rows
    x_copies = copies_of(gather_pairs(blocks, rows, packs, xs), sems, 0)
    base = len(x_copies)
    w_copies = copies_of(((wt_in, wt), (wl_in, wl), (mt_in, mt), (et_in, et), (st_in, st)), sems, base)
    base += 5
    wait_all(x_copies)
    wait_all(w_copies[:2])

    text_bias = bt[...].astype(F32)
    layout_bias = bl[...].astype(F32)
    for pack in range(packs):
        own = pl.ds(pack * keys, rows)
        mine = pl.ds(pack * rows, rows)
        q_t[mine, :] = (dot(xs[own, :DT], wt[:, :DT]) + text_bias[0:1, :]).astype(BF16) * 0.125
        q_l[mine, :] = (dot(xs[own, DT:], wl[:, :SLAB]) + layout_bias[0:1, :]).astype(BF16) * 0.25

    step = 256

    def key_rows(at, unused):
        span = pl.ds(pl.multiple_of(at * step, step), step)
        k_t[span, :] = dot(xs[span, :DT], wt[:, DT : 2 * DT]).astype(BF16)
        v_t[span, :] = (dot(xs[span, :DT], wt[:, 2 * DT :]) + text_bias[1:2, :]).astype(BF16)
        k_l[span, :] = dot(xs[span, DT:], wl[:, SLAB : 2 * SLAB]).astype(BF16)
        v_l[span, :] = (dot(xs[span, DT:], wl[:, 2 * SLAB :]) + layout_bias[1:2, :]).astype(BF16)
        return unused

    lax.fori_loop(0, packs * keys // step, key_rows, 0)
    kv_copies = copies_of(((k_t, kt_out), (k_l, kl_out), (v_t, vt_out), (v_l, vl_out)), sems, base)
    base += 4

    marks = lax.broadcasted_iota(jnp.int32, (1, LANES), 1) - 64
    for pack in range(packs):
        slab = xs[pl.ds(pack * keys, keys), DT + LANES : DT + 2 * LANES].astype(F32)
        hot = jnp.where((slab == marks.astype(F32)) & (marks >= 0), 1.0, 0.0).astype(BF16)
        same = dot_nt(hot[:rows], hot)
        bias[pack] = jnp.where(same > 0.5, 0.0, MASKED)

    ctx_l[...] = jnp.zeros_like(ctx_l)

    def head_pair(pair_at, unused):
        masks = lane_masks(pair_at)
        text_lanes = pl.ds(pl.multiple_of(pair_at * LANES, LANES), LANES)
        layout_lanes = pl.ds(pl.multiple_of(pair_at // 4 * LANES, LANES), LANES)
        for pack in range(packs):
            mine = pl.ds(pack * rows, rows)
            span = pl.ds(pack * keys, keys)
            queries = stacked_heads(q_t[mine, text_lanes], q_l[mine, layout_lanes], masks)
            both_keys = jnp.concatenate([k_t[span, text_lanes], k_l[span, layout_lanes]], axis=1)
            both_values = jnp.concatenate([v_t[span, text_lanes], v_l[span, layout_lanes]], axis=1)
            allowed = bias[pack]
            logit = dot_nt(queries, both_keys) + jnp.concatenate([allowed, allowed], axis=0)
            raised = jnp.exp(logit - jnp.max(logit, axis=1, keepdims=True))
            low = (raised * (1.0 / jnp.sum(raised, axis=1, keepdims=True))).astype(BF16)
            prob[pair_at, pack] = low
            mixed = dot(low, both_values).astype(BF16)
            ctx_t[mine, text_lanes] = jnp.where(masks[0], mixed[:rows, :LANES], mixed[rows:, :LANES])
            kept = ctx_l[mine, layout_lanes]
            kept = jnp.where(masks[1], mixed[:rows, LANES:], kept)
            ctx_l[mine, layout_lanes] = jnp.where(masks[2], mixed[rows:, LANES:], kept)
        return unused

    lax.fori_loop(0, HEADS // 2, head_pair, 0)
    p_copies = copies_of(((prob, p_out),), sems, base)
    base += 1

    wait_all(w_copies[2:])

    def own_rows(lanes):
        return jnp.concatenate(
            [xs[pl.ds(pack * keys, rows), lanes].astype(F32) for pack in range(packs)], axis=0
        )

    def tail(x, ctx, merge, expand, offsets, shrink, b, g, cot, active, slope, branch, chunk, out, hid, unit, inv, delta, sv):
        width = merge.shape[1]
        middle = x + dot(ctx, merge[...]) + b[2:3, :width]
        unit_first, inverse_first = normalized(middle)
        hidden = unit_first * g[0:1, :] + b[3:4, :width]
        hidden_low = hidden.astype(BF16)
        hid[...] = hidden_low
        unit[...] = unit_first
        inv[...] = inverse_first
        feed_forward(hidden_low, expand, offsets, shrink, active, slope, chunk, branch)
        unit_second, inverse_second = normalized(hidden + branch[...] + b[4:5, :width])
        out[...] = (unit_second * g[1:2, :] + b[5:6, :width]).astype(BF16)
        cotangent = cot[...].astype(F32)
        sv[1:2, :] = column_sum(cotangent)
        sv[2:3, :] = column_sum(cotangent * unit_second)
        sum_delta = norm_back(cotangent * g[1:2, :], unit_second, inverse_second)
        delta[...] = sum_delta
        rounded = sum_delta.astype(BF16).astype(F32)
        sv[0:1, :] = column_sum(rounded)
        return rounded

    rounded = tail(
        own_rows(slice(0, DT)), ctx_t[...], mt, et, ot, st, text_bias, gt[...].astype(F32),
        cot_t, act_t, slope_t, branch_t, 512, res_t, hid_t, unit_t, inv_t, sum_t, sv_t,
    )
    turned[...] = rounded.T.astype(BF16)
    s = place[0]
    out_copies = []
    share = DT // 4
    for at, target in ((3, g3), (1, g1), (2, g2), (0, g0)):
        mark = pl.multiple_of(jnp.bitwise_xor(s, at) * share, share)
        own = turned[pl.ds(mark, share), :]
        for block in range(FT // DT):
            grads[at, pl.ds(block * share, share), :] = dot(
                own, act_t[:, block * DT : (block + 1) * DT]
            ).astype(BF16)
        out_copies += copies_of(((grads.at[at], target),), sems, base)
        base += 1
    tail(
        own_rows(slice(DT, DT + DL)), ctx_l[...], ml, el, ol, sl, layout_bias, gl[...].astype(F32),
        cot_l, act_l, slope_l, branch_l, 256, res_l, hid_l, unit_l, inv_l, sum_l, sv_l,
    )
    wait_all(kv_copies)
    wait_all(p_copies)
    wait_all(out_copies)


def forward_call(place, blocks, wt, wl, mt, et, st, ml, el, sl, cot_t, cot_l, bt, gt, ot, bl, gl, ol, packs, rows):
    tokens = packs * rows
    every = tokens * len(blocks)
    keys = rows * len(blocks)
    pairs = HEADS // 2
    outs = (
        shape_of((tokens, DT), BF16),
        shape_of((tokens, DL), BF16),
        shape_of((tokens, DT), BF16),
        shape_of((tokens, SLAB), BF16),
        shape_of((every, DT), BF16),
        shape_of((every, SLAB), BF16),
        shape_of((every, DT), BF16),
        shape_of((every, SLAB), BF16),
        shape_of((pairs, packs, 2 * rows, keys), BF16),
        shape_of((tokens, DT), BF16),
        shape_of((tokens, SLAB), BF16),
        shape_of((tokens, DT), BF16),
        shape_of((tokens, DT), F32),
        shape_of((tokens, 1), F32),
        shape_of((tokens, DT), F32),
        shape_of((tokens, FT), BF16),
        shape_of((tokens, DL), BF16),
        shape_of((tokens, DL), F32),
        shape_of((tokens, 1), F32),
        shape_of((tokens, DL), F32),
        shape_of((tokens, FL), BF16),
        shape_of((tokens, FL), BF16),
        shape_of((8, DT), F32),
        shape_of((8, DL), F32),
    ) + (shape_of((DT, DT), BF16),) * 4
    out_specs = [VMEM] * 4 + [ANY] * 5 + [VMEM] * 15 + [ANY] * 4
    scratch = [
        pltpu.VMEM((every, DT + SLAB), BF16),
        pltpu.VMEM(wt.shape, BF16),
        pltpu.VMEM(wl.shape, BF16),
        pltpu.VMEM(mt.shape, BF16),
        pltpu.VMEM(et.shape, BF16),
        pltpu.VMEM(st.shape, BF16),
        pltpu.VMEM((every, DT), BF16),
        pltpu.VMEM((every, SLAB), BF16),
        pltpu.VMEM((every, DT), BF16),
        pltpu.VMEM((every, SLAB), BF16),
        pltpu.VMEM((pairs, packs, 2 * rows, keys), BF16),
        pltpu.VMEM((packs, rows, keys), F32),
        pltpu.VMEM((tokens, FT), BF16),
        pltpu.VMEM((DT, tokens), BF16),
        pltpu.VMEM((tokens, DT), F32),
        pltpu.VMEM((tokens, DL), F32),
        pltpu.VMEM((4, DT, DT), BF16),
        pltpu.SemaphoreType.DMA((32,)),
    ]
    return pl.pallas_call(
        functools.partial(forward_kernel, packs, rows),
        out_shape=outs,
        in_specs=[SMEM] + [ANY] * 9 + [VMEM] * 11,
        out_specs=out_specs,
        scratch_shapes=scratch,
        compiler_params=pltpu.CompilerParams(vmem_limit_bytes=56 * MIB),
        name="forward",
    )(place, *blocks, wt, wl, mt, et, st, ml, el, sl, cot_t, cot_l, bt, gt, ot, bl, gl, ol)


E_ROWS = 896
P_ROWS = 896


def middle_kernel(
    place,
    hid_t,
    unit_t,
    inv_t,
    sum_t,
    slope_t,
    hid_l,
    unit_l,
    inv_l,
    sum_l,
    slope_l,
    act_l,
    st_in,
    et_in,
    mt_in,
    sl,
    el,
    ml,
    gt,
    gl,
    g0,
    g1,
    g2,
    g3,
    mid_t,
    mid_l,
    ad_t,
    ad_l,
    dctx_t,
    dctx_l,
    sv_t,
    sv_l,
    so_t,
    so_l,
    st,
    et,
    mt,
    before_t,
    before_l,
    hidden_t,
    hidden_l,
    turned,
    grads,
    sems,
):
    w_copies = copies_of(((st_in, st), (et_in, et), (mt_in, mt)), sems, 0)
    base = 3

    def feed_back(branch_delta, shrink, expand, slope, before, so, hidden_delta, chunk):
        width = slope.shape[1]
        for at in range(width // chunk):
            part = pl.ds(at * chunk, chunk)
            active_delta = dot_nt(branch_delta, shrink[part, :])
            low = (active_delta * slope[:, part].astype(F32)).astype(BF16)
            before[:, part] = low
            so[:, part] = column_sum(low.astype(F32))
            product = dot_nt(low, expand[:, part])
            if at == 0:
                hidden_delta[...] = product
            else:
                hidden_delta[...] += product

    def front(hidden_delta, total, unit, inv, g, merge, mid, ad, dctx, sv):
        delta = total[...] + hidden_delta[...]
        sv[0:1, :] = column_sum(delta * unit[...])
        sv[1:2, :] = column_sum(delta)
        middle = norm_back(delta * g, unit[...], inv[...])
        mid[...] = middle
        low = middle.astype(BF16)
        rounded = low.astype(F32)
        sv[2:3, :] = column_sum(rounded)
        ad[...] = rounded.T.astype(BF16)
        back = dot_nt(low, merge[...]).astype(BF16)
        dctx[...] = back
        sv[3:4, :] = column_sum(back.astype(F32)[:, : sv.shape[1]])

    s = place[0]
    text_delta = sum_t[...].astype(BF16)
    layout_delta = sum_l[...].astype(BF16)
    feed_back(layout_delta, sl, el, slope_l, before_l, so_l, hidden_l, 256)
    turned_l = before_l[...].astype(F32).T.astype(BF16)
    grown_l = dot(turned_l, hid_l[...]).astype(BF16)
    shrunk_l = dot(layout_delta.astype(F32).T.astype(BF16), act_l[...]).astype(BF16)
    for shard in range(4):
        for at in range(3):
            grads[shard, pl.ds(DT + 0, 64), pl.ds(at * SLAB, DL)] = grown_l[
                shard * DL + at * 64 : shard * DL + at * 64 + 64, :
            ]
        grads[shard, pl.ds(DT + 64, 48), :] = shrunk_l[shard * 48 : shard * 48 + 48, :]
    front(hidden_l, sum_l, unit_l, inv_l, gl[0:1, :].astype(F32), ml, mid_l, ad_l, dctx_l, sv_l)
    turned[...] = hid_t[...].astype(F32).T.astype(BF16)
    wait_all(w_copies)
    feed_back(text_delta, st, et, slope_t, before_t, so_t, hidden_t, 512)
    for shard in range(4):
        grads[shard, pl.ds(0, DT), :] = dot(
            turned[...], before_t[:, shard * DT : (shard + 1) * DT]
        ).astype(BF16)
    out_copies = copies_of(
        tuple(
            (grads.at[jnp.bitwise_xor(s, at)], target)
            for at, target in ((3, g3), (1, g1), (2, g2), (0, g0))
        ),
        sems,
        base,
    )
    front(hidden_t, sum_t, unit_t, inv_t, gt[0:1, :].astype(F32), mt, mid_t, ad_t, dctx_t, sv_t)
    wait_all(out_copies)


def middle_call(place, hid_t, unit_t, inv_t, sum_t, slope_t, hid_l, unit_l, inv_l, sum_l, slope_l, act_l, st, et, mt, sl, el, ml, gt, gl):
    tokens = hid_t.shape[0]
    outs = (shape_of((E_ROWS, DT), BF16),) * 4 + (
        shape_of((tokens, DT), F32),
        shape_of((tokens, DL), F32),
        shape_of((DT, tokens), BF16),
        shape_of((DL, tokens), BF16),
        shape_of((tokens, DT), BF16),
        shape_of((tokens, SLAB), BF16),
        shape_of((8, DT), F32),
        shape_of((8, DL), F32),
        shape_of((1, FT), F32),
        shape_of((1, FL), F32),
    )
    scratch = [
        pltpu.VMEM(st.shape, BF16),
        pltpu.VMEM(et.shape, BF16),
        pltpu.VMEM(mt.shape, BF16),
        pltpu.VMEM((tokens, FT), BF16),
        pltpu.VMEM((tokens, FL), BF16),
        pltpu.VMEM((tokens, DT), F32),
        pltpu.VMEM((tokens, DL), F32),
        pltpu.VMEM((DT, tokens), BF16),
        pltpu.VMEM((4, E_ROWS, DT), BF16),
        pltpu.SemaphoreType.DMA((8,)),
    ]
    return pl.pallas_call(
        middle_kernel,
        out_shape=outs,
        in_specs=[SMEM] + [VMEM] * 11 + [ANY] * 3 + [VMEM] * 5,
        out_specs=[ANY] * 4 + [VMEM] * 10,
        scratch_shapes=scratch,
        compiler_params=pltpu.CompilerParams(vmem_limit_bytes=48 * MIB),
        name="middle",
    )(place, hid_t, unit_t, inv_t, sum_t, slope_t, hid_l, unit_l, inv_l, sum_l, slope_l, act_l, st, et, mt, sl, el, ml, gt, gl)


def attention_kernel(
    packs,
    rows,
    place,
    x0,
    x1,
    x2,
    x3,
    kt_in,
    kl_in,
    vt_in,
    vl_in,
    p_in,
    q_t,
    q_l,
    dctx_t,
    dctx_l,
    ctx_t,
    ctx_l,
    ad_t,
    ad_l,
    sf_t,
    sf_l,
    sm_t,
    sm_l,
    so_t,
    so_l,
    g0,
    g1,
    g2,
    g3,
    joined_t,
    joined_l,
    query_t,
    query_l,
    xs,
    k_t,
    k_l,
    v_t,
    v_l,
    prob,
    dq_t,
    dq_l,
    dk_l,
    dv_l,
    text_grads,
    merge_grads,
    layout_grads,
    layout_merge,
    smalls,
    sems,
):
    blocks = (x0, x1, x2, x3)
    keys = rows * len(blocks)
    kv_copies = copies_of(((kt_in, k_t), (kl_in, k_l), (vt_in, v_t), (vl_in, v_l), (p_in, prob)), sems, 0)
    x_copies = copies_of(gather_pairs(blocks, rows, packs, xs), sems, 5)
    base = 5 + len(x_copies)
    dq_l[...] = jnp.zeros_like(dq_l)
    dk_l[...] = jnp.zeros_like(dk_l)
    dv_l[...] = jnp.zeros_like(dv_l)
    merge_grads[...] = dot(ad_t[...], ctx_t[...]).astype(BF16)
    layout_merge[...] = dot(ad_l[...], ctx_l[...]).astype(BF16)
    wait_all(kv_copies)

    def head_pair(pair_at, unused):
        masks = lane_masks(pair_at)
        text_lanes = pl.ds(pl.multiple_of(pair_at * LANES, LANES), LANES)
        layout_lanes = pl.ds(pl.multiple_of(pair_at // 4 * LANES, LANES), LANES)
        for pack in range(packs):
            mine = pl.ds(pack * rows, rows)
            span = pl.ds(pack * keys, keys)
            queries = stacked_heads(q_t[mine, text_lanes], q_l[mine, layout_lanes], masks)
            deltas = stacked_heads(dctx_t[mine, text_lanes], dctx_l[mine, layout_lanes], masks)
            one = jnp.concatenate([ctx_t[mine, text_lanes], ctx_l[mine, layout_lanes]], axis=1)
            contexts = jnp.concatenate([one, one], axis=0).astype(F32)
            products = deltas.astype(F32) * contexts
            layout_mean = jnp.sum(products[:, LANES:], axis=1, keepdims=True)
            both_mean = jnp.sum(products, axis=1, keepdims=True)
            text_values = v_t[span, text_lanes]
            layout_values = v_l[span, layout_lanes]
            both_values = jnp.concatenate([text_values, layout_values], axis=1)
            low = prob[pair_at, pack]
            chance = low.astype(F32)
            both_change = (chance * (dot_nt(deltas, both_values) - both_mean)).astype(BF16)
            layout_change = (
                chance * (dot_nt(deltas[:, LANES:], layout_values) - layout_mean)
            ).astype(BF16)
            from_text = dot(both_change, k_t[span, text_lanes])
            dq_t[mine, text_lanes] = (
                jnp.where(masks[0], from_text[:rows], from_text[rows:]) * 0.125
            ).astype(BF16)
            from_layout = dot(layout_change, k_l[span, layout_lanes]) * 0.25
            kept = dq_l[mine, layout_lanes]
            kept = jnp.where(masks[1], from_layout[:rows], kept)
            dq_l[mine, layout_lanes] = jnp.where(masks[2], from_layout[rows:], kept)
            turned_queries = queries.T
            turned_deltas = deltas.T
            joined_t[text_lanes, span] = dot(turned_queries[:LANES], both_change).astype(BF16)
            dk_l[layout_lanes, span] += dot(turned_queries[LANES:], layout_change)
            value_change = dot(turned_deltas, low)
            text_at = pl.ds(pl.multiple_of(pair_at * LANES + DT, LANES), LANES)
            joined_t[text_at, span] = value_change[:LANES].astype(BF16)
            dv_l[layout_lanes, span] += value_change[LANES:]
        return unused

    lax.fori_loop(0, HEADS // 2, head_pair, 0)
    joined_l[:SLAB, :] = dk_l[...].astype(BF16)
    joined_l[SLAB:, :] = dv_l[...].astype(BF16)
    whole_t = dq_t[...].astype(F32)
    whole_l = dq_l[...]
    low_l = whole_l.astype(BF16)
    query_t[...] = whole_t.T.astype(BF16)
    query_l[...] = whole_l.T.astype(BF16)
    wait_all(x_copies)
    own = jnp.concatenate([xs[pl.ds(pack * keys, rows), :] for pack in range(packs)], axis=0)
    text_grads[:DT, :] = dot(query_t[...], own[:, :DT]).astype(BF16)
    step = 256
    for at in range(2 * DT // step):
        text_grads[pl.ds(DT + at * step, step), :] = dot(
            joined_t[pl.ds(at * step, step), :], xs[:, :DT]
        ).astype(BF16)
    layout_grads[:DL, :] = dot(query_l[:DL, :], own[:, DT:]).astype(BF16)
    layout_grads[DL : 2 * DL, :] = dot(joined_l[:DL, :], xs[:, DT:]).astype(BF16)
    layout_grads[2 * DL :, :] = dot(joined_l[SLAB : SLAB + DL, :], xs[:, DT:]).astype(BF16)

    smalls[...] = jnp.zeros_like(smalls)
    text_lines = jnp.concatenate(
        [
            column_sum(whole_t),
            sm_t[3:4, :],
            sm_t[2:3, :],
            sm_t[1:2, :],
            sf_t[0:2, :],
            sm_t[0:1, :],
            sf_t[2:3, :],
            so_t[:, :DT],
            so_t[:, DT : 2 * DT],
            so_t[:, 2 * DT : 3 * DT],
            so_t[:, 3 * DT :],
            so_l[...],
            jnp.zeros((3, DT), F32),
        ],
        axis=0,
    )
    smalls[:16, :] = text_lines.astype(BF16)
    layout_lines = jnp.concatenate(
        [
            column_sum(low_l.astype(F32))[:, :DL],
            sm_l[3:4, :],
            sm_l[2:3, :],
            sm_l[1:2, :],
            sf_l[0:2, :],
            sm_l[0:1, :],
            sf_l[2:3, :],
            jnp.zeros((8, DL), F32),
        ],
        axis=0,
    )
    smalls[16:32, :DL] = layout_lines.astype(BF16)

    s = place[0]
    out_copies = []
    for at, target in ((3, g3), (1, g1), (2, g2), (0, g0)):
        shard = jnp.bitwise_xor(s, at)

        pairs = [
            (text_grads.at[pl.ds(pl.multiple_of(shard * 576, 64), 576), :], target.at[pl.ds(0, 576), :]),
            (merge_grads.at[pl.ds(pl.multiple_of(shard * 192, 64), 192), :], target.at[pl.ds(576, 192), :]),
            (smalls, target.at[pl.ds(832, 32), :]),
        ]
        for piece in range(3):
            lanes = pl.ds(piece * SLAB, SLAB)
            pairs.append(
                (
                    layout_grads.at[pl.ds(pl.multiple_of(shard * 144 + piece * 48, 16), 48), :],
                    target.at[pl.ds(768, 48), lanes],
                )
            )
            pairs.append(
                (
                    layout_merge.at[pl.ds(pl.multiple_of(shard * 48 + piece * 16, 16), 16), :],
                    target.at[pl.ds(816, 16), lanes],
                )
            )
        pairs.append((smalls, target.at[pl.ds(864, 32), :]))
        out_copies += copies_of(pairs, sems, base)
        base += len(pairs)
    wait_all(out_copies)


def attention_call(place, blocks, kt, kl, vt, vl, p, q_t, q_l, dctx_t, dctx_l, ctx_t, ctx_l, ad_t, ad_l, sf_t, sf_l, sm_t, sm_l, so_t, so_l, packs, rows):
    tokens = packs * rows
    every = tokens * len(blocks)
    outs = (shape_of((P_ROWS, DT), BF16),) * 4 + (
        shape_of((2 * DT, every), BF16),
        shape_of((2 * SLAB, every), BF16),
        shape_of((DT, tokens), BF16),
        shape_of((SLAB, tokens), BF16),
    )
    scratch = [
        pltpu.VMEM((every, DT + SLAB), BF16),
        pltpu.VMEM(kt.shape, BF16),
        pltpu.VMEM(kl.shape, BF16),
        pltpu.VMEM(vt.shape, BF16),
        pltpu.VMEM(vl.shape, BF16),
        pltpu.VMEM(p.shape, BF16),
        pltpu.VMEM((tokens, DT), BF16),
        pltpu.VMEM((tokens, SLAB), F32),
        pltpu.VMEM((SLAB, every), F32),
        pltpu.VMEM((SLAB, every), F32),
        pltpu.VMEM((3 * DT, DT), BF16),
        pltpu.VMEM((DT, DT), BF16),
        pltpu.VMEM((3 * DL, SLAB), BF16),
        pltpu.VMEM((DL, SLAB), BF16),
        pltpu.VMEM((32, DT), BF16),
        pltpu.SemaphoreType.DMA((64,)),
    ]
    return pl.pallas_call(
        functools.partial(attention_kernel, packs, rows),
        out_shape=outs,
        in_specs=[SMEM] + [ANY] * 9 + [VMEM] * 14,
        out_specs=[ANY] * 4 + [VMEM] * 4,
        scratch_shapes=scratch,
        compiler_params=pltpu.CompilerParams(vmem_limit_bytes=48 * MIB),
        name="attention_back",
    )(place, *blocks, kt, kl, vt, vl, p, q_t, q_l, dctx_t, dctx_l, ctx_t, ctx_l, ad_t, ad_l, sf_t, sf_l, sm_t, sm_l, so_t, so_l)


def input_kernel(packs, rows, joined_t, joined_l, query_t, query_l, wt, wl, g0, g1, g2, g3):
    keys = joined_t.shape[1] // packs
    for at, target in ((3, g3), (1, g1), (2, g2), (0, g0)):
        spans = [slice(pack * keys + at * rows, pack * keys + (at + 1) * rows) for pack in range(packs)]
        text_part = jnp.concatenate([joined_t[:, span] for span in spans], axis=1)
        layout_part = jnp.concatenate([joined_l[:, span] for span in spans], axis=1)
        text_sum = dot(wt[:, DT:], text_part)
        layout_sum = dot(wl[:DL, SLAB:], layout_part)
        if at == 0:
            text_sum += dot(wt[:, :DT], query_t[...])
            layout_sum += dot(wl[:DL, :SLAB], query_l[...])
        target[:DT, :] = text_sum.astype(target.dtype)
        target[DT:, :] = layout_sum.astype(target.dtype)


def input_call(joined_t, joined_l, query_t, query_l, wt, wl, packs, rows):
    tokens = packs * rows
    return pl.pallas_call(
        functools.partial(input_kernel, packs, rows),
        out_shape=(shape_of((DT + DL, tokens), F32),) + (shape_of((DT + DL, tokens), BF16),) * 3,
        in_specs=[VMEM] * 6,
        out_specs=[VMEM] * 4,
        compiler_params=pltpu.CompilerParams(vmem_limit_bytes=32 * MIB),
        name="input_back",
    )(joined_t, joined_l, query_t, query_l, wt, wl)


def sensitivity_kernel(own, near, far, mid_t, mid_l, out_t, out_l):
    total = own[...] + near[...].astype(F32) + far[...].astype(F32)
    out_t[...] = mid_t[...] + total[:DT, :].T
    out_l[...] = mid_l[...] + total[DT:, :].T


def sensitivity_call(own, near, far, mid_t, mid_l):
    return pl.pallas_call(
        sensitivity_kernel,
        out_shape=(shape_of(mid_t.shape, F32), shape_of(mid_l.shape, F32)),
        in_specs=[VMEM] * 5,
        out_specs=[VMEM] * 2,
        compiler_params=pltpu.CompilerParams(vmem_limit_bytes=16 * MIB),
        name="sensitivity",
    )(own, near, far, mid_t, mid_l)


def pieces_in_order(index, total, whole, pieces):
    size = total.shape[0] // pieces
    for at in range(pieces):
        mark = pl.multiple_of(jnp.bitwise_xor(index, at) * size, 16)
        whole[at * size : (at + 1) * size, :] = total[pl.ds(mark, size), :].astype(F32)


def shrink_kernel(pieces, index, total, out, whole):
    pieces_in_order(index[0], total, whole, pieces)
    share = DT // 4
    for block in range(FT // DT):
        out[block * DT : (block + 1) * DT, :] = whole[block * share : (block + 1) * share, :].T


def expand_kernel(pieces, index, total, out, out_grow, out_shrink, whole):
    pieces_in_order(index[0], total, whole, pieces)
    out[...] = whole[:DT, :]
    grown = jnp.concatenate(
        [whole[DT : DT + 64, at * SLAB : at * SLAB + DL] for at in range(3)], axis=0
    )
    out_grow[...] = grown.T
    out_shrink[...] = whole[DT + 64 : DT + 112, :].T


def project_kernel(pieces, index, total, out, out_merge, out_layout, out_layout_merge, out_small, whole):
    pieces_in_order(index[0], total, whole, pieces)
    out[...] = whole[:576, :].T
    out_merge[...] = whole[576:768, :].T
    layout = jnp.concatenate([whole[768:816, at * SLAB : at * SLAB + DL] for at in range(3)], axis=0)
    out_layout[...] = layout.T
    merge = jnp.concatenate([whole[816:832, at * SLAB : at * SLAB + DL] for at in range(3)], axis=0)
    out_layout_merge[...] = merge.T
    out_small[...] = whole[832:864, :]


def final_call(kernel, name, index, total, pieces, outs):
    return pl.pallas_call(
        functools.partial(kernel, pieces),
        out_shape=tuple(shape_of(shape, F32) for shape in outs),
        in_specs=[SMEM, VMEM],
        out_specs=[VMEM] * len(outs),
        scratch_shapes=[pltpu.VMEM(total.shape, F32)],
        compiler_params=pltpu.CompilerParams(vmem_limit_bytes=24 * MIB),
        name=name,
    )(index, total)


def partners(size, bit):
    return [(at, at ^ bit) for at in range(size)]


def low_sum(parts):
    total = parts[0].astype(F32)
    for part in parts[1:]:
        total = total + part.astype(F32)
    return total


def over_seq(shards, size):
    own, near, far, corner = shards
    from_corner = lax.ppermute(corner, "seq", partners(size, 1))
    from_near = lax.ppermute(near, "seq", partners(size, 1))
    onward = low_sum([far, from_corner]).astype(BF16)
    from_far = lax.ppermute(onward, "seq", partners(size, 2))
    return [own, from_near, from_far]


def padded_rows(shards, multiple):
    short = -shards[0].shape[0] % multiple
    if short:
        return [jnp.pad(shard, ((0, short), (0, 0))) for shard in shards]
    return list(shards)


def summed(shards, seq_size, dp_size, order):
    shards = padded_rows(shards, 16 * dp_size)
    parts = over_seq(shards, seq_size)
    device = lax.axis_index("dp")
    rows = shards[0].shape[0]
    index = 0
    for bit in order:
        mine = jnp.bitwise_and(device // bit, 1)
        half = rows // 2
        send = low_sum([lax.dynamic_slice_in_dim(part, (1 - mine) * half, half) for part in parts])
        keep = low_sum([lax.dynamic_slice_in_dim(part, mine * half, half) for part in parts])
        parts = [keep, lax.ppermute(send.astype(BF16), "dp", partners(dp_size, bit))]
        index = 2 * index + mine
        rows = half
    total = low_sum(parts).astype(BF16)
    for bit in reversed(order):
        total = jnp.concatenate([total, lax.ppermute(total, "dp", partners(dp_size, bit))], axis=0)
    return total, index.reshape(1).astype(jnp.int32)


def local(
    dp_size,
    seq_size,
    text_input,
    layout_input,
    segments,
    text_cotangent,
    layout_cotangent,
    text_project,
    text_biases,
    text_gains,
    text_merge,
    text_expand,
    text_offsets,
    text_shrink,
    layout_project,
    layout_biases,
    layout_gains,
    layout_merge,
    layout_expand,
    layout_offsets,
    layout_shrink,
):
    packs, rows, unused = text_input.shape
    tokens = packs * rows
    shard = lax.axis_index("seq")
    place = shard.reshape(1).astype(jnp.int32)
    marks = jnp.broadcast_to(segments.astype(BF16)[:, :, None], (packs, rows, SLAB - DL))
    own = jnp.concatenate([text_input, layout_input, marks], axis=2).reshape(tokens, DT + SLAB)
    far = lax.ppermute(own, "seq", partners(seq_size, 2))
    near = lax.ppermute(own, "seq", partners(seq_size, 1))
    corner = lax.ppermute(far, "seq", partners(seq_size, 1))
    blocks = (own, near, far, corner)

    pad = SLAB - DL
    wl = jnp.pad(layout_project.reshape(DL, 3, DL), ((0, pad), (0, 0), (0, pad))).reshape(SLAB, 3 * SLAB)
    bl = jnp.pad(layout_biases, ((0, 0), (0, pad)))
    ml = jnp.pad(layout_merge, ((0, pad), (0, 0)))
    (
        res_t, res_l, q_t, q_l, kt, kl, vt, vl, p, ctx_t, ctx_l,
        hid_t, unit_t, inv_t, sum_t, slope_t,
        hid_l, unit_l, inv_l, sum_l, slope_l, act_l, sf_t, sf_l,
        *shrink_parts,
    ) = forward_call(
        place, blocks, text_project, wl, text_merge, text_expand, text_shrink,
        ml, layout_expand, layout_shrink,
        text_cotangent.reshape(tokens, DT), layout_cotangent.reshape(tokens, DL),
        text_biases, text_gains, text_offsets.reshape(1, FT), bl, layout_gains, layout_offsets.reshape(1, FL),
        packs, rows,
    )
    order = [1 << at for at in range((dp_size - 1).bit_length())]
    shrink_total, shrink_index = summed(shrink_parts, seq_size, dp_size, order)
    *expand_parts, mid_t, mid_l, ad_t, ad_l, dctx_t, dctx_l, sm_t, sm_l, so_t, so_l = middle_call(
        place, hid_t, unit_t, inv_t, sum_t, slope_t, hid_l, unit_l, inv_l, sum_l, slope_l, act_l,
        text_shrink, text_expand, text_merge, layout_shrink, layout_expand, ml, text_gains, layout_gains,
    )
    expand_total, expand_index = summed(expand_parts, seq_size, dp_size, order)
    *project_parts, joined_t, joined_l, query_t, query_l = attention_call(
        place, blocks, kt, kl, vt, vl, p, q_t, q_l, dctx_t, dctx_l, ctx_t, ctx_l, ad_t, ad_l,
        sf_t, sf_l, sm_t, sm_l, so_t, so_l, packs, rows,
    )
    project_total, project_index = summed(project_parts, seq_size, dp_size, order)
    input_parts = input_call(joined_t, joined_l, query_t, query_l, text_project, wl, packs, rows)
    sens_t, sens_l = sensitivity_call(*over_seq(input_parts, seq_size), mid_t, mid_l)

    (shrink_t,) = final_call(shrink_kernel, "shrink_out", shrink_index, shrink_total, dp_size, [(FT, DT // 4)])
    expand_t, expand_l, shrink_l = final_call(
        expand_kernel, "expand_out", expand_index, expand_total, dp_size, [(DT, DT), (DL, DL), (FL, DL // 4)]
    )
    project_t, merge_t, project_l, merge_l, small = final_call(
        project_kernel, "project_out", project_index, project_total, dp_size,
        [(DT, 576), (DT, 192), (DL, 144), (DL, 48), (32, DT)],
    )
    text_small = lax.dynamic_slice_in_dim(small[:8], shard * (DT // 4), DT // 4, 1)
    layout_small = lax.dynamic_slice_in_dim(small[16:24, :DL], shard * (DL // 4), DL // 4, 1)
    offsets_t = lax.dynamic_slice_in_dim(small[8:12], shard, 1, 0).reshape(DT)
    offsets_l = lax.dynamic_slice_in_dim(small[12:13].reshape(FL), shard * (FL // 4), FL // 4, 0)
    return (
        res_t.reshape(packs, rows, DT),
        res_l.reshape(packs, rows, DL),
        sens_t.reshape(packs, rows, DT),
        sens_l.reshape(packs, rows, DL),
        project_t,
        text_small[:6],
        text_small[6:8],
        merge_t,
        expand_t,
        offsets_t,
        shrink_t,
        project_l,
        layout_small[:6],
        layout_small[6:8],
        merge_l,
        expand_l,
        offsets_l,
        shrink_l,
    )


def solution(mesh):
    rows = P("dp", "seq", None)
    columns = P(None, "seq")
    in_specs = (rows, rows, P("dp", "seq"), rows, rows) + (P(),) * 14
    out_specs = (
        (rows,) * 4 + (columns,) * 5 + (P("seq"),) + (columns,) * 6 + (P("seq"),) + (columns,)
    )
    body = functools.partial(local, mesh.shape["dp"], mesh.shape["seq"])
    return jax.shard_map(body, mesh=mesh, in_specs=in_specs, out_specs=out_specs, check_vma=False)
```

time: 780 us -> 318 us (0.41)
  waiting for transfers between devices: 384 us -> 149 us
  matrix products: 161 us -> 0 us
  local copies, waits for them, and re-layouts: 113 us -> 35.3 us
  blocking collectives: 66.6 us -> 0 us
  Pallas kernels: 0 us -> 64.3 us
  starting transfers between devices: 0.46 us -> 30.9 us
  between operations: 15.1 us -> 1.35 us
    psum x1 -> x0, waiting for transfers between devices: 383 us -> none  [local(): lax.psum((text_back[0], text_bias_total, text_tail[6], text_tail[4], layo...]
    dot_general x35 -> x0, matrix products: 151 us -> none  [the longest x2 27.4 us: input_change(): jnp.einsum('ghij,gjhe->gihe', score_delta, head_split(key_rows, HEADS), p...]
    ppermute x0 -> x33, waiting for transfers between devices: none -> 149 us  [the longest x4 78 us: over_seq(): from_far = lax.ppermute(onward, 'seq', partners(size, 2))]
    pallas_call x0 -> x8, Pallas kernels: none -> 64.3 us  [the longest x1 25.2 us: forward_call(): pl.pallas_call(functools.partial(forward_kernel, packs, rows), out_shape=...]
    psum x1 -> x0, blocking collectives: 44 us -> none  [local(): lax.psum((text_back[0], text_bias_total, text_tail[6], text_tail[4], layo...]
    ppermute x0 -> x33, starting transfers between devices: none -> 30.9 us  [the longest x9 10.6 us: summed(): lax.ppermute(send.astype(BF16), 'dp', partners(dp_size, bit))]
    dynamic_slice x14 -> x3, local copies, waits for them, and re-layouts: 25.8 us -> 1.32 us  [the longest x1 0.63 us: local(): lax.dynamic_slice_in_dim(small[12:13].reshape(FL), shard * (FL // 4), FL...]
    all_gather x3 -> x0, blocking collectives: 22.6 us -> none  [the longest x1 9.11 us: local(): lax.all_gather(layout_value, 'seq', axis=1, tiled=True)]
  transfers between devices with their start and end apart: 7 -> 33, of which waited for: 1 -> 16; matrix products, arithmetic and copies ran while one was open for 33% -> 13% of each run, Pallas kernels for 0% -> 2%
where the time goes in v1:
time: 318 us; the launch traced here: 317 us
  waiting for transfers between devices  149 us (47%)
  Pallas kernels  64.3 us (20%)
  other arithmetic  35.7 us (11%)
  local copies, waits for them, and re-layouts  35.3 us (11%)
  starting transfers between devices  30.9 us (10%)
    ppermute x4, waiting for transfers between devices, over_seq(): from_far = lax.ppermute(onward, 'seq', partners(size, 2))  78 us
    ppermute x9, waiting for transfers between devices, summed(): lax.ppermute(total, 'dp', partners(dp_size, bit))  43.6 us
    unnamed x160, local copies, waits for them, and re-layouts  28.5 us
    pallas_call x1, Pallas kernels, forward_call(): pl.pallas_call(functools.partial(forward_kernel, packs, rows), out_shape=...  25.2 us
    convert_element_type x9, other arithmetic, summed(): send.astype(BF16)  18.5 us
    pallas_call x1, Pallas kernels, attention_call(): pl.pallas_call(functools.partial(attention_kernel, packs, rows), out_shap...  17.5 us
    pallas_call x1, Pallas kernels, middle_call(): pl.pallas_call(middle_kernel, out_shape=outs, in_specs=[SMEM] + [VMEM] *...  14 us
    ppermute x9, waiting for transfers between devices, summed(): lax.ppermute(send.astype(BF16), 'dp', partners(dp_size, bit))  12.1 us
  transfers between devices with their start and end apart: 33, of which 16 were waited for; matrix products, arithmetic and copies ran while one was open for 13% of the time, Pallas kernels for 2%

profile of v1, /device:TPU:0, one launch (start us, length us, event | category | flops | bytes accessed | tf_op | source)
XLA Modules:
  0.0 316.9 jit_solution(13130478702057476199)
XLA Ops:
  0.7 1.0 copy.49
  2.5 1.1 pad_maximum_fusion.6
  3.7 3.0 collective-permute-start.1
  6.7 11.9 %collective-permute-done.1.x2 = bf16[256,1024]{1,0:T(8,128)(2,1)S(1)} collective-permute-done((bf16[256,1024]{1,0:T(8,128)(2,1)S(1)}, bf16[256,1024]{1,0:T(8,128)(2,1)S(1)}, u32[]{:S(2)}, u32[]{:S(2)}) %collective-permute-start.1) | collective-permute-done | bytes 524320 | tf_op jit(solution)/shard_map/ppermute | solution.py:929
  25.1 25.2 %forward.1 = (bf16[256,768]{1,0:T(8,128)(2,1)}, bf16[256,192]{1,0:T(8,128)(2,1)}, bf16[256,768]{1,0:T(8,128)(2,1)}, bf16[256,256]{1,0:T(8,128)(2,1)}, bf16[1024,...) custom-call(s32[1]{0:T(128)} %bitcast.place, ...), custom_call_target="tpu_custom_call" | custom-call | tf_op jit(solution)/shard_map/forward/pallas_call | solution.py:372
  50.3 1.1 copy-done.17
  51.4 1.0 copy-done.26
  52.4 1.0 copy-done.27
  53.4 1.0 copy-done.28
  59.1 14.0 %middle.1 = (bf16[896,768]{1,0:T(8,128)(2,1)}, bf16[896,768]{1,0:T(8,128)(2,1)}, bf16[896,768]{1,0:T(8,128)(2,1)}, bf16[896,768]{1,0:T(8,128)(2,1)}, f32[256,768...) custom-call(s32[1]{0:T(128)} %bitcast.place, ...), custom_call_target="tpu_custom_call" | custom-call | tf_op jit(solution)/shard_map/middle/pallas_call | solution.py:523
  74.1 17.5 %attention_back.1 = (bf16[896,768]{1,0:T(8,128)(2,1)}, bf16[896,768]{1,0:T(8,128)(2,1)}, bf16[896,768]{1,0:T(8,128)(2,1)}, bf16[896,768]{1,0:T(8,128)(2,1)}, bf1...) custom-call(s32[1]{0:T(128)} %bitcast.place, ...), custom_call_target="tpu_custom_call" | custom-call | tf_op jit(solution)/shard_map/attention_back/pallas_call | solution.py:751
  93.2 1.9 collective-permute-done.7
  95.5 2.8 add_convert_fusion.1
  98.4 1.8 collective-permute-done.25
  100.2 1.8 collective-permute-start.8
  102.0 1.3 add_convert_fusion.2
  103.6 1.5 add_convert_fusion
  105.1 1.7 collective-permute-start.17
  106.8 52.0 %collective-permute-done.26 = bf16[768,768]{1,0:T(8,128)(2,1)} collective-permute-done((bf16[768,768]{1,0:T(8,128)(2,1)}, bf16[768,768]{1,0:T(8,128)(2,1)}, u32[]{:S(2)}, u32[]{:S(2)}) %collective-permute-start.26) | collective-permute-done | bytes 1179680 | tf_op jit(solution)/shard_map/ppermute | solution.py:869
  158.8 3.5 %add_convert_fusion.5 = (bf16[384,768]{1,0:T(8,128)(2,1)S(1)}, f32[384,768]{1,0:T(8,128)}) fusion(bf16[768,768]{1,0:T(8,128)(2,1)} %collective-permute-done.26, s32[]{:T(128)S(6)} %select_n.103, bf16[768,768]{1,0:T(8,128)(2,1)} %collective-permute-done.24, bf16[768,768]{1,0:T(8,128)(2,1)} %get-tuple-element.138, s32[]{:T(128)S(6)} %select_n.101), kind=kLoop, calls=%fused_computation.10 | loop fusion | flops 3244032 | bytes 5308424 | tf_op jit(solution)/shard_map/convert_element_type | solution.py:891
  162.3 1.7 collective-permute-start.27
  164.1 3.2 %add_convert_fusion.4 = (bf16[448,768]{1,0:T(8,128)(2,1)}, f32[448,768]{1,0:T(8,128)}) fusion(bf16[896,768]{1,0:T(8,128)(2,1)} %collective-permute-done.8, s32[]{:T(128)S(6)} %select_n.95, bf16[896,768]{1,0:T(8,128)(2,1)S(1)} %collective-permute-done.6, bf16[896,768]{1,0:T(8,128)(2,1)S(1)} %copy-done.55, s32[]{:T(128)S(6)} %select_n.47), kind=kLoop, calls=%fused_computation.7 | loop fusion | flops 3784704 | bytes 6193160 | tf_op jit(solution)/shard_map/convert_element_type | solution.py:891
  167.6 20.2 %collective-permute-done.17 = bf16[896,768]{1,0:T(8,128)(2,1)} collective-permute-done((bf16[896,768]{1,0:T(8,128)(2,1)}, bf16[896,768]{1,0:T(8,128)(2,1)}, u32[]{:S(2)}, u32[]{:S(2)}) %collective-permute-start.17) | collective-permute-done | bytes 1376288 | tf_op jit(solution)/shard_map/ppermute | solution.py:869
  187.8 3.1 add_convert_fusion.3
  190.9 1.7 collective-permute-start.18
  192.6 2.6 add_convert_fusion.9
  195.2 1.6 collective-permute-start.28
  196.8 2.6 add_convert_fusion.8
  199.8 1.0 copy-done.3
  200.8 1.9 copy-done.5
  202.7 1.2 copy-done.14
  204.0 1.0 copy-done.23
  205.9 3.8 %input_back.1 = (f32[960,256]{1,0:T(8,128)S(1)}, bf16[960,256]{1,0:T(8,128)(2,1)}, bf16[960,256]{1,0:T(8,128)(2,1)S(1)}, bf16[960,256]{1,0:T(8,128)(2,1)S(1)}) custom-call(bf16[1536,1024]{1,0:T(8,128)(2,1)S(1)} %copy-done.5, bf16[512,1024]{1,0:T(8,128)(2,1)S(1)} %copy-done.14, bf16[768,256]{1,0:T(8,128)(2,1)S(1)} %copy-done.23, ...), custom_call_target="tpu_custom_call" | custom-call | tf_op jit(solution)/shard_map/input_back/pallas_call | solution.py:779
  209.7 1.1 add_convert_fusion.15
  210.8 2.7 collective-permute-start.29
  213.5 1.3 add_convert_fusion.7
  214.8 1.6 collective-permute-start.19
  216.4 0.9 add_convert_fusion.13
  217.8 3.6 %collective-permute-done.29 = bf16[96,768]{1,0:T(8,128)(2,1)S(1)} collective-permute-done((bf16[96,768]{1,0:T(8,128)(2,1)S(1)}, bf16[96,768]{1,0:T(8,128)(2,1)S(1)}, u32[]{:S(2)}, u32[]{:S(2)}) %collective-permute-start.29) | collective-permute-done | bytes 147488 | tf_op jit(solution)/shard_map/ppermute | solution.py:891
  221.4 1.0 add_convert_fusion.14
  222.4 6.3 %collective-permute-done.11 = bf16[112,768]{1,0:T(8,128)(2,1)S(1)} collective-permute-done((bf16[112,768]{1,0:T(8,128)(2,1)S(1)}, bf16[112,768]{1,0:T(8,128)(2,1)S(1)}, u32[]{:S(2)}, u32[]{:S(2)}) %collective-permute-start.11) | collective-permute-done | bytes 172064 | tf_op jit(solution)/shard_map/ppermute | solution.py:891
  228.7 1.0 add_convert_fusion.12
  229.7 3.5 %collective-permute-start.12 = (bf16[112,768]{1,0:T(8,128)(2,1)S(1)}, bf16[112,768]{1,0:T(8,128)(2,1)S(1)}, u32[]{:S(2)}, u32[]{:S(2)}) collective-permute-start(bf16[112,768]{1,0:T(8,128)(2,1)S(1)} %add_convert_fusion.12), channel_id=1, source_target_pairs={{0,16},{4,20},{8,24},{12,28},{16,0},{20,4},{24,8},{28,12},{1,17},{... | collective-permute-start | bytes 516104 | tf_op jit(solution)/shard_map/ppermute | solution.py:896
  233.3 10.4 %collective-permute-done.30 = bf16[96,768]{1,0:T(8,128)(2,1)S(1)} collective-permute-done((bf16[96,768]{1,0:T(8,128)(2,1)S(1)}, bf16[96,768]{1,0:T(8,128)(2,1)S(1)}, u32[]{:S(2)}, u32[]{:S(2)}) %collective-permute-start.30) | collective-permute-done | bytes 147488 | tf_op jit(solution)/shard_map/ppermute | solution.py:896
  243.8 3.7 %collective-permute-done.12 = bf16[112,768]{1,0:T(8,128)(2,1)S(1)} collective-permute-done((bf16[112,768]{1,0:T(8,128)(2,1)S(1)}, bf16[112,768]{1,0:T(8,128)(2,1)S(1)}, u32[]{:S(2)}, u32[]{:S(2)}) %collective-permute-start.12) | collective-permute-done | bytes 172064 | tf_op jit(solution)/shard_map/ppermute | solution.py:896
  247.6 2.3 collective-permute-done.20
  250.8 9.0 %collective-permute-done.31 = bf16[192,768]{1,0:T(8,128)(2,1)S(1)} collective-permute-done((bf16[192,768]{1,0:T(8,128)(2,1)S(1)}, bf16[192,768]{1,0:T(8,128)(2,1)S(1)}, u32[]{:S(2)}, u32[]{:S(2)}) %collective-permute-start.31) | collective-permute-done | bytes 294944 | tf_op jit(solution)/shard_map/ppermute | solution.py:896
  261.6 3.4 %collective-permute-start.22 = (bf16[224,768]{1,0:T(8,128)(2,1)S(1)}, bf16[224,768]{1,0:T(8,128)(2,1)S(1)}, u32[]{:S(2)}, u32[]{:S(2)}) collective-permute-start(bf16[224,768]{1,0:T(8,128)(2,1)S(1)} %pad_maximum_fusion.8), channel_id=1, source_target_pairs={{0,8},{4,12},{8,0},{12,4},{16,24},{20,28},{24,16},{28,20},{1,9},{5... | collective-permute-start | bytes 1032200 | tf_op jit(solution)/shard_map/ppermute | solution.py:896
  265.0 2.2 collective-permute-done.13
  267.2 1.0 pad_maximum_fusion.3
  269.9 1.3 collective-permute-start.5
  271.2 3.3 %collective-permute-done.22 = bf16[224,768]{1,0:T(8,128)(2,1)S(1)} collective-permute-done((bf16[224,768]{1,0:T(8,128)(2,1)S(1)}, bf16[224,768]{1,0:T(8,128)(2,1)S(1)}, u32[]{:S(2)}, u32[]{:S(2)}) %collective-permute-start.22) | collective-permute-done | bytes 344096 | tf_op jit(solution)/shard_map/ppermute | solution.py:896
  274.5 1.2 pad_maximum_fusion.4
  277.2 5.8 %collective-permute-done.5.far = bf16[960,256]{1,0:T(8,128)(2,1)S(1)} collective-permute-done((bf16[960,256]{1,0:T(8,128)(2,1)}, bf16[960,256]{1,0:T(8,128)(2,1)S(1)}, u32[]{:S(2)}, u32[]{:S(2)}) %collective-permute-start.5) | collective-permute-done | bytes 491552 | tf_op jit(solution)/shard_map/ppermute | solution.py:869
  283.0 1.2 sensitivity.1
  285.0 1.3 pad_maximum_fusion.2.total
  286.8 2.2 copy.60
  288.9 3.1 collective-permute-done.14
  292.1 1.3 pad_maximum_fusion.total
  294.0 11.8 %collective-permute-done.23 = bf16[448,768]{1,0:T(8,128)(2,1)} collective-permute-done((bf16[448,768]{1,0:T(8,128)(2,1)}, bf16[448,768]{1,0:T(8,128)(2,1)}, u32[]{:S(2)}, u32[]{:S(2)}) %collective-permute-start.23) | collective-permute-done | bytes 688160 | tf_op jit(solution)/shard_map/ppermute | solution.py:896
  305.8 1.2 pad_maximum_fusion.1.total
  307.0 1.7 expand_out.1
  309.5 1.7 copy.58
  311.2 1.1 copy.59
  (214 shorter events, 30.7 us)
Async XLA Ops:
  0.7 18.0 %copy-start.64 = (bf16[192,576]{1,0:T(8,128)(2,1)S(1)}, bf16[192,576]{1,0:T(8,128)(2,1)}, u32[]{:S(2)}) copy-start(bf16[192,576]{1,0:T(8,128)(2,1)} %param.31) | copy-start | bytes 663556
  2.5 17.4 %copy-start.63 = (bf16[768,192]{0,1:T(8,128)(2,1)S(1)}, bf16[768,192]{0,1:T(8,128)(2,1)}, u32[]{:S(2)}) copy-start(bf16[768,192]{0,1:T(8,128)(2,1)} %param.37) | copy-start | bytes 884740
  3.7 17.8 %copy-start.1 = (bf16[2,128,1024]{2,1,0:T(8,128)(2,1)}, bf16[2,128,1024]{2,1,0:T(8,128)(2,1)S(1)}, u32[]{:S(2)}) copy-start(bf16[2,128,1024]{2,1,0:T(8,128)(2,1)S(1)} %pad_maximum_fusion.6) | copy-start | bytes 1572868
  3.7 17.1 %copy-start.66 = (bf16[192,192]{1,0:T(8,128)(2,1)S(1)}, bf16[192,192]{1,0:T(8,128)(2,1)}, u32[]{:S(2)}) copy-start(bf16[192,192]{1,0:T(8,128)(2,1)} %param.34) | copy-start | bytes 221188
  3.7 15.0 %collective-permute-start.1 = (bf16[256,1024]{1,0:T(8,128)(2,1)S(1)}, bf16[256,1024]{1,0:T(8,128)(2,1)S(1)}, u32[]{:S(2)}, u32[]{:S(2)}) collective-permute-start(bf16[256,1024]{1,0:T(8,128)(2,1)S(1)} %bitcast.13), channel_id=1, source_target_pairs={{0,2},{1,3},{2,0},{3,1},{4,6},{5,7},{6,4},{7,5},{8,10},{9,11},{10,... | collective-permute-start | bytes 1572872 | tf_op jit(solution)/shard_map/ppermute | solution.py:929
  6.7 17.3 %collective-permute-start = (bf16[256,1024]{1,0:T(8,128)(2,1)S(1)}, bf16[256,1024]{1,0:T(8,128)(2,1)S(1)}, u32[]{:S(2)}, u32[]{:S(2)}) collective-permute-start(bf16[256,1024]{1,0:T(8,128)(2,1)S(1)} %bitcast.14), channel_id=1, source_target_pairs={{0,1},{1,0},{2,3},{3,2},{4,5},{5,4},{6,7},{7,6},{8,9},{9,8},{10,11... | collective-permute-start | bytes 1572872 | tf_op jit(solution)/shard_map/ppermute | solution.py:930
  18.6 5.4 %collective-permute-start.2 = (bf16[256,1024]{1,0:T(8,128)(2,1)S(1)}, bf16[256,1024]{1,0:T(8,128)(2,1)S(1)}, u32[]{:S(2)}, u32[]{:S(2)}) collective-permute-start(bf16[256,1024]{1,0:T(8,128)(2,1)S(1)} %collective-permute-done.1.x2), channel_id=1, source_target_pairs={{0,1},{1,0},{2,3},{3,2},{4,5},{5,4},{6,7},{7,6},{8,9},{9,8},{10,11... | collective-permute-start | bytes 1572872 | tf_op jit(solution)/shard_map/ppermute | solution.py:931
  25.0 25.2 %copy-start.4 = (bf16[768,192]{1,0:T(8,128)(2,1)S(1)}, bf16[768,192]{1,0:T(8,128)(2,1)}, u32[]{:S(2)}) copy-start(bf16[768,192]{1,0:T(8,128)(2,1)} %copy.53.sl) | copy-start | bytes 884740
  25.0 25.2 %copy-start.12 = (bf16[256,192]{1,0:T(8,128)(2,1)S(1)}, bf16[256,192]{1,0:T(8,128)(2,1)}, u32[]{:S(2)}) copy-start(bf16[256,192]{1,0:T(8,128)(2,1)} %pad.13.ml) | copy-start | bytes 294916
  25.0 25.2 %copy-start.13 = (bf16[192,768]{1,0:T(8,128)(2,1)S(1)}, bf16[192,768]{1,0:T(8,128)(2,1)}, u32[]{:S(2)}) copy-start(bf16[192,768]{1,0:T(8,128)(2,1)} %el.3) | copy-start | bytes 884740
  25.0 25.2 %copy-start.41 = (bf16[2,768]{1,0:T(2,128)(2,1)S(1)}, bf16[2,768]{1,0:T(2,128)(2,1)}, u32[]{:S(2)}) copy-start(bf16[2,768]{1,0:T(2,128)(2,1)} %gt.3) | copy-start | bytes 9220
  25.1 25.2 %copy-start.43 = (bf16[2,192]{1,0:T(2,128)(2,1)S(1)}, bf16[2,192]{1,0:T(2,128)(2,1)}, u32[]{:S(2)}) copy-start(bf16[2,192]{1,0:T(2,128)(2,1)} %gl.3) | copy-start | bytes 2308
  59.0 15.0 %copy-start.2 = (bf16[2,128,1024]{2,1,0:T(8,128)(2,1)S(1)}, bf16[2,128,1024]{2,1,0:T(8,128)(2,1)}, u32[]{:S(2)}) copy-start(bf16[2,128,1024]{2,1,0:T(8,128)(2,1)} %copy-done.1) | copy-start | bytes 1572868
  59.1 15.0 %copy-start.7 = (bf16[256,1024]{1,0:T(8,128)(2,1)S(1)}, bf16[256,1024]{1,0:T(8,128)(2,1)}, u32[]{:S(2)}) copy-start(bf16[256,1024]{1,0:T(8,128)(2,1)} %copy-done.6) | copy-start | bytes 1572868
  59.1 15.0 %copy-start.9 = (bf16[256,1024]{1,0:T(8,128)(2,1)S(1)}, bf16[256,1024]{1,0:T(8,128)(2,1)}, u32[]{:S(2)}) copy-start(bf16[256,1024]{1,0:T(8,128)(2,1)} %copy-done.8) | copy-start | bytes 1572868
  59.1 15.0 %copy-start.11 = (bf16[256,1024]{1,0:T(8,128)(2,1)S(1)}, bf16[256,1024]{1,0:T(8,128)(2,1)}, u32[]{:S(2)}) copy-start(bf16[256,1024]{1,0:T(8,128)(2,1)} %copy-done.10) | copy-start | bytes 1572868
  59.1 15.0 %copy-start.20 = (bf16[1024,256]{1,0:T(8,128)(2,1)S(1)}, bf16[1024,256]{1,0:T(8,128)(2,1)}, u32[]{:S(2)}) copy-start(bf16[1024,256]{1,0:T(8,128)(2,1)} %get-tuple-element.85.kl_in) | copy-start | bytes 1572868
  59.1 15.0 %copy-start.21 = (bf16[1024,256]{1,0:T(8,128)(2,1)S(1)}, bf16[1024,256]{1,0:T(8,128)(2,1)}, u32[]{:S(2)}) copy-start(bf16[1024,256]{1,0:T(8,128)(2,1)} %get-tuple-element.87.vl_in) | copy-start | bytes 1572868
  59.1 15.0 %copy-start.24 = (bf16[256,768]{1,0:T(8,128)(2,1)S(1)}, bf16[256,768]{1,0:T(8,128)(2,1)}, u32[]{:S(2)}) copy-start(bf16[256,768]{1,0:T(8,128)(2,1)} %get-tuple-element.89.q_t) | copy-start | bytes 1179652
  59.1 15.0 %copy-start.25 = (bf16[256,768]{1,0:T(8,128)(2,1)S(1)}, bf16[256,768]{1,0:T(8,128)(2,1)}, u32[]{:S(2)}) copy-start(bf16[256,768]{1,0:T(8,128)(2,1)} %get-tuple-element.104.ctx_t) | copy-start | bytes 1179652
  59.1 15.0 %copy-start.35 = (bf16[256,256]{1,0:T(8,128)(2,1)S(1)}, bf16[256,256]{1,0:T(8,128)(2,1)}, u32[]{:S(2)}) copy-start(bf16[256,256]{1,0:T(8,128)(2,1)} %get-tuple-element.90.q_l) | copy-start | bytes 393220
  59.1 15.0 %copy-start.36 = (bf16[256,256]{1,0:T(8,128)(2,1)S(1)}, bf16[256,256]{1,0:T(8,128)(2,1)}, u32[]{:S(2)}) copy-start(bf16[256,256]{1,0:T(8,128)(2,1)} %get-tuple-element.105.ctx_l) | copy-start | bytes 393220
  59.1 15.0 %copy-start.40 = (f32[8,768]{1,0:T(8,128)S(1)}, f32[8,768]{1,0:T(8,128)}, u32[]{:S(2)}) copy-start(f32[8,768]{1,0:T(8,128)} %get-tuple-element.108.sf_t) | copy-start | bytes 73732
  59.1 15.0 %copy-start.42 = (f32[8,192]{1,0:T(8,128)S(1)}, f32[8,192]{1,0:T(8,128)}, u32[]{:S(2)}) copy-start(f32[8,192]{1,0:T(8,128)} %get-tuple-element.109.sf_l) | copy-start | bytes 18436
  74.0 17.6 %copy-start.31 = (f32[256,192]{1,0:T(8,128)}, f32[256,192]{1,0:T(8,128)S(1)}, u32[]{:S(2)}) copy-start(f32[256,192]{1,0:T(8,128)S(1)} %get-tuple-element.123.mid_l) | copy-start | bytes 589828
  74.1 18.2 %copy-start.72 = (bf16[896,768]{1,0:T(8,128)(2,1)S(1)}, bf16[896,768]{1,0:T(8,128)(2,1)}, u32[]{:S(2)}) copy-start(bf16[896,768]{1,0:T(8,128)(2,1)} %get-tuple-element.136) | copy-start | bytes 4128772
  74.1 18.6 %copy-start.73 = (bf16[768,768]{1,0:T(8,128)(2,1)S(1)}, bf16[768,768]{1,0:T(8,128)(2,1)}, u32[]{:S(2)}) copy-start(bf16[768,768]{1,0:T(8,128)(2,1)} %get-tuple-element.139) | copy-start | bytes 3538948
  91.6 3.5 %collective-permute-start.7 = (bf16[896,768]{1,0:T(8,128)(2,1)}, bf16[896,768]{1,0:T(8,128)(2,1)S(1)}, u32[]{:S(2)}, u32[]{:S(2)}) collective-permute-start(bf16[896,768]{1,0:T(8,128)(2,1)} %get-tuple-element.129), channel_id=1, source_target_pairs={{0,1},{1,0},{2,3},{3,2},{4,5},{5,4},{6,7},{7,6},{8,9},{9,8},{10,11... | collective-permute-start | bytes 4128776 | tf_op jit(solution)/shard_map/ppermute | solution.py:866
  92.2 8.0 %collective-permute-start.25 = (bf16[768,768]{1,0:T(8,128)(2,1)}, bf16[768,768]{1,0:T(8,128)(2,1)S(1)}, u32[]{:S(2)}, u32[]{:S(2)}) collective-permute-start(bf16[768,768]{1,0:T(8,128)(2,1)} %get-tuple-element.141), channel_id=1, source_target_pairs={{0,1},{1,0},{2,3},{3,2},{4,5},{5,4},{6,7},{7,6},{8,9},{9,8},{10,11... | collective-permute-start | bytes 3538952 | tf_op jit(solution)/shard_map/ppermute | solution.py:866
  92.3 11.0 %collective-permute-start.16 = (bf16[896,768]{1,0:T(8,128)(2,1)S(1)}, bf16[896,768]{1,0:T(8,128)(2,1)S(1)}, u32[]{:S(2)}, u32[]{:S(2)}) collective-permute-start(bf16[896,768]{1,0:T(8,128)(2,1)S(1)} %copy-done.72), channel_id=1, source_target_pairs={{0,1},{1,0},{2,3},{3,2},{4,5},{5,4},{6,7},{7,6},{8,9},{9,8},{10,11... | collective-permute-start | bytes 4128776 | tf_op jit(solution)/shard_map/ppermute | solution.py:866
  92.7 12.4 %collective-permute-start.24 = (bf16[768,768]{1,0:T(8,128)(2,1)S(1)}, bf16[768,768]{1,0:T(8,128)(2,1)}, u32[]{:S(2)}, u32[]{:S(2)}) collective-permute-start(bf16[768,768]{1,0:T(8,128)(2,1)S(1)} %copy-done.73), channel_id=1, source_target_pairs={{0,1},{1,0},{2,3},{3,2},{4,5},{5,4},{6,7},{7,6},{8,9},{9,8},{10,11... | collective-permute-start | bytes 3538952 | tf_op jit(solution)/shard_map/ppermute | solution.py:867
  92.8 74.8 %collective-permute-start.15 = (bf16[896,768]{1,0:T(8,128)(2,1)}, bf16[896,768]{1,0:T(8,128)(2,1)S(1)}, u32[]{:S(2)}, u32[]{:S(2)}) collective-permute-start(bf16[896,768]{1,0:T(8,128)(2,1)} %get-tuple-element.134), channel_id=1, source_target_pairs={{0,1},{1,0},{2,3},{3,2},{4,5},{5,4},{6,7},{7,6},{8,9},{9,8},{10,11... | collective-permute-start | bytes 4128776 | tf_op jit(solution)/shard_map/ppermute | solution.py:867
  95.1 68.9 %collective-permute-start.6 = (bf16[896,768]{1,0:T(8,128)(2,1)}, bf16[896,768]{1,0:T(8,128)(2,1)S(1)}, u32[]{:S(2)}, u32[]{:S(2)}) collective-permute-start(bf16[896,768]{1,0:T(8,128)(2,1)} %get-tuple-element.127), channel_id=1, source_target_pairs={{0,1},{1,0},{2,3},{3,2},{4,5},{5,4},{6,7},{7,6},{8,9},{9,8},{10,11... | collective-permute-start | bytes 4128776 | tf_op jit(solution)/shard_map/ppermute | solution.py:867
  100.2 63.8 %collective-permute-start.8 = (bf16[896,768]{1,0:T(8,128)(2,1)}, bf16[896,768]{1,0:T(8,128)(2,1)}, u32[]{:S(2)}, u32[]{:S(2)}) collective-permute-start(bf16[896,768]{1,0:T(8,128)(2,1)} %add_convert_fusion.1), channel_id=1, source_target_pairs={{0,2},{1,3},{2,0},{3,1},{4,6},{5,7},{6,4},{7,5},{8,10},{9,11},{10,... | collective-permute-start | bytes 4128776 | tf_op jit(solution)/shard_map/ppermute | solution.py:869
  103.3 55.5 %collective-permute-start.26 = (bf16[768,768]{1,0:T(8,128)(2,1)}, bf16[768,768]{1,0:T(8,128)(2,1)}, u32[]{:S(2)}, u32[]{:S(2)}) collective-permute-start(bf16[768,768]{1,0:T(8,128)(2,1)} %add_convert_fusion.2), channel_id=1, source_target_pairs={{0,2},{1,3},{2,0},{3,1},{4,6},{5,7},{6,4},{7,5},{8,10},{9,11},{10,... | collective-permute-start | bytes 3538952 | tf_op jit(solution)/shard_map/ppermute | solution.py:869
  105.1 82.7 %collective-permute-start.17 = (bf16[896,768]{1,0:T(8,128)(2,1)}, bf16[896,768]{1,0:T(8,128)(2,1)}, u32[]{:S(2)}, u32[]{:S(2)}) collective-permute-start(bf16[896,768]{1,0:T(8,128)(2,1)} %add_convert_fusion), channel_id=1, source_target_pairs={{0,2},{1,3},{2,0},{3,1},{4,6},{5,7},{6,4},{7,5},{8,10},{9,11},{10,... | collective-permute-start | bytes 4128776 | tf_op jit(solution)/shard_map/ppermute | solution.py:869
  162.3 30.3 %collective-permute-start.27 = (bf16[384,768]{1,0:T(8,128)(2,1)S(1)}, bf16[384,768]{1,0:T(8,128)(2,1)}, u32[]{:S(2)}, u32[]{:S(2)}) collective-permute-start(bf16[384,768]{1,0:T(8,128)(2,1)S(1)} %get-tuple-element.186), channel_id=1, source_target_pairs={{0,4},{4,0},{8,12},{12,8},{16,20},{20,16},{24,28},{28,24},{1,5},{5... | collective-permute-start | bytes 1769480 | tf_op jit(solution)/shard_map/ppermute | solution.py:891
  164.0 23.7 %copy-start.54 = (bf16[896,768]{1,0:T(8,128)(2,1)S(1)}, bf16[896,768]{1,0:T(8,128)(2,1)}, u32[]{:S(2)}) copy-start(bf16[896,768]{1,0:T(8,128)(2,1)} %get-tuple-element.133) | copy-start | bytes 4128772
  167.3 29.5 %collective-permute-start.9 = (bf16[448,768]{1,0:T(8,128)(2,1)}, bf16[448,768]{1,0:T(8,128)(2,1)}, u32[]{:S(2)}, u32[]{:S(2)}) collective-permute-start(bf16[448,768]{1,0:T(8,128)(2,1)} %get-tuple-element.184), channel_id=1, source_target_pairs={{0,4},{4,0},{8,12},{12,8},{16,20},{20,16},{24,28},{28,24},{1,5},{5... | collective-permute-start | bytes 2064392 | tf_op jit(solution)/shard_map/ppermute | solution.py:891
  190.9 22.6 %collective-permute-start.18 = (bf16[448,768]{1,0:T(8,128)(2,1)}, bf16[448,768]{1,0:T(8,128)(2,1)}, u32[]{:S(2)}, u32[]{:S(2)}) collective-permute-start(bf16[448,768]{1,0:T(8,128)(2,1)} %get-tuple-element.182), channel_id=1, source_target_pairs={{0,4},{4,0},{8,12},{12,8},{16,20},{20,16},{24,28},{28,24},{1,5},{5... | collective-permute-start | bytes 2064392 | tf_op jit(solution)/shard_map/ppermute | solution.py:891
  195.2 14.4 %collective-permute-start.28 = (bf16[192,768]{1,0:T(8,128)(2,1)}, bf16[192,768]{1,0:T(8,128)(2,1)}, u32[]{:S(2)}, u32[]{:S(2)}) collective-permute-start(bf16[192,768]{1,0:T(8,128)(2,1)} %get-tuple-element.192), channel_id=1, source_target_pairs={{0,8},{4,12},{8,0},{12,4},{16,24},{20,28},{24,16},{28,20},{1,9},{5... | collective-permute-start | bytes 884744 | tf_op jit(solution)/shard_map/ppermute | solution.py:891
  199.4 17.0 %collective-permute-start.10 = (bf16[224,768]{1,0:T(8,128)(2,1)}, bf16[224,768]{1,0:T(8,128)(2,1)}, u32[]{:S(2)}, u32[]{:S(2)}) collective-permute-start(bf16[224,768]{1,0:T(8,128)(2,1)} %get-tuple-element.190), channel_id=1, source_target_pairs={{0,8},{4,12},{8,0},{12,4},{16,24},{20,28},{24,16},{28,20},{1,9},{5... | collective-permute-start | bytes 1032200 | tf_op jit(solution)/shard_map/ppermute | solution.py:891
  209.6 59.3 %collective-permute-start.4 = (bf16[960,256]{1,0:T(8,128)(2,1)S(1)}, bf16[960,256]{1,0:T(8,128)(2,1)S(1)}, u32[]{:S(2)}, u32[]{:S(2)}) collective-permute-start(bf16[960,256]{1,0:T(8,128)(2,1)S(1)} %get-tuple-element.121), channel_id=1, source_target_pairs={{0,1},{1,0},{2,3},{3,2},{4,5},{5,4},{6,7},{7,6},{8,9},{9,8},{10,11... | collective-permute-start | bytes 1474568 | tf_op jit(solution)/shard_map/ppermute | solution.py:866
  210.8 10.6 %collective-permute-start.29 = (bf16[96,768]{1,0:T(8,128)(2,1)S(1)}, bf16[96,768]{1,0:T(8,128)(2,1)S(1)}, u32[]{:S(2)}, u32[]{:S(2)}) collective-permute-start(bf16[96,768]{1,0:T(8,128)(2,1)S(1)} %add_convert_fusion.15), channel_id=1, source_target_pairs={{0,16},{4,20},{8,24},{12,28},{16,0},{20,4},{24,8},{28,12},{1,17},{... | collective-permute-start | bytes 442376 | tf_op jit(solution)/shard_map/ppermute | solution.py:891
  214.8 18.4 %collective-permute-start.19 = (bf16[224,768]{1,0:T(8,128)(2,1)S(1)}, bf16[224,768]{1,0:T(8,128)(2,1)S(1)}, u32[]{:S(2)}, u32[]{:S(2)}) collective-permute-start(bf16[224,768]{1,0:T(8,128)(2,1)S(1)} %get-tuple-element.188), channel_id=1, source_target_pairs={{0,8},{4,12},{8,0},{12,4},{16,24},{20,28},{24,16},{28,20},{1,9},{5... | collective-permute-start | bytes 1032200 | tf_op jit(solution)/shard_map/ppermute | solution.py:891
  217.4 11.3 %collective-permute-start.11 = (bf16[112,768]{1,0:T(8,128)(2,1)S(1)}, bf16[112,768]{1,0:T(8,128)(2,1)S(1)}, u32[]{:S(2)}, u32[]{:S(2)}) collective-permute-start(bf16[112,768]{1,0:T(8,128)(2,1)S(1)} %add_convert_fusion.13), channel_id=1, source_target_pairs={{0,16},{4,20},{8,24},{12,28},{16,0},{20,4},{24,8},{28,12},{1,17},{... | collective-permute-start | bytes 516104 | tf_op jit(solution)/shard_map/ppermute | solution.py:891
  222.3 37.5 %copy-start.48 = (bf16[96,768]{1,0:T(8,128)(2,1)}, bf16[96,768]{1,0:T(8,128)(2,1)S(1)}, u32[]{:S(2)}) copy-start(bf16[96,768]{1,0:T(8,128)(2,1)S(1)} %add_convert_fusion.14) | copy-start | bytes 442372
  222.3 21.4 %collective-permute-start.30 = (bf16[96,768]{1,0:T(8,128)(2,1)S(1)}, bf16[96,768]{1,0:T(8,128)(2,1)S(1)}, u32[]{:S(2)}, u32[]{:S(2)}) collective-permute-start(bf16[96,768]{1,0:T(8,128)(2,1)S(1)} %add_convert_fusion.14), channel_id=1, source_target_pairs={{0,16},{4,20},{8,24},{12,28},{16,0},{20,4},{24,8},{28,12},{1,17},{... | collective-permute-start | bytes 442376 | tf_op jit(solution)/shard_map/ppermute | solution.py:896
  229.7 17.8 %collective-permute-start.12 = (bf16[112,768]{1,0:T(8,128)(2,1)S(1)}, bf16[112,768]{1,0:T(8,128)(2,1)S(1)}, u32[]{:S(2)}, u32[]{:S(2)}) collective-permute-start(bf16[112,768]{1,0:T(8,128)(2,1)S(1)} %add_convert_fusion.12), channel_id=1, source_target_pairs={{0,16},{4,20},{8,24},{12,28},{16,0},{20,4},{24,8},{28,12},{1,17},{... | collective-permute-start | bytes 516104 | tf_op jit(solution)/shard_map/ppermute | solution.py:896
  233.2 16.7 %collective-permute-start.20 = (bf16[112,768]{1,0:T(8,128)(2,1)S(1)}, bf16[112,768]{1,0:T(8,128)(2,1)S(1)}, u32[]{:S(2)}, u32[]{:S(2)}) collective-permute-start(bf16[112,768]{1,0:T(8,128)(2,1)S(1)} %add_convert_fusion.11), channel_id=1, source_target_pairs={{0,16},{4,20},{8,24},{12,28},{16,0},{20,4},{24,8},{28,12},{1,17},{... | collective-permute-start | bytes 516104 | tf_op jit(solution)/shard_map/ppermute | solution.py:891
  243.7 17.1 %copy-start.60 = (bf16[96,768]{1,0:T(8,128)(2,1)}, bf16[96,768]{1,0:T(8,128)(2,1)S(1)}, u32[]{:S(2)}) copy-start(bf16[96,768]{1,0:T(8,128)(2,1)S(1)} %collective-permute-done.30) | copy-start | bytes 442372
  243.7 16.1 %collective-permute-start.31 = (bf16[192,768]{1,0:T(8,128)(2,1)S(1)}, bf16[192,768]{1,0:T(8,128)(2,1)S(1)}, u32[]{:S(2)}, u32[]{:S(2)}) collective-permute-start(bf16[192,768]{1,0:T(8,128)(2,1)S(1)} %pad_maximum_fusion.9), channel_id=1, source_target_pairs={{0,8},{4,12},{8,0},{12,4},{16,24},{20,28},{24,16},{28,20},{1,9},{5... | collective-permute-start | bytes 884744 | tf_op jit(solution)/shard_map/ppermute | solution.py:896
  247.5 19.7 %copy-start.50 = (bf16[112,768]{1,0:T(8,128)(2,1)}, bf16[112,768]{1,0:T(8,128)(2,1)S(1)}, u32[]{:S(2)}) copy-start(bf16[112,768]{1,0:T(8,128)(2,1)S(1)} %collective-permute-done.12) | copy-start | bytes 516100
  247.5 19.7 %collective-permute-start.13 = (bf16[224,768]{1,0:T(8,128)(2,1)S(1)}, bf16[224,768]{1,0:T(8,128)(2,1)S(1)}, u32[]{:S(2)}, u32[]{:S(2)}) collective-permute-start(bf16[224,768]{1,0:T(8,128)(2,1)S(1)} %pad_maximum_fusion.7), channel_id=1, source_target_pairs={{0,8},{4,12},{8,0},{12,4},{16,24},{20,28},{24,16},{28,20},{1,9},{5... | collective-permute-start | bytes 1032200 | tf_op jit(solution)/shard_map/ppermute | solution.py:896
  249.9 24.6 %copy-start.46 = (bf16[112,768]{1,0:T(8,128)(2,1)}, bf16[112,768]{1,0:T(8,128)(2,1)S(1)}, u32[]{:S(2)}) copy-start(bf16[112,768]{1,0:T(8,128)(2,1)S(1)} %add_convert_fusion.10) | copy-start | bytes 516100
  249.9 11.6 %collective-permute-start.21 = (bf16[112,768]{1,0:T(8,128)(2,1)S(1)}, bf16[112,768]{1,0:T(8,128)(2,1)S(1)}, u32[]{:S(2)}, u32[]{:S(2)}) collective-permute-start(bf16[112,768]{1,0:T(8,128)(2,1)S(1)} %add_convert_fusion.10), channel_id=1, source_target_pairs={{0,16},{4,20},{8,24},{12,28},{16,0},{20,4},{24,8},{28,12},{1,17},{... | collective-permute-start | bytes 516104 | tf_op jit(solution)/shard_map/ppermute | solution.py:896
  250.8 26.4 %collective-permute-start.3 = (bf16[960,256]{1,0:T(8,128)(2,1)}, bf16[960,256]{1,0:T(8,128)(2,1)S(1)}, u32[]{:S(2)}, u32[]{:S(2)}) collective-permute-start(bf16[960,256]{1,0:T(8,128)(2,1)} %get-tuple-element.119), channel_id=1, source_target_pairs={{0,1},{1,0},{2,3},{3,2},{4,5},{5,4},{6,7},{7,6},{8,9},{9,8},{10,11... | collective-permute-start | bytes 1474568 | tf_op jit(solution)/shard_map/ppermute | solution.py:867
  260.8 24.2 %collective-permute-start.32 = (bf16[384,768]{1,0:T(8,128)(2,1)}, bf16[384,768]{1,0:T(8,128)(2,1)}, u32[]{:S(2)}, u32[]{:S(2)}) collective-permute-start(bf16[384,768]{1,0:T(8,128)(2,1)} %pad_maximum_fusion.5), channel_id=1, source_target_pairs={{0,4},{4,0},{8,12},{12,8},{16,20},{20,16},{24,28},{28,24},{1,5},{5... | collective-permute-start | bytes 1769480 | tf_op jit(solution)/shard_map/ppermute | solution.py:896
  261.6 12.9 %collective-permute-start.22 = (bf16[224,768]{1,0:T(8,128)(2,1)S(1)}, bf16[224,768]{1,0:T(8,128)(2,1)S(1)}, u32[]{:S(2)}, u32[]{:S(2)}) collective-permute-start(bf16[224,768]{1,0:T(8,128)(2,1)S(1)} %pad_maximum_fusion.8), channel_id=1, source_target_pairs={{0,8},{4,12},{8,0},{12,4},{16,24},{20,28},{24,16},{28,20},{1,9},{5... | collective-permute-start | bytes 1032200 | tf_op jit(solution)/shard_map/ppermute | solution.py:896
  268.2 23.8 %collective-permute-start.14 = (bf16[448,768]{1,0:T(8,128)(2,1)}, bf16[448,768]{1,0:T(8,128)(2,1)}, u32[]{:S(2)}, u32[]{:S(2)}) collective-permute-start(bf16[448,768]{1,0:T(8,128)(2,1)} %pad_maximum_fusion.3), channel_id=1, source_target_pairs={{0,4},{4,0},{8,12},{12,8},{16,20},{20,16},{24,28},{28,24},{1,5},{5... | collective-permute-start | bytes 2064392 | tf_op jit(solution)/shard_map/ppermute | solution.py:896
  269.0 14.0 %copy-start.16 = (f32[960,256]{1,0:T(8,128)S(1)}, f32[960,256]{1,0:T(8,128)}, u32[]{:S(2)}) copy-start(f32[960,256]{1,0:T(8,128)} %copy-done.15) | copy-start | bytes 2949124
  269.0 14.0 %copy-start.19 = (f32[256,768]{1,0:T(8,128)S(1)}, f32[256,768]{1,0:T(8,128)}, u32[]{:S(2)}) copy-start(f32[256,768]{1,0:T(8,128)} %copy-done.18) | copy-start | bytes 2359300
  269.9 13.1 %collective-permute-start.5 = (bf16[960,256]{1,0:T(8,128)(2,1)}, bf16[960,256]{1,0:T(8,128)(2,1)S(1)}, u32[]{:S(2)}, u32[]{:S(2)}) collective-permute-start(bf16[960,256]{1,0:T(8,128)(2,1)} %add_convert_fusion.6), channel_id=1, source_target_pairs={{0,2},{1,3},{2,0},{3,1},{4,6},{5,7},{6,4},{7,5},{8,10},{9,11},{10,... | collective-permute-start | bytes 1474568 | tf_op jit(solution)/shard_map/ppermute | solution.py:869
  275.7 30.1 %collective-permute-start.23 = (bf16[448,768]{1,0:T(8,128)(2,1)}, bf16[448,768]{1,0:T(8,128)(2,1)}, u32[]{:S(2)}, u32[]{:S(2)}) collective-permute-start(bf16[448,768]{1,0:T(8,128)(2,1)} %pad_maximum_fusion.4), channel_id=1, source_target_pairs={{0,4},{4,0},{8,12},{12,8},{16,20},{20,16},{24,28},{28,24},{1,5},{5... | collective-permute-start | bytes 2064392 | tf_op jit(solution)/shard_map/ppermute | solution.py:896
  (43 other events, 172.9 us)

commit v2 on v1

v2 whole, which is shorter than its diff:
```python
import functools

import jax
import jax.numpy as jnp
from jax import lax
from jax.experimental import pallas as pl
from jax.experimental.pallas import tpu as pltpu
from jax.sharding import PartitionSpec as P

HEADS = 12
EPSILON = 1e-05
MASKED = -1000000000.0
F32 = jnp.float32
BF16 = jnp.bfloat16
DT = 768
DL = 192
FT = 3072
FL = 768
LANES = 128
SLAB = 256
S_ROWS = 768
E_ROWS = 1152
P_ROWS = 640
MIB = 1024 * 1024

VMEM = pl.BlockSpec(memory_space=pltpu.VMEM)
ANY = pl.BlockSpec(memory_space=pl.ANY)


def dot(left, right):
    return jnp.dot(left, right, preferred_element_type=F32)


def dot_nt(left, right):
    return lax.dot_general(left, right, (((1,), (1,)), ((), ())), preferred_element_type=F32)


LIMIT = 60 * MIB
FIRST = 60 * MIB
SMALL = 16 * MIB


COST = pl.CostEstimate(flops=1, bytes_accessed=1, transcendentals=0)


def shape_of(shape, dtype):
    return jax.ShapeDtypeStruct(shape, dtype)


def copies_of(pairs, sems, base):
    made = []
    for at, (source, target) in enumerate(pairs):
        copy = pltpu.make_async_copy(source, target, sems.at[base + at])
        copy.start()
        made.append(copy)
    return made


def wait_all(made):
    for copy in made:
        copy.wait()


def gather_pairs(blocks, rows, packs, target):
    span = rows * len(blocks)
    return [
        (block.at[pack], target.at[pl.ds(pack * span + at * rows, rows), :])
        for at, block in enumerate(blocks)
        for pack in range(packs)
    ]


def in_lines(shards, subs, dp_size, targets):
    place = (lax.axis_index("seq"), lax.axis_index("dp"))
    pairs = []
    for core in (1, 0):
        for at, (first, rows, hops, growth) in enumerate(subs):
            size = rows // dp_size
            target = targets[2 * at + 1 - core]
            for across in range(2):
                shard = jnp.bitwise_xor(place[0], core + 2 * across)
                for other in range(dp_size):
                    piece = jnp.bitwise_xor(place[1], other)
                    mark = pl.multiple_of(first + piece * size, 16)
                    line = position(hops, across, other) * size
                    pairs.append(
                        (shards.at[shard, pl.ds(mark, size), :], target.at[pl.ds(line, size), :])
                    )
    return pairs


def position(hops, across, other):
    at = 0
    for group in hops:
        index = 0
        for n, (axis, bit) in enumerate(group):
            if across if axis == "seq" else other & bit:
                index += 1 << n
        at = (at << len(group)) + index
    return at


def sub_chunks(rows, split, dp_size):
    step = 16 * dp_size
    total = (rows + step - 1) // step * step
    subs = []
    first = 0
    for at, (share, hops, growth) in enumerate(split):
        size = total - first if at == len(split) - 1 else (share + step - 1) // step * step
        subs.append((first, size, hops, growth))
        first += size
    return tuple(subs)


def total_lines(subs):
    return sum(rows for first, rows, hops, growth in subs)


def pair_shapes(subs):
    return tuple(shape_of((2 * rows, DT), BF16) for first, rows, hops, growth in subs for unused in range(2))


def lane_masks(pair_at):
    lanes = lax.broadcasted_iota(jnp.int32, (1, LANES), 1)
    low_half = lanes < 64
    group_of_16 = lax.shift_right_logical(lanes, 4)
    first = group_of_16 == 2 * lax.rem(pair_at, 4)
    second = group_of_16 == 2 * lax.rem(pair_at, 4) + 1
    return (low_half, first, second)


def stacked_heads(text_rows, layout_rows, masks):
    low_half, first, second = masks
    zero_text = jnp.zeros_like(text_rows)
    zero_layout = jnp.zeros_like(layout_rows)
    top = jnp.concatenate(
        [jnp.where(low_half, text_rows, zero_text), jnp.where(first, layout_rows, zero_layout)],
        axis=1,
    )
    bottom = jnp.concatenate(
        [jnp.where(low_half, zero_text, text_rows), jnp.where(second, layout_rows, zero_layout)],
        axis=1,
    )
    return jnp.concatenate([top, bottom], axis=0)


def normalized(values):
    centre = values - jnp.mean(values, axis=-1, keepdims=True)
    spread = jnp.mean(centre * centre, axis=-1, keepdims=True)
    inverse = lax.rsqrt(spread + EPSILON)
    return (centre * inverse, inverse)


def norm_back(delta, unit, inverse):
    return inverse * (
        delta
        - jnp.mean(delta, axis=-1, keepdims=True)
        - unit * jnp.mean(delta * unit, axis=-1, keepdims=True)
    )


def column_sum(values):
    return jnp.sum(values, axis=0, keepdims=True)


def feed_forward(hidden_low, expand, offsets, shrink, turned, active, slope, chunk, branch_ref):
    width = expand.shape[1]
    for at in range(width // chunk):
        part = pl.ds(at * chunk, chunk)
        before = dot(hidden_low, expand[:, part]) + offsets[:, part].astype(F32)
        share = 0.5 + 0.5 * lax.erf(before * (0.5**0.5))
        density = jnp.exp(-0.5 * (before * before)) * 0.3989422804014327
        active_part = (before * share).astype(BF16)
        active[:, part] = active_part
        slope[:, part] = (share + before * density).astype(BF16)
        product = dot_nt(active_part, shrink[:, part]) if turned else dot(active_part, shrink[part, :])
        if at == 0:
            branch_ref[...] = product
        else:
            branch_ref[...] += product


def prepare_kernel(text_rows, layout_rows, segments, project, offsets_t, offsets_l, joined, padded, line_t, line_l):
    packs, width, rows = layout_rows.shape
    for pack in range(packs):
        marks = jnp.broadcast_to(segments[pack : pack + 1, :].astype(F32), (SLAB - width, rows))
        lines = jnp.concatenate([layout_rows[pack].astype(F32), marks], axis=0)
        joined[pack, :, :DT] = text_rows[pack]
        joined[pack, :, DT:] = lines.T.astype(BF16)
    line_t[...] = offsets_t[...].reshape(line_t.shape)
    line_l[...] = offsets_l[...].reshape(line_l.shape)
    padded[...] = jnp.zeros_like(padded)
    for third in range(3):
        padded[:, third * SLAB : third * SLAB + DL] = project[:, third * DL : (third + 1) * DL]


def prepare_call(text_rows, layout_rows, segments, project, offsets_t, offsets_l):
    packs, rows, unused = text_rows.shape
    return pl.pallas_call(
        prepare_kernel,
        out_shape=(
            shape_of((packs, rows, DT + SLAB), BF16),
            shape_of((DL, 3 * SLAB), BF16),
            shape_of((1, FT), BF16),
            shape_of((1, FL), BF16),
        ),
        in_specs=[VMEM] * 6,
        out_specs=[VMEM] * 4,
        compiler_params=pltpu.CompilerParams(vmem_limit_bytes=LIMIT),
        cost_estimate=COST,
        name="prepare",
    )(text_rows, layout_rows, segments, project, offsets_t, offsets_l)


def forward_kernel(
    packs,
    rows,
    dp_size,
    subs,
    x0,
    x1,
    x2,
    x3,
    wt_in,
    wl_in,
    mt_in,
    et_in,
    st_in,
    ml,
    el,
    sl,
    cot_t,
    cot_l,
    bt,
    gt,
    ot,
    bl,
    gl,
    ol,
    res_t,
    res_l,
    q_t,
    q_l,
    kt_out,
    kl_out,
    vt_out,
    vl_out,
    p_out,
    ctx_t,
    ctx_l,
    hid_t,
    unit_t,
    inv_t,
    sum_t,
    slope_t,
    hid_l,
    unit_l,
    inv_l,
    sum_l,
    slope_l,
    act_l,
    sv_t,
    sv_l,
    *rest,
):
    targets, rest = rest[: 2 * len(subs)], rest[2 * len(subs) :]
    (
        xs,
        layout_bias_ref,
        wt,
        wl,
        mt,
        et,
        st,
        k_t,
        k_l,
        v_t,
        v_l,
        prob,
        bias,
        act_t,
        turned,
        branch_t,
        branch_l,
        grads,
        sems,
    ) = rest
    blocks = (x0, x1, x2, x3)
    keys = rows * len(blocks)
    tokens = packs * rows
    x_copies = copies_of(
        gather_pairs(blocks, rows, packs, xs), sems, 0
    )
    base = len(x_copies)
    w_copies = copies_of(((wt_in, wt), (wl_in, wl), (mt_in, mt), (et_in, et), (st_in, st)), sems, base)
    base += 5
    text_bias = bt[...].astype(F32)
    layout_bias_ref[...] = jnp.zeros_like(layout_bias_ref)
    layout_bias_ref[:, :DL] = bl[...].astype(F32)
    layout_bias = layout_bias_ref[...]
    wait_all(x_copies)
    wait_all(w_copies[:2])

    for pack in range(packs):
        own = pl.ds(pack * keys, rows)
        mine = pl.ds(pack * rows, rows)
        q_t[mine, :] = (dot(xs[own, :DT], wt[:, :DT]) + text_bias[0:1, :]).astype(BF16) * 0.125
        q_l[mine, :] = (dot(xs[own, DT : DT + DL], wl[:, :SLAB]) + layout_bias[0:1, :]).astype(BF16) * 0.25

    step = 256

    def key_rows(at, unused):
        span = pl.ds(pl.multiple_of(at * step, step), step)
        k_t[span, :] = dot(xs[span, :DT], wt[:, DT : 2 * DT]).astype(BF16)
        v_t[span, :] = (dot(xs[span, :DT], wt[:, 2 * DT :]) + text_bias[1:2, :]).astype(BF16)
        k_l[span, :] = dot(xs[span, DT : DT + DL], wl[:, SLAB : 2 * SLAB]).astype(BF16)
        v_l[span, :] = (dot(xs[span, DT : DT + DL], wl[:, 2 * SLAB :]) + layout_bias[1:2, :]).astype(BF16)
        return unused

    lax.fori_loop(0, packs * keys // step, key_rows, 0)
    kv_copies = copies_of(((k_t, kt_out), (k_l, kl_out), (v_t, vt_out), (v_l, vl_out)), sems, base)
    base += 4

    marks = lax.broadcasted_iota(jnp.int32, (1, LANES), 1) - 64
    for pack in range(packs):
        slab = xs[pl.ds(pack * keys, keys), DT + LANES : DT + 2 * LANES].astype(F32)
        hot = jnp.where((slab == marks.astype(F32)) & (marks >= 0) & (marks < 16), 1.0, 0.0).astype(BF16)
        same = dot_nt(hot[:rows], hot)
        bias[pack] = jnp.where(same > 0.5, 0.0, MASKED)

    ctx_l[...] = jnp.zeros_like(ctx_l)

    def head_pair(pair_at, unused):
        masks = lane_masks(pair_at)
        text_lanes = pl.ds(pl.multiple_of(pair_at * LANES, LANES), LANES)
        layout_lanes = pl.ds(pl.multiple_of(pair_at // 4 * LANES, LANES), LANES)
        for pack in range(packs):
            mine = pl.ds(pack * rows, rows)
            span = pl.ds(pack * keys, keys)
            queries = stacked_heads(q_t[mine, text_lanes], q_l[mine, layout_lanes], masks)
            both_keys = jnp.concatenate([k_t[span, text_lanes], k_l[span, layout_lanes]], axis=1)
            both_values = jnp.concatenate([v_t[span, text_lanes], v_l[span, layout_lanes]], axis=1)
            allowed = bias[pack]
            logit = dot_nt(queries, both_keys) + jnp.concatenate([allowed, allowed], axis=0)
            raised = jnp.exp(logit - jnp.max(logit, axis=1, keepdims=True))
            low = (raised * (1.0 / jnp.sum(raised, axis=1, keepdims=True))).astype(BF16)
            prob[pair_at, pack] = low
            mixed = dot(low, both_values).astype(BF16)
            ctx_t[mine, text_lanes] = jnp.where(masks[0], mixed[:rows, :LANES], mixed[rows:, :LANES])
            kept = ctx_l[mine, layout_lanes]
            kept = jnp.where(masks[1], mixed[:rows, LANES:], kept)
            ctx_l[mine, layout_lanes] = jnp.where(masks[2], mixed[rows:, LANES:], kept)
        return unused

    lax.fori_loop(0, HEADS // 2, head_pair, 0)
    p_copies = copies_of(((prob, p_out),), sems, base)
    base += 1

    wait_all(w_copies[2:])

    def own_rows(lanes):
        return jnp.concatenate(
            [xs[pl.ds(pack * keys, rows), lanes].astype(F32) for pack in range(packs)], axis=0
        )

    def tail(x, attended, expand, offsets, shrink, turned, b, g, cotangent, active, slope, branch, chunk, hid, unit, inv, delta, sv):
        width = x.shape[1]
        middle = x + attended + b[2:3, :width]
        unit_first, inverse_first = normalized(middle)
        hidden = unit_first * g[0:1, :] + b[3:4, :width]
        hidden_low = hidden.astype(BF16)
        hid[...] = hidden_low
        unit[...] = unit_first
        inv[...] = inverse_first
        feed_forward(hidden_low, expand, offsets, shrink, turned, active, slope, chunk, branch)
        unit_second, inverse_second = normalized(hidden + branch[...] + b[4:5, :width])
        result = unit_second * g[1:2, :] + b[5:6, :width]
        sv[1:2, :] = column_sum(cotangent)
        sv[2:3, :] = column_sum(cotangent * unit_second)
        sum_delta = norm_back(cotangent * g[1:2, :], unit_second, inverse_second)
        delta[...] = sum_delta
        rounded = sum_delta.astype(BF16).astype(F32)
        sv[0:1, :] = column_sum(rounded)
        return result, rounded

    result, rounded = tail(
        own_rows(slice(0, DT)), dot(ctx_t[...], mt[...]), et, ot, st, False, text_bias, gt[...].astype(F32),
        jnp.concatenate([cot_t[pack] for pack in range(packs)], axis=0).astype(F32),
        act_t, slope_t, branch_t, 512, hid_t, unit_t, inv_t, sum_t, sv_t,
    )
    res_t[...] = result.astype(BF16)
    turned[...] = rounded.T.astype(BF16)
    share = DT // 4
    for shard in range(4):
        own = turned[shard * share : (shard + 1) * share, :]
        for block in range(FT // DT):
            grads[shard, pl.ds(block * share, share), :] = dot(
                own, act_t[:, block * DT : (block + 1) * DT]
            ).astype(BF16)
    if grads.shape[1] > S_ROWS:
        grads[:, S_ROWS:, :] = jnp.zeros((4, grads.shape[1] - S_ROWS, DT), BF16)
    out_copies = copies_of(
        in_lines(grads, subs, dp_size, targets), sems, base
    )
    result, unused = tail(
        own_rows(slice(DT, DT + DL)), dot(ctx_l[:, :DL], ml[...]), el, ol, sl, True, layout_bias,
        gl[...].astype(F32),
        jnp.concatenate([cot_l[pack].astype(F32).T for pack in range(packs)], axis=0),
        act_l, slope_l, branch_l, 256, hid_l, unit_l, inv_l, sum_l, sv_l,
    )
    for pack in range(packs):
        res_l[pack] = result[pack * rows : (pack + 1) * rows, :].T.astype(BF16)
    wait_all(kv_copies)
    wait_all(p_copies)
    wait_all(out_copies)


def forward_call(blocks, wt, wl, mt, et, st, ml, el, sl, cot_t, cot_l, bt, gt, ot, bl, gl, ol, packs, rows, dp_size, subs):
    tokens = packs * rows
    lines = total_lines(subs)
    every = tokens * len(blocks)
    keys = rows * len(blocks)
    pairs = HEADS // 2
    outs = (
        shape_of((tokens, DT), BF16),
        shape_of((packs, DL, rows), BF16),
        shape_of((tokens, DT), BF16),
        shape_of((tokens, SLAB), BF16),
        shape_of((every, DT), BF16),
        shape_of((every, SLAB), BF16),
        shape_of((every, DT), BF16),
        shape_of((every, SLAB), BF16),
        shape_of((pairs, packs, 2 * rows, keys), BF16),
        shape_of((tokens, DT), BF16),
        shape_of((tokens, SLAB), BF16),
        shape_of((tokens, DT), BF16),
        shape_of((tokens, DT), F32),
        shape_of((tokens, 1), F32),
        shape_of((tokens, DT), F32),
        shape_of((tokens, FT), BF16),
        shape_of((tokens, DL), BF16),
        shape_of((tokens, DL), F32),
        shape_of((tokens, 1), F32),
        shape_of((tokens, DL), F32),
        shape_of((tokens, FL), BF16),
        shape_of((tokens, FL), BF16),
        shape_of((8, DT), F32),
        shape_of((8, DL), F32),
    ) + pair_shapes(subs)
    out_specs = [VMEM] * 4 + [ANY] * 5 + [VMEM] * 15 + [ANY] * (2 * len(subs))
    scratch = [
        pltpu.VMEM((every, DT + SLAB), BF16),
        pltpu.VMEM((6, SLAB), F32),
        pltpu.VMEM(wt.shape, BF16),
        pltpu.VMEM(wl.shape, BF16),
        pltpu.VMEM(mt.shape, BF16),
        pltpu.VMEM(et.shape, BF16),
        pltpu.VMEM(st.shape, BF16),
        pltpu.VMEM((every, DT), BF16),
        pltpu.VMEM((every, SLAB), BF16),
        pltpu.VMEM((every, DT), BF16),
        pltpu.VMEM((every, SLAB), BF16),
        pltpu.VMEM((pairs, packs, 2 * rows, keys), BF16),
        pltpu.VMEM((packs, rows, keys), F32),
        pltpu.VMEM((tokens, FT), BF16),
        pltpu.VMEM((DT, tokens), BF16),
        pltpu.VMEM((tokens, DT), F32),
        pltpu.VMEM((tokens, DL), F32),
        pltpu.VMEM((4, lines, DT), BF16),
        pltpu.SemaphoreType.DMA((24 + 4 * dp_size * len(subs),)),
    ]
    return pl.pallas_call(
        functools.partial(forward_kernel, packs, rows, dp_size, subs),
        out_shape=outs,
        in_specs=[ANY] * 9 + [VMEM] * 11,
        out_specs=out_specs,
        scratch_shapes=scratch,
        compiler_params=pltpu.CompilerParams(vmem_limit_bytes=FIRST),
        cost_estimate=COST,
        name="forward",
    )(*blocks, wt, wl, mt, et, st, ml, el, sl, cot_t, cot_l, bt, gt, ot, bl, gl, ol)


def middle_kernel(
    dp_size,
    subs,
    hid_t,
    unit_t,
    inv_t,
    sum_t,
    slope_t,
    hid_l,
    unit_l,
    inv_l,
    sum_l,
    slope_l,
    act_l,
    ctx_t,
    ctx_l,
    st_in,
    et_in,
    mt_in,
    sl,
    el,
    ml,
    gt,
    gl,
    after,
    mid_t,
    mid_l,
    dctx_t,
    dctx_l,
    sv_t,
    sv_l,
    so_t,
    so_l,
    *rest,
):
    targets, rest = rest[: 2 * len(subs)], rest[2 * len(subs) :]
    (
        st,
        et,
        mt,
        before_t,
        before_l,
        hidden_t,
        hidden_l,
        turned,
        grads,
        sems,
    ) = rest
    w_copies = copies_of(((st_in, st), (et_in, et), (mt_in, mt)), sems, 0)
    base = 3

    def feed_back(branch_delta, shrink, turned, expand, slope, before, so, hidden_delta, chunk):
        width = slope.shape[1]
        for at in range(width // chunk):
            part = pl.ds(at * chunk, chunk)
            if turned:
                active_delta = dot(branch_delta, shrink[:, part])
            else:
                active_delta = dot_nt(branch_delta, shrink[part, :])
            low = (active_delta * slope[:, part].astype(F32)).astype(BF16)
            before[:, part] = low
            so[:, part] = column_sum(low.astype(F32))
            product = dot_nt(low, expand[:, part])
            if at == 0:
                hidden_delta[...] = product
            else:
                hidden_delta[...] += product

    def front(hidden_delta, total, unit, inv, g, merge, sv):
        delta = total[...] + hidden_delta[...]
        sv[0:1, :] = column_sum(delta * unit[...])
        sv[1:2, :] = column_sum(delta)
        middle = norm_back(delta * g, unit[...], inv[...])
        low = middle.astype(BF16)
        rounded = low.astype(F32)
        sv[2:3, :] = column_sum(rounded)
        back = dot_nt(low, merge).astype(BF16)
        sv[3:4, :] = column_sum(back.astype(F32))
        return middle, rounded.T.astype(BF16), back

    text_delta = sum_t[...].astype(BF16)
    layout_delta = sum_l[...].astype(BF16)
    feed_back(layout_delta, sl, True, el, slope_l, before_l, so_l, hidden_l, 256)
    turned_l = before_l[...].astype(F32).T.astype(BF16)
    grown_l = dot(turned_l, hid_l[...]).astype(BF16)
    shrunk_l = dot(layout_delta.astype(F32).T.astype(BF16), act_l[...]).astype(BF16)
    middle, low_turned, back = front(
        hidden_l, sum_l, unit_l, inv_l, gl[0:1, :].astype(F32), ml[...], sv_l
    )
    for pack in range(mid_l.shape[0]):
        size = mid_l.shape[2]
        mid_l[pack] = middle[pack * size : (pack + 1) * size, :].T
    dctx_l[...] = jnp.zeros_like(dctx_l)
    dctx_l[:, :DL] = back
    merged_l = dot(low_turned, ctx_l[...]).astype(BF16)
    turned[...] = hid_t[...].astype(F32).T.astype(BF16)
    wait_all(w_copies)
    feed_back(text_delta, st, False, et, slope_t, before_t, so_t, hidden_t, 512)
    middle, low_turned, back = front(
        hidden_t, sum_t, unit_t, inv_t, gt[0:1, :].astype(F32), mt[...], sv_t
    )
    mid_t[...] = middle
    dctx_t[...] = back
    for shard in range(4):
        grads[shard, pl.ds(0, DT), :] = dot(
            turned[...], before_t[:, shard * DT : (shard + 1) * DT]
        ).astype(BF16)
        grads[shard, pl.ds(DT, 192), :] = dot(
            low_turned[shard * 192 : (shard + 1) * 192, :], ctx_t[...]
        ).astype(BF16)
    for shard in range(4):
        grads[shard, 960:, :] = jnp.zeros((grads.shape[1] - 960, DT), BF16)
        for at in range(3):
            lanes = slice(at * SLAB, at * SLAB + DL)
            line = shard * DL + at * 64
            grads[shard, 960:1024, lanes] = grown_l[line : line + 64, :]
            line = shard * 48 + at * 16
            grads[shard, 1072:1088, at * SLAB : (at + 1) * SLAB] = merged_l[line : line + 16, :]
        grads[shard, 1024:1072, :] = shrunk_l[shard * 48 : shard * 48 + 48, :]
    wait_all(
        copies_of(in_lines(grads, subs, dp_size, targets), sems, base)
    )


def middle_call(operands, packs, rows, dp_size, subs):
    tokens = packs * rows
    lines = total_lines(subs)
    outs = (
        shape_of((tokens, DT), F32),
        shape_of((packs, DL, rows), F32),
        shape_of((tokens, DT), BF16),
        shape_of((tokens, SLAB), BF16),
        shape_of((8, DT), F32),
        shape_of((8, DL), F32),
        shape_of((1, FT), F32),
        shape_of((1, FL), F32),
    ) + pair_shapes(subs)
    scratch = [
        pltpu.VMEM((FT, DT), BF16),
        pltpu.VMEM((DT, FT), BF16),
        pltpu.VMEM((DT, DT), BF16),
        pltpu.VMEM((tokens, FT), BF16),
        pltpu.VMEM((tokens, FL), BF16),
        pltpu.VMEM((tokens, DT), F32),
        pltpu.VMEM((tokens, DL), F32),
        pltpu.VMEM((DT, tokens), BF16),
        pltpu.VMEM((4, lines, DT), BF16),
        pltpu.SemaphoreType.DMA((8 + 4 * dp_size * len(subs),)),
    ]
    return pl.pallas_call(
        functools.partial(middle_kernel, dp_size, subs),
        out_shape=outs,
        in_specs=[VMEM] * 13 + [ANY] * 3 + [VMEM] * 5 + [ANY],
        out_specs=[VMEM] * 8 + [ANY] * (2 * len(subs)),
        scratch_shapes=scratch,
        compiler_params=pltpu.CompilerParams(vmem_limit_bytes=LIMIT),
        cost_estimate=COST,
        name="middle",
    )(*operands)


def attention_kernel(
    packs,
    rows,
    dp_size,
    subs,
    x0,
    x1,
    x2,
    x3,
    kt_in,
    kl_in,
    vt_in,
    vl_in,
    p_in,
    q_t,
    q_l,
    dctx_t,
    dctx_l,
    ctx_t,
    ctx_l,
    sf_t,
    sf_l,
    sm_t,
    sm_l,
    so_t,
    so_l,
    after,
    joined_t,
    joined_l,
    query_t,
    query_l,
    *rest,
):
    targets, rest = rest[: 2 * len(subs)], rest[2 * len(subs) :]
    (
        xs,
        k_t,
        k_l,
        v_t,
        v_l,
        prob,
        dq_t,
        dq_l,
        dk_l,
        dv_l,
        layout_grads,
        grads,
        smalls,
        sems,
    ) = rest
    blocks = (x0, x1, x2, x3)
    keys = rows * len(blocks)
    kv_copies = copies_of(((kt_in, k_t), (kl_in, k_l), (vt_in, v_t), (vl_in, v_l), (p_in, prob)), sems, 0)
    x_copies = copies_of(
        gather_pairs(blocks, rows, packs, xs), sems, 5
    )
    base = 5 + len(x_copies)
    dq_l[...] = jnp.zeros_like(dq_l)
    dk_l[...] = jnp.zeros_like(dk_l)
    dv_l[...] = jnp.zeros_like(dv_l)
    wait_all(kv_copies)

    def head_pair(pair_at, unused):
        masks = lane_masks(pair_at)
        text_lanes = pl.ds(pl.multiple_of(pair_at * LANES, LANES), LANES)
        layout_lanes = pl.ds(pl.multiple_of(pair_at // 4 * LANES, LANES), LANES)
        for pack in range(packs):
            mine = pl.ds(pack * rows, rows)
            span = pl.ds(pack * keys, keys)
            queries = stacked_heads(q_t[mine, text_lanes], q_l[mine, layout_lanes], masks)
            deltas = stacked_heads(dctx_t[mine, text_lanes], dctx_l[mine, layout_lanes], masks)
            one = jnp.concatenate([ctx_t[mine, text_lanes], ctx_l[mine, layout_lanes]], axis=1)
            contexts = jnp.concatenate([one, one], axis=0).astype(F32)
            products = deltas.astype(F32) * contexts
            layout_mean = jnp.sum(products[:, LANES:], axis=1, keepdims=True)
            both_mean = jnp.sum(products, axis=1, keepdims=True)
            text_values = v_t[span, text_lanes]
            layout_values = v_l[span, layout_lanes]
            both_values = jnp.concatenate([text_values, layout_values], axis=1)
            low = prob[pair_at, pack]
            chance = low.astype(F32)
            both_change = (chance * (dot_nt(deltas, both_values) - both_mean)).astype(BF16)
            layout_change = (
                chance * (dot_nt(deltas[:, LANES:], layout_values) - layout_mean)
            ).astype(BF16)
            from_text = dot(both_change, k_t[span, text_lanes])
            dq_t[mine, text_lanes] = (
                jnp.where(masks[0], from_text[:rows], from_text[rows:]) * 0.125
            ).astype(BF16)
            from_layout = dot(layout_change, k_l[span, layout_lanes]) * 0.25
            kept = dq_l[mine, layout_lanes]
            kept = jnp.where(masks[1], from_layout[:rows], kept)
            dq_l[mine, layout_lanes] = jnp.where(masks[2], from_layout[rows:], kept)
            turned_queries = queries.T
            turned_deltas = deltas.T
            joined_t[text_lanes, span] = dot(turned_queries[:LANES], both_change).astype(BF16)
            dk_l[layout_lanes, span] += dot(turned_queries[LANES:], layout_change)
            value_change = dot(turned_deltas, low)
            text_at = pl.ds(pl.multiple_of(pair_at * LANES + DT, LANES), LANES)
            joined_t[text_at, span] = value_change[:LANES].astype(BF16)
            dv_l[layout_lanes, span] += value_change[LANES:]
        return unused

    lax.fori_loop(0, HEADS // 2, head_pair, 0)
    joined_l[:SLAB, :] = dk_l[...].astype(BF16)
    joined_l[SLAB:, :] = dv_l[...].astype(BF16)
    whole_t = dq_t[...].astype(F32)
    whole_l = dq_l[...]
    low_l = whole_l.astype(BF16)
    query_t[...] = whole_t.T.astype(BF16)
    query_l[...] = whole_l.T.astype(BF16)
    wait_all(x_copies)
    own = jnp.concatenate([xs[pl.ds(pack * keys, rows), :] for pack in range(packs)], axis=0)
    step = 192
    for at in range(3 * DT // step):
        shard, line = at // 3, at % 3 * step
        if at < DT // step:
            product = dot(query_t[at * step : (at + 1) * step, :], own[:, :DT])
        else:
            product = dot(joined_t[at * step - DT : (at + 1) * step - DT, :], xs[:, :DT])
        grads[shard, line : line + step, :] = product.astype(BF16)
    layout_grads[:DL, :] = dot(query_l[:DL, :], own[:, DT:]).astype(BF16)
    layout_grads[DL : 2 * DL, :] = dot(joined_l[:DL, :], xs[:, DT:]).astype(BF16)
    layout_grads[2 * DL :, :] = dot(joined_l[SLAB : SLAB + DL, :], xs[:, DT:]).astype(BF16)
    text_lines = jnp.concatenate(
        [column_sum(whole_t), sm_t[3:4, :], sm_t[2:3, :], sm_t[1:2, :], sf_t[0:2, :], sm_t[0:1, :], sf_t[2:3, :]],
        axis=0,
    )
    layout_lines = jnp.concatenate(
        [
            column_sum(low_l.astype(F32))[:, :DL],
            sm_l[3:4, :], sm_l[2:3, :], sm_l[1:2, :], sf_l[0:2, :], sm_l[0:1, :], sf_l[2:3, :],
        ],
        axis=0,
    )
    for shard in range(4):
        for at in range(3):
            line = shard * 144 + at * 48
            grads[shard, 576:624, at * SLAB : (at + 1) * SLAB] = layout_grads[line : line + 48, :]
        smalls[...] = jnp.zeros_like(smalls)
        share = DT // 4
        smalls[0:8, 0:share] = text_lines[:, shard * share : (shard + 1) * share]
        smalls[8:9, :] = so_t[:, shard * DT : (shard + 1) * DT]
        share = DL // 4
        smalls[0:8, SLAB : SLAB + share] = layout_lines[:, shard * share : (shard + 1) * share]
        share = FL // 4
        smalls[9:10, 0:share] = so_l[:, shard * share : (shard + 1) * share]
        grads[shard, 624:640, :] = smalls[...].astype(BF16)
        if grads.shape[1] > P_ROWS:
            grads[shard, P_ROWS:, :] = jnp.zeros((grads.shape[1] - P_ROWS, DT), BF16)
    wait_all(copies_of(in_lines(grads, subs, dp_size, targets), sems, base))


def attention_call(operands, packs, rows, dp_size, subs):
    tokens = packs * rows
    every = tokens * 4
    lines = total_lines(subs)
    pairs = HEADS // 2
    outs = (
        shape_of((2 * DT, every), BF16),
        shape_of((2 * SLAB, every), BF16),
        shape_of((DT, tokens), BF16),
        shape_of((SLAB, tokens), BF16),
    ) + pair_shapes(subs)
    scratch = [
        pltpu.VMEM((every, DT + SLAB), BF16),
        pltpu.VMEM((every, DT), BF16),
        pltpu.VMEM((every, SLAB), BF16),
        pltpu.VMEM((every, DT), BF16),
        pltpu.VMEM((every, SLAB), BF16),
        pltpu.VMEM((pairs, packs, 2 * rows, 4 * rows), BF16),
        pltpu.VMEM((tokens, DT), BF16),
        pltpu.VMEM((tokens, SLAB), F32),
        pltpu.VMEM((SLAB, every), F32),
        pltpu.VMEM((SLAB, every), F32),
        pltpu.VMEM((3 * DL, SLAB), BF16),
        pltpu.VMEM((4, lines, DT), BF16),
        pltpu.VMEM((16, DT), F32),
        pltpu.SemaphoreType.DMA((24 + 4 * dp_size * len(subs),)),
    ]
    return pl.pallas_call(
        functools.partial(attention_kernel, packs, rows, dp_size, subs),
        out_shape=outs,
        in_specs=[ANY] * 9 + [VMEM] * 12 + [ANY],
        out_specs=[VMEM] * 4 + [ANY] * (2 * len(subs)),
        scratch_shapes=scratch,
        compiler_params=pltpu.CompilerParams(vmem_limit_bytes=LIMIT),
        cost_estimate=COST,
        name="attention_back",
    )(*operands)


def input_kernel(packs, rows, joined_t, joined_l, query_t, query_l, wt, wl, after, give, hold):
    keys = joined_t.shape[1] // packs
    for at in (3, 1, 2, 0):
        target = (hold, give)[at % 2].at[at // 2]
        spans = [slice(pack * keys + at * rows, pack * keys + (at + 1) * rows) for pack in range(packs)]
        text_part = jnp.concatenate([joined_t[:, span] for span in spans], axis=1)
        layout_part = jnp.concatenate([joined_l[:, span] for span in spans], axis=1)
        text_sum = dot(wt[:, DT:], text_part)
        layout_sum = dot(wl[:, SLAB:], layout_part)
        if at == 0:
            text_sum += dot(wt[:, :DT], query_t[...])
            layout_sum += dot(wl[:, :SLAB], query_l[...])
        target[:DT, :] = text_sum.astype(target.dtype)
        target[DT:, :] = layout_sum.astype(target.dtype)


def input_call(joined_t, joined_l, query_t, query_l, wt, wl, after, packs, rows):
    tokens = packs * rows
    return pl.pallas_call(
        functools.partial(input_kernel, packs, rows),
        out_shape=(shape_of((2, DT + DL, tokens), BF16),) * 2,
        in_specs=[VMEM] * 6 + [ANY],
        out_specs=[VMEM] * 2,
        compiler_params=pltpu.CompilerParams(vmem_limit_bytes=LIMIT),
        cost_estimate=COST,
        name="input_back",
    )(joined_t, joined_l, query_t, query_l, wt, wl, after)


def sensitivity_kernel(own, far, mid_t, mid_l, after, out_t, out_l):
    total = own[...].astype(F32) + far[...].astype(F32)
    out_t[...] = mid_t[...] + total[:DT, :].T
    packs, unused, rows = mid_l.shape
    for pack in range(packs):
        out_l[pack] = mid_l[pack] + total[DT:, pack * rows : (pack + 1) * rows]


def sensitivity_call(own, far, mid_t, mid_l, after):
    return pl.pallas_call(
        sensitivity_kernel,
        out_shape=(shape_of(mid_t.shape, F32), shape_of(mid_l.shape, F32)),
        in_specs=[VMEM] * 4 + [ANY],
        out_specs=[VMEM] * 2,
        compiler_params=pltpu.CompilerParams(vmem_limit_bytes=SMALL),
        cost_estimate=COST,
        name="sensitivity",
    )(own, far, mid_t, mid_l, after)


def lines_in_order(dp_size, sources, subs, whole):
    device = lax.axis_index("dp")
    for at, (first, rows, hops, growth) in enumerate(subs):
        half, other = sources[2 * at : 2 * at + 2]
        size = rows // dp_size
        for index in range(dp_size):
            line = position(growth[::-1], 0, index) * size
            source = half if line < rows // 2 else other
            line = line % (rows // 2)
            mark = pl.multiple_of(first + jnp.bitwise_xor(device, index) * size, 16)
            whole[pl.ds(mark, size), :] = source[line : line + size, :].astype(F32)


def shrink_store(whole, out):
    share = DT // 4
    for block in range(FT // DT):
        out[:, block * DT : (block + 1) * DT] = whole[block * share : (block + 1) * share, :]


def expand_store(whole, out, out_merge, out_grow, out_shrink, out_layout_merge):
    out[...] = whole[:DT, :]
    out_merge[...] = whole[DT:960, :]
    grown = jnp.concatenate(
        [whole[960:1024, at * SLAB : at * SLAB + DL] for at in range(3)], axis=0
    )
    out_grow[...] = grown.T
    out_shrink[...] = whole[1024:1072, :]
    out_layout_merge[...] = jnp.concatenate(
        [whole[1072:1088, at * SLAB : at * SLAB + DL] for at in range(3)], axis=0
    )


def project_store(whole, out, out_layout, biases_t, gains_t, offsets_t, biases_l, gains_l, offsets_l):
    out[...] = whole[:576, :]
    out_layout[...] = jnp.concatenate(
        [whole[576:624, at * SLAB : at * SLAB + DL] for at in range(3)], axis=0
    )
    biases_t[...] = whole[624:630, : DT // 4]
    gains_t[...] = whole[630:632, : DT // 4]
    offsets_t[...] = whole[632:633, :].reshape(DT)
    biases_l[...] = whole[624:630, SLAB : SLAB + DL // 4]
    gains_l[...] = whole[630:632, SLAB : SLAB + DL // 4]
    offsets_l[...] = whole[633:634, : FL // 4].reshape(FL // 4)


def final_kernel(store, dp_size, subs, *refs):
    sources, outs, whole = refs[: 2 * len(subs)], refs[2 * len(subs) + 1 : -1], refs[-1]
    lines_in_order(dp_size, sources, subs, whole)
    store(whole, *outs)


def final_call(store, name, sources, after, dp_size, subs, outs):
    return pl.pallas_call(
        functools.partial(final_kernel, store, dp_size, subs),
        out_shape=tuple(shape_of(shape, F32) for shape in outs),
        in_specs=[VMEM] * len(sources) + [ANY],
        out_specs=[VMEM] * len(outs),
        scratch_shapes=[pltpu.VMEM((total_lines(subs), DT), F32)],
        compiler_params=pltpu.CompilerParams(vmem_limit_bytes=SMALL),
        cost_estimate=COST,
        name=name,
    )(*sources, after)


def add_kernel(count, parts, *refs):
    sources, targets = refs[: count * parts], refs[count * parts + 1 :]
    for at, target in enumerate(targets):
        total = sources[at][...].astype(F32)
        for n in range(1, count):
            total += sources[n * parts + at][...].astype(F32)
        target[...] = total.astype(BF16)


def add_call(sources, parts, after):
    lines, width = sources[0].shape
    size = lines // parts
    steps = max(n for n in (1, 2, 3, 4) if size % (16 * n) == 0 and (n == 1 or lines // n >= 256))
    block = size // steps
    specs = [
        pl.BlockSpec((block, width), functools.partial(lambda at, i: (at * steps + i, 0), at))
        for unused in sources
        for at in range(parts)
    ]
    return pl.pallas_call(
        functools.partial(add_kernel, len(sources), parts),
        grid=(steps,),
        out_shape=(shape_of((size, width), BF16),) * parts,
        in_specs=specs + [ANY],
        out_specs=[pl.BlockSpec((block, width), lambda i: (i, 0))] * parts,
        compiler_params=pltpu.CompilerParams(vmem_limit_bytes=SMALL),
        cost_estimate=COST,
        name="add",
    )(*[source for source in sources for unused in range(parts)], after)


def gate_call(arrays, after):
    count = len(arrays)
    return pl.pallas_call(
        lambda *refs: None,
        out_shape=tuple(shape_of(array.shape, array.dtype) for array in arrays),
        in_specs=[ANY] * (count + 1),
        out_specs=[ANY] * count,
        input_output_aliases={at: at for at in range(count)},
        compiler_params=pltpu.CompilerParams(vmem_limit_bytes=SMALL),
        cost_estimate=COST,
        name="gate",
    )(*arrays, after)


def join_kernel(count, *refs):
    sources, target = refs[:count], refs[-1]
    size = sources[0].shape[0]
    for at, source in enumerate(sources):
        target[at * size : (at + 1) * size, :] = source[...]


def join_call(sources, after):
    lines, width = sources[0].shape
    return pl.pallas_call(
        functools.partial(join_kernel, len(sources)),
        out_shape=shape_of((len(sources) * lines, width), BF16),
        in_specs=[VMEM] * len(sources) + [ANY],
        out_specs=VMEM,
        compiler_params=pltpu.CompilerParams(vmem_limit_bytes=SMALL),
        cost_estimate=COST,
        name="join",
    )(*sources, after)


def sent(array, group, index, seq_size, dp_size):
    across = other = 0
    for n, (axis, bit) in enumerate(group):
        if index & (1 << n):
            if axis == "seq":
                across |= bit
            else:
                other |= bit
    if not other:
        return lax.ppermute(array, "seq", [(at, at ^ across) for at in range(seq_size)])
    if not across:
        return lax.ppermute(array, "dp", [(at, at ^ other) for at in range(dp_size)])
    pairs = [
        (d * seq_size + s, (d ^ other) * seq_size + (s ^ across))
        for d in range(dp_size)
        for s in range(seq_size)
    ]
    return lax.ppermute(array, ("dp", "seq"), pairs)


def steps_of(give, hold, hops, growth, send):
    parts = [hold, send(give, (("seq", 1),), 1)]
    for group in hops:
        keep, *sends = yield functools.partial(add_call, parts, 1 << len(group))
        parts = [keep] + [send(array, group, at + 1) for at, array in enumerate(sends)]
    (piece,) = yield functools.partial(add_call, parts, 1)
    gathered = [piece]
    for group in growth:
        if len(gathered) > 1:
            piece = yield functools.partial(join_call, gathered)
        gathered = [piece] + [send(piece, group, at) for at in range(1, 1 << len(group))]
    return gathered


X = ("dp", 1)
Y = ("seq", 2)
Z1 = ("dp", 2)
Z2 = ("dp", 4)


def hops_of(text, extra):
    groups = {"x": (X,), "y": (Y,), "1": (Z1,), "2": (Z2,), "d": (Y, X), "z": (Z1, Z2)}
    return tuple(groups[letter] for letter in text) + extra


SPLIT_S = ((768, "y1x2B"), )
SPLIT_E = ((640, "1xy2B"), (512, "xyzB"), )
SPLIT_P = ((256, "xy12B"), (384, "yxzB"), )
ORDER = "B S0 GE E1 E0 C E1 S0 E0 GP D E1 P0 S0 E0 P1 GX E1 X0 E0 E1 S0 P0 E0 FX E1 S0 P0 E0 P0 P1 S0 P0 E0 P1 P0 S0 P0 P1 FE P1 P1 FS FP"


def local(
    dp_size,
    seq_size,
    text_input,
    layout_input,
    segments,
    text_cotangent,
    layout_cotangent,
    text_project,
    text_biases,
    text_gains,
    text_merge,
    text_expand,
    text_offsets,
    text_shrink,
    layout_project,
    layout_biases,
    layout_gains,
    layout_merge,
    layout_expand,
    layout_offsets,
    layout_shrink,
):
    packs, rows, unused = text_input.shape

    def send(array, group, index):
        return sent(array, group, index, seq_size, dp_size)

    core = (("seq", 1),)
    own, wl, line_t, line_l = prepare_call(
        text_input, layout_input.transpose(0, 2, 1), segments, layout_project, text_offsets, layout_offsets
    )
    far, near = send(own, (Y,), 1), send(own, core, 1)
    blocks = (own, near, far, send(far, core, 1))
    turned_shrink = layout_shrink.T

    bits = [1 << at for at in range((dp_size - 1).bit_length())]
    extra = tuple((("dp", bit),) for bit in bits[3:])
    growths = {
        "B": tuple(reversed(extra)) + ((Z2,), (Z1,), (X,)),
        "D": tuple(reversed(extra)) + ((Z1, Z2), (X,)),
    }
    subs = {
        name: sub_chunks(count, [(share, hops_of(text[:-1], extra), growths[text[-1]]) for share, text in split], dp_size)
        for name, count, split in (
            ("S", S_ROWS, SPLIT_S),
            ("E", E_ROWS, SPLIT_E),
            ("P", P_ROWS, SPLIT_P),
        )
    }
    reductions = {}
    calls = {}
    halves = {}
    values = {}
    token = None

    def begin(name, pairs):
        for at, (first, count, hops, growth) in enumerate(subs[name]):
            steps = steps_of(pairs[2 * at], pairs[2 * at + 1], hops, growth, send)
            reductions[name + str(at)] = steps
            calls[name + str(at)] = next(steps)

    def forward(after):
        (
            res_t, res_l, q_t, q_l, kt, kl, vt, vl, p, ctx_t, ctx_l,
            hid_t, unit_t, inv_t, sum_t, slope_t,
            hid_l, unit_l, inv_l, sum_l, slope_l, act_l, sf_t, sf_l,
            *pairs,
        ) = forward_call(
            blocks, text_project, wl, text_merge, text_expand, text_shrink,
            layout_merge, layout_expand, turned_shrink,
            text_cotangent, layout_cotangent.transpose(0, 2, 1),
            text_biases, text_gains, line_t, layout_biases, layout_gains,
            line_l, packs, rows, dp_size, subs["S"],
        )
        begin("S", pairs)
        values.update(
            results=(res_t, res_l),
            tail=(
                hid_t, unit_t, inv_t, sum_t, slope_t, hid_l, unit_l, inv_l, sum_l, slope_l, act_l,
                ctx_t, ctx_l,
            ),
            attended=(kt, kl, vt, vl, p, q_t, q_l),
            contexts=(ctx_t, ctx_l),
            first_sums=(sf_t, sf_l),
        )
        return sf_t

    def middle(after):
        mid_t, mid_l, dctx_t, dctx_l, sm_t, sm_l, so_t, so_l, *pairs = middle_call(
            (
                *values["tail"], text_shrink, text_expand, text_merge, turned_shrink,
                layout_expand, layout_merge, text_gains, layout_gains, after,
            ),
            packs, rows, dp_size, subs["E"],
        )
        values["E pairs"] = pairs
        values.update(
            middles=(mid_t, mid_l), deltas=(dctx_t, dctx_l), second_sums=(sm_t, sm_l, so_t, so_l)
        )
        return sm_t

    def attention(after):
        joined_t, joined_l, query_t, query_l, *pairs = attention_call(
            (
                *blocks, *values["attended"], *values["deltas"],
                *values["contexts"], *values["first_sums"], *values["second_sums"], after,
            ),
            packs, rows, dp_size, subs["P"],
        )
        values["P pairs"] = pairs
        values.update(joined=(joined_t, joined_l, query_t, query_l))
        return query_l

    def inputs(after):
        give, hold = input_call(*values["joined"], text_project, wl, after, packs, rows)
        values["X pairs"] = [give, hold]
        return hold

    def inputs_gate(after):
        give, hold = gate_call(values["X pairs"], after)
        lines = 2 * (DT + DL)
        values.update(inputs=[hold.reshape(lines, -1), send(give, core, 1).reshape(lines, -1)])
        return hold

    def gate(name):
        def call(after):
            pairs = gate_call(values[name + " pairs"], after)
            begin(name, pairs)
            return pairs[1]

        return call

    def inputs_add(after):
        own, onward = add_call(values["inputs"], 2, after)
        values.update(onward=(own, send(onward, (Y,), 1)))
        return own

    def inputs_end(after):
        values.update(sens=sensitivity_call(*values["onward"], *values["middles"], after))
        return values["sens"][1]

    def end(name, store, label, outs):
        def call(after):
            sources = [array for at in range(len(subs[name])) for array in halves[name + str(at)]]
            values[name] = final_call(
                store, label, sources, after, dp_size, subs[name], outs
            )
            return values[name][-1]

        return call

    kernels = {
        "A": forward,
        "B": middle,
        "C": attention,
        "D": inputs,
        "GE": gate("E"),
        "GP": gate("P"),
        "GX": inputs_gate,
        "X0": inputs_add,
        "FX": inputs_end,
        "FS": end("S", shrink_store, "shrink_out", [(DT // 4, FT)]),
        "FE": end(
            "E", expand_store, "expand_out",
            [(DT, DT), (DT // 4, DT), (DL, DL), (DL // 4, FL), (DL // 4, DL)],
        ),
        "FP": end(
            "P", project_store, "project_out",
            [
                (576, DT), (144, DL), (6, DT // 4), (2, DT // 4), (DT,),
                (6, DL // 4), (2, DL // 4), (FL // 4,),
            ],
        ),
    }

    def advance(name, after):
        outs = calls[name](after)
        try:
            calls[name] = reductions[name].send(outs)
        except StopIteration as stop:
            halves[name] = stop.value
            del calls[name]
        return outs[0] if isinstance(outs, (tuple, list)) else outs

    def finish(name, after):
        for at in range(len(subs[name])):
            while name + str(at) in calls:
                after = advance(name + str(at), after)
        return after

    token = forward(None)
    for label in ORDER.split():
        if label in kernels:
            if label[0] == "F" and label[1] in subs:
                token = finish(label[1], token)
            token = kernels[label](token)
        elif label in calls:
            token = advance(label, token)

    res_t, res_l = values["results"]
    sens_t, sens_l = values["sens"]
    (shrink_t,) = values["S"]
    expand_t, merge_t, expand_l, shrink_l, merge_l = values["E"]
    project_t, project_l, biases_t, gains_t, offsets_t, biases_l, gains_l, offsets_l = values["P"]
    return (
        res_t.reshape(packs, rows, DT),
        res_l.transpose(0, 2, 1),
        sens_t.reshape(packs, rows, DT),
        sens_l.transpose(0, 2, 1),
        project_t.T,
        biases_t,
        gains_t,
        merge_t.T,
        expand_t,
        offsets_t,
        shrink_t.T,
        project_l.T,
        biases_l,
        gains_l,
        merge_l.T,
        expand_l,
        offsets_l,
        shrink_l.T,
    )


def solution(mesh):
    rows = P("dp", "seq", None)
    columns = P(None, "seq")
    in_specs = (rows, rows, P("dp", "seq"), rows, rows) + (P(),) * 14
    out_specs = (
        (rows,) * 4 + (columns,) * 5 + (P("seq"),) + (columns,) * 6 + (P("seq"),) + (columns,)
    )
    body = functools.partial(local, mesh.shape["dp"], mesh.shape["seq"])
    return jax.shard_map(body, mesh=mesh, in_specs=in_specs, out_specs=out_specs, check_vma=False)
```

time: 318 us -> 244 us (0.77)
  waiting for transfers between devices: 149 us -> 75.9 us
  other arithmetic: 35.7 us -> 0 us
  Pallas kernels: 64.3 us -> 96.8 us
  starting transfers between devices: 30.9 us -> 55.3 us
  local copies, waits for them, and re-layouts: 35.3 us -> 13.9 us
    ppermute x33 -> x47, waiting for transfers between devices: 149 us -> 75.9 us  [the longest x32 56.3 us: sent(): lax.ppermute(array, 'dp', [(at, at ^ other) for at in range(dp_size)])]
    pallas_call x6 -> x44, Pallas kernels: 59.3 us -> 88 us  [the longest x1 26.2 us: forward_call(): pl.pallas_call(functools.partial(forward_kernel, packs, rows, dp_size, su...]
    convert_element_type x17 -> x0, other arithmetic: 27.7 us -> none  [the longest x9 18.5 us: summed(): send.astype(BF16)]
    ppermute x33 -> x47, starting transfers between devices: 30.9 us -> 55.3 us  [the longest x32 43.6 us: sent(): lax.ppermute(array, 'dp', [(at, at ^ other) for at in range(dp_size)])]
    unnamed x160 -> x56, local copies, waits for them, and re-layouts: 28.5 us -> 13.9 us
    concatenate x10 -> x0, other arithmetic: 8.04 us -> none  [the longest x9 6.9 us: summed(): jnp.concatenate([total, lax.ppermute(total, 'dp', partners(dp_size, bit))...]
    pallas_call x1, Pallas kernels: 3.78 us -> 7.54 us  [input_call(): pl.pallas_call(functools.partial(input_kernel, packs, rows), out_shape=(s...]
  transfers between devices with their start and end apart: 33 -> 47, of which waited for: 16 -> 21; matrix products, arithmetic and copies ran while one was open for 13% -> 0% of each run, Pallas kernels for 2% -> 25%
where the time goes in v2:
time: 244 us; the launch traced here: 243 us
  Pallas kernels  96.8 us (40%)
  waiting for transfers between devices  75.9 us (31%)
  starting transfers between devices  55.3 us (23%)
  local copies, waits for them, and re-layouts  13.9 us (6%)
    ppermute x32, waiting for transfers between devices, sent(): lax.ppermute(array, 'dp', [(at, at ^ other) for at in range(dp_size)])  56.3 us
    ppermute x32, starting transfers between devices, sent(): lax.ppermute(array, 'dp', [(at, at ^ other) for at in range(dp_size)])  43.6 us
    pallas_call x1, Pallas kernels, forward_call(): pl.pallas_call(functools.partial(forward_kernel, packs, rows, dp_size, su...  26.2 us
    ppermute x15, waiting for transfers between devices, sent(): lax.ppermute(array, 'seq', [(at, at ^ across) for at in range(seq_size)])  19.6 us
    pallas_call x1, Pallas kernels, attention_call(): pl.pallas_call(functools.partial(attention_kernel, packs, rows, dp_size,...  19.2 us
    pallas_call x24, Pallas kernels, add_call(): pl.pallas_call(functools.partial(add_kernel, len(sources), parts), grid=(...  17.7 us
    pallas_call x1, Pallas kernels, middle_call(): pl.pallas_call(functools.partial(middle_kernel, dp_size, subs), out_shape...  17.4 us
    unnamed x56, local copies, waits for them, and re-layouts  13.9 us
  transfers between devices with their start and end apart: 47, of which 21 were waited for; matrix products, arithmetic and copies ran while one was open for 0% of the time, Pallas kernels for 25%

profile of v2, /device:TPU:0, one launch (start us, length us, event | category | flops | bytes accessed | tf_op | source)
XLA Modules:
  0.0 243.0 jit_solution(2189740858562329931)
XLA Ops:
  0.7 2.2 prepare.1
  2.9 3.0 %collective-permute-start.1 = (bf16[2,128,1024]{2,1,0:T(8,128)(2,1)}, bf16[2,128,1024]{2,1,0:T(8,128)(2,1)S(1)}, u32[]{:S(2)}, u32[]{:S(2)}) collective-permute-start(bf16[2,128,1024]{2,1,0:T(8,128)(2,1)} %get-tuple-element.137.x0), channel_id=1, source_target_pairs={{0,2},{1,3},{2,0},{3,1},{4,6},{5,7},{6,4},{7,5},{8,10},{9,11},{10,... | collective-permute-start | bytes 1572872 | tf_op jit(solution)/shard_map/ppermute | solution.py:1024
  5.8 12.1 %collective-permute-done.1.x2 = bf16[2,128,1024]{2,1,0:T(8,128)(2,1)S(1)} collective-permute-done((bf16[2,128,1024]{2,1,0:T(8,128)(2,1)}, bf16[2,128,1024]{2,1,0:T(8,128)(2,1)S(1)}, u32[]{:S(2)}, u32[]{:S(2)}) %collective-permute-start.1) | collective-permute-done | bytes 524320 | tf_op jit(solution)/shard_map/ppermute | solution.py:1024
  18.0 1.9 collective-permute-done.2.x3
  20.7 26.2 %forward.1 = (bf16[256,768]{1,0:T(8,128)(2,1)}, bf16[2,192,128]{2,1,0:T(8,128)(2,1)}, bf16[256,768]{1,0:T(8,128)(2,1)}, bf16[256,256]{1,0:T(8,128)(2,1)}, bf16[1...) custom-call(bf16[2,128,1024]{2,1,0:T(8,128)(2,1)} %get-tuple-element, ...), custom_call_target="tpu_custom_call" | custom-call | flops 1 | bytes 1 | tf_op jit(solution)/shard_map/forward/pallas_call | solution.py:472
  47.0 17.4 %middle.1 = (f32[256,768]{1,0:T(8,128)}, f32[2,192,128]{2,1,0:T(8,128)}, bf16[256,768]{1,0:T(8,128)(2,1)}, bf16[256,256]{1,0:T(8,128)(2,1)}, f32[8,768]{1,0:T(8,...) custom-call(bf16[256,768]{1,0:T(8,128)(2,1)} %get-tuple-element.150., ...), custom_call_target="tpu_custom_call" | custom-call | flops 1 | bytes 1 | tf_op jit(solution)/shard_map/middle/pallas_call | solution.py:633
  65.2 4.6 %add.24 = (bf16[768,768]{1,0:T(8,128)(2,1)S(1)}, bf16[768,768]{1,0:T(8,128)(2,1)}) custom-call(bf16[1536,768]{1,0:T(8,128)(2,1)S(1)} %copy-done.9, bf16[1536,768]{1,0:T(8,128)(2,1)S(1)} %copy-done.9, bf16[1536,768]{1,0:T(8,128)(2,1)} %collective-permute-done.3.refs_2_.refs_3_, bf16[1536,768]{1,0:T(8,128)(2,1)} %collective-permute-done.3.refs_2_.refs_3_, ...), custom_call_target="tpu_custom_call" | custom-call | flops 1 | bytes 1 | tf_op jit(solution)/shard_map/add/pallas_call | solution.py:969
  70.4 1.8 collective-permute-start.7
  72.2 4.0 %collective-permute-done.5.refs_2_.refs_3_ = bf16[1024,768]{1,0:T(8,128)(2,1)S(1)} collective-permute-done((bf16[1024,768]{1,0:T(8,128)(2,1)S(1)}, bf16[1024,768]{1,0:T(8,128)(2,1)S(1)}, u32[]{:S(2)}, u32[]{:S(2)}) %collective-permute-start.5) | collective-permute-done | bytes 1572896 | tf_op jit(solution)/shard_map/ppermute | solution.py:1024
  76.2 1.6 add.25
  77.7 1.6 add.26
  79.4 0.9 copy-done.10
  80.3 1.8 collective-permute-start.6
  82.1 1.5 collective-permute-start.8
  83.6 19.2 %attention_back.1 = (bf16[1536,1024]{1,0:T(8,128)(2,1)}, bf16[512,1024]{1,0:T(8,128)(2,1)}, bf16[768,256]{1,0:T(8,128)(2,1)}, bf16[256,256]{1,0:T(8,128)(2,1)}, ...) custom-call(bf16[2,128,1024]{2,1,0:T(8,128)(2,1)} %get-tuple-element.1, ...), custom_call_target="tpu_custom_call" | custom-call | flops 1 | bytes 1 | tf_op jit(solution)/shard_map/attention_back/pallas_call | solution.py:825
  103.7 1.1 copy-done.15
  106.5 1.4 add.28
  108.0 2.2 add.29
  113.4 1.5 collective-permute-start.13
  114.9 7.5 %input_back.1 = (bf16[2,960,256]{2,1,0:T(8,128)(2,1)}, bf16[2,960,256]{2,1,0:T(8,128)(2,1)}) custom-call(bf16[1536,1024]{1,0:T(8,128)(2,1)} %get-tuple-element.184.joined_t, bf16[512,1024]{1,0:T(8,128)(2,1)} %get-tuple-element.185.joined_l, bf16[768,256]{1,0:T(8,128)(2,1)} %get-tuple-element.186.query_t, ...), custom_call_target="tpu_custom_call" | custom-call | flops 1 | bytes 1 | tf_op jit(solution)/shard_map/input_back/pallas_call | solution.py:855
  122.5 1.6 collective-permute-done.13.refs_4_.refs_5_.refs_6_.refs_7_
  124.1 1.2 copy-done.1
  125.4 1.0 copy-done.6
  126.4 1.3 add.31
  128.0 1.2 add.32
  129.2 1.2 add.33
  131.9 1.4 collective-permute-start.15
  133.3 2.6 %collective-permute-start.16 = (bf16[64,768]{1,0:T(8,128)(2,1)S(1)}, bf16[64,768]{1,0:T(8,128)(2,1)S(1)}, u32[]{:S(2)}, u32[]{:S(2)}) collective-permute-start(bf16[64,768]{1,0:T(8,128)(2,1)S(1)} %get-tuple-element.215), channel_id=1, source_target_pairs={{0,16},{4,20},{8,24},{12,28},{16,0},{20,4},{24,8},{28,12},{1,17},{... | collective-permute-start | bytes 294920 | tf_op jit(solution)/shard_map/ppermute | solution.py:1026
  136.3 1.5 collective-permute-start.19
  137.8 6.3 %collective-permute-done.16.refs_2_ = bf16[64,768]{1,0:T(8,128)(2,1)S(1)} collective-permute-done((bf16[64,768]{1,0:T(8,128)(2,1)S(1)}, bf16[64,768]{1,0:T(8,128)(2,1)S(1)}, u32[]{:S(2)}, u32[]{:S(2)}) %collective-permute-start.16) | collective-permute-done | bytes 98336 | tf_op jit(solution)/shard_map/ppermute | solution.py:1026
  144.7 1.6 collective-permute-start.18
  146.3 1.5 collective-permute-start.21
  148.8 3.1 %collective-permute-start.23 = (bf16[64,768]{1,0:T(8,128)(2,1)S(1)}, bf16[64,768]{1,0:T(8,128)(2,1)S(1)}, u32[]{:S(2)}, u32[]{:S(2)}) collective-permute-start(bf16[64,768]{1,0:T(8,128)(2,1)S(1)} %add.35.refs_4_.refs_0_), channel_id=1, source_target_pairs={{0,16},{4,20},{8,24},{12,28},{16,0},{20,4},{24,8},{28,12},{1,17},{... | collective-permute-start | bytes 294920 | tf_op jit(solution)/shard_map/ppermute | solution.py:1026
  152.0 2.5 %collective-permute-done.23.refs_1_ = bf16[64,768]{1,0:T(8,128)(2,1)S(1)} collective-permute-done((bf16[64,768]{1,0:T(8,128)(2,1)S(1)}, bf16[64,768]{1,0:T(8,128)(2,1)S(1)}, u32[]{:S(2)}, u32[]{:S(2)}) %collective-permute-start.23) | collective-permute-done | bytes 98336 | tf_op jit(solution)/shard_map/ppermute | solution.py:1026
  154.5 3.0 %collective-permute-start.20 = (bf16[80,768]{1,0:T(8,128)(2,1)S(1)}, bf16[80,768]{1,0:T(8,128)(2,1)S(1)}, u32[]{:S(2)}, u32[]{:S(2)}) collective-permute-start(bf16[80,768]{1,0:T(8,128)(2,1)S(1)} %get-tuple-element.223), channel_id=1, source_target_pairs={{0,16},{4,20},{8,24},{12,28},{16,0},{20,4},{24,8},{28,12},{1,17},{... | collective-permute-start | bytes 368648 | tf_op jit(solution)/shard_map/ppermute | solution.py:1026
  157.6 4.8 %collective-permute-done.22.refs_2_.refs_3_ = bf16[192,768]{1,0:T(8,128)(2,1)S(1)} collective-permute-done((bf16[192,768]{1,0:T(8,128)(2,1)S(1)}, bf16[192,768]{1,0:T(8,128)(2,1)S(1)}, u32[]{:S(2)}, u32[]{:S(2)}) %collective-permute-start.22) | collective-permute-done | bytes 294944 | tf_op jit(solution)/shard_map/ppermute | solution.py:1026
  162.4 2.3 collective-permute-start.26
  165.5 1.2 collective-permute-start.25
  166.7 1.8 collective-permute-start.28
  168.5 1.2 sensitivity.1
  169.7 1.2 collective-permute-done.26.refs_1_
  171.9 5.1 %collective-permute-done.25.refs_1_ = bf16[96,768]{1,0:T(8,128)(2,1)S(1)} collective-permute-done((bf16[96,768]{1,0:T(8,128)(2,1)S(1)}, bf16[96,768]{1,0:T(8,128)(2,1)S(1)}, u32[]{:S(2)}, u32[]{:S(2)}) %collective-permute-start.25) | collective-permute-done | bytes 147488 | tf_op jit(solution)/shard_map/ppermute | solution.py:1026
  177.0 1.3 collective-permute-done.28.refs_1_
  178.4 2.0 collective-permute-start.27
  180.4 1.1 collective-permute-start.30
  181.6 7.2 %collective-permute-done.27.refs_2_.refs_3_ = bf16[64,768]{1,0:T(8,128)(2,1)S(1)} collective-permute-done((bf16[64,768]{1,0:T(8,128)(2,1)S(1)}, bf16[64,768]{1,0:T(8,128)(2,1)S(1)}, u32[]{:S(2)}, u32[]{:S(2)}) %collective-permute-start.27) | collective-permute-done | bytes 98336 | tf_op jit(solution)/shard_map/ppermute | solution.py:1026
  188.8 2.1 collective-permute-start.29
  191.0 1.4 collective-permute-start.33
  192.4 1.4 collective-permute-done.29.refs_1_
  193.9 2.9 %collective-permute-start.42 = (bf16[320,768]{1,0:T(8,128)(2,1)S(1)}, bf16[320,768]{1,0:T(8,128)(2,1)S(1)}, u32[]{:S(2)}, u32[]{:S(2)}) collective-permute-start(bf16[320,768]{1,0:T(8,128)(2,1)S(1)} %join.14.refs_8_.refs_0_), channel_id=1, source_target_pairs={{0,4},{4,0},{8,12},{12,8},{16,20},{20,16},{24,28},{28,24},{1,5},{5... | collective-permute-start | bytes 1474568 | tf_op jit(solution)/shard_map/ppermute | solution.py:1026
  197.6 2.9 %collective-permute-start.32 = (bf16[32,768]{1,0:T(8,128)(2,1)S(1)}, bf16[32,768]{1,0:T(8,128)(2,1)S(1)}, u32[]{:S(2)}, u32[]{:S(2)}) collective-permute-start(bf16[32,768]{1,0:T(8,128)(2,1)S(1)} %add.45.refs_2_.refs_0_), channel_id=1, source_target_pairs={{0,16},{4,20},{8,24},{12,28},{16,0},{20,4},{24,8},{28,12},{1,17},{... | collective-permute-start | bytes 147464 | tf_op jit(solution)/shard_map/ppermute | solution.py:1026
  201.0 1.8 collective-permute-done.32.refs_1_
  202.9 4.2 %collective-permute-start.35 = (bf16[64,768]{1,0:T(8,128)(2,1)S(1)}, bf16[64,768]{1,0:T(8,128)(2,1)S(1)}, u32[]{:S(2)}, u32[]{:S(2)}) collective-permute-start(bf16[64,768]{1,0:T(8,128)(2,1)S(1)} %join.15.refs_2_.refs_0_), channel_id=1, source_target_pairs={{0,8},{4,12},{8,0},{12,4},{16,24},{20,28},{24,16},{28,20},{1,9},{5... | collective-permute-start | bytes 294920 | tf_op jit(solution)/shard_map/ppermute | solution.py:1026
  207.1 1.2 collective-permute-start.39
  208.3 4.6 %collective-permute-done.38.refs_1_ = bf16[48,768]{1,0:T(8,128)(2,1)S(1)} collective-permute-done((bf16[48,768]{1,0:T(8,128)(2,1)S(1)}, bf16[48,768]{1,0:T(8,128)(2,1)S(1)}, u32[]{:S(2)}, u32[]{:S(2)}) %collective-permute-start.38) | collective-permute-done | bytes 73760 | tf_op jit(solution)/shard_map/ppermute | solution.py:1026
  213.5 5.6 %collective-permute-done.40.refs_3_ = bf16[48,768]{1,0:T(8,128)(2,1)S(1)} collective-permute-done((bf16[48,768]{1,0:T(8,128)(2,1)S(1)}, bf16[48,768]{1,0:T(8,128)(2,1)S(1)}, u32[]{:S(2)}, u32[]{:S(2)}) %collective-permute-start.40) | collective-permute-done | bytes 73760 | tf_op jit(solution)/shard_map/ppermute | solution.py:1026
  219.9 2.0 expand_out.1
  222.0 2.5 %collective-permute-done.41.refs_1_ = bf16[48,768]{1,0:T(8,128)(2,1)S(1)} collective-permute-done((bf16[48,768]{1,0:T(8,128)(2,1)S(1)}, bf16[48,768]{1,0:T(8,128)(2,1)S(1)}, u32[]{:S(2)}, u32[]{:S(2)}) %collective-permute-start.41) | collective-permute-done | bytes 73760 | tf_op jit(solution)/shard_map/ppermute | solution.py:1026
  225.4 5.1 %collective-permute-done.44.refs_1_ = bf16[96,768]{1,0:T(8,128)(2,1)S(1)} collective-permute-done((bf16[96,768]{1,0:T(8,128)(2,1)S(1)}, bf16[96,768]{1,0:T(8,128)(2,1)S(1)}, u32[]{:S(2)}, u32[]{:S(2)}) %collective-permute-start.44) | collective-permute-done | bytes 147488 | tf_op jit(solution)/shard_map/ppermute | solution.py:1026
  231.0 1.6 collective-permute-start.37
  232.6 1.7 shrink_out.1.refs_4_
  234.4 5.4 %collective-permute-done.37.refs_1_ = bf16[128,768]{1,0:T(8,128)(2,1)S(1)} collective-permute-done((bf16[128,768]{1,0:T(8,128)(2,1)S(1)}, bf16[128,768]{1,0:T(8,128)(2,1)S(1)}, u32[]{:S(2)}, u32[]{:S(2)}) %collective-permute-start.37) | collective-permute-done | bytes 196640 | tf_op jit(solution)/shard_map/ppermute | solution.py:1026
  239.8 1.7 copy-done.8
  241.5 1.5 project_out.1
  (132 shorter events, 18.2 us)
Async XLA Ops:
  2.9 15.1 %collective-permute-start.1 = (bf16[2,128,1024]{2,1,0:T(8,128)(2,1)}, bf16[2,128,1024]{2,1,0:T(8,128)(2,1)S(1)}, u32[]{:S(2)}, u32[]{:S(2)}) collective-permute-start(bf16[2,128,1024]{2,1,0:T(8,128)(2,1)} %get-tuple-element.137.x0), channel_id=1, source_target_pairs={{0,2},{1,3},{2,0},{3,1},{4,6},{5,7},{6,4},{7,5},{8,10},{9,11},{10,... | collective-permute-start | bytes 1572872 | tf_op jit(solution)/shard_map/ppermute | solution.py:1024
  5.8 12.1 %collective-permute-start = (bf16[2,128,1024]{2,1,0:T(8,128)(2,1)}, bf16[2,128,1024]{2,1,0:T(8,128)(2,1)S(1)}, u32[]{:S(2)}, u32[]{:S(2)}) collective-permute-start(bf16[2,128,1024]{2,1,0:T(8,128)(2,1)} %get-tuple-element.137.x0), channel_id=1, source_target_pairs={{0,1},{1,0},{2,3},{3,2},{4,5},{5,4},{6,7},{7,6},{8,9},{9,8},{10,11... | collective-permute-start | bytes 1572872 | tf_op jit(solution)/shard_map/ppermute | solution.py:1024
  18.0 1.9 copy-start.25
  18.0 1.9 collective-permute-start.2
  18.0 1.9 copy-start.26
  46.8 17.6 %collective-permute-start.3 = (bf16[1536,768]{1,0:T(8,128)(2,1)}, bf16[1536,768]{1,0:T(8,128)(2,1)}, u32[]{:S(2)}, u32[]{:S(2)}) collective-permute-start(bf16[1536,768]{1,0:T(8,128)(2,1)} %get-tuple-element.176), channel_id=1, source_target_pairs={{0,1},{1,0},{2,3},{3,2},{4,5},{5,4},{6,7},{7,6},{8,9},{9,8},{10,11... | collective-permute-start | bytes 7077896 | tf_op jit(solution)/shard_map/ppermute | solution.py:1024
  47.0 17.4 %copy-start.9 = (bf16[1536,768]{1,0:T(8,128)(2,1)S(1)}, bf16[1536,768]{1,0:T(8,128)(2,1)}, u32[]{:S(2)}) copy-start(bf16[1536,768]{1,0:T(8,128)(2,1)} %get-tuple-element.175.refs_0_.refs_1_) | copy-start | bytes 7077892
  65.2 4.6 %copy-start = (bf16[1280,768]{1,0:T(8,128)(2,1)S(1)}, bf16[1280,768]{1,0:T(8,128)(2,1)}, u32[]{:S(2)}) copy-start(bf16[1280,768]{1,0:T(8,128)(2,1)} %get-tuple-element.172.refs_1_) | copy-start | bytes 5898244
  65.2 4.6 %copy-start.3 = (bf16[1024,768]{1,0:T(8,128)(2,1)S(1)}, bf16[1024,768]{1,0:T(8,128)(2,1)}, u32[]{:S(2)}) copy-start(bf16[1024,768]{1,0:T(8,128)(2,1)} %get-tuple-element.174.refs_3_) | copy-start | bytes 4718596
  65.2 4.6 %copy-start.16 = (bf16[1280,768]{1,0:T(8,128)(2,1)S(1)}, bf16[1280,768]{1,0:T(8,128)(2,1)}, u32[]{:S(2)}) copy-start(bf16[1280,768]{1,0:T(8,128)(2,1)} %get-tuple-element.171.refs_0_) | copy-start | bytes 5898244
  65.2 4.6 %copy-start.17 = (bf16[1024,768]{1,0:T(8,128)(2,1)S(1)}, bf16[1024,768]{1,0:T(8,128)(2,1)}, u32[]{:S(2)}) copy-start(bf16[1024,768]{1,0:T(8,128)(2,1)} %get-tuple-element.173.refs_2_) | copy-start | bytes 4718596
  69.9 7.9 %collective-permute-start.4 = (bf16[1280,768]{1,0:T(8,128)(2,1)S(1)}, bf16[1280,768]{1,0:T(8,128)(2,1)S(1)}, u32[]{:S(2)}, u32[]{:S(2)}) collective-permute-start(bf16[1280,768]{1,0:T(8,128)(2,1)S(1)} %get-tuple-element.179), channel_id=1, source_target_pairs={{0,1},{1,0},{2,3},{3,2},{4,5},{5,4},{6,7},{7,6},{8,9},{9,8},{10,11... | collective-permute-start | bytes 5898248 | tf_op jit(solution)/shard_map/ppermute | solution.py:1024
  70.3 5.8 %collective-permute-start.5 = (bf16[1024,768]{1,0:T(8,128)(2,1)S(1)}, bf16[1024,768]{1,0:T(8,128)(2,1)S(1)}, u32[]{:S(2)}, u32[]{:S(2)}) collective-permute-start(bf16[1024,768]{1,0:T(8,128)(2,1)S(1)} %get-tuple-element.181), channel_id=1, source_target_pairs={{0,1},{1,0},{2,3},{3,2},{4,5},{5,4},{6,7},{7,6},{8,9},{9,8},{10,11... | collective-permute-start | bytes 4718600 | tf_op jit(solution)/shard_map/ppermute | solution.py:1024
  70.4 36.1 %collective-permute-start.7 = (bf16[768,768]{1,0:T(8,128)(2,1)}, bf16[768,768]{1,0:T(8,128)(2,1)S(1)}, u32[]{:S(2)}, u32[]{:S(2)}) collective-permute-start(bf16[768,768]{1,0:T(8,128)(2,1)} %get-tuple-element.193), channel_id=1, source_target_pairs={{0,2},{1,3},{2,0},{3,1},{4,6},{5,7},{6,4},{7,5},{8,10},{9,11},{10,... | collective-permute-start | bytes 3538952 | tf_op jit(solution)/shard_map/ppermute | solution.py:1024
  80.3 27.7 %collective-permute-start.6 = (bf16[640,768]{1,0:T(8,128)(2,1)}, bf16[640,768]{1,0:T(8,128)(2,1)}, u32[]{:S(2)}, u32[]{:S(2)}) collective-permute-start(bf16[640,768]{1,0:T(8,128)(2,1)} %get-tuple-element.192), channel_id=1, source_target_pairs={{0,8},{4,12},{8,0},{12,4},{16,24},{20,28},{24,16},{28,20},{1,9},{5... | collective-permute-start | bytes 2949128 | tf_op jit(solution)/shard_map/ppermute | solution.py:1026
  82.1 20.7 %collective-permute-start.8 = (bf16[512,768]{1,0:T(8,128)(2,1)}, bf16[512,768]{1,0:T(8,128)(2,1)S(1)}, u32[]{:S(2)}, u32[]{:S(2)}) collective-permute-start(bf16[512,768]{1,0:T(8,128)(2,1)} %get-tuple-element.194), channel_id=1, source_target_pairs={{0,4},{4,0},{8,12},{12,8},{16,20},{20,16},{24,28},{28,24},{1,5},{5... | collective-permute-start | bytes 2359304 | tf_op jit(solution)/shard_map/ppermute | solution.py:1026
  106.5 1.5 copy-start.11
  108.0 2.2 copy-start.4
  108.0 2.2 copy-start.7
  111.9 18.5 %collective-permute-start.9 = (bf16[768,768]{1,0:T(8,128)(2,1)}, bf16[768,768]{1,0:T(8,128)(2,1)S(1)}, u32[]{:S(2)}, u32[]{:S(2)}) collective-permute-start(bf16[768,768]{1,0:T(8,128)(2,1)} %get-tuple-element.202), channel_id=1, source_target_pairs={{0,1},{1,0},{2,3},{3,2},{4,5},{5,4},{6,7},{7,6},{8,9},{9,8},{10,11... | collective-permute-start | bytes 3538952 | tf_op jit(solution)/shard_map/ppermute | solution.py:1024
  111.9 13.5 %collective-permute-start.12 = (bf16[512,768]{1,0:T(8,128)(2,1)}, bf16[512,768]{1,0:T(8,128)(2,1)}, u32[]{:S(2)}, u32[]{:S(2)}) collective-permute-start(bf16[512,768]{1,0:T(8,128)(2,1)} %get-tuple-element.205), channel_id=1, source_target_pairs={{0,1},{1,0},{2,3},{3,2},{4,5},{5,4},{6,7},{7,6},{8,9},{9,8},{10,11... | collective-permute-start | bytes 2359304 | tf_op jit(solution)/shard_map/ppermute | solution.py:1024
  112.4 15.6 %collective-permute-start.11 = (bf16[384,768]{1,0:T(8,128)(2,1)}, bf16[384,768]{1,0:T(8,128)(2,1)}, u32[]{:S(2)}, u32[]{:S(2)}) collective-permute-start(bf16[384,768]{1,0:T(8,128)(2,1)} %get-tuple-element.204), channel_id=1, source_target_pairs={{0,8},{4,12},{8,0},{12,4},{16,24},{20,28},{24,16},{28,20},{1,9},{5... | collective-permute-start | bytes 1769480 | tf_op jit(solution)/shard_map/ppermute | solution.py:1026
  112.9 16.3 %collective-permute-start.10 = (bf16[320,768]{1,0:T(8,128)(2,1)}, bf16[320,768]{1,0:T(8,128)(2,1)}, u32[]{:S(2)}, u32[]{:S(2)}) collective-permute-start(bf16[320,768]{1,0:T(8,128)(2,1)} %get-tuple-element.203), channel_id=1, source_target_pairs={{0,4},{4,0},{8,12},{12,8},{16,20},{20,16},{24,28},{28,24},{1,5},{5... | collective-permute-start | bytes 1474568 | tf_op jit(solution)/shard_map/ppermute | solution.py:1026
  113.4 10.7 %collective-permute-start.13 = (bf16[256,768]{1,0:T(8,128)(2,1)}, bf16[256,768]{1,0:T(8,128)(2,1)S(1)}, u32[]{:S(2)}, u32[]{:S(2)}) collective-permute-start(bf16[256,768]{1,0:T(8,128)(2,1)} %get-tuple-element.206), channel_id=1, source_target_pairs={{0,2},{1,3},{2,0},{3,1},{4,6},{5,7},{6,4},{7,5},{8,10},{9,11},{10,... | collective-permute-start | bytes 1179656 | tf_op jit(solution)/shard_map/ppermute | solution.py:1024
  124.1 1.2 copy-start.1
  127.8 1.4 copy-start.13
  130.4 1.2 copy-start.2
  130.4 1.5 copy-start.18
  131.9 12.3 %collective-permute-start.14 = (bf16[2,960,256]{2,1,0:T(8,128)(2,1)S(1)}, bf16[2,960,256]{2,1,0:T(8,128)(2,1)S(1)}, u32[]{:S(2)}, u32[]{:S(2)}) collective-permute-start(bf16[2,960,256]{2,1,0:T(8,128)(2,1)S(1)} %get-tuple-element.213), channel_id=1, source_target_pairs={{0,1},{1,0},{2,3},{3,2},{4,5},{5,4},{6,7},{7,6},{8,9},{9,8},{10,11... | collective-permute-start | bytes 2949128 | tf_op jit(solution)/shard_map/ppermute | solution.py:1024
  131.9 5.9 %collective-permute-start.15 = (bf16[64,768]{1,0:T(8,128)(2,1)S(1)}, bf16[64,768]{1,0:T(8,128)(2,1)S(1)}, u32[]{:S(2)}, u32[]{:S(2)}) collective-permute-start(bf16[64,768]{1,0:T(8,128)(2,1)S(1)} %get-tuple-element.214), channel_id=1, source_target_pairs={{0,8},{4,12},{8,0},{12,4},{16,24},{20,28},{24,16},{28,20},{1,9},{5... | collective-permute-start | bytes 294920 | tf_op jit(solution)/shard_map/ppermute | solution.py:1026
  133.3 10.7 %collective-permute-start.16 = (bf16[64,768]{1,0:T(8,128)(2,1)S(1)}, bf16[64,768]{1,0:T(8,128)(2,1)S(1)}, u32[]{:S(2)}, u32[]{:S(2)}) collective-permute-start(bf16[64,768]{1,0:T(8,128)(2,1)S(1)} %get-tuple-element.215), channel_id=1, source_target_pairs={{0,16},{4,20},{8,24},{12,28},{16,0},{20,4},{24,8},{28,12},{1,17},{... | collective-permute-start | bytes 294920 | tf_op jit(solution)/shard_map/ppermute | solution.py:1026
  135.9 8.2 %collective-permute-start.17 = (bf16[64,768]{1,0:T(8,128)(2,1)S(1)}, bf16[64,768]{1,0:T(8,128)(2,1)S(1)}, u32[]{:S(2)}, u32[]{:S(2)}) collective-permute-start(bf16[64,768]{1,0:T(8,128)(2,1)S(1)} %get-tuple-element.216), channel_id=1, source_target_pairs={{0,24},{4,28},{8,16},{12,20},{16,8},{20,12},{24,0},{28,4},{1,25},{... | collective-permute-start | bytes 294920 | tf_op jit(solution)/shard_map/ppermute | solution.py:1026
  136.3 12.6 %collective-permute-start.19 = (bf16[160,768]{1,0:T(8,128)(2,1)S(1)}, bf16[160,768]{1,0:T(8,128)(2,1)S(1)}, u32[]{:S(2)}, u32[]{:S(2)}) collective-permute-start(bf16[160,768]{1,0:T(8,128)(2,1)S(1)} %get-tuple-element.221), channel_id=1, source_target_pairs={{0,2},{1,3},{2,0},{3,1},{4,6},{5,7},{6,4},{7,5},{8,10},{9,11},{10,... | collective-permute-start | bytes 737288 | tf_op jit(solution)/shard_map/ppermute | solution.py:1024
  144.7 22.0 %collective-permute-start.18 = (bf16[960,256]{1,0:T(8,128)(2,1)S(1)}, bf16[960,256]{1,0:T(8,128)(2,1)S(1)}, u32[]{:S(2)}, u32[]{:S(2)}) collective-permute-start(bf16[960,256]{1,0:T(8,128)(2,1)S(1)} %get-tuple-element.218), channel_id=1, source_target_pairs={{0,2},{1,3},{2,0},{3,1},{4,6},{5,7},{6,4},{7,5},{8,10},{9,11},{10,... | collective-permute-start | bytes 1474568 | tf_op jit(solution)/shard_map/ppermute | solution.py:1024
  146.3 18.5 %collective-permute-start.21 = (bf16[256,768]{1,0:T(8,128)(2,1)S(1)}, bf16[256,768]{1,0:T(8,128)(2,1)S(1)}, u32[]{:S(2)}, u32[]{:S(2)}) collective-permute-start(bf16[256,768]{1,0:T(8,128)(2,1)S(1)} %get-tuple-element.224), channel_id=1, source_target_pairs={{0,4},{4,0},{8,12},{12,8},{16,20},{20,16},{24,28},{28,24},{1,5},{5... | collective-permute-start | bytes 1179656 | tf_op jit(solution)/shard_map/ppermute | solution.py:1026
  147.8 14.6 %collective-permute-start.22 = (bf16[192,768]{1,0:T(8,128)(2,1)S(1)}, bf16[192,768]{1,0:T(8,128)(2,1)S(1)}, u32[]{:S(2)}, u32[]{:S(2)}) collective-permute-start(bf16[192,768]{1,0:T(8,128)(2,1)S(1)} %get-tuple-element.225), channel_id=1, source_target_pairs={{0,4},{4,0},{8,12},{12,8},{16,20},{20,16},{24,28},{28,24},{1,5},{5... | collective-permute-start | bytes 884744 | tf_op jit(solution)/shard_map/ppermute | solution.py:1026
  148.3 42.6 %collective-permute-start.31 = (bf16[384,768]{1,0:T(8,128)(2,1)S(1)}, bf16[384,768]{1,0:T(8,128)(2,1)S(1)}, u32[]{:S(2)}, u32[]{:S(2)}) collective-permute-start(bf16[384,768]{1,0:T(8,128)(2,1)S(1)} %get-tuple-element.236), channel_id=1, source_target_pairs={{0,2},{1,3},{2,0},{3,1},{4,6},{5,7},{6,4},{7,5},{8,10},{9,11},{10,... | collective-permute-start | bytes 1769480 | tf_op jit(solution)/shard_map/ppermute | solution.py:1024
  148.8 5.7 %collective-permute-start.23 = (bf16[64,768]{1,0:T(8,128)(2,1)S(1)}, bf16[64,768]{1,0:T(8,128)(2,1)S(1)}, u32[]{:S(2)}, u32[]{:S(2)}) collective-permute-start(bf16[64,768]{1,0:T(8,128)(2,1)S(1)} %add.35.refs_4_.refs_0_), channel_id=1, source_target_pairs={{0,16},{4,20},{8,24},{12,28},{16,0},{20,4},{24,8},{28,12},{1,17},{... | collective-permute-start | bytes 294920 | tf_op jit(solution)/shard_map/ppermute | solution.py:1026
  154.5 10.9 %collective-permute-start.20 = (bf16[80,768]{1,0:T(8,128)(2,1)S(1)}, bf16[80,768]{1,0:T(8,128)(2,1)S(1)}, u32[]{:S(2)}, u32[]{:S(2)}) collective-permute-start(bf16[80,768]{1,0:T(8,128)(2,1)S(1)} %get-tuple-element.223), channel_id=1, source_target_pairs={{0,16},{4,20},{8,24},{12,28},{16,0},{20,4},{24,8},{28,12},{1,17},{... | collective-permute-start | bytes 368648 | tf_op jit(solution)/shard_map/ppermute | solution.py:1026
  157.6 10.9 %copy-start.19 = (f32[256,768]{1,0:T(8,128)S(1)}, f32[256,768]{1,0:T(8,128)}, u32[]{:S(2)}) copy-start(f32[256,768]{1,0:T(8,128)} %get-tuple-element.219.mid_t) | copy-start | bytes 2359300
  157.6 10.9 %copy-start.21 = (f32[2,192,128]{2,1,0:T(8,128)S(1)}, f32[2,192,128]{2,1,0:T(8,128)}, u32[]{:S(2)}) copy-start(f32[2,192,128]{2,1,0:T(8,128)} %get-tuple-element.220.mid_l) | copy-start | bytes 589828
  162.4 8.5 %collective-permute-start.26 = (bf16[128,768]{1,0:T(8,128)(2,1)S(1)}, bf16[128,768]{1,0:T(8,128)(2,1)S(1)}, u32[]{:S(2)}, u32[]{:S(2)}) collective-permute-start(bf16[128,768]{1,0:T(8,128)(2,1)S(1)} %join.10.refs_4_.refs_0_), channel_id=1, source_target_pairs={{0,8},{4,12},{8,0},{12,4},{16,24},{20,28},{24,16},{28,20},{1,9},{5... | collective-permute-start | bytes 589832 | tf_op jit(solution)/shard_map/ppermute | solution.py:1026
  164.9 12.1 %collective-permute-start.24 = (bf16[128,768]{1,0:T(8,128)(2,1)S(1)}, bf16[128,768]{1,0:T(8,128)(2,1)S(1)}, u32[]{:S(2)}, u32[]{:S(2)}) collective-permute-start(bf16[128,768]{1,0:T(8,128)(2,1)S(1)} %get-tuple-element.230), channel_id=1, source_target_pairs={{0,2},{1,3},{2,0},{3,1},{4,6},{5,7},{6,4},{7,5},{8,10},{9,11},{10,... | collective-permute-start | bytes 589832 | tf_op jit(solution)/shard_map/ppermute | solution.py:1024
  165.5 11.4 %collective-permute-start.25 = (bf16[96,768]{1,0:T(8,128)(2,1)S(1)}, bf16[96,768]{1,0:T(8,128)(2,1)S(1)}, u32[]{:S(2)}, u32[]{:S(2)}) collective-permute-start(bf16[96,768]{1,0:T(8,128)(2,1)S(1)} %get-tuple-element.231), channel_id=1, source_target_pairs={{0,16},{4,20},{8,24},{12,28},{16,0},{20,4},{24,8},{28,12},{1,17},{... | collective-permute-start | bytes 442376 | tf_op jit(solution)/shard_map/ppermute | solution.py:1026
  166.7 11.6 %collective-permute-start.28 = (bf16[80,768]{1,0:T(8,128)(2,1)S(1)}, bf16[80,768]{1,0:T(8,128)(2,1)S(1)}, u32[]{:S(2)}, u32[]{:S(2)}) collective-permute-start(bf16[80,768]{1,0:T(8,128)(2,1)S(1)} %add.40.after.refs_0_), channel_id=1, source_target_pairs={{0,16},{4,20},{8,24},{12,28},{16,0},{20,4},{24,8},{28,12},{1,17},{... | collective-permute-start | bytes 368648 | tf_op jit(solution)/shard_map/ppermute | solution.py:1026
  178.3 15.6 %collective-permute-start.34 = (bf16[160,768]{1,0:T(8,128)(2,1)S(1)}, bf16[160,768]{1,0:T(8,128)(2,1)S(1)}, u32[]{:S(2)}, u32[]{:S(2)}) collective-permute-start(bf16[160,768]{1,0:T(8,128)(2,1)S(1)} %join.12.refs_4_.refs_0_), channel_id=1, source_target_pairs={{0,8},{4,12},{8,0},{12,4},{16,24},{20,28},{24,16},{28,20},{1,9},{5... | collective-permute-start | bytes 737288 | tf_op jit(solution)/shard_map/ppermute | solution.py:1026
  178.4 10.4 %collective-permute-start.27 = (bf16[64,768]{1,0:T(8,128)(2,1)S(1)}, bf16[64,768]{1,0:T(8,128)(2,1)S(1)}, u32[]{:S(2)}, u32[]{:S(2)}) collective-permute-start(bf16[64,768]{1,0:T(8,128)(2,1)S(1)} %get-tuple-element.233), channel_id=1, source_target_pairs={{0,8},{4,12},{8,0},{12,4},{16,24},{20,28},{24,16},{28,20},{1,9},{5... | collective-permute-start | bytes 294920 | tf_op jit(solution)/shard_map/ppermute | solution.py:1026
  180.4 12.0 %collective-permute-start.30 = (bf16[96,768]{1,0:T(8,128)(2,1)S(1)}, bf16[96,768]{1,0:T(8,128)(2,1)S(1)}, u32[]{:S(2)}, u32[]{:S(2)}) collective-permute-start(bf16[96,768]{1,0:T(8,128)(2,1)S(1)} %add.41.refs_4_.refs_0_), channel_id=1, source_target_pairs={{0,16},{4,20},{8,24},{12,28},{16,0},{20,4},{24,8},{28,12},{1,17},{... | collective-permute-start | bytes 442376 | tf_op jit(solution)/shard_map/ppermute | solution.py:1026
  188.8 5.1 %collective-permute-start.29 = (bf16[32,768]{1,0:T(8,128)(2,1)S(1)}, bf16[32,768]{1,0:T(8,128)(2,1)S(1)}, u32[]{:S(2)}, u32[]{:S(2)}) collective-permute-start(bf16[32,768]{1,0:T(8,128)(2,1)S(1)} %get-tuple-element.235), channel_id=1, source_target_pairs={{0,16},{4,20},{8,24},{12,28},{16,0},{20,4},{24,8},{28,12},{1,17},{... | collective-permute-start | bytes 147464 | tf_op jit(solution)/shard_map/ppermute | solution.py:1026
  191.0 9.9 %collective-permute-start.33 = (bf16[192,768]{1,0:T(8,128)(2,1)S(1)}, bf16[192,768]{1,0:T(8,128)(2,1)S(1)}, u32[]{:S(2)}, u32[]{:S(2)}) collective-permute-start(bf16[192,768]{1,0:T(8,128)(2,1)S(1)} %get-tuple-element.238), channel_id=1, source_target_pairs={{0,4},{4,0},{8,12},{12,8},{16,20},{20,16},{24,28},{28,24},{1,5},{5... | collective-permute-start | bytes 884744 | tf_op jit(solution)/shard_map/ppermute | solution.py:1026
  193.9 26.0 %collective-permute-start.42 = (bf16[320,768]{1,0:T(8,128)(2,1)S(1)}, bf16[320,768]{1,0:T(8,128)(2,1)S(1)}, u32[]{:S(2)}, u32[]{:S(2)}) collective-permute-start(bf16[320,768]{1,0:T(8,128)(2,1)S(1)} %join.14.refs_8_.refs_0_), channel_id=1, source_target_pairs={{0,4},{4,0},{8,12},{12,8},{16,20},{20,16},{24,28},{28,24},{1,5},{5... | collective-permute-start | bytes 1474568 | tf_op jit(solution)/shard_map/ppermute | solution.py:1026
  196.8 10.3 %collective-permute-start.36 = (bf16[192,768]{1,0:T(8,128)(2,1)S(1)}, bf16[192,768]{1,0:T(8,128)(2,1)S(1)}, u32[]{:S(2)}, u32[]{:S(2)}) collective-permute-start(bf16[192,768]{1,0:T(8,128)(2,1)S(1)} %join.13.refs_2_.refs_0_), channel_id=1, source_target_pairs={{0,8},{4,12},{8,0},{12,4},{16,24},{20,28},{24,16},{28,20},{1,9},{5... | collective-permute-start | bytes 884744 | tf_op jit(solution)/shard_map/ppermute | solution.py:1026
  197.0 22.9 %collective-permute-start.43 = (bf16[256,768]{1,0:T(8,128)(2,1)S(1)}, bf16[256,768]{1,0:T(8,128)(2,1)S(1)}, u32[]{:S(2)}, u32[]{:S(2)}) collective-permute-start(bf16[256,768]{1,0:T(8,128)(2,1)S(1)} %join.11.refs_2_), channel_id=1, source_target_pairs={{0,4},{4,0},{8,12},{12,8},{16,20},{20,16},{24,28},{28,24},{1,5},{5... | collective-permute-start | bytes 1179656 | tf_op jit(solution)/shard_map/ppermute | solution.py:1026
  197.6 5.3 %collective-permute-start.32 = (bf16[32,768]{1,0:T(8,128)(2,1)S(1)}, bf16[32,768]{1,0:T(8,128)(2,1)S(1)}, u32[]{:S(2)}, u32[]{:S(2)}) collective-permute-start(bf16[32,768]{1,0:T(8,128)(2,1)S(1)} %add.45.refs_2_.refs_0_), channel_id=1, source_target_pairs={{0,16},{4,20},{8,24},{12,28},{16,0},{20,4},{24,8},{28,12},{1,17},{... | collective-permute-start | bytes 147464 | tf_op jit(solution)/shard_map/ppermute | solution.py:1026
  202.9 10.2 %collective-permute-start.35 = (bf16[64,768]{1,0:T(8,128)(2,1)S(1)}, bf16[64,768]{1,0:T(8,128)(2,1)S(1)}, u32[]{:S(2)}, u32[]{:S(2)}) collective-permute-start(bf16[64,768]{1,0:T(8,128)(2,1)S(1)} %join.15.refs_2_.refs_0_), channel_id=1, source_target_pairs={{0,8},{4,12},{8,0},{12,4},{16,24},{20,28},{24,16},{28,20},{1,9},{5... | collective-permute-start | bytes 294920 | tf_op jit(solution)/shard_map/ppermute | solution.py:1026
  207.1 5.9 %collective-permute-start.38 = (bf16[48,768]{1,0:T(8,128)(2,1)S(1)}, bf16[48,768]{1,0:T(8,128)(2,1)S(1)}, u32[]{:S(2)}, u32[]{:S(2)}) collective-permute-start(bf16[48,768]{1,0:T(8,128)(2,1)S(1)} %get-tuple-element.240), channel_id=1, source_target_pairs={{0,8},{4,12},{8,0},{12,4},{16,24},{20,28},{24,16},{28,20},{1,9},{5... | collective-permute-start | bytes 221192 | tf_op jit(solution)/shard_map/ppermute | solution.py:1026
  207.1 6.4 %collective-permute-start.39 = (bf16[48,768]{1,0:T(8,128)(2,1)S(1)}, bf16[48,768]{1,0:T(8,128)(2,1)S(1)}, u32[]{:S(2)}, u32[]{:S(2)}) collective-permute-start(bf16[48,768]{1,0:T(8,128)(2,1)S(1)} %get-tuple-element.241), channel_id=1, source_target_pairs={{0,16},{4,20},{8,24},{12,28},{16,0},{20,4},{24,8},{28,12},{1,17},{... | collective-permute-start | bytes 221192 | tf_op jit(solution)/shard_map/ppermute | solution.py:1026
  213.0 6.2 %collective-permute-start.40 = (bf16[48,768]{1,0:T(8,128)(2,1)S(1)}, bf16[48,768]{1,0:T(8,128)(2,1)S(1)}, u32[]{:S(2)}, u32[]{:S(2)}) collective-permute-start(bf16[48,768]{1,0:T(8,128)(2,1)S(1)} %get-tuple-element.242), channel_id=1, source_target_pairs={{0,24},{4,28},{8,16},{12,20},{16,8},{20,12},{24,0},{28,4},{1,25},{... | collective-permute-start | bytes 221192 | tf_op jit(solution)/shard_map/ppermute | solution.py:1026
  213.0 19.6 %collective-permute-start.46 = (bf16[384,768]{1,0:T(8,128)(2,1)S(1)}, bf16[384,768]{1,0:T(8,128)(2,1)S(1)}, u32[]{:S(2)}, u32[]{:S(2)}) collective-permute-start(bf16[384,768]{1,0:T(8,128)(2,1)S(1)} %join.16.refs_2_.refs_0_), channel_id=1, source_target_pairs={{0,4},{4,0},{8,12},{12,8},{16,20},{20,16},{24,28},{28,24},{1,5},{5... | collective-permute-start | bytes 1769480 | tf_op jit(solution)/shard_map/ppermute | solution.py:1026
  219.2 5.3 %collective-permute-start.41 = (bf16[48,768]{1,0:T(8,128)(2,1)S(1)}, bf16[48,768]{1,0:T(8,128)(2,1)S(1)}, u32[]{:S(2)}, u32[]{:S(2)}) collective-permute-start(bf16[48,768]{1,0:T(8,128)(2,1)S(1)} %add.47.refs_4_.refs_0_), channel_id=1, source_target_pairs={{0,16},{4,20},{8,24},{12,28},{16,0},{20,4},{24,8},{28,12},{1,17},{... | collective-permute-start | bytes 221192 | tf_op jit(solution)/shard_map/ppermute | solution.py:1026
  225.3 5.2 %collective-permute-start.44 = (bf16[96,768]{1,0:T(8,128)(2,1)S(1)}, bf16[96,768]{1,0:T(8,128)(2,1)S(1)}, u32[]{:S(2)}, u32[]{:S(2)}) collective-permute-start(bf16[96,768]{1,0:T(8,128)(2,1)S(1)} %join.18.refs_0_.refs_2_), channel_id=1, source_target_pairs={{0,8},{4,12},{8,0},{12,4},{16,24},{20,28},{24,16},{28,20},{1,9},{5... | collective-permute-start | bytes 442376 | tf_op jit(solution)/shard_map/ppermute | solution.py:1026
  230.5 9.3 %collective-permute-start.45 = (bf16[192,768]{1,0:T(8,128)(2,1)S(1)}, bf16[192,768]{1,0:T(8,128)(2,1)S(1)}, u32[]{:S(2)}, u32[]{:S(2)}) collective-permute-start(bf16[192,768]{1,0:T(8,128)(2,1)S(1)} %join.19.refs_2_), channel_id=1, source_target_pairs={{0,4},{4,0},{8,12},{12,8},{16,20},{20,16},{24,28},{28,24},{1,5},{5... | collective-permute-start | bytes 884744 | tf_op jit(solution)/shard_map/ppermute | solution.py:1026
  231.0 8.8 %collective-permute-start.37 = (bf16[128,768]{1,0:T(8,128)(2,1)S(1)}, bf16[128,768]{1,0:T(8,128)(2,1)S(1)}, u32[]{:S(2)}, u32[]{:S(2)}) collective-permute-start(bf16[128,768]{1,0:T(8,128)(2,1)S(1)} %join.17.refs_4_.refs_0_), channel_id=1, source_target_pairs={{0,4},{4,0},{8,12},{12,8},{16,20},{20,16},{24,28},{28,24},{1,5},{5... | collective-permute-start | bytes 589832 | tf_op jit(solution)/shard_map/ppermute | solution.py:1026
  239.8 1.7 copy-start.8
  (11 other events, 10.0 us)

commit v3 on v2

--- a/solution.py
+++ b/solution.py
@@ -25,6 +25,7 @@
 
 VMEM = pl.BlockSpec(memory_space=pltpu.VMEM)
 ANY = pl.BlockSpec(memory_space=pl.ANY)
+HBM = pl.BlockSpec(memory_space=pltpu.HBM)
 
 
 def dot(left, right):
@@ -37,7 +38,11 @@
 
 LIMIT = 60 * MIB
 FIRST = 60 * MIB
+SECOND = 60 * MIB
+LAST = 30 * MIB
 SMALL = 16 * MIB
+UNROLL = 6
+UNROLL_BACK = 1
 
 
 COST = pl.CostEstimate(flops=1, bytes_accessed=1, transcendentals=0)
@@ -70,11 +75,13 @@
     ]
 
 
-def in_lines(shards, subs, dp_size, targets):
+def in_lines(shards, subs, dp_size, targets, low=0, high=1 << 30):
     place = (lax.axis_index("seq"), lax.axis_index("dp"))
     pairs = []
     for core in (1, 0):
         for at, (first, rows, hops, growth) in enumerate(subs):
+            if not low < first + rows <= high:
+                continue
             size = rows // dp_size
             target = targets[2 * at + 1 - core]
             for across in range(2):
@@ -237,35 +244,54 @@
     bl,
     gl,
     ol,
-    res_t,
-    res_l,
-    q_t,
-    q_l,
+    res_t_out,
+    res_l_out,
+    q_t_out,
+    q_l_out,
     kt_out,
     kl_out,
     vt_out,
     vl_out,
     p_out,
-    ctx_t,
-    ctx_l,
-    hid_t,
-    unit_t,
-    inv_t,
-    sum_t,
-    slope_t,
-    hid_l,
-    unit_l,
-    inv_l,
-    sum_l,
-    slope_l,
-    act_l,
-    sv_t,
-    sv_l,
+    ctx_t_out,
+    ctx_l_out,
+    hid_t_out,
+    unit_t_out,
+    inv_t_out,
+    sum_t_out,
+    slope_t_out,
+    hid_l_out,
+    unit_l_out,
+    inv_l_out,
+    sum_l_out,
+    slope_l_out,
+    act_l_out,
+    sv_t_out,
+    sv_l_out,
     *rest,
 ):
     targets, rest = rest[: 2 * len(subs)], rest[2 * len(subs) :]
     (
         xs,
+        res_t,
+        res_l,
+        q_t,
+        q_l,
+        ctx_t,
+        ctx_l,
+        hid_t,
+        unit_t,
+        inv_t,
+        sum_t,
+        slope_t,
+        hid_l,
+        unit_l,
+        inv_l,
+        sum_l,
+        slope_l,
+        act_l,
+        sv_t,
+        sv_l,
         layout_bias_ref,
         wt,
         wl,
@@ -292,14 +318,21 @@
         gather_pairs(blocks, rows, packs, xs), sems, 0
     )
     base = len(x_copies)
-    w_copies = copies_of(((wt_in, wt), (wl_in, wl), (mt_in, mt), (et_in, et), (st_in, st)), sems, base)
-    base += 5
+    w_copies = copies_of(((wt_in, wt), (wl_in, wl)), sems, base)
+    base += 2
+    pending = []
+
+    def emit(*pairs):
+        pending.extend(copies_of(pairs, sems, base + len(pending)))
+
     text_bias = bt[...].astype(F32)
     layout_bias_ref[...] = jnp.zeros_like(layout_bias_ref)
     layout_bias_ref[:, :DL] = bl[...].astype(F32)
     layout_bias = layout_bias_ref[...]
     wait_all(x_copies)
-    wait_all(w_copies[:2])
+    wait_all(w_copies)
+    w_copies = copies_of(((mt_in, mt), (et_in, et), (st_in, st)), sems, base)
+    base += 3
 
     for pack in range(packs):
         own = pl.ds(pack * keys, rows)
@@ -318,8 +351,7 @@
         return unused
 
     lax.fori_loop(0, packs * keys // step, key_rows, 0)
-    kv_copies = copies_of(((k_t, kt_out), (k_l, kl_out), (v_t, vt_out), (v_l, vl_out)), sems, base)
-    base += 4
+    emit((k_t, kt_out), (k_l, kl_out), (v_t, vt_out), (v_l, vl_out), (q_t, q_t_out), (q_l, q_l_out))
 
     marks = lax.broadcasted_iota(jnp.int32, (1, LANES), 1) - 64
     for pack in range(packs):
@@ -352,18 +384,16 @@
             ctx_l[mine, layout_lanes] = jnp.where(masks[2], mixed[rows:, LANES:], kept)
         return unused
 
-    lax.fori_loop(0, HEADS // 2, head_pair, 0)
-    p_copies = copies_of(((prob, p_out),), sems, base)
-    base += 1
-
-    wait_all(w_copies[2:])
+    lax.fori_loop(0, HEADS // 2, head_pair, 0, unroll=UNROLL)
+    emit((prob, p_out), (ctx_t, ctx_t_out), (ctx_l, ctx_l_out))
+    wait_all(w_copies)
 
     def own_rows(lanes):
         return jnp.concatenate(
             [xs[pl.ds(pack * keys, rows), lanes].astype(F32) for pack in range(packs)], axis=0
         )
 
-    def tail(x, attended, expand, offsets, shrink, turned, b, g, cotangent, active, slope, branch, chunk, hid, unit, inv, delta, sv):
+    def tail(x, attended, expand, offsets, shrink, turned, b, g, cotangent, active, slope, branch, chunk, hid, unit, inv, delta, sv, outs):
         width = x.shape[1]
         middle = x + attended + b[2:3, :width]
         unit_first, inverse_first = normalized(middle)
@@ -372,23 +402,29 @@
         hid[...] = hidden_low
         unit[...] = unit_first
         inv[...] = inverse_first
+        emit((hid, outs[0]), (unit, outs[1]), (inv, outs[2]))
         feed_forward(hidden_low, expand, offsets, shrink, turned, active, slope, chunk, branch)
+        emit((slope, outs[3]))
         unit_second, inverse_second = normalized(hidden + branch[...] + b[4:5, :width])
         result = unit_second * g[1:2, :] + b[5:6, :width]
         sv[1:2, :] = column_sum(cotangent)
         sv[2:3, :] = column_sum(cotangent * unit_second)
         sum_delta = norm_back(cotangent * g[1:2, :], unit_second, inverse_second)
         delta[...] = sum_delta
+        emit((delta, outs[4]))
         rounded = sum_delta.astype(BF16).astype(F32)
         sv[0:1, :] = column_sum(rounded)
+        emit((sv, outs[5]))
         return result, rounded
 
     result, rounded = tail(
         own_rows(slice(0, DT)), dot(ctx_t[...], mt[...]), et, ot, st, False, text_bias, gt[...].astype(F32),
         jnp.concatenate([cot_t[pack] for pack in range(packs)], axis=0).astype(F32),
         act_t, slope_t, branch_t, 512, hid_t, unit_t, inv_t, sum_t, sv_t,
+        (hid_t_out, unit_t_out, inv_t_out, slope_t_out, sum_t_out, sv_t_out),
     )
     res_t[...] = result.astype(BF16)
+    emit((res_t, res_t_out))
     turned[...] = rounded.T.astype(BF16)
     share = DT // 4
     for shard in range(4):
@@ -399,20 +435,18 @@
             ).astype(BF16)
     if grads.shape[1] > S_ROWS:
         grads[:, S_ROWS:, :] = jnp.zeros((4, grads.shape[1] - S_ROWS, DT), BF16)
-    out_copies = copies_of(
-        in_lines(grads, subs, dp_size, targets), sems, base
-    )
+    emit(*in_lines(grads, subs, dp_size, targets))
     result, unused = tail(
         own_rows(slice(DT, DT + DL)), dot(ctx_l[:, :DL], ml[...]), el, ol, sl, True, layout_bias,
         gl[...].astype(F32),
         jnp.concatenate([cot_l[pack].astype(F32).T for pack in range(packs)], axis=0),
         act_l, slope_l, branch_l, 256, hid_l, unit_l, inv_l, sum_l, sv_l,
+        (hid_l_out, unit_l_out, inv_l_out, slope_l_out, sum_l_out, sv_l_out),
     )
     for pack in range(packs):
         res_l[pack] = result[pack * rows : (pack + 1) * rows, :].T.astype(BF16)
-    wait_all(kv_copies)
-    wait_all(p_copies)
-    wait_all(out_copies)
+    emit((res_l, res_l_out), (act_l, act_l_out))
+    wait_all(pending)
 
 
 def forward_call(blocks, wt, wl, mt, et, st, ml, el, sl, cot_t, cot_l, bt, gt, ot, bl, gl, ol, packs, rows, dp_size, subs):
@@ -447,9 +481,11 @@
         shape_of((8, DT), F32),
         shape_of((8, DL), F32),
     ) + pair_shapes(subs)
-    out_specs = [VMEM] * 4 + [ANY] * 5 + [VMEM] * 15 + [ANY] * (2 * len(subs))
+    out_specs = [ANY] * len(outs)
+    kept = (0, 1, 2, 3, 9, 10) + tuple(range(11, 24))
     scratch = [
         pltpu.VMEM((every, DT + SLAB), BF16),
+        *(pltpu.VMEM(outs[at].shape, outs[at].dtype) for at in kept),
         pltpu.VMEM((6, SLAB), F32),
         pltpu.VMEM(wt.shape, BF16),
         pltpu.VMEM(wl.shape, BF16),
@@ -467,7 +503,7 @@
         pltpu.VMEM((tokens, DT), F32),
         pltpu.VMEM((tokens, DL), F32),
         pltpu.VMEM((4, lines, DT), BF16),
-        pltpu.SemaphoreType.DMA((24 + 4 * dp_size * len(subs),)),
+        pltpu.SemaphoreType.DMA((48 + 4 * dp_size * len(subs),)),
     ]
     return pl.pallas_call(
         functools.partial(forward_kernel, packs, rows, dp_size, subs),
@@ -484,18 +520,18 @@
 def middle_kernel(
     dp_size,
     subs,
-    hid_t,
-    unit_t,
-    inv_t,
-    sum_t,
-    slope_t,
+    hid_t_in,
+    unit_t_in,
+    inv_t_in,
+    sum_t_in,
+    slope_t_in,
     hid_l,
     unit_l,
     inv_l,
     sum_l,
     slope_l,
     act_l,
-    ctx_t,
+    ctx_t_in,
     ctx_l,
     st_in,
     et_in,
@@ -518,23 +554,33 @@
 ):
     targets, rest = rest[: 2 * len(subs)], rest[2 * len(subs) :]
     (
+        hid_t,
+        unit_t,
+        inv_t,
+        sum_t,
+        slope_t,
+        ctx_t,
         st,
         et,
         mt,
         before_t,
         before_l,
-        hidden_t,
-        hidden_l,
         turned,
         grads,
         sems,
     ) = rest
-    w_copies = copies_of(((st_in, st), (et_in, et), (mt_in, mt)), sems, 0)
-    base = 3
-
-    def feed_back(branch_delta, shrink, turned, expand, slope, before, so, hidden_delta, chunk):
-        width = slope.shape[1]
-        for at in range(width // chunk):
+    w_copies = copies_of(
+        (
+            (sum_t_in, sum_t), (st_in, st), (slope_t_in, slope_t), (hid_t_in, hid_t), (et_in, et),
+            (unit_t_in, unit_t), (inv_t_in, inv_t), (ctx_t_in, ctx_t), (mt_in, mt),
+        ),
+        sems,
+        0,
+    )
+    base = len(w_copies)
+
+    def feed_back(branch_delta, shrink, turned, slope, before, so, chunk):
+        for at in range(slope.shape[1] // chunk):
             part = pl.ds(at * chunk, chunk)
             if turned:
                 active_delta = dot(branch_delta, shrink[:, part])
@@ -543,14 +589,9 @@
             low = (active_delta * slope[:, part].astype(F32)).astype(BF16)
             before[:, part] = low
             so[:, part] = column_sum(low.astype(F32))
-            product = dot_nt(low, expand[:, part])
-            if at == 0:
-                hidden_delta[...] = product
-            else:
-                hidden_delta[...] += product
 
     def front(hidden_delta, total, unit, inv, g, merge, sv):
-        delta = total[...] + hidden_delta[...]
+        delta = total[...] + hidden_delta
         sv[0:1, :] = column_sum(delta * unit[...])
         sv[1:2, :] = column_sum(delta)
         middle = norm_back(delta * g, unit[...], inv[...])
@@ -561,14 +602,13 @@
         sv[3:4, :] = column_sum(back.astype(F32))
         return middle, rounded.T.astype(BF16), back
 
-    text_delta = sum_t[...].astype(BF16)
     layout_delta = sum_l[...].astype(BF16)
-    feed_back(layout_delta, sl, True, el, slope_l, before_l, so_l, hidden_l, 256)
+    feed_back(layout_delta, sl, True, slope_l, before_l, so_l, 256)
     turned_l = before_l[...].astype(F32).T.astype(BF16)
     grown_l = dot(turned_l, hid_l[...]).astype(BF16)
     shrunk_l = dot(layout_delta.astype(F32).T.astype(BF16), act_l[...]).astype(BF16)
     middle, low_turned, back = front(
-        hidden_l, sum_l, unit_l, inv_l, gl[0:1, :].astype(F32), ml[...], sv_l
+        dot_nt(before_l[...], el[...]), sum_l, unit_l, inv_l, gl[0:1, :].astype(F32), ml[...], sv_l
     )
     for pack in range(mid_l.shape[0]):
         size = mid_l.shape[2]
@@ -576,18 +616,23 @@
     dctx_l[...] = jnp.zeros_like(dctx_l)
     dctx_l[:, :DL] = back
     merged_l = dot(low_turned, ctx_l[...]).astype(BF16)
+    wait_all(w_copies[:3])
+    feed_back(sum_t[...].astype(BF16), st, False, slope_t, before_t, so_t, 512)
+    wait_all(w_copies[3:4])
     turned[...] = hid_t[...].astype(F32).T.astype(BF16)
-    wait_all(w_copies)
-    feed_back(text_delta, st, False, et, slope_t, before_t, so_t, hidden_t, 512)
-    middle, low_turned, back = front(
-        hidden_t, sum_t, unit_t, inv_t, gt[0:1, :].astype(F32), mt[...], sv_t
-    )
-    mid_t[...] = middle
-    dctx_t[...] = back
     for shard in range(4):
         grads[shard, pl.ds(0, DT), :] = dot(
             turned[...], before_t[:, shard * DT : (shard + 1) * DT]
         ).astype(BF16)
+    early = copies_of(in_lines(grads, subs, dp_size, targets, 0, DT), sems, base)
+    base += len(early)
+    wait_all(w_copies[4:])
+    middle, low_turned, back = front(
+        dot_nt(before_t[...], et[...]), sum_t, unit_t, inv_t, gt[0:1, :].astype(F32), mt[...], sv_t
+    )
+    mid_t[...] = middle
+    dctx_t[...] = back
+    for shard in range(4):
         grads[shard, pl.ds(DT, 192), :] = dot(
             low_turned[shard * 192 : (shard + 1) * 192, :], ctx_t[...]
         ).astype(BF16)
@@ -600,9 +645,8 @@
             line = shard * 48 + at * 16
             grads[shard, 1072:1088, at * SLAB : (at + 1) * SLAB] = merged_l[line : line + 16, :]
         grads[shard, 1024:1072, :] = shrunk_l[shard * 48 : shard * 48 + 48, :]
-    wait_all(
-        copies_of(in_lines(grads, subs, dp_size, targets), sems, base)
-    )
+    wait_all(copies_of(in_lines(grads, subs, dp_size, targets, DT), sems, base))
+    wait_all(early)
 
 
 def middle_call(operands, packs, rows, dp_size, subs):
@@ -619,24 +663,23 @@
         shape_of((1, FL), F32),
     ) + pair_shapes(subs)
     scratch = [
+        *(pltpu.VMEM(operands[at].shape, operands[at].dtype) for at in (0, 1, 2, 3, 4, 11)),
         pltpu.VMEM((FT, DT), BF16),
         pltpu.VMEM((DT, FT), BF16),
         pltpu.VMEM((DT, DT), BF16),
         pltpu.VMEM((tokens, FT), BF16),
         pltpu.VMEM((tokens, FL), BF16),
-        pltpu.VMEM((tokens, DT), F32),
-        pltpu.VMEM((tokens, DL), F32),
         pltpu.VMEM((DT, tokens), BF16),
         pltpu.VMEM((4, lines, DT), BF16),
-        pltpu.SemaphoreType.DMA((8 + 4 * dp_size * len(subs),)),
+        pltpu.SemaphoreType.DMA((16 + 4 * dp_size * len(subs),)),
     ]
     return pl.pallas_call(
         functools.partial(middle_kernel, dp_size, subs),
         out_shape=outs,
-        in_specs=[VMEM] * 13 + [ANY] * 3 + [VMEM] * 5 + [ANY],
+        in_specs=[ANY] * 5 + [VMEM] * 6 + [ANY, VMEM] + [ANY] * 3 + [VMEM] * 5 + [ANY],
         out_specs=[VMEM] * 8 + [ANY] * (2 * len(subs)),
         scratch_shapes=scratch,
-        compiler_params=pltpu.CompilerParams(vmem_limit_bytes=LIMIT),
+        compiler_params=pltpu.CompilerParams(vmem_limit_bytes=SECOND),
         cost_estimate=COST,
         name="middle",
     )(*operands)
@@ -669,15 +712,19 @@
     so_t,
     so_l,
     after,
-    joined_t,
-    joined_l,
-    query_t,
-    query_l,
+    joined_t_out,
+    joined_l_out,
+    query_t_out,
+    query_l_out,
     *rest,
 ):
     targets, rest = rest[: 2 * len(subs)], rest[2 * len(subs) :]
     (
         xs,
+        joined_t,
+        joined_l,
+        query_t,
+        query_l,
         k_t,
         k_l,
         v_t,
@@ -694,17 +741,23 @@
     ) = rest
     blocks = (x0, x1, x2, x3)
     keys = rows * len(blocks)
-    kv_copies = copies_of(((kt_in, k_t), (kl_in, k_l), (vt_in, v_t), (vl_in, v_l), (p_in, prob)), sems, 0)
-    x_copies = copies_of(
-        gather_pairs(blocks, rows, packs, xs), sems, 5
-    )
-    base = 5 + len(x_copies)
+    kv_copies = copies_of(((kt_in, k_t), (vt_in, v_t), (kl_in, k_l), (vl_in, v_l)), sems, 0)
+
+    def chances(at):
+        return pltpu.make_async_copy(p_in.at[at], prob.at[at], sems.at[4 + at])
+
+    for at in range(HEADS // 2):
+        chances(at).start()
+    base = 4 + HEADS // 2
     dq_l[...] = jnp.zeros_like(dq_l)
     dk_l[...] = jnp.zeros_like(dk_l)
     dv_l[...] = jnp.zeros_like(dv_l)
     wait_all(kv_copies)
+    x_copies = copies_of(gather_pairs(blocks, rows, packs, xs), sems, base)
+    base += len(x_copies)
 
     def head_pair(pair_at, unused):
+        chances(pair_at).wait()
         masks = lane_masks(pair_at)
         text_lanes = pl.ds(pl.multiple_of(pair_at * LANES, LANES), LANES)
         layout_lanes = pl.ds(pl.multiple_of(pair_at // 4 * LANES, LANES), LANES)
@@ -745,7 +798,7 @@
             dv_l[layout_lanes, span] += value_change[LANES:]
         return unused
 
-    lax.fori_loop(0, HEADS // 2, head_pair, 0)
+    lax.fori_loop(0, HEADS // 2, head_pair, 0, unroll=UNROLL_BACK)
     joined_l[:SLAB, :] = dk_l[...].astype(BF16)
     joined_l[SLAB:, :] = dv_l[...].astype(BF16)
     whole_t = dq_t[...].astype(F32)
@@ -753,6 +806,12 @@
     low_l = whole_l.astype(BF16)
     query_t[...] = whole_t.T.astype(BF16)
     query_l[...] = whole_l.T.astype(BF16)
+    out_copies = copies_of(
+        ((joined_t, joined_t_out), (joined_l, joined_l_out), (query_t, query_t_out), (query_l, query_l_out)),
+        sems,
+        base,
+    )
+    base += 4
     wait_all(x_copies)
     own = jnp.concatenate([xs[pl.ds(pack * keys, rows), :] for pack in range(packs)], axis=0)
     step = 192
@@ -793,6 +852,7 @@
         if grads.shape[1] > P_ROWS:
             grads[shard, P_ROWS:, :] = jnp.zeros((grads.shape[1] - P_ROWS, DT), BF16)
     wait_all(copies_of(in_lines(grads, subs, dp_size, targets), sems, base))
+    wait_all(out_copies)
 
 
 def attention_call(operands, packs, rows, dp_size, subs):
@@ -808,6 +868,7 @@
     ) + pair_shapes(subs)
     scratch = [
         pltpu.VMEM((every, DT + SLAB), BF16),
+        *(pltpu.VMEM(outs[at].shape, outs[at].dtype) for at in range(4)),
         pltpu.VMEM((every, DT), BF16),
         pltpu.VMEM((every, SLAB), BF16),
         pltpu.VMEM((every, DT), BF16),
@@ -820,34 +881,54 @@
         pltpu.VMEM((3 * DL, SLAB), BF16),
         pltpu.VMEM((4, lines, DT), BF16),
         pltpu.VMEM((16, DT), F32),
-        pltpu.SemaphoreType.DMA((24 + 4 * dp_size * len(subs),)),
+        pltpu.SemaphoreType.DMA((32 + 4 * dp_size * len(subs),)),
     ]
     return pl.pallas_call(
         functools.partial(attention_kernel, packs, rows, dp_size, subs),
         out_shape=outs,
         in_specs=[ANY] * 9 + [VMEM] * 12 + [ANY],
-        out_specs=[VMEM] * 4 + [ANY] * (2 * len(subs)),
+        out_specs=[ANY] * len(outs),
         scratch_shapes=scratch,
-        compiler_params=pltpu.CompilerParams(vmem_limit_bytes=LIMIT),
+        compiler_params=pltpu.CompilerParams(vmem_limit_bytes=LAST),
         cost_estimate=COST,
         name="attention_back",
     )(*operands)
 
 
-def input_kernel(packs, rows, joined_t, joined_l, query_t, query_l, wt, wl, after, give, hold):
+def input_kernel(
+    packs, rows, joined_in, joined_l, query_t, query_l, wt_in, wl, after, give, hold, joined_t, wt, totals, sums, sems
+):
     keys = joined_t.shape[1] // packs
+    pairs = []
+    for third in (1, 2):
+        lanes = pl.ds(third * DT, DT)
+        lines = pl.ds((third - 1) * DT, DT)
+        pairs += [(wt_in.at[:, lanes], wt.at[:, lanes]), (joined_in.at[lines, :], joined_t.at[lines, :])]
+    pairs.append((wt_in.at[:, pl.ds(0, DT)], wt.at[:, pl.ds(0, DT)]))
+    copies = copies_of(pairs, sems, 0)
+
+    def tokens_of(ref, lines, at):
+        spans = [slice(pack * keys + at * rows, pack * keys + (at + 1) * rows) for pack in range(packs)]
+        return jnp.concatenate([ref[lines, span] for span in spans], axis=1)
+
+    everything = slice(None)
+    for at in range(4):
+        sums[at, DT:, :] = dot(wl[:, SLAB:], tokens_of(joined_l, everything, at)).astype(BF16)
+    layout_own = dot(wl[:, :SLAB], query_l[...])
+    sums[0, DT:, :] = (sums[0, DT:, :].astype(F32) + layout_own).astype(BF16)
+    wait_all(copies[:2])
+    for at in range(4):
+        totals[at] = dot(wt[:, DT : 2 * DT], tokens_of(joined_t, slice(0, DT), at))
+    wait_all(copies[2:])
+    out = []
     for at in (3, 1, 2, 0):
+        total = totals[at] + dot(wt[:, 2 * DT :], tokens_of(joined_t, slice(DT, 2 * DT), at))
+        if at == 0:
+            total += dot(wt[:, :DT], query_t[...])
+        sums[at, :DT, :] = total.astype(BF16)
         target = (hold, give)[at % 2].at[at // 2]
-        spans = [slice(pack * keys + at * rows, pack * keys + (at + 1) * rows) for pack in range(packs)]
-        text_part = jnp.concatenate([joined_t[:, span] for span in spans], axis=1)
-        layout_part = jnp.concatenate([joined_l[:, span] for span in spans], axis=1)
-        text_sum = dot(wt[:, DT:], text_part)
-        layout_sum = dot(wl[:, SLAB:], layout_part)
-        if at == 0:
-            text_sum += dot(wt[:, :DT], query_t[...])
-            layout_sum += dot(wl[:, :SLAB], query_l[...])
-        target[:DT, :] = text_sum.astype(target.dtype)
-        target[DT:, :] = layout_sum.astype(target.dtype)
+        out += copies_of(((sums.at[at], target),), sems, 5 + at)
+    wait_all(out)
 
 
 def input_call(joined_t, joined_l, query_t, query_l, wt, wl, after, packs, rows):
@@ -855,12 +936,19 @@
     return pl.pallas_call(
         functools.partial(input_kernel, packs, rows),
         out_shape=(shape_of((2, DT + DL, tokens), BF16),) * 2,
-        in_specs=[VMEM] * 6 + [ANY],
-        out_specs=[VMEM] * 2,
+        in_specs=[ANY] + [VMEM] * 3 + [ANY, VMEM, after[1]],
+        out_specs=[ANY] * 2,
+        scratch_shapes=[
+            pltpu.VMEM(joined_t.shape, BF16),
+            pltpu.VMEM(wt.shape, BF16),
+            pltpu.VMEM((4, DT, tokens), F32),
+            pltpu.VMEM((4, DT + DL, tokens), BF16),
+            pltpu.SemaphoreType.DMA((9,)),
+        ],
         compiler_params=pltpu.CompilerParams(vmem_limit_bytes=LIMIT),
         cost_estimate=COST,
         name="input_back",
-    )(joined_t, joined_l, query_t, query_l, wt, wl, after)
+    )(joined_t, joined_l, query_t, query_l, wt, wl, after[0])
 
 
 def sensitivity_kernel(own, far, mid_t, mid_l, after, out_t, out_l):
@@ -875,12 +963,12 @@
     return pl.pallas_call(
         sensitivity_kernel,
         out_shape=(shape_of(mid_t.shape, F32), shape_of(mid_l.shape, F32)),
-        in_specs=[VMEM] * 4 + [ANY],
+        in_specs=[VMEM] * 4 + [after[1]],
         out_specs=[VMEM] * 2,
         compiler_params=pltpu.CompilerParams(vmem_limit_bytes=SMALL),
         cost_estimate=COST,
         name="sensitivity",
-    )(own, far, mid_t, mid_l, after)
+    )(own, far, mid_t, mid_l, after[0])
 
 
 def lines_in_order(dp_size, sources, subs, whole):
@@ -938,13 +1026,13 @@
     return pl.pallas_call(
         functools.partial(final_kernel, store, dp_size, subs),
         out_shape=tuple(shape_of(shape, F32) for shape in outs),
-        in_specs=[VMEM] * len(sources) + [ANY],
+        in_specs=[VMEM] * len(sources) + [after[1]],
         out_specs=[VMEM] * len(outs),
         scratch_shapes=[pltpu.VMEM((total_lines(subs), DT), F32)],
         compiler_params=pltpu.CompilerParams(vmem_limit_bytes=SMALL),
         cost_estimate=COST,
         name=name,
-    )(*sources, after)
+    )(*sources, after[0])
 
 
 def add_kernel(count, parts, *refs):
@@ -970,12 +1058,12 @@
         functools.partial(add_kernel, len(sources), parts),
         grid=(steps,),
         out_shape=(shape_of((size, width), BF16),) * parts,
-        in_specs=specs + [ANY],
+        in_specs=specs + [after[1]],
         out_specs=[pl.BlockSpec((block, width), lambda i: (i, 0))] * parts,
         compiler_params=pltpu.CompilerParams(vmem_limit_bytes=SMALL),
         cost_estimate=COST,
         name="add",
-    )(*[source for source in sources for unused in range(parts)], after)
+    )(*[source for source in sources for unused in range(parts)], after[0])
 
 
 def gate_call(arrays, after):
@@ -983,13 +1071,13 @@
     return pl.pallas_call(
         lambda *refs: None,
         out_shape=tuple(shape_of(array.shape, array.dtype) for array in arrays),
-        in_specs=[ANY] * (count + 1),
+        in_specs=[ANY] * count + [after[1]],
         out_specs=[ANY] * count,
         input_output_aliases={at: at for at in range(count)},
         compiler_params=pltpu.CompilerParams(vmem_limit_bytes=SMALL),
         cost_estimate=COST,
         name="gate",
-    )(*arrays, after)
+    )(*arrays, after[0])
 
 
 def join_kernel(count, *refs):
@@ -1004,12 +1092,12 @@
     return pl.pallas_call(
         functools.partial(join_kernel, len(sources)),
         out_shape=shape_of((len(sources) * lines, width), BF16),
-        in_specs=[VMEM] * len(sources) + [ANY],
+        in_specs=[VMEM] * len(sources) + [after[1]],
         out_specs=VMEM,
         compiler_params=pltpu.CompilerParams(vmem_limit_bytes=SMALL),
         cost_estimate=COST,
         name="join",
-    )(*sources, after)
+    )(*sources, after[0])
 
 
 def sent(array, group, index, seq_size, dp_size):
@@ -1060,7 +1148,7 @@
 SPLIT_S = ((768, "y1x2B"), )
 SPLIT_E = ((640, "1xy2B"), (512, "xyzB"), )
 SPLIT_P = ((256, "xy12B"), (384, "yxzB"), )
-ORDER = "B S0 GE E1 E0 C E1 S0 E0 GP D E1 P0 S0 E0 P1 GX E1 X0 E0 E1 S0 P0 E0 FX E1 S0 P0 E0 P0 P1 S0 P0 E0 P1 P0 S0 P0 P1 FE P1 P1 FS FP"
+ORDER = ('B', 'S0', 'GE', 'E1', 'E0', 'C', 'E1', 'S0', 'E0', 'GP', 'D', 'E1', 'P0', 'S0', 'E0', 'P1', 'GX', 'E1', 'X0', 'E0', 'E1', 'S0', 'P0', 'E0', 'FX', 'E1', 'S0', 'P0', 'E0', 'P0', 'P1', 'S0', 'P0', 'E0', 'P1', 'P0', 'S0', 'P0', 'P1', 'FE', 'P1', 'P1', 'FS', 'FP')
 
 
 def local(
@@ -1149,13 +1237,13 @@
             contexts=(ctx_t, ctx_l),
             first_sums=(sf_t, sf_l),
         )
-        return sf_t
+        return sf_t, HBM
 
     def middle(after):
         mid_t, mid_l, dctx_t, dctx_l, sm_t, sm_l, so_t, so_l, *pairs = middle_call(
             (
                 *values["tail"], text_shrink, text_expand, text_merge, turned_shrink,
-                layout_expand, layout_merge, text_gains, layout_gains, after,
+                layout_expand, layout_merge, text_gains, layout_gains, after[0],
             ),
             packs, rows, dp_size, subs["E"],
         )
@@ -1163,47 +1251,47 @@
         values.update(
             middles=(mid_t, mid_l), deltas=(dctx_t, dctx_l), second_sums=(sm_t, sm_l, so_t, so_l)
         )
-        return sm_t
+        return sm_t, HBM
 
     def attention(after):
         joined_t, joined_l, query_t, query_l, *pairs = attention_call(
             (
                 *blocks, *values["attended"], *values["deltas"],
-                *values["contexts"], *values["first_sums"], *values["second_sums"], after,
+                *values["contexts"], *values["first_sums"], *values["second_sums"], after[0],
             ),
             packs, rows, dp_size, subs["P"],
         )
         values["P pairs"] = pairs
         values.update(joined=(joined_t, joined_l, query_t, query_l))
-        return query_l
+        return query_l, HBM
 
     def inputs(after):
         give, hold = input_call(*values["joined"], text_project, wl, after, packs, rows)
         values["X pairs"] = [give, hold]
-        return hold
+        return hold, HBM
 
     def inputs_gate(after):
         give, hold = gate_call(values["X pairs"], after)
         lines = 2 * (DT + DL)
         values.update(inputs=[hold.reshape(lines, -1), send(give, core, 1).reshape(lines, -1)])
-        return hold
+        return hold, ANY
 
     def gate(name):
         def call(after):
             pairs = gate_call(values[name + " pairs"], after)
             begin(name, pairs)
-            return pairs[1]
+            return pairs[1], ANY
 
         return call
 
     def inputs_add(after):
         own, onward = add_call(values["inputs"], 2, after)
         values.update(onward=(own, send(onward, (Y,), 1)))
-        return own
+        return own, ANY
 
     def inputs_end(after):
         values.update(sens=sensitivity_call(*values["onward"], *values["middles"], after))
-        return values["sens"][1]
+        return values["sens"][1], HBM
 
     def end(name, store, label, outs):
         def call(after):
@@ -1211,7 +1299,7 @@
             values[name] = final_call(
                 store, label, sources, after, dp_size, subs[name], outs
             )
-            return values[name][-1]
+            return values[name][-1], HBM
 
         return call
 
@@ -1246,7 +1334,7 @@
         except StopIteration as stop:
             halves[name] = stop.value
             del calls[name]
-        return outs[0] if isinstance(outs, (tuple, list)) else outs
+        return (outs[0] if isinstance(outs, (tuple, list)) else outs), ANY
 
     def finish(name, after):
         for at in range(len(subs[name])):
@@ -1255,7 +1343,7 @@
         return after
 
     token = forward(None)
-    for label in ORDER.split():
+    for label in ORDER:
         if label in kernels:
             if label[0] == "F" and label[1] in subs:
                 token = finish(label[1], token)

time: 244 us -> 232 us (0.951)
  Pallas kernels: 96.8 us -> 81.8 us
  starting transfers between devices: 55.3 us -> 59.4 us
    pallas_call x24, Pallas kernels: 17.7 us -> 13.1 us  [add_call(): pl.pallas_call(functools.partial(add_kernel, len(sources), parts), grid=(...]
    ppermute x32, starting transfers between devices: 43.6 us -> 47.7 us  [sent(): lax.ppermute(array, 'dp', [(at, at ^ other) for at in range(dp_size)])]
    pallas_call x1, Pallas kernels: 26.2 us -> 22.3 us  [forward_call(): pl.pallas_call(functools.partial(forward_kernel, packs, rows, dp_size, su...]
    pallas_call x1, Pallas kernels: 19.2 us -> 15.4 us  [attention_call(): pl.pallas_call(functools.partial(attention_kernel, packs, rows, dp_size,...]
    pallas_call x1, Pallas kernels: 17.4 us -> 14.5 us  [middle_call(): pl.pallas_call(functools.partial(middle_kernel, dp_size, subs), out_shape...]
    unnamed x56 -> x92, local copies, waits for them, and re-layouts: 13.9 us -> 12.1 us
  transfers between devices with their start and end apart: 47 -> 47, of which waited for: 21 -> 24; matrix products, arithmetic and copies ran while one was open for 0% -> 0% of each run, Pallas kernels for 25% -> 22%
where the time goes in v3:
time: 232 us; the launch traced here: 230 us
  Pallas kernels  81.8 us (35%)
  waiting for transfers between devices  75.7 us (33%)
  starting transfers between devices  59.4 us (26%)
  local copies, waits for them, and re-layouts  12.1 us (5%)
    ppermute x32, waiting for transfers between devices, sent(): lax.ppermute(array, 'dp', [(at, at ^ other) for at in range(dp_size)])  56.3 us
    ppermute x32, starting transfers between devices, sent(): lax.ppermute(array, 'dp', [(at, at ^ other) for at in range(dp_size)])  47.7 us
    pallas_call x1, Pallas kernels, forward_call(): pl.pallas_call(functools.partial(forward_kernel, packs, rows, dp_size, su...  22.3 us
    ppermute x15, waiting for transfers between devices, sent(): lax.ppermute(array, 'seq', [(at, at ^ across) for at in range(seq_size)])  19.5 us
    pallas_call x1, Pallas kernels, attention_call(): pl.pallas_call(functools.partial(attention_kernel, packs, rows, dp_size,...  15.4 us
    pallas_call x1, Pallas kernels, middle_call(): pl.pallas_call(functools.partial(middle_kernel, dp_size, subs), out_shape...  14.5 us
    pallas_call x24, Pallas kernels, add_call(): pl.pallas_call(functools.partial(add_kernel, len(sources), parts), grid=(...  13.1 us
    unnamed x92, local copies, waits for them, and re-layouts  12.1 us
  transfers between devices with their start and end apart: 47, of which 24 were waited for; matrix products, arithmetic and copies ran while one was open for 0% of the time, Pallas kernels for 22%

profile of v3, /device:TPU:0, one launch (start us, length us, event | category | flops | bytes accessed | tf_op | source)
XLA Modules:
  0.0 230.5 jit_solution(1120700532487145063)
XLA Ops:
  0.7 2.2 prepare.1
  2.8 3.0 %collective-permute-start.1 = (bf16[2,128,1024]{2,1,0:T(8,128)(2,1)}, bf16[2,128,1024]{2,1,0:T(8,128)(2,1)S(1)}, u32[]{:S(2)}, u32[]{:S(2)}) collective-permute-start(bf16[2,128,1024]{2,1,0:T(8,128)(2,1)} %get-tuple-element.137.x0), channel_id=1, source_target_pairs={{0,2},{1,3},{2,0},{3,1},{4,6},{5,7},{6,4},{7,5},{8,10},{9,11},{10,... | collective-permute-start | bytes 1572872 | tf_op jit(solution)/shard_map/ppermute | solution.py:1112
  5.8 12.1 %collective-permute-done.1.x2 = bf16[2,128,1024]{2,1,0:T(8,128)(2,1)S(1)} collective-permute-done((bf16[2,128,1024]{2,1,0:T(8,128)(2,1)}, bf16[2,128,1024]{2,1,0:T(8,128)(2,1)S(1)}, u32[]{:S(2)}, u32[]{:S(2)}) %collective-permute-start.1) | collective-permute-done | bytes 524320 | tf_op jit(solution)/shard_map/ppermute | solution.py:1112
  17.9 1.9 collective-permute-done.2.x3
  20.6 22.3 %forward.1 = (bf16[256,768]{1,0:T(8,128)(2,1)}, bf16[2,192,128]{2,1,0:T(8,128)(2,1)}, bf16[256,768]{1,0:T(8,128)(2,1)}, bf16[256,256]{1,0:T(8,128)(2,1)}, bf16[1...) custom-call(bf16[2,128,1024]{2,1,0:T(8,128)(2,1)} %get-tuple-element, ...), custom_call_target="tpu_custom_call" | custom-call | flops 1 | bytes 1 | tf_op jit(solution)/shard_map/forward/pallas_call | solution.py:508
  43.2 14.5 %middle.1 = (f32[256,768]{1,0:T(8,128)}, f32[2,192,128]{2,1,0:T(8,128)}, bf16[256,768]{1,0:T(8,128)(2,1)}, bf16[256,256]{1,0:T(8,128)(2,1)}, f32[8,768]{1,0:T(8,...) custom-call(bf16[256,768]{1,0:T(8,128)(2,1)} %get-tuple-element.150., ...), custom_call_target="tpu_custom_call" | custom-call | flops 1 | bytes 1 | tf_op jit(solution)/shard_map/middle/pallas_call | solution.py:676
  58.5 3.5 %add.24 = (bf16[768,768]{1,0:T(8,128)(2,1)S(1)}, bf16[768,768]{1,0:T(8,128)(2,1)S(1)}) custom-call(bf16[1536,768]{1,0:T(8,128)(2,1)S(1)} %copy-done.7, bf16[1536,768]{1,0:T(8,128)(2,1)S(1)} %copy-done.7, bf16[1536,768]{1,0:T(8,128)(2,1)} %collective-permute-done.3.refs_2_.refs_3_, bf16[1536,768]{1,0:T(8,128)(2,1)} %collective-permute-done.3.refs_2_.refs_3_, ...), custom_call_target="tpu_custom_call" | custom-call | flops 1 | bytes 1 | tf_op jit(solution)/shard_map/add/pallas_call | solution.py:1057
  62.7 1.8 collective-permute-start.7
  64.5 4.0 %collective-permute-done.5.refs_2_.refs_3_ = bf16[1024,768]{1,0:T(8,128)(2,1)S(1)} collective-permute-done((bf16[1024,768]{1,0:T(8,128)(2,1)S(1)}, bf16[1024,768]{1,0:T(8,128)(2,1)S(1)}, u32[]{:S(2)}, u32[]{:S(2)}) %collective-permute-start.5) | collective-permute-done | bytes 1572896 | tf_op jit(solution)/shard_map/ppermute | solution.py:1112
  69.6 1.9 collective-permute-start.6
  71.5 1.5 collective-permute-start.8
  73.2 15.4 %attention_back.1 = (bf16[1536,1024]{1,0:T(8,128)(2,1)S(1)}, bf16[512,1024]{1,0:T(8,128)(2,1)S(1)}, bf16[768,256]{1,0:T(8,128)(2,1)S(1)}, bf16[256,256]{1,0:T(8,...) custom-call(bf16[2,128,1024]{2,1,0:T(8,128)(2,1)S(1)} %copy-done.12,, ...), custom_call_target="tpu_custom_call" | custom-call | flops 1 | bytes 1 | tf_op jit(solution)/shard_map/attention_back/pallas_call | solution.py:886
  91.0 1.1 add.27
  92.2 1.5 add.28
  97.0 1.7 collective-permute-start.11
  98.7 1.5 collective-permute-start.10
  100.2 1.5 collective-permute-start.13
  101.7 7.7 %input_back.1 = (bf16[2,960,256]{2,1,0:T(8,128)(2,1)}, bf16[2,960,256]{2,1,0:T(8,128)(2,1)}) custom-call(bf16[1536,1024]{1,0:T(8,128)(2,1)} %copy-done.11, bf16[512,1024]{1,0:T(8,128)(2,1)} %copy-done.24, bf16[768,256]{1,0:T(8,128)(2,1)} %copy-done.33, bf16[256,256]{1,0:T(8,128)(2,1)} %copy-done.28, bf16[768,2304]{1,0:T(8,128)(2,1)} %wt_in.3, ...), custom_call_target="tpu_custom_call" | custom-call | flops 1 | bytes 1 | tf_op jit(solution)/shard_map/input_back/pallas_call | solution.py:936
  109.4 1.5 collective-permute-done.13.refs_4_.refs_5_.refs_6_.refs_7_
  110.9 1.2 copy-done.1
  113.2 1.3 add.31
  114.6 1.2 add.32
  115.8 1.2 add.33
  119.0 2.6 %collective-permute-start.16 = (bf16[64,768]{1,0:T(8,128)(2,1)S(1)}, bf16[64,768]{1,0:T(8,128)(2,1)S(1)}, u32[]{:S(2)}, u32[]{:S(2)}) collective-permute-start(bf16[64,768]{1,0:T(8,128)(2,1)S(1)} %get-tuple-element.215), channel_id=1, source_target_pairs={{0,16},{4,20},{8,24},{12,28},{16,0},{20,4},{24,8},{28,12},{1,17},{... | collective-permute-start | bytes 294920 | tf_op jit(solution)/shard_map/ppermute | solution.py:1114
  121.6 1.3 collective-permute-start.17
  122.9 1.5 collective-permute-start.19
  124.4 1.4 collective-permute-done.15.refs_1_
  125.8 4.2 %collective-permute-done.17.refs_3_ = bf16[64,768]{1,0:T(8,128)(2,1)S(1)} collective-permute-done((bf16[64,768]{1,0:T(8,128)(2,1)S(1)}, bf16[64,768]{1,0:T(8,128)(2,1)S(1)}, u32[]{:S(2)}, u32[]{:S(2)}) %collective-permute-start.17) | collective-permute-done | bytes 98336 | tf_op jit(solution)/shard_map/ppermute | solution.py:1114
  130.5 1.6 collective-permute-start.18
  132.6 1.5 collective-permute-start.22
  134.6 3.6 %collective-permute-start.23 = (bf16[64,768]{1,0:T(8,128)(2,1)S(1)}, bf16[64,768]{1,0:T(8,128)(2,1)S(1)}, u32[]{:S(2)}, u32[]{:S(2)}) collective-permute-start(bf16[64,768]{1,0:T(8,128)(2,1)S(1)} %add.35.refs_4_.refs_0_), channel_id=1, source_target_pairs={{0,16},{4,20},{8,24},{12,28},{16,0},{20,4},{24,8},{28,12},{1,17},{... | collective-permute-start | bytes 294920 | tf_op jit(solution)/shard_map/ppermute | solution.py:1114
  138.3 3.9 %collective-permute-done.23.refs_1_ = bf16[64,768]{1,0:T(8,128)(2,1)S(1)} collective-permute-done((bf16[64,768]{1,0:T(8,128)(2,1)S(1)}, bf16[64,768]{1,0:T(8,128)(2,1)S(1)}, u32[]{:S(2)}, u32[]{:S(2)}) %collective-permute-start.23) | collective-permute-done | bytes 98336 | tf_op jit(solution)/shard_map/ppermute | solution.py:1114
  142.2 1.6 collective-permute-start.20
  143.9 4.9 %collective-permute-done.22.refs_2_.refs_3_ = bf16[192,768]{1,0:T(8,128)(2,1)S(1)} collective-permute-done((bf16[192,768]{1,0:T(8,128)(2,1)S(1)}, bf16[192,768]{1,0:T(8,128)(2,1)S(1)}, u32[]{:S(2)}, u32[]{:S(2)}) %collective-permute-start.22) | collective-permute-done | bytes 294944 | tf_op jit(solution)/shard_map/ppermute | solution.py:1114
  148.8 2.1 collective-permute-start.26
  151.6 1.9 collective-permute-start.25
  154.7 1.2 sensitivity.1
  155.9 1.2 collective-permute-done.26.refs_1_
  158.1 6.1 %collective-permute-done.25.refs_1_ = bf16[96,768]{1,0:T(8,128)(2,1)S(1)} collective-permute-done((bf16[96,768]{1,0:T(8,128)(2,1)S(1)}, bf16[96,768]{1,0:T(8,128)(2,1)S(1)}, u32[]{:S(2)}, u32[]{:S(2)}) %collective-permute-start.25) | collective-permute-done | bytes 147488 | tf_op jit(solution)/shard_map/ppermute | solution.py:1114
  164.3 1.2 collective-permute-done.28.refs_1_
  165.6 2.0 collective-permute-start.27
  167.6 1.4 collective-permute-start.30
  169.0 7.0 %collective-permute-done.27.refs_2_.refs_3_ = bf16[64,768]{1,0:T(8,128)(2,1)S(1)} collective-permute-done((bf16[64,768]{1,0:T(8,128)(2,1)S(1)}, bf16[64,768]{1,0:T(8,128)(2,1)S(1)}, u32[]{:S(2)}, u32[]{:S(2)}) %collective-permute-start.27) | collective-permute-done | bytes 98336 | tf_op jit(solution)/shard_map/ppermute | solution.py:1114
  176.0 2.3 %collective-permute-start.29 = (bf16[32,768]{1,0:T(8,128)(2,1)S(1)}, bf16[32,768]{1,0:T(8,128)(2,1)S(1)}, u32[]{:S(2)}, u32[]{:S(2)}) collective-permute-start(bf16[32,768]{1,0:T(8,128)(2,1)S(1)} %get-tuple-element.235), channel_id=1, source_target_pairs={{0,16},{4,20},{8,24},{12,28},{16,0},{20,4},{24,8},{28,12},{1,17},{... | collective-permute-start | bytes 147464 | tf_op jit(solution)/shard_map/ppermute | solution.py:1114
  179.1 2.0 collective-permute-done.29.refs_1_
  181.8 1.8 collective-permute-start.36
  183.6 1.5 collective-permute-start.43
  185.1 3.0 %collective-permute-start.32 = (bf16[32,768]{1,0:T(8,128)(2,1)S(1)}, bf16[32,768]{1,0:T(8,128)(2,1)S(1)}, u32[]{:S(2)}, u32[]{:S(2)}) collective-permute-start(bf16[32,768]{1,0:T(8,128)(2,1)S(1)} %add.45.refs_2_.refs_0_), channel_id=1, source_target_pairs={{0,16},{4,20},{8,24},{12,28},{16,0},{20,4},{24,8},{28,12},{1,17},{... | collective-permute-start | bytes 147464 | tf_op jit(solution)/shard_map/ppermute | solution.py:1114
  188.5 1.7 collective-permute-done.32.refs_1_
  190.3 2.9 %collective-permute-start.35 = (bf16[64,768]{1,0:T(8,128)(2,1)S(1)}, bf16[64,768]{1,0:T(8,128)(2,1)S(1)}, u32[]{:S(2)}, u32[]{:S(2)}) collective-permute-start(bf16[64,768]{1,0:T(8,128)(2,1)S(1)} %join.15.refs_2_.refs_0_), channel_id=1, source_target_pairs={{0,8},{4,12},{8,0},{12,4},{16,24},{20,28},{24,16},{28,20},{1,9},{5... | collective-permute-start | bytes 294920 | tf_op jit(solution)/shard_map/ppermute | solution.py:1114
  193.2 2.5 %collective-permute-start.39 = (bf16[48,768]{1,0:T(8,128)(2,1)S(1)}, bf16[48,768]{1,0:T(8,128)(2,1)S(1)}, u32[]{:S(2)}, u32[]{:S(2)}) collective-permute-start(bf16[48,768]{1,0:T(8,128)(2,1)S(1)} %get-tuple-element.241), channel_id=1, source_target_pairs={{0,16},{4,20},{8,24},{12,28},{16,0},{20,4},{24,8},{28,12},{1,17},{... | collective-permute-start | bytes 221192 | tf_op jit(solution)/shard_map/ppermute | solution.py:1114
  195.7 3.3 %collective-permute-done.38.refs_1_ = bf16[48,768]{1,0:T(8,128)(2,1)S(1)} collective-permute-done((bf16[48,768]{1,0:T(8,128)(2,1)S(1)}, bf16[48,768]{1,0:T(8,128)(2,1)S(1)}, u32[]{:S(2)}, u32[]{:S(2)}) %collective-permute-start.38) | collective-permute-done | bytes 73760 | tf_op jit(solution)/shard_map/ppermute | solution.py:1114
  199.6 1.4 collective-permute-start.46
  201.0 4.2 %collective-permute-done.40.refs_3_ = bf16[48,768]{1,0:T(8,128)(2,1)S(1)} collective-permute-done((bf16[48,768]{1,0:T(8,128)(2,1)S(1)}, bf16[48,768]{1,0:T(8,128)(2,1)S(1)}, u32[]{:S(2)}, u32[]{:S(2)}) %collective-permute-start.40) | collective-permute-done | bytes 73760 | tf_op jit(solution)/shard_map/ppermute | solution.py:1114
  205.7 1.8 collective-permute-done.43.refs_3_
  207.4 2.0 expand_out.1
  209.5 1.4 collective-permute-done.41.refs_1_
  211.7 1.2 collective-permute-start.44
  212.9 4.0 %collective-permute-done.44.refs_1_ = bf16[96,768]{1,0:T(8,128)(2,1)S(1)} collective-permute-done((bf16[96,768]{1,0:T(8,128)(2,1)S(1)}, bf16[96,768]{1,0:T(8,128)(2,1)S(1)}, u32[]{:S(2)}, u32[]{:S(2)}) %collective-permute-start.44) | collective-permute-done | bytes 147488 | tf_op jit(solution)/shard_map/ppermute | solution.py:1114
  216.9 1.6 collective-permute-start.45
  220.1 1.7 shrink_out.1.refs_4_
  221.8 5.6 %collective-permute-done.37.refs_1_ = bf16[128,768]{1,0:T(8,128)(2,1)S(1)} collective-permute-done((bf16[128,768]{1,0:T(8,128)(2,1)S(1)}, bf16[128,768]{1,0:T(8,128)(2,1)S(1)}, u32[]{:S(2)}, u32[]{:S(2)}) %collective-permute-start.37) | collective-permute-done | bytes 196640 | tf_op jit(solution)/shard_map/ppermute | solution.py:1114
  227.4 1.7 copy-done.6
  229.0 1.5 project_out.1
  (168 shorter events, 22.2 us)
Async XLA Ops:
  2.8 15.1 %collective-permute-start.1 = (bf16[2,128,1024]{2,1,0:T(8,128)(2,1)}, bf16[2,128,1024]{2,1,0:T(8,128)(2,1)S(1)}, u32[]{:S(2)}, u32[]{:S(2)}) collective-permute-start(bf16[2,128,1024]{2,1,0:T(8,128)(2,1)} %get-tuple-element.137.x0), channel_id=1, source_target_pairs={{0,2},{1,3},{2,0},{3,1},{4,6},{5,7},{6,4},{7,5},{8,10},{9,11},{10,... | collective-permute-start | bytes 1572872 | tf_op jit(solution)/shard_map/ppermute | solution.py:1112
  5.8 12.1 %collective-permute-start = (bf16[2,128,1024]{2,1,0:T(8,128)(2,1)}, bf16[2,128,1024]{2,1,0:T(8,128)(2,1)S(1)}, u32[]{:S(2)}, u32[]{:S(2)}) collective-permute-start(bf16[2,128,1024]{2,1,0:T(8,128)(2,1)} %get-tuple-element.137.x0), channel_id=1, source_target_pairs={{0,1},{1,0},{2,3},{3,2},{4,5},{5,4},{6,7},{7,6},{8,9},{9,8},{10,11... | collective-permute-start | bytes 1572872 | tf_op jit(solution)/shard_map/ppermute | solution.py:1112
  17.9 1.9 collective-permute-start.2
  43.0 14.7 %collective-permute-start.3 = (bf16[1536,768]{1,0:T(8,128)(2,1)}, bf16[1536,768]{1,0:T(8,128)(2,1)}, u32[]{:S(2)}, u32[]{:S(2)}) collective-permute-start(bf16[1536,768]{1,0:T(8,128)(2,1)} %get-tuple-element.176), channel_id=1, source_target_pairs={{0,1},{1,0},{2,3},{3,2},{4,5},{5,4},{6,7},{7,6},{8,9},{9,8},{10,11... | collective-permute-start | bytes 7077896 | tf_op jit(solution)/shard_map/ppermute | solution.py:1112
  43.2 14.5 %copy-start.7 = (bf16[1536,768]{1,0:T(8,128)(2,1)S(1)}, bf16[1536,768]{1,0:T(8,128)(2,1)}, u32[]{:S(2)}) copy-start(bf16[1536,768]{1,0:T(8,128)(2,1)} %get-tuple-element.175.refs_0_.refs_1_) | copy-start | bytes 7077892
  62.2 6.7 %collective-permute-start.4 = (bf16[1280,768]{1,0:T(8,128)(2,1)S(1)}, bf16[1280,768]{1,0:T(8,128)(2,1)S(1)}, u32[]{:S(2)}, u32[]{:S(2)}) collective-permute-start(bf16[1280,768]{1,0:T(8,128)(2,1)S(1)} %get-tuple-element.179), channel_id=1, source_target_pairs={{0,1},{1,0},{2,3},{3,2},{4,5},{5,4},{6,7},{7,6},{8,9},{9,8},{10,11... | collective-permute-start | bytes 5898248 | tf_op jit(solution)/shard_map/ppermute | solution.py:1112
  62.6 5.8 %collective-permute-start.5 = (bf16[1024,768]{1,0:T(8,128)(2,1)S(1)}, bf16[1024,768]{1,0:T(8,128)(2,1)S(1)}, u32[]{:S(2)}, u32[]{:S(2)}) collective-permute-start(bf16[1024,768]{1,0:T(8,128)(2,1)S(1)} %get-tuple-element.181), channel_id=1, source_target_pairs={{0,1},{1,0},{2,3},{3,2},{4,5},{5,4},{6,7},{7,6},{8,9},{9,8},{10,11... | collective-permute-start | bytes 4718600 | tf_op jit(solution)/shard_map/ppermute | solution.py:1112
  62.7 29.4 %collective-permute-start.7 = (bf16[768,768]{1,0:T(8,128)(2,1)S(1)}, bf16[768,768]{1,0:T(8,128)(2,1)S(1)}, u32[]{:S(2)}, u32[]{:S(2)}) collective-permute-start(bf16[768,768]{1,0:T(8,128)(2,1)S(1)} %get-tuple-element.193), channel_id=1, source_target_pairs={{0,2},{1,3},{2,0},{3,1},{4,6},{5,7},{6,4},{7,5},{8,10},{9,11},{10,... | collective-permute-start | bytes 3538952 | tf_op jit(solution)/shard_map/ppermute | solution.py:1112
  68.4 4.6 %copy-start.22 = (bf16[1024,768]{1,0:T(8,128)(2,1)S(1)}, bf16[1024,768]{1,0:T(8,128)(2,1)}, u32[]{:S(2)}) copy-start(bf16[1024,768]{1,0:T(8,128)(2,1)} %get-tuple-element.145.vt_in) | copy-start | bytes 4718596
  68.4 4.6 %copy-start.31 = (bf16[256,768]{1,0:T(8,128)(2,1)S(1)}, bf16[256,768]{1,0:T(8,128)(2,1)}, u32[]{:S(2)}) copy-start(bf16[256,768]{1,0:T(8,128)(2,1)} %get-tuple-element.148.q_t) | copy-start | bytes 1179652
  68.4 4.6 %copy-start.32 = (bf16[256,768]{1,0:T(8,128)(2,1)S(1)}, bf16[256,768]{1,0:T(8,128)(2,1)}, u32[]{:S(2)}) copy-start(bf16[256,768]{1,0:T(8,128)(2,1)} %get-tuple-element.164.dctx_t) | copy-start | bytes 1179652
  68.4 4.6 %copy-start.40 = (f32[8,768]{1,0:T(8,128)S(1)}, f32[8,768]{1,0:T(8,128)}, u32[]{:S(2)}) copy-start(f32[8,768]{1,0:T(8,128)} %get-tuple-element.167.refs_4_.sm_t) | copy-start | bytes 73732
  68.4 4.6 %copy-start.42 = (f32[1,3072]{1,0:T(1,128)S(1)}, f32[1,3072]{1,0:T(1,128)}, u32[]{:S(2)}) copy-start(f32[1,3072]{1,0:T(1,128)} %get-tuple-element.169.so_t) | copy-start | bytes 36868
  68.5 4.6 %copy-start.43 = (f32[8,192]{1,0:T(8,128)S(1)}, f32[8,192]{1,0:T(8,128)}, u32[]{:S(2)}) copy-start(f32[8,192]{1,0:T(8,128)} %get-tuple-element.166.sf_l) | copy-start | bytes 18436
  68.5 4.6 %copy-start.44 = (f32[8,192]{1,0:T(8,128)S(1)}, f32[8,192]{1,0:T(8,128)}, u32[]{:S(2)}) copy-start(f32[8,192]{1,0:T(8,128)} %get-tuple-element.168.sm_l) | copy-start | bytes 18436
  68.9 4.1 %copy-start.10 = (bf16[6,2,256,512]{3,2,1,0:T(8,128)(2,1)S(1)}, bf16[6,2,256,512]{3,2,1,0:T(8,128)(2,1)}, u32[]{:S(2)}) copy-start(bf16[6,2,256,512]{3,2,1,0:T(8,128)(2,1)} %get-tuple-element.147.p_in) | copy-start | bytes 9437188
  68.9 4.1 %copy-start.12 = (bf16[2,128,1024]{2,1,0:T(8,128)(2,1)S(1)}, bf16[2,128,1024]{2,1,0:T(8,128)(2,1)}, u32[]{:S(2)}) copy-start(bf16[2,128,1024]{2,1,0:T(8,128)(2,1)} %get-tuple-element.137.x0) | copy-start | bytes 1572868
  69.0 4.1 %copy-start.14 = (bf16[2,128,1024]{2,1,0:T(8,128)(2,1)S(1)}, bf16[2,128,1024]{2,1,0:T(8,128)(2,1)}, u32[]{:S(2)}) copy-start(bf16[2,128,1024]{2,1,0:T(8,128)(2,1)} %copy-done.13) | copy-start | bytes 1572868
  69.0 4.1 %copy-start.16 = (bf16[2,128,1024]{2,1,0:T(8,128)(2,1)S(1)}, bf16[2,128,1024]{2,1,0:T(8,128)(2,1)}, u32[]{:S(2)}) copy-start(bf16[2,128,1024]{2,1,0:T(8,128)(2,1)} %copy-done.15) | copy-start | bytes 1572868
  69.0 4.1 %copy-start.18 = (bf16[2,128,1024]{2,1,0:T(8,128)(2,1)S(1)}, bf16[2,128,1024]{2,1,0:T(8,128)(2,1)}, u32[]{:S(2)}) copy-start(bf16[2,128,1024]{2,1,0:T(8,128)(2,1)} %copy-done.17) | copy-start | bytes 1572868
  69.0 4.1 %copy-start.20 = (bf16[256,768]{1,0:T(8,128)(2,1)S(1)}, bf16[256,768]{1,0:T(8,128)(2,1)}, u32[]{:S(2)}) copy-start(bf16[256,768]{1,0:T(8,128)(2,1)} %get-tuple-element.161.ctx_t_in.ctx_t) | copy-start | bytes 1179652
  69.0 4.1 %copy-start.21 = (bf16[1024,768]{1,0:T(8,128)(2,1)S(1)}, bf16[1024,768]{1,0:T(8,128)(2,1)}, u32[]{:S(2)}) copy-start(bf16[1024,768]{1,0:T(8,128)(2,1)} %get-tuple-element.143.kt_in) | copy-start | bytes 4718596
  69.6 24.2 %collective-permute-start.6 = (bf16[640,768]{1,0:T(8,128)(2,1)S(1)}, bf16[640,768]{1,0:T(8,128)(2,1)S(1)}, u32[]{:S(2)}, u32[]{:S(2)}) collective-permute-start(bf16[640,768]{1,0:T(8,128)(2,1)S(1)} %get-tuple-element.192), channel_id=1, source_target_pairs={{0,8},{4,12},{8,0},{12,4},{16,24},{20,28},{24,16},{28,20},{1,9},{5... | collective-permute-start | bytes 2949128 | tf_op jit(solution)/shard_map/ppermute | solution.py:1114
  71.5 19.5 %collective-permute-start.8 = (bf16[512,768]{1,0:T(8,128)(2,1)S(1)}, bf16[512,768]{1,0:T(8,128)(2,1)S(1)}, u32[]{:S(2)}, u32[]{:S(2)}) collective-permute-start(bf16[512,768]{1,0:T(8,128)(2,1)S(1)} %get-tuple-element.194), channel_id=1, source_target_pairs={{0,4},{4,0},{8,12},{12,8},{16,20},{20,16},{24,28},{28,24},{1,5},{5... | collective-permute-start | bytes 2359304 | tf_op jit(solution)/shard_map/ppermute | solution.py:1114
  96.4 20.6 %collective-permute-start.9 = (bf16[768,768]{1,0:T(8,128)(2,1)}, bf16[768,768]{1,0:T(8,128)(2,1)S(1)}, u32[]{:S(2)}, u32[]{:S(2)}) collective-permute-start(bf16[768,768]{1,0:T(8,128)(2,1)} %get-tuple-element.202), channel_id=1, source_target_pairs={{0,1},{1,0},{2,3},{3,2},{4,5},{5,4},{6,7},{7,6},{8,9},{9,8},{10,11... | collective-permute-start | bytes 3538952 | tf_op jit(solution)/shard_map/ppermute | solution.py:1112
  96.4 15.7 %collective-permute-start.12 = (bf16[512,768]{1,0:T(8,128)(2,1)}, bf16[512,768]{1,0:T(8,128)(2,1)}, u32[]{:S(2)}, u32[]{:S(2)}) collective-permute-start(bf16[512,768]{1,0:T(8,128)(2,1)} %get-tuple-element.205), channel_id=1, source_target_pairs={{0,1},{1,0},{2,3},{3,2},{4,5},{5,4},{6,7},{7,6},{8,9},{9,8},{10,11... | collective-permute-start | bytes 2359304 | tf_op jit(solution)/shard_map/ppermute | solution.py:1112
  97.0 17.6 %collective-permute-start.11 = (bf16[384,768]{1,0:T(8,128)(2,1)}, bf16[384,768]{1,0:T(8,128)(2,1)}, u32[]{:S(2)}, u32[]{:S(2)}) collective-permute-start(bf16[384,768]{1,0:T(8,128)(2,1)} %get-tuple-element.204), channel_id=1, source_target_pairs={{0,8},{4,12},{8,0},{12,4},{16,24},{20,28},{24,16},{28,20},{1,9},{5... | collective-permute-start | bytes 1769480 | tf_op jit(solution)/shard_map/ppermute | solution.py:1114
  98.7 17.1 %collective-permute-start.10 = (bf16[320,768]{1,0:T(8,128)(2,1)}, bf16[320,768]{1,0:T(8,128)(2,1)}, u32[]{:S(2)}, u32[]{:S(2)}) collective-permute-start(bf16[320,768]{1,0:T(8,128)(2,1)} %get-tuple-element.203), channel_id=1, source_target_pairs={{0,4},{4,0},{8,12},{12,8},{16,20},{20,16},{24,28},{28,24},{1,5},{5... | collective-permute-start | bytes 1474568 | tf_op jit(solution)/shard_map/ppermute | solution.py:1114
  100.2 10.7 %collective-permute-start.13 = (bf16[256,768]{1,0:T(8,128)(2,1)}, bf16[256,768]{1,0:T(8,128)(2,1)S(1)}, u32[]{:S(2)}, u32[]{:S(2)}) collective-permute-start(bf16[256,768]{1,0:T(8,128)(2,1)} %get-tuple-element.206), channel_id=1, source_target_pairs={{0,2},{1,3},{2,0},{3,1},{4,6},{5,7},{6,4},{7,5},{8,10},{9,11},{10,... | collective-permute-start | bytes 1179656 | tf_op jit(solution)/shard_map/ppermute | solution.py:1112
  118.5 11.6 %collective-permute-start.14 = (bf16[2,960,256]{2,1,0:T(8,128)(2,1)S(1)}, bf16[2,960,256]{2,1,0:T(8,128)(2,1)S(1)}, u32[]{:S(2)}, u32[]{:S(2)}) collective-permute-start(bf16[2,960,256]{2,1,0:T(8,128)(2,1)S(1)} %get-tuple-element.213), channel_id=1, source_target_pairs={{0,1},{1,0},{2,3},{3,2},{4,5},{5,4},{6,7},{7,6},{8,9},{9,8},{10,11... | collective-permute-start | bytes 2949128 | tf_op jit(solution)/shard_map/ppermute | solution.py:1112
  118.5 7.3 %collective-permute-start.15 = (bf16[64,768]{1,0:T(8,128)(2,1)S(1)}, bf16[64,768]{1,0:T(8,128)(2,1)S(1)}, u32[]{:S(2)}, u32[]{:S(2)}) collective-permute-start(bf16[64,768]{1,0:T(8,128)(2,1)S(1)} %get-tuple-element.214), channel_id=1, source_target_pairs={{0,8},{4,12},{8,0},{12,4},{16,24},{20,28},{24,16},{28,20},{1,9},{5... | collective-permute-start | bytes 294920 | tf_op jit(solution)/shard_map/ppermute | solution.py:1114
  119.0 6.9 %collective-permute-start.16 = (bf16[64,768]{1,0:T(8,128)(2,1)S(1)}, bf16[64,768]{1,0:T(8,128)(2,1)S(1)}, u32[]{:S(2)}, u32[]{:S(2)}) collective-permute-start(bf16[64,768]{1,0:T(8,128)(2,1)S(1)} %get-tuple-element.215), channel_id=1, source_target_pairs={{0,16},{4,20},{8,24},{12,28},{16,0},{20,4},{24,8},{28,12},{1,17},{... | collective-permute-start | bytes 294920 | tf_op jit(solution)/shard_map/ppermute | solution.py:1114
  121.6 8.5 %collective-permute-start.17 = (bf16[64,768]{1,0:T(8,128)(2,1)S(1)}, bf16[64,768]{1,0:T(8,128)(2,1)S(1)}, u32[]{:S(2)}, u32[]{:S(2)}) collective-permute-start(bf16[64,768]{1,0:T(8,128)(2,1)S(1)} %get-tuple-element.216), channel_id=1, source_target_pairs={{0,24},{4,28},{8,16},{12,20},{16,8},{20,12},{24,0},{28,4},{1,25},{... | collective-permute-start | bytes 294920 | tf_op jit(solution)/shard_map/ppermute | solution.py:1114
  122.9 11.7 %collective-permute-start.19 = (bf16[160,768]{1,0:T(8,128)(2,1)S(1)}, bf16[160,768]{1,0:T(8,128)(2,1)S(1)}, u32[]{:S(2)}, u32[]{:S(2)}) collective-permute-start(bf16[160,768]{1,0:T(8,128)(2,1)S(1)} %get-tuple-element.221), channel_id=1, source_target_pairs={{0,2},{1,3},{2,0},{3,1},{4,6},{5,7},{6,4},{7,5},{8,10},{9,11},{10,... | collective-permute-start | bytes 737288 | tf_op jit(solution)/shard_map/ppermute | solution.py:1112
  130.5 23.1 %collective-permute-start.18 = (bf16[960,256]{1,0:T(8,128)(2,1)S(1)}, bf16[960,256]{1,0:T(8,128)(2,1)S(1)}, u32[]{:S(2)}, u32[]{:S(2)}) collective-permute-start(bf16[960,256]{1,0:T(8,128)(2,1)S(1)} %get-tuple-element.218), channel_id=1, source_target_pairs={{0,2},{1,3},{2,0},{3,1},{4,6},{5,7},{6,4},{7,5},{8,10},{9,11},{10,... | collective-permute-start | bytes 1474568 | tf_op jit(solution)/shard_map/ppermute | solution.py:1112
  132.0 18.9 %collective-permute-start.21 = (bf16[256,768]{1,0:T(8,128)(2,1)S(1)}, bf16[256,768]{1,0:T(8,128)(2,1)S(1)}, u32[]{:S(2)}, u32[]{:S(2)}) collective-permute-start(bf16[256,768]{1,0:T(8,128)(2,1)S(1)} %get-tuple-element.224), channel_id=1, source_target_pairs={{0,4},{4,0},{8,12},{12,8},{16,20},{20,16},{24,28},{28,24},{1,5},{5... | collective-permute-start | bytes 1179656 | tf_op jit(solution)/shard_map/ppermute | solution.py:1114
  132.6 16.2 %collective-permute-start.22 = (bf16[192,768]{1,0:T(8,128)(2,1)S(1)}, bf16[192,768]{1,0:T(8,128)(2,1)S(1)}, u32[]{:S(2)}, u32[]{:S(2)}) collective-permute-start(bf16[192,768]{1,0:T(8,128)(2,1)S(1)} %get-tuple-element.225), channel_id=1, source_target_pairs={{0,4},{4,0},{8,12},{12,8},{16,20},{20,16},{24,28},{28,24},{1,5},{5... | collective-permute-start | bytes 884744 | tf_op jit(solution)/shard_map/ppermute | solution.py:1114
  134.1 44.3 %collective-permute-start.31 = (bf16[384,768]{1,0:T(8,128)(2,1)S(1)}, bf16[384,768]{1,0:T(8,128)(2,1)S(1)}, u32[]{:S(2)}, u32[]{:S(2)}) collective-permute-start(bf16[384,768]{1,0:T(8,128)(2,1)S(1)} %get-tuple-element.236), channel_id=1, source_target_pairs={{0,2},{1,3},{2,0},{3,1},{4,6},{5,7},{6,4},{7,5},{8,10},{9,11},{10,... | collective-permute-start | bytes 1769480 | tf_op jit(solution)/shard_map/ppermute | solution.py:1112
  134.6 7.6 %collective-permute-start.23 = (bf16[64,768]{1,0:T(8,128)(2,1)S(1)}, bf16[64,768]{1,0:T(8,128)(2,1)S(1)}, u32[]{:S(2)}, u32[]{:S(2)}) collective-permute-start(bf16[64,768]{1,0:T(8,128)(2,1)S(1)} %add.35.refs_4_.refs_0_), channel_id=1, source_target_pairs={{0,16},{4,20},{8,24},{12,28},{16,0},{20,4},{24,8},{28,12},{1,17},{... | collective-permute-start | bytes 294920 | tf_op jit(solution)/shard_map/ppermute | solution.py:1114
  142.2 9.4 %collective-permute-start.20 = (bf16[80,768]{1,0:T(8,128)(2,1)S(1)}, bf16[80,768]{1,0:T(8,128)(2,1)S(1)}, u32[]{:S(2)}, u32[]{:S(2)}) collective-permute-start(bf16[80,768]{1,0:T(8,128)(2,1)S(1)} %get-tuple-element.223), channel_id=1, source_target_pairs={{0,16},{4,20},{8,24},{12,28},{16,0},{20,4},{24,8},{28,12},{1,17},{... | collective-permute-start | bytes 368648 | tf_op jit(solution)/shard_map/ppermute | solution.py:1114
  143.9 10.8 %copy-start.26 = (f32[256,768]{1,0:T(8,128)S(1)}, f32[256,768]{1,0:T(8,128)}, u32[]{:S(2)}) copy-start(f32[256,768]{1,0:T(8,128)} %get-tuple-element.219.mid_t) | copy-start | bytes 2359300
  143.9 10.8 %copy-start.34 = (f32[2,192,128]{2,1,0:T(8,128)S(1)}, f32[2,192,128]{2,1,0:T(8,128)}, u32[]{:S(2)}) copy-start(f32[2,192,128]{2,1,0:T(8,128)} %get-tuple-element.220.mid_l) | copy-start | bytes 589828
  148.8 8.3 %collective-permute-start.26 = (bf16[128,768]{1,0:T(8,128)(2,1)S(1)}, bf16[128,768]{1,0:T(8,128)(2,1)S(1)}, u32[]{:S(2)}, u32[]{:S(2)}) collective-permute-start(bf16[128,768]{1,0:T(8,128)(2,1)S(1)} %join.10.refs_4_.refs_0_), channel_id=1, source_target_pairs={{0,8},{4,12},{8,0},{12,4},{16,24},{20,28},{24,16},{28,20},{1,9},{5... | collective-permute-start | bytes 589832 | tf_op jit(solution)/shard_map/ppermute | solution.py:1114
  151.0 13.2 %collective-permute-start.24 = (bf16[128,768]{1,0:T(8,128)(2,1)S(1)}, bf16[128,768]{1,0:T(8,128)(2,1)S(1)}, u32[]{:S(2)}, u32[]{:S(2)}) collective-permute-start(bf16[128,768]{1,0:T(8,128)(2,1)S(1)} %get-tuple-element.230), channel_id=1, source_target_pairs={{0,2},{1,3},{2,0},{3,1},{4,6},{5,7},{6,4},{7,5},{8,10},{9,11},{10,... | collective-permute-start | bytes 589832 | tf_op jit(solution)/shard_map/ppermute | solution.py:1112
  151.6 12.5 %collective-permute-start.25 = (bf16[96,768]{1,0:T(8,128)(2,1)S(1)}, bf16[96,768]{1,0:T(8,128)(2,1)S(1)}, u32[]{:S(2)}, u32[]{:S(2)}) collective-permute-start(bf16[96,768]{1,0:T(8,128)(2,1)S(1)} %get-tuple-element.231), channel_id=1, source_target_pairs={{0,16},{4,20},{8,24},{12,28},{16,0},{20,4},{24,8},{28,12},{1,17},{... | collective-permute-start | bytes 442376 | tf_op jit(solution)/shard_map/ppermute | solution.py:1114
  153.6 11.9 %collective-permute-start.28 = (bf16[80,768]{1,0:T(8,128)(2,1)S(1)}, bf16[80,768]{1,0:T(8,128)(2,1)S(1)}, u32[]{:S(2)}, u32[]{:S(2)}) collective-permute-start(bf16[80,768]{1,0:T(8,128)(2,1)S(1)} %add.40.after.refs_0_), channel_id=1, source_target_pairs={{0,16},{4,20},{8,24},{12,28},{16,0},{20,4},{24,8},{28,12},{1,17},{... | collective-permute-start | bytes 368648 | tf_op jit(solution)/shard_map/ppermute | solution.py:1114
  165.5 15.6 %collective-permute-start.34 = (bf16[160,768]{1,0:T(8,128)(2,1)S(1)}, bf16[160,768]{1,0:T(8,128)(2,1)S(1)}, u32[]{:S(2)}, u32[]{:S(2)}) collective-permute-start(bf16[160,768]{1,0:T(8,128)(2,1)S(1)} %join.12.refs_4_.refs_0_), channel_id=1, source_target_pairs={{0,8},{4,12},{8,0},{12,4},{16,24},{20,28},{24,16},{28,20},{1,9},{5... | collective-permute-start | bytes 737288 | tf_op jit(solution)/shard_map/ppermute | solution.py:1114
  165.6 10.4 %collective-permute-start.27 = (bf16[64,768]{1,0:T(8,128)(2,1)S(1)}, bf16[64,768]{1,0:T(8,128)(2,1)S(1)}, u32[]{:S(2)}, u32[]{:S(2)}) collective-permute-start(bf16[64,768]{1,0:T(8,128)(2,1)S(1)} %get-tuple-element.233), channel_id=1, source_target_pairs={{0,8},{4,12},{8,0},{12,4},{16,24},{20,28},{24,16},{28,20},{1,9},{5... | collective-permute-start | bytes 294920 | tf_op jit(solution)/shard_map/ppermute | solution.py:1114
  167.6 11.5 %collective-permute-start.30 = (bf16[96,768]{1,0:T(8,128)(2,1)S(1)}, bf16[96,768]{1,0:T(8,128)(2,1)S(1)}, u32[]{:S(2)}, u32[]{:S(2)}) collective-permute-start(bf16[96,768]{1,0:T(8,128)(2,1)S(1)} %add.41.refs_4_.refs_0_), channel_id=1, source_target_pairs={{0,16},{4,20},{8,24},{12,28},{16,0},{20,4},{24,8},{28,12},{1,17},{... | collective-permute-start | bytes 442376 | tf_op jit(solution)/shard_map/ppermute | solution.py:1114
  176.0 5.1 %collective-permute-start.29 = (bf16[32,768]{1,0:T(8,128)(2,1)S(1)}, bf16[32,768]{1,0:T(8,128)(2,1)S(1)}, u32[]{:S(2)}, u32[]{:S(2)}) collective-permute-start(bf16[32,768]{1,0:T(8,128)(2,1)S(1)} %get-tuple-element.235), channel_id=1, source_target_pairs={{0,16},{4,20},{8,24},{12,28},{16,0},{20,4},{24,8},{28,12},{1,17},{... | collective-permute-start | bytes 147464 | tf_op jit(solution)/shard_map/ppermute | solution.py:1114
  178.5 9.9 %collective-permute-start.33 = (bf16[192,768]{1,0:T(8,128)(2,1)S(1)}, bf16[192,768]{1,0:T(8,128)(2,1)S(1)}, u32[]{:S(2)}, u32[]{:S(2)}) collective-permute-start(bf16[192,768]{1,0:T(8,128)(2,1)S(1)} %get-tuple-element.238), channel_id=1, source_target_pairs={{0,4},{4,0},{8,12},{12,8},{16,20},{20,16},{24,28},{28,24},{1,5},{5... | collective-permute-start | bytes 884744 | tf_op jit(solution)/shard_map/ppermute | solution.py:1114
  181.2 26.3 %collective-permute-start.42 = (bf16[320,768]{1,0:T(8,128)(2,1)S(1)}, bf16[320,768]{1,0:T(8,128)(2,1)S(1)}, u32[]{:S(2)}, u32[]{:S(2)}) collective-permute-start(bf16[320,768]{1,0:T(8,128)(2,1)S(1)} %join.14.refs_8_.refs_0_), channel_id=1, source_target_pairs={{0,4},{4,0},{8,12},{12,8},{16,20},{20,16},{24,28},{28,24},{1,5},{5... | collective-permute-start | bytes 1474568 | tf_op jit(solution)/shard_map/ppermute | solution.py:1114
  181.8 11.4 %collective-permute-start.36 = (bf16[192,768]{1,0:T(8,128)(2,1)S(1)}, bf16[192,768]{1,0:T(8,128)(2,1)S(1)}, u32[]{:S(2)}, u32[]{:S(2)}) collective-permute-start(bf16[192,768]{1,0:T(8,128)(2,1)S(1)} %join.13.refs_2_.refs_0_), channel_id=1, source_target_pairs={{0,8},{4,12},{8,0},{12,4},{16,24},{20,28},{24,16},{28,20},{1,9},{5... | collective-permute-start | bytes 884744 | tf_op jit(solution)/shard_map/ppermute | solution.py:1114
  183.6 23.8 %collective-permute-start.43 = (bf16[256,768]{1,0:T(8,128)(2,1)S(1)}, bf16[256,768]{1,0:T(8,128)(2,1)S(1)}, u32[]{:S(2)}, u32[]{:S(2)}) collective-permute-start(bf16[256,768]{1,0:T(8,128)(2,1)S(1)} %join.11.refs_2_), channel_id=1, source_target_pairs={{0,4},{4,0},{8,12},{12,8},{16,20},{20,16},{24,28},{28,24},{1,5},{5... | collective-permute-start | bytes 1179656 | tf_op jit(solution)/shard_map/ppermute | solution.py:1114
  185.1 5.2 %collective-permute-start.32 = (bf16[32,768]{1,0:T(8,128)(2,1)S(1)}, bf16[32,768]{1,0:T(8,128)(2,1)S(1)}, u32[]{:S(2)}, u32[]{:S(2)}) collective-permute-start(bf16[32,768]{1,0:T(8,128)(2,1)S(1)} %add.45.refs_2_.refs_0_), channel_id=1, source_target_pairs={{0,16},{4,20},{8,24},{12,28},{16,0},{20,4},{24,8},{28,12},{1,17},{... | collective-permute-start | bytes 147464 | tf_op jit(solution)/shard_map/ppermute | solution.py:1114
  190.3 9.3 %collective-permute-start.35 = (bf16[64,768]{1,0:T(8,128)(2,1)S(1)}, bf16[64,768]{1,0:T(8,128)(2,1)S(1)}, u32[]{:S(2)}, u32[]{:S(2)}) collective-permute-start(bf16[64,768]{1,0:T(8,128)(2,1)S(1)} %join.15.refs_2_.refs_0_), channel_id=1, source_target_pairs={{0,8},{4,12},{8,0},{12,4},{16,24},{20,28},{24,16},{28,20},{1,9},{5... | collective-permute-start | bytes 294920 | tf_op jit(solution)/shard_map/ppermute | solution.py:1114
  193.1 5.9 %collective-permute-start.38 = (bf16[48,768]{1,0:T(8,128)(2,1)S(1)}, bf16[48,768]{1,0:T(8,128)(2,1)S(1)}, u32[]{:S(2)}, u32[]{:S(2)}) collective-permute-start(bf16[48,768]{1,0:T(8,128)(2,1)S(1)} %get-tuple-element.240), channel_id=1, source_target_pairs={{0,8},{4,12},{8,0},{12,4},{16,24},{20,28},{24,16},{28,20},{1,9},{5... | collective-permute-start | bytes 221192 | tf_op jit(solution)/shard_map/ppermute | solution.py:1114
  193.2 7.8 %collective-permute-start.39 = (bf16[48,768]{1,0:T(8,128)(2,1)S(1)}, bf16[48,768]{1,0:T(8,128)(2,1)S(1)}, u32[]{:S(2)}, u32[]{:S(2)}) collective-permute-start(bf16[48,768]{1,0:T(8,128)(2,1)S(1)} %get-tuple-element.241), channel_id=1, source_target_pairs={{0,16},{4,20},{8,24},{12,28},{16,0},{20,4},{24,8},{28,12},{1,17},{... | collective-permute-start | bytes 221192 | tf_op jit(solution)/shard_map/ppermute | solution.py:1114
  199.1 6.2 %collective-permute-start.40 = (bf16[48,768]{1,0:T(8,128)(2,1)S(1)}, bf16[48,768]{1,0:T(8,128)(2,1)S(1)}, u32[]{:S(2)}, u32[]{:S(2)}) collective-permute-start(bf16[48,768]{1,0:T(8,128)(2,1)S(1)} %get-tuple-element.242), channel_id=1, source_target_pairs={{0,24},{4,28},{8,16},{12,20},{16,8},{20,12},{24,0},{28,4},{1,25},{... | collective-permute-start | bytes 221192 | tf_op jit(solution)/shard_map/ppermute | solution.py:1114
  199.6 20.5 %collective-permute-start.46 = (bf16[384,768]{1,0:T(8,128)(2,1)S(1)}, bf16[384,768]{1,0:T(8,128)(2,1)S(1)}, u32[]{:S(2)}, u32[]{:S(2)}) collective-permute-start(bf16[384,768]{1,0:T(8,128)(2,1)S(1)} %join.16.refs_2_.refs_0_), channel_id=1, source_target_pairs={{0,4},{4,0},{8,12},{12,8},{16,20},{20,16},{24,28},{28,24},{1,5},{5... | collective-permute-start | bytes 1769480 | tf_op jit(solution)/shard_map/ppermute | solution.py:1114
  205.3 5.6 %collective-permute-start.41 = (bf16[48,768]{1,0:T(8,128)(2,1)S(1)}, bf16[48,768]{1,0:T(8,128)(2,1)S(1)}, u32[]{:S(2)}, u32[]{:S(2)}) collective-permute-start(bf16[48,768]{1,0:T(8,128)(2,1)S(1)} %add.47.refs_4_.refs_0_), channel_id=1, source_target_pairs={{0,16},{4,20},{8,24},{12,28},{16,0},{20,4},{24,8},{28,12},{1,17},{... | collective-permute-start | bytes 221192 | tf_op jit(solution)/shard_map/ppermute | solution.py:1114
  211.7 5.2 %collective-permute-start.44 = (bf16[96,768]{1,0:T(8,128)(2,1)S(1)}, bf16[96,768]{1,0:T(8,128)(2,1)S(1)}, u32[]{:S(2)}, u32[]{:S(2)}) collective-permute-start(bf16[96,768]{1,0:T(8,128)(2,1)S(1)} %join.18.refs_0_.refs_2_), channel_id=1, source_target_pairs={{0,8},{4,12},{8,0},{12,4},{16,24},{20,28},{24,16},{28,20},{1,9},{5... | collective-permute-start | bytes 442376 | tf_op jit(solution)/shard_map/ppermute | solution.py:1114
  216.9 10.5 %collective-permute-start.45 = (bf16[192,768]{1,0:T(8,128)(2,1)S(1)}, bf16[192,768]{1,0:T(8,128)(2,1)S(1)}, u32[]{:S(2)}, u32[]{:S(2)}) collective-permute-start(bf16[192,768]{1,0:T(8,128)(2,1)S(1)} %join.19.refs_2_), channel_id=1, source_target_pairs={{0,4},{4,0},{8,12},{12,8},{16,20},{20,16},{24,28},{28,24},{1,5},{5... | collective-permute-start | bytes 884744 | tf_op jit(solution)/shard_map/ppermute | solution.py:1114
  218.5 8.8 %collective-permute-start.37 = (bf16[128,768]{1,0:T(8,128)(2,1)S(1)}, bf16[128,768]{1,0:T(8,128)(2,1)S(1)}, u32[]{:S(2)}, u32[]{:S(2)}) collective-permute-start(bf16[128,768]{1,0:T(8,128)(2,1)S(1)} %join.17.refs_4_.refs_0_), channel_id=1, source_target_pairs={{0,4},{4,0},{8,12},{12,8},{16,20},{20,16},{24,28},{28,24},{1,5},{5... | collective-permute-start | bytes 589832 | tf_op jit(solution)/shard_map/ppermute | solution.py:1114
  (29 other events, 65.2 us)

commit v4 on v3

--- a/solution.py
+++ b/solution.py
@@ -896,7 +896,7 @@
 
 
 def input_kernel(
-    packs, rows, joined_in, joined_l, query_t, query_l, wt_in, wl, after, give, hold, joined_t, wt, totals, sums, sems
+    packs, rows, joined_in, joined_l, query_t, query_l, wt_in, wl, after, give, hold, mark, joined_t, wt, totals, sums, sems
 ):
     keys = joined_t.shape[1] // packs
     pairs = []
@@ -916,6 +916,7 @@
         sums[at, DT:, :] = dot(wl[:, SLAB:], tokens_of(joined_l, everything, at)).astype(BF16)
     layout_own = dot(wl[:, :SLAB], query_l[...])
     sums[0, DT:, :] = (sums[0, DT:, :].astype(F32) + layout_own).astype(BF16)
+    mark[...] = layout_own[:8, :LANES]
     wait_all(copies[:2])
     for at in range(4):
         totals[at] = dot(wt[:, DT : 2 * DT], tokens_of(joined_t, slice(0, DT), at))
@@ -935,9 +936,9 @@
     tokens = packs * rows
     return pl.pallas_call(
         functools.partial(input_kernel, packs, rows),
-        out_shape=(shape_of((2, DT + DL, tokens), BF16),) * 2,
+        out_shape=(shape_of((2, DT + DL, tokens), BF16),) * 2 + (shape_of((8, LANES), F32),),
         in_specs=[ANY] + [VMEM] * 3 + [ANY, VMEM, after[1]],
-        out_specs=[ANY] * 2,
+        out_specs=[ANY] * 2 + [VMEM],
         scratch_shapes=[
             pltpu.VMEM(joined_t.shape, BF16),
             pltpu.VMEM(wt.shape, BF16),
@@ -951,7 +952,8 @@
     )(joined_t, joined_l, query_t, query_l, wt, wl, after[0])
 
 
-def sensitivity_kernel(own, far, mid_t, mid_l, after, out_t, out_l):
+def sensitivity_kernel(own, far, mid_t, mid_l, after, out_t, out_l, mark):
+    mark[...] = mid_t[:8, :LANES]
     total = own[...].astype(F32) + far[...].astype(F32)
     out_t[...] = mid_t[...] + total[:DT, :].T
     packs, unused, rows = mid_l.shape
@@ -962,9 +964,9 @@
 def sensitivity_call(own, far, mid_t, mid_l, after):
     return pl.pallas_call(
         sensitivity_kernel,
-        out_shape=(shape_of(mid_t.shape, F32), shape_of(mid_l.shape, F32)),
+        out_shape=(shape_of(mid_t.shape, F32), shape_of(mid_l.shape, F32), shape_of((8, LANES), F32)),
         in_specs=[VMEM] * 4 + [after[1]],
-        out_specs=[VMEM] * 2,
+        out_specs=[VMEM] * 3,
         compiler_params=pltpu.CompilerParams(vmem_limit_bytes=SMALL),
         cost_estimate=COST,
         name="sensitivity",
@@ -1019,15 +1021,16 @@
 def final_kernel(store, dp_size, subs, *refs):
     sources, outs, whole = refs[: 2 * len(subs)], refs[2 * len(subs) + 1 : -1], refs[-1]
     lines_in_order(dp_size, sources, subs, whole)
-    store(whole, *outs)
+    store(whole, *outs[:-1])
+    outs[-1][...] = whole[:8, :LANES]
 
 
 def final_call(store, name, sources, after, dp_size, subs, outs):
     return pl.pallas_call(
         functools.partial(final_kernel, store, dp_size, subs),
-        out_shape=tuple(shape_of(shape, F32) for shape in outs),
+        out_shape=tuple(shape_of(shape, F32) for shape in outs) + (shape_of((8, LANES), F32),),
         in_specs=[VMEM] * len(sources) + [after[1]],
-        out_specs=[VMEM] * len(outs),
+        out_specs=[VMEM] * (len(outs) + 1),
         scratch_shapes=[pltpu.VMEM((total_lines(subs), DT), F32)],
         compiler_params=pltpu.CompilerParams(vmem_limit_bytes=SMALL),
         cost_estimate=COST,
@@ -1146,9 +1149,9 @@
 
 
 SPLIT_S = ((768, "y1x2B"), )
-SPLIT_E = ((640, "1xy2B"), (512, "xyzB"), )
+SPLIT_E = ((576, "1xy2B"), (576, "xyzB"), )
 SPLIT_P = ((256, "xy12B"), (384, "yxzB"), )
-ORDER = ('B', 'S0', 'GE', 'E1', 'E0', 'C', 'E1', 'S0', 'E0', 'GP', 'D', 'E1', 'P0', 'S0', 'E0', 'P1', 'GX', 'E1', 'X0', 'E0', 'E1', 'S0', 'P0', 'E0', 'FX', 'E1', 'S0', 'P0', 'E0', 'P0', 'P1', 'S0', 'P0', 'E0', 'P1', 'P0', 'S0', 'P0', 'P1', 'FE', 'P1', 'P1', 'FS', 'FP')
+ORDER = ('B', 'NE', 'S0', 'E1', 'E0', 'C', 'GP', 'E1', 'S0', 'E0', 'P0', 'P1', 'D', 'E1', 'S0', 'E0', 'GX', 'E1', 'X0', 'E0', 'E1', 'S0', 'P0', 'E0', 'FX', 'E1', 'S0', 'P0', 'E0', 'P0', 'P1', 'S0', 'P0', 'E0', 'P1', 'P0', 'S0', 'P0', 'P1', 'FE', 'P1', 'P1', 'FS', 'FP')
 
 
 def local(
@@ -1266,21 +1269,21 @@
         return query_l, HBM
 
     def inputs(after):
-        give, hold = input_call(*values["joined"], text_project, wl, after, packs, rows)
+        give, hold, mark = input_call(*values["joined"], text_project, wl, after, packs, rows)
         values["X pairs"] = [give, hold]
-        return hold, HBM
-
-    def inputs_gate(after):
-        give, hold = gate_call(values["X pairs"], after)
+        return mark, ANY
+
+    def inputs_gate(after, gated=True):
+        give, hold = gate_call(values["X pairs"], after) if gated else values["X pairs"]
         lines = 2 * (DT + DL)
         values.update(inputs=[hold.reshape(lines, -1), send(give, core, 1).reshape(lines, -1)])
-        return hold, ANY
-
-    def gate(name):
+        return (hold, ANY) if gated else after
+
+    def gate(name, gated=True):
         def call(after):
-            pairs = gate_call(values[name + " pairs"], after)
+            pairs = gate_call(values[name + " pairs"], after) if gated else values[name + " pairs"]
             begin(name, pairs)
-            return pairs[1], ANY
+            return (pairs[1], ANY) if gated else after
 
         return call
 
@@ -1291,7 +1294,7 @@
 
     def inputs_end(after):
         values.update(sens=sensitivity_call(*values["onward"], *values["middles"], after))
-        return values["sens"][1], HBM
+        return values["sens"][2], ANY
 
     def end(name, store, label, outs):
         def call(after):
@@ -1299,7 +1302,7 @@
             values[name] = final_call(
                 store, label, sources, after, dp_size, subs[name], outs
             )
-            return values[name][-1], HBM
+            return values[name][-1], ANY
 
         return call
 
@@ -1311,6 +1314,9 @@
         "GE": gate("E"),
         "GP": gate("P"),
         "GX": inputs_gate,
+        "NE": gate("E", False),
+        "NP": gate("P", False),
+        "NX": functools.partial(inputs_gate, gated=False),
         "X0": inputs_add,
         "FX": inputs_end,
         "FS": end("S", shrink_store, "shrink_out", [(DT // 4, FT)]),
@@ -1352,10 +1358,10 @@
             token = advance(label, token)
 
     res_t, res_l = values["results"]
-    sens_t, sens_l = values["sens"]
-    (shrink_t,) = values["S"]
-    expand_t, merge_t, expand_l, shrink_l, merge_l = values["E"]
-    project_t, project_l, biases_t, gains_t, offsets_t, biases_l, gains_l, offsets_l = values["P"]
+    sens_t, sens_l, unused = values["sens"]
+    shrink_t, unused = values["S"]
+    expand_t, merge_t, expand_l, shrink_l, merge_l, unused = values["E"]
+    project_t, project_l, biases_t, gains_t, offsets_t, biases_l, gains_l, offsets_l, unused = values["P"]
     return (
         res_t.reshape(packs, rows, DT),
         res_l.transpose(0, 2, 1),

time: 232 us -> 221 us (0.953)
  starting transfers between devices: 59.4 us -> 54 us
  local copies, waits for them, and re-layouts: 12.1 us -> 8.73 us
    ppermute x32, starting transfers between devices: 47.7 us -> 42 us  [sent(): lax.ppermute(array, 'dp', [(at, at ^ other) for at in range(dp_size)])]
    ppermute x15, waiting for transfers between devices: 19.5 us -> 14.7 us  [sent(): lax.ppermute(array, 'seq', [(at, at ^ across) for at in range(seq_size)])]
    ppermute x32, waiting for transfers between devices: 56.3 us -> 60.8 us  [sent(): lax.ppermute(array, 'dp', [(at, at ^ other) for at in range(dp_size)])]
    pallas_call x24, Pallas kernels: 13.1 us -> 8.76 us  [add_call(): pl.pallas_call(functools.partial(add_kernel, len(sources), parts), grid=(...]
    unnamed x92 -> x82, local copies, waits for them, and re-layouts: 12.1 us -> 8.73 us
    pallas_call x1, Pallas kernels: 15.4 us -> 18 us  [attention_call(): pl.pallas_call(functools.partial(attention_kernel, packs, rows, dp_size,...]
  transfers between devices with their start and end apart: 47 -> 47, of which waited for: 24 -> 21; matrix products, arithmetic and copies ran while one was open for 0% -> 0% of each run, Pallas kernels for 22% -> 25%
where the time goes in v4:
time: 221 us; the launch traced here: 220 us
  Pallas kernels  80.6 us (36%)
  waiting for transfers between devices  75.5 us (34%)
  starting transfers between devices  54 us (24%)
  local copies, waits for them, and re-layouts  8.73 us (4%)
    ppermute x32, waiting for transfers between devices, sent(): lax.ppermute(array, 'dp', [(at, at ^ other) for at in range(dp_size)])  60.8 us
    ppermute x32, starting transfers between devices, sent(): lax.ppermute(array, 'dp', [(at, at ^ other) for at in range(dp_size)])  42 us
    pallas_call x1, Pallas kernels, forward_call(): pl.pallas_call(functools.partial(forward_kernel, packs, rows, dp_size, su...  22.3 us
    pallas_call x1, Pallas kernels, attention_call(): pl.pallas_call(functools.partial(attention_kernel, packs, rows, dp_size,...  18 us
    ppermute x15, waiting for transfers between devices, sent(): lax.ppermute(array, 'seq', [(at, at ^ across) for at in range(seq_size)])  14.7 us
    pallas_call x1, Pallas kernels, middle_call(): pl.pallas_call(functools.partial(middle_kernel, dp_size, subs), out_shape...  14.5 us
    ppermute x15, starting transfers between devices, sent(): lax.ppermute(array, 'seq', [(at, at ^ across) for at in range(seq_size)])  12.1 us
    pallas_call x24, Pallas kernels, add_call(): pl.pallas_call(functools.partial(add_kernel, len(sources), parts), grid=(...  8.76 us
  transfers between devices with their start and end apart: 47, of which 21 were waited for; matrix products, arithmetic and copies ran while one was open for 0% of the time, Pallas kernels for 25%

profile of v4, /device:TPU:0, one launch (start us, length us, event | category | flops | bytes accessed | tf_op | source)
XLA Modules:
  0.0 220.3 jit_solution(14495337025216648345)
XLA Ops:
  0.7 2.2 prepare.1
  2.8 3.0 %collective-permute-start.1 = (bf16[2,128,1024]{2,1,0:T(8,128)(2,1)}, bf16[2,128,1024]{2,1,0:T(8,128)(2,1)S(1)}, u32[]{:S(2)}, u32[]{:S(2)}) collective-permute-start(bf16[2,128,1024]{2,1,0:T(8,128)(2,1)} %get-tuple-element.138.x0), channel_id=1, source_target_pairs={{0,2},{1,3},{2,0},{3,1},{4,6},{5,7},{6,4},{7,5},{8,10},{9,11},{10,... | collective-permute-start | bytes 1572872 | tf_op jit(solution)/shard_map/ppermute | solution.py:1115
  5.8 12.1 %collective-permute-done.1.x2 = bf16[2,128,1024]{2,1,0:T(8,128)(2,1)S(1)} collective-permute-done((bf16[2,128,1024]{2,1,0:T(8,128)(2,1)}, bf16[2,128,1024]{2,1,0:T(8,128)(2,1)S(1)}, u32[]{:S(2)}, u32[]{:S(2)}) %collective-permute-start.1) | collective-permute-done | bytes 524320 | tf_op jit(solution)/shard_map/ppermute | solution.py:1115
  17.9 1.9 collective-permute-done.2.x3
  19.8 0.8 copy-done.13
  20.6 22.3 %forward.1 = (bf16[256,768]{1,0:T(8,128)(2,1)}, bf16[2,192,128]{2,1,0:T(8,128)(2,1)}, bf16[256,768]{1,0:T(8,128)(2,1)}, bf16[256,256]{1,0:T(8,128)(2,1)}, bf16[1...) custom-call(bf16[2,128,1024]{2,1,0:T(8,128)(2,1)} %get-tuple-element, ...), custom_call_target="tpu_custom_call" | custom-call | flops 1 | bytes 1 | tf_op jit(solution)/shard_map/forward/pallas_call | solution.py:508
  43.2 14.5 %middle.1 = (f32[256,768]{1,0:T(8,128)}, f32[2,192,128]{2,1,0:T(8,128)}, bf16[256,768]{1,0:T(8,128)(2,1)}, bf16[256,256]{1,0:T(8,128)(2,1)}, f32[8,768]{1,0:T(8,...) custom-call(bf16[256,768]{1,0:T(8,128)(2,1)} %get-tuple-element.151., ...), custom_call_target="tpu_custom_call" | custom-call | flops 1 | bytes 1 | tf_op jit(solution)/shard_map/middle/pallas_call | solution.py:676
  58.3 0.7 copy-done.32
  59.0 2.7 %add.24 = (bf16[768,768]{1,0:T(8,128)(2,1)S(1)}, bf16[768,768]{1,0:T(8,128)(2,1)S(1)}) custom-call(bf16[1536,768]{1,0:T(8,128)(2,1)S(1)} %copy-done.1, bf16[1536,768]{1,0:T(8,128)(2,1)S(1)} %copy-done.1, bf16[1536,768]{1,0:T(8,128)(2,1)} %collective-permute-done.5.refs_2_.refs_3_, bf16[1536,768]{1,0:T(8,128)(2,1)} %collective-permute-done.5.refs_2_.refs_3_, ...), custom_call_target="tpu_custom_call" | custom-call | flops 1 | bytes 1 | tf_op jit(solution)/shard_map/add/pallas_call | solution.py:1060
  61.8 1.8 collective-permute-start.9
  64.7 1.0 copy-done.2
  66.4 1.9 collective-permute-start.8
  68.3 1.5 collective-permute-start.10
  69.9 18.0 %attention_back.1 = (bf16[1536,1024]{1,0:T(8,128)(2,1)S(1)}, bf16[512,1024]{1,0:T(8,128)(2,1)S(1)}, bf16[768,256]{1,0:T(8,128)(2,1)S(1)}, bf16[256,256]{1,0:T(8,...) custom-call(bf16[2,128,1024]{2,1,0:T(8,128)(2,1)S(1)} %copy-done.8, ...), custom_call_target="tpu_custom_call" | custom-call | flops 1 | bytes 1 | tf_op jit(solution)/shard_map/attention_back/pallas_call | solution.py:886
  87.9 1.0 copy-done.18
  88.9 1.7 copy-done.6
  91.2 0.8 add.27
  92.1 1.4 add.28
  93.5 1.1 collective-permute-start.12
  94.6 0.9 add.29
  95.5 1.5 collective-permute-start.11
  97.0 1.5 collective-permute-start.13
  99.5 0.8 copy-done.4
  100.3 8.3 %input_back.1 = (bf16[2,960,256]{2,1,0:T(8,128)(2,1)}, bf16[2,960,256]{2,1,0:T(8,128)(2,1)}, f32[8,128]{1,0:T(8,128)}) custom-call(bf16[1536,1024]{1,0:T(8,128)(2,1)} %copy-done.6, bf16[512,1024]{1,0:T(8,128)(2,1)} %copy-done.18, bf16[768,256]{1,0:T(8,128)(2,1)} %copy-done.25, bf16[256,256]{1,0:T(8,128)(2,1)} %copy-done.22, bf16[768,2304]{1,0:T(8,128)(2,1)} %wt_in.3, ...), custom_call_target="tpu_custom_call" | custom-call | flops 1 | bytes 1 | tf_op jit(solution)/shard_map/input_back/pallas_call | solution.py:937
  109.7 1.0 copy-done
  111.1 1.0 collective-permute-start.15
  112.1 2.6 %collective-permute-start.16 = (bf16[64,768]{1,0:T(8,128)(2,1)S(1)}, bf16[64,768]{1,0:T(8,128)(2,1)S(1)}, u32[]{:S(2)}, u32[]{:S(2)}) collective-permute-start(bf16[64,768]{1,0:T(8,128)(2,1)S(1)} %get-tuple-element.213), channel_id=1, source_target_pairs={{0,16},{4,20},{8,24},{12,28},{16,0},{20,4},{24,8},{28,12},{1,17},{... | collective-permute-start | bytes 294920 | tf_op jit(solution)/shard_map/ppermute | solution.py:1117
  114.6 0.8 collective-permute-start.17
  115.4 1.1 collective-permute-start.19
  116.5 1.8 collective-permute-done.15.refs_1_
  118.4 4.2 %collective-permute-done.17.refs_3_ = bf16[64,768]{1,0:T(8,128)(2,1)S(1)} collective-permute-done((bf16[64,768]{1,0:T(8,128)(2,1)S(1)}, bf16[64,768]{1,0:T(8,128)(2,1)S(1)}, u32[]{:S(2)}, u32[]{:S(2)}) %collective-permute-start.17) | collective-permute-done | bytes 98336 | tf_op jit(solution)/shard_map/ppermute | solution.py:1117
  123.0 1.8 collective-permute-start.18
  124.8 1.5 collective-permute-start.21
  127.4 3.4 %collective-permute-start.23 = (bf16[64,768]{1,0:T(8,128)(2,1)S(1)}, bf16[64,768]{1,0:T(8,128)(2,1)S(1)}, u32[]{:S(2)}, u32[]{:S(2)}) collective-permute-start(bf16[64,768]{1,0:T(8,128)(2,1)S(1)} %add.35.refs_4_.refs_0_), channel_id=1, source_target_pairs={{0,16},{4,20},{8,24},{12,28},{16,0},{20,4},{24,8},{28,12},{1,17},{... | collective-permute-start | bytes 294920 | tf_op jit(solution)/shard_map/ppermute | solution.py:1117
  130.9 3.6 %collective-permute-done.23.refs_1_ = bf16[64,768]{1,0:T(8,128)(2,1)S(1)} collective-permute-done((bf16[64,768]{1,0:T(8,128)(2,1)S(1)}, bf16[64,768]{1,0:T(8,128)(2,1)S(1)}, u32[]{:S(2)}, u32[]{:S(2)}) %collective-permute-start.23) | collective-permute-done | bytes 98336 | tf_op jit(solution)/shard_map/ppermute | solution.py:1117
  134.5 2.0 collective-permute-start.20
  136.5 4.3 %collective-permute-done.22.refs_2_.refs_3_ = bf16[192,768]{1,0:T(8,128)(2,1)S(1)} collective-permute-done((bf16[192,768]{1,0:T(8,128)(2,1)S(1)}, bf16[192,768]{1,0:T(8,128)(2,1)S(1)}, u32[]{:S(2)}, u32[]{:S(2)}) %collective-permute-start.22) | collective-permute-done | bytes 294944 | tf_op jit(solution)/shard_map/ppermute | solution.py:1117
  140.9 2.3 %collective-permute-start.26 = (bf16[128,768]{1,0:T(8,128)(2,1)S(1)}, bf16[128,768]{1,0:T(8,128)(2,1)S(1)}, u32[]{:S(2)}, u32[]{:S(2)}) collective-permute-start(bf16[128,768]{1,0:T(8,128)(2,1)S(1)} %join.10.refs_4_.refs_0_), channel_id=1, source_target_pairs={{0,8},{4,12},{8,0},{12,4},{16,24},{20,28},{24,16},{28,20},{1,9},{5... | collective-permute-start | bytes 589832 | tf_op jit(solution)/shard_map/ppermute | solution.py:1117
  143.4 1.0 collective-permute-start.24
  144.4 1.4 collective-permute-start.25
  145.8 1.6 collective-permute-start.28
  147.4 1.2 sensitivity.1
  148.6 7.4 %collective-permute-done.25.refs_1_ = bf16[96,768]{1,0:T(8,128)(2,1)S(1)} collective-permute-done((bf16[96,768]{1,0:T(8,128)(2,1)S(1)}, bf16[96,768]{1,0:T(8,128)(2,1)S(1)}, u32[]{:S(2)}, u32[]{:S(2)}) %collective-permute-start.25) | collective-permute-done | bytes 147488 | tf_op jit(solution)/shard_map/ppermute | solution.py:1117
  156.2 1.2 collective-permute-done.28.refs_1_
  157.5 2.0 collective-permute-start.27
  159.5 1.2 collective-permute-start.30
  160.7 8.3 %collective-permute-done.27.refs_2_.refs_3_ = bf16[64,768]{1,0:T(8,128)(2,1)S(1)} collective-permute-done((bf16[64,768]{1,0:T(8,128)(2,1)S(1)}, bf16[64,768]{1,0:T(8,128)(2,1)S(1)}, u32[]{:S(2)}, u32[]{:S(2)}) %collective-permute-start.27) | collective-permute-done | bytes 98336 | tf_op jit(solution)/shard_map/ppermute | solution.py:1117
  169.0 0.8 collective-permute-start.29
  170.0 1.4 collective-permute-start.33
  171.4 3.0 %collective-permute-done.29.refs_1_ = bf16[32,768]{1,0:T(8,128)(2,1)S(1)} collective-permute-done((bf16[32,768]{1,0:T(8,128)(2,1)S(1)}, bf16[32,768]{1,0:T(8,128)(2,1)S(1)}, u32[]{:S(2)}, u32[]{:S(2)}) %collective-permute-start.29) | collective-permute-done | bytes 49184 | tf_op jit(solution)/shard_map/ppermute | solution.py:1117
  174.4 1.4 collective-permute-start.42
  176.5 2.9 %collective-permute-start.32 = (bf16[32,768]{1,0:T(8,128)(2,1)S(1)}, bf16[32,768]{1,0:T(8,128)(2,1)S(1)}, u32[]{:S(2)}, u32[]{:S(2)}) collective-permute-start(bf16[32,768]{1,0:T(8,128)(2,1)S(1)} %add.45.refs_2_.refs_0_), channel_id=1, source_target_pairs={{0,16},{4,20},{8,24},{12,28},{16,0},{20,4},{24,8},{28,12},{1,17},{... | collective-permute-start | bytes 147464 | tf_op jit(solution)/shard_map/ppermute | solution.py:1117
  180.0 1.8 collective-permute-done.32.refs_1_
  181.8 4.3 %collective-permute-start.35 = (bf16[64,768]{1,0:T(8,128)(2,1)S(1)}, bf16[64,768]{1,0:T(8,128)(2,1)S(1)}, u32[]{:S(2)}, u32[]{:S(2)}) collective-permute-start(bf16[64,768]{1,0:T(8,128)(2,1)S(1)} %join.15.refs_2_.refs_0_), channel_id=1, source_target_pairs={{0,8},{4,12},{8,0},{12,4},{16,24},{20,28},{24,16},{28,20},{1,9},{5... | collective-permute-start | bytes 294920 | tf_op jit(solution)/shard_map/ppermute | solution.py:1117
  186.2 1.1 collective-permute-start.39
  187.3 4.7 %collective-permute-done.38.refs_1_ = bf16[48,768]{1,0:T(8,128)(2,1)S(1)} collective-permute-done((bf16[48,768]{1,0:T(8,128)(2,1)S(1)}, bf16[48,768]{1,0:T(8,128)(2,1)S(1)}, u32[]{:S(2)}, u32[]{:S(2)}) %collective-permute-start.38) | collective-permute-done | bytes 73760 | tf_op jit(solution)/shard_map/ppermute | solution.py:1117
  192.8 5.4 %collective-permute-done.40.refs_3_ = bf16[48,768]{1,0:T(8,128)(2,1)S(1)} collective-permute-done((bf16[48,768]{1,0:T(8,128)(2,1)S(1)}, bf16[48,768]{1,0:T(8,128)(2,1)S(1)}, u32[]{:S(2)}, u32[]{:S(2)}) %collective-permute-start.40) | collective-permute-done | bytes 73760 | tf_op jit(solution)/shard_map/ppermute | solution.py:1117
  198.9 2.0 expand_out.1
  200.9 2.6 %collective-permute-done.41.refs_1_ = bf16[48,768]{1,0:T(8,128)(2,1)S(1)} collective-permute-done((bf16[48,768]{1,0:T(8,128)(2,1)S(1)}, bf16[48,768]{1,0:T(8,128)(2,1)S(1)}, u32[]{:S(2)}, u32[]{:S(2)}) %collective-permute-start.41) | collective-permute-done | bytes 73760 | tf_op jit(solution)/shard_map/ppermute | solution.py:1117
  203.6 5.1 %collective-permute-done.44.refs_1_ = bf16[96,768]{1,0:T(8,128)(2,1)S(1)} collective-permute-done((bf16[96,768]{1,0:T(8,128)(2,1)S(1)}, bf16[96,768]{1,0:T(8,128)(2,1)S(1)}, u32[]{:S(2)}, u32[]{:S(2)}) %collective-permute-start.44) | collective-permute-done | bytes 147488 | tf_op jit(solution)/shard_map/ppermute | solution.py:1117
  209.2 1.6 collective-permute-start.37
  211.5 1.7 shrink_out.1
  213.2 5.6 %collective-permute-done.37.refs_1_ = bf16[128,768]{1,0:T(8,128)(2,1)S(1)} collective-permute-done((bf16[128,768]{1,0:T(8,128)(2,1)S(1)}, bf16[128,768]{1,0:T(8,128)(2,1)S(1)}, u32[]{:S(2)}, u32[]{:S(2)}) %collective-permute-start.37) | collective-permute-done | bytes 196640 | tf_op jit(solution)/shard_map/ppermute | solution.py:1117
  218.8 1.5 project_out.1
  (157 shorter events, 12.0 us)
Async XLA Ops:
  2.8 15.1 %collective-permute-start.1 = (bf16[2,128,1024]{2,1,0:T(8,128)(2,1)}, bf16[2,128,1024]{2,1,0:T(8,128)(2,1)S(1)}, u32[]{:S(2)}, u32[]{:S(2)}) collective-permute-start(bf16[2,128,1024]{2,1,0:T(8,128)(2,1)} %get-tuple-element.138.x0), channel_id=1, source_target_pairs={{0,2},{1,3},{2,0},{3,1},{4,6},{5,7},{6,4},{7,5},{8,10},{9,11},{10,... | collective-permute-start | bytes 1572872 | tf_op jit(solution)/shard_map/ppermute | solution.py:1115
  5.8 12.1 %collective-permute-start = (bf16[2,128,1024]{2,1,0:T(8,128)(2,1)}, bf16[2,128,1024]{2,1,0:T(8,128)(2,1)S(1)}, u32[]{:S(2)}, u32[]{:S(2)}) collective-permute-start(bf16[2,128,1024]{2,1,0:T(8,128)(2,1)} %get-tuple-element.138.x0), channel_id=1, source_target_pairs={{0,1},{1,0},{2,3},{3,2},{4,5},{5,4},{6,7},{7,6},{8,9},{9,8},{10,11... | collective-permute-start | bytes 1572872 | tf_op jit(solution)/shard_map/ppermute | solution.py:1115
  17.9 1.9 collective-permute-start.2
  43.0 15.3 %collective-permute-start.5 = (bf16[1536,768]{1,0:T(8,128)(2,1)}, bf16[1536,768]{1,0:T(8,128)(2,1)}, u32[]{:S(2)}, u32[]{:S(2)}) collective-permute-start(bf16[1536,768]{1,0:T(8,128)(2,1)} %get-tuple-element.177), channel_id=1, source_target_pairs={{0,1},{1,0},{2,3},{3,2},{4,5},{5,4},{6,7},{7,6},{8,9},{9,8},{10,11... | collective-permute-start | bytes 7077896 | tf_op jit(solution)/shard_map/ppermute | solution.py:1115
  43.2 15.1 %copy-start.1 = (bf16[1536,768]{1,0:T(8,128)(2,1)S(1)}, bf16[1536,768]{1,0:T(8,128)(2,1)}, u32[]{:S(2)}) copy-start(bf16[1536,768]{1,0:T(8,128)(2,1)} %get-tuple-element.176.refs_0_.refs_1_) | copy-start | bytes 7077892
  57.7 7.0 %collective-permute-start.3 = (bf16[1280,768]{1,0:T(8,128)(2,1)}, bf16[1280,768]{1,0:T(8,128)(2,1)S(1)}, u32[]{:S(2)}, u32[]{:S(2)}) collective-permute-start(bf16[1280,768]{1,0:T(8,128)(2,1)} %get-tuple-element.173), channel_id=1, source_target_pairs={{0,1},{1,0},{2,3},{3,2},{4,5},{5,4},{6,7},{7,6},{8,9},{9,8},{10,11... | collective-permute-start | bytes 5898248 | tf_op jit(solution)/shard_map/ppermute | solution.py:1115
  58.1 6.1 %collective-permute-start.4 = (bf16[1024,768]{1,0:T(8,128)(2,1)}, bf16[1024,768]{1,0:T(8,128)(2,1)S(1)}, u32[]{:S(2)}, u32[]{:S(2)}) collective-permute-start(bf16[1024,768]{1,0:T(8,128)(2,1)} %get-tuple-element.175), channel_id=1, source_target_pairs={{0,1},{1,0},{2,3},{3,2},{4,5},{5,4},{6,7},{7,6},{8,9},{9,8},{10,11... | collective-permute-start | bytes 4718600 | tf_op jit(solution)/shard_map/ppermute | solution.py:1115
  59.0 5.2 %copy-start.3 = (bf16[1024,768]{1,0:T(8,128)(2,1)S(1)}, bf16[1024,768]{1,0:T(8,128)(2,1)}, u32[]{:S(2)}) copy-start(bf16[1024,768]{1,0:T(8,128)(2,1)} %get-tuple-element.174.refs_0_.refs_1_) | copy-start | bytes 4718596
  61.8 30.3 %collective-permute-start.9 = (bf16[768,768]{1,0:T(8,128)(2,1)S(1)}, bf16[768,768]{1,0:T(8,128)(2,1)S(1)}, u32[]{:S(2)}, u32[]{:S(2)}) collective-permute-start(bf16[768,768]{1,0:T(8,128)(2,1)S(1)} %get-tuple-element.194), channel_id=1, source_target_pairs={{0,2},{1,3},{2,0},{3,1},{4,6},{5,7},{6,4},{7,5},{8,10},{9,11},{10,... | collective-permute-start | bytes 3538952 | tf_op jit(solution)/shard_map/ppermute | solution.py:1115
  64.2 5.6 %copy-start.17 = (bf16[1024,768]{1,0:T(8,128)(2,1)S(1)}, bf16[1024,768]{1,0:T(8,128)(2,1)}, u32[]{:S(2)}) copy-start(bf16[1024,768]{1,0:T(8,128)(2,1)} %get-tuple-element.146.vt_in) | copy-start | bytes 4718596
  64.2 5.6 %copy-start.26 = (bf16[256,768]{1,0:T(8,128)(2,1)S(1)}, bf16[256,768]{1,0:T(8,128)(2,1)}, u32[]{:S(2)}) copy-start(bf16[256,768]{1,0:T(8,128)(2,1)} %get-tuple-element.149.q_t) | copy-start | bytes 1179652
  64.2 5.6 %copy-start.27 = (bf16[256,768]{1,0:T(8,128)(2,1)S(1)}, bf16[256,768]{1,0:T(8,128)(2,1)}, u32[]{:S(2)}) copy-start(bf16[256,768]{1,0:T(8,128)(2,1)} %get-tuple-element.165.dctx_t) | copy-start | bytes 1179652
  64.2 5.6 %copy-start.33 = (f32[8,768]{1,0:T(8,128)S(1)}, f32[8,768]{1,0:T(8,128)}, u32[]{:S(2)}) copy-start(f32[8,768]{1,0:T(8,128)} %get-tuple-element.168.refs_4_.sm_t) | copy-start | bytes 73732
  64.2 5.6 %copy-start.34 = (f32[1,3072]{1,0:T(1,128)S(1)}, f32[1,3072]{1,0:T(1,128)}, u32[]{:S(2)}) copy-start(f32[1,3072]{1,0:T(1,128)} %get-tuple-element.170.so_t) | copy-start | bytes 36868
  64.2 5.6 %copy-start.35 = (f32[8,192]{1,0:T(8,128)S(1)}, f32[8,192]{1,0:T(8,128)}, u32[]{:S(2)}) copy-start(f32[8,192]{1,0:T(8,128)} %get-tuple-element.167.sf_l) | copy-start | bytes 18436
  64.2 5.6 %copy-start.36 = (f32[8,192]{1,0:T(8,128)S(1)}, f32[8,192]{1,0:T(8,128)}, u32[]{:S(2)}) copy-start(f32[8,192]{1,0:T(8,128)} %get-tuple-element.169.sm_l) | copy-start | bytes 18436
  65.7 4.1 %copy-start.14 = (bf16[2,128,1024]{2,1,0:T(8,128)(2,1)S(1)}, bf16[2,128,1024]{2,1,0:T(8,128)(2,1)}, u32[]{:S(2)}) copy-start(bf16[2,128,1024]{2,1,0:T(8,128)(2,1)} %copy-done.13) | copy-start | bytes 1572868
  65.8 4.1 %copy-start.15 = (bf16[256,768]{1,0:T(8,128)(2,1)S(1)}, bf16[256,768]{1,0:T(8,128)(2,1)}, u32[]{:S(2)}) copy-start(bf16[256,768]{1,0:T(8,128)(2,1)} %get-tuple-element.162.ctx_t_in.ctx_t) | copy-start | bytes 1179652
  65.8 4.1 %copy-start.16 = (bf16[1024,768]{1,0:T(8,128)(2,1)S(1)}, bf16[1024,768]{1,0:T(8,128)(2,1)}, u32[]{:S(2)}) copy-start(bf16[1024,768]{1,0:T(8,128)(2,1)} %get-tuple-element.144.kt_in) | copy-start | bytes 4718596
  65.8 4.1 %copy-start.21 = (bf16[256,256]{1,0:T(8,128)(2,1)S(1)}, bf16[256,256]{1,0:T(8,128)(2,1)}, u32[]{:S(2)}) copy-start(bf16[256,256]{1,0:T(8,128)(2,1)} %get-tuple-element.163.ctx_l) | copy-start | bytes 393220
  65.8 4.1 %copy-start.23 = (bf16[1024,256]{1,0:T(8,128)(2,1)S(1)}, bf16[1024,256]{1,0:T(8,128)(2,1)}, u32[]{:S(2)}) copy-start(bf16[1024,256]{1,0:T(8,128)(2,1)} %get-tuple-element.145.kl_in) | copy-start | bytes 1572868
  66.4 28.2 %collective-permute-start.8 = (bf16[640,768]{1,0:T(8,128)(2,1)S(1)}, bf16[640,768]{1,0:T(8,128)(2,1)S(1)}, u32[]{:S(2)}, u32[]{:S(2)}) collective-permute-start(bf16[640,768]{1,0:T(8,128)(2,1)S(1)} %get-tuple-element.193), channel_id=1, source_target_pairs={{0,8},{4,12},{8,0},{12,4},{16,24},{20,28},{24,16},{28,20},{1,9},{5... | collective-permute-start | bytes 2949128 | tf_op jit(solution)/shard_map/ppermute | solution.py:1117
  68.3 23.0 %collective-permute-start.10 = (bf16[512,768]{1,0:T(8,128)(2,1)S(1)}, bf16[512,768]{1,0:T(8,128)(2,1)S(1)}, u32[]{:S(2)}, u32[]{:S(2)}) collective-permute-start(bf16[512,768]{1,0:T(8,128)(2,1)S(1)} %get-tuple-element.195), channel_id=1, source_target_pairs={{0,4},{4,0},{8,12},{12,8},{16,20},{20,16},{24,28},{28,24},{1,5},{5... | collective-permute-start | bytes 2359304 | tf_op jit(solution)/shard_map/ppermute | solution.py:1117
  90.7 8.0 %collective-permute-start.6 = (bf16[768,768]{1,0:T(8,128)(2,1)S(1)}, bf16[768,768]{1,0:T(8,128)(2,1)S(1)}, u32[]{:S(2)}, u32[]{:S(2)}) collective-permute-start(bf16[768,768]{1,0:T(8,128)(2,1)S(1)} %get-tuple-element.190), channel_id=1, source_target_pairs={{0,1},{1,0},{2,3},{3,2},{4,5},{5,4},{6,7},{7,6},{8,9},{9,8},{10,11... | collective-permute-start | bytes 3538952 | tf_op jit(solution)/shard_map/ppermute | solution.py:1115
  90.7 7.8 %collective-permute-start.7 = (bf16[512,768]{1,0:T(8,128)(2,1)S(1)}, bf16[512,768]{1,0:T(8,128)(2,1)S(1)}, u32[]{:S(2)}, u32[]{:S(2)}) collective-permute-start(bf16[512,768]{1,0:T(8,128)(2,1)S(1)} %get-tuple-element.192), channel_id=1, source_target_pairs={{0,1},{1,0},{2,3},{3,2},{4,5},{5,4},{6,7},{7,6},{8,9},{9,8},{10,11... | collective-permute-start | bytes 2359304 | tf_op jit(solution)/shard_map/ppermute | solution.py:1115
  93.5 15.9 %collective-permute-start.12 = (bf16[384,768]{1,0:T(8,128)(2,1)}, bf16[384,768]{1,0:T(8,128)(2,1)S(1)}, u32[]{:S(2)}, u32[]{:S(2)}) collective-permute-start(bf16[384,768]{1,0:T(8,128)(2,1)} %get-tuple-element.204), channel_id=1, source_target_pairs={{0,8},{4,12},{8,0},{12,4},{16,24},{20,28},{24,16},{28,20},{1,9},{5... | collective-permute-start | bytes 1769480 | tf_op jit(solution)/shard_map/ppermute | solution.py:1117
  95.5 14.1 %collective-permute-start.11 = (bf16[320,768]{1,0:T(8,128)(2,1)}, bf16[320,768]{1,0:T(8,128)(2,1)S(1)}, u32[]{:S(2)}, u32[]{:S(2)}) collective-permute-start(bf16[320,768]{1,0:T(8,128)(2,1)} %get-tuple-element.203), channel_id=1, source_target_pairs={{0,4},{4,0},{8,12},{12,8},{16,20},{20,16},{24,28},{28,24},{1,5},{5... | collective-permute-start | bytes 1474568 | tf_op jit(solution)/shard_map/ppermute | solution.py:1117
  97.0 11.6 %collective-permute-start.13 = (bf16[256,768]{1,0:T(8,128)(2,1)}, bf16[256,768]{1,0:T(8,128)(2,1)S(1)}, u32[]{:S(2)}, u32[]{:S(2)}) collective-permute-start(bf16[256,768]{1,0:T(8,128)(2,1)} %get-tuple-element.205), channel_id=1, source_target_pairs={{0,2},{1,3},{2,0},{3,1},{4,6},{5,7},{6,4},{7,5},{8,10},{9,11},{10,... | collective-permute-start | bytes 1179656 | tf_op jit(solution)/shard_map/ppermute | solution.py:1115
  111.1 11.6 %collective-permute-start.14 = (bf16[2,960,256]{2,1,0:T(8,128)(2,1)S(1)}, bf16[2,960,256]{2,1,0:T(8,128)(2,1)S(1)}, u32[]{:S(2)}, u32[]{:S(2)}) collective-permute-start(bf16[2,960,256]{2,1,0:T(8,128)(2,1)S(1)} %get-tuple-element.211), channel_id=1, source_target_pairs={{0,1},{1,0},{2,3},{3,2},{4,5},{5,4},{6,7},{7,6},{8,9},{9,8},{10,11... | collective-permute-start | bytes 2949128 | tf_op jit(solution)/shard_map/ppermute | solution.py:1115
  111.1 7.3 %collective-permute-start.15 = (bf16[64,768]{1,0:T(8,128)(2,1)S(1)}, bf16[64,768]{1,0:T(8,128)(2,1)S(1)}, u32[]{:S(2)}, u32[]{:S(2)}) collective-permute-start(bf16[64,768]{1,0:T(8,128)(2,1)S(1)} %get-tuple-element.212), channel_id=1, source_target_pairs={{0,8},{4,12},{8,0},{12,4},{16,24},{20,28},{24,16},{28,20},{1,9},{5... | collective-permute-start | bytes 294920 | tf_op jit(solution)/shard_map/ppermute | solution.py:1117
  112.1 6.4 %collective-permute-start.16 = (bf16[64,768]{1,0:T(8,128)(2,1)S(1)}, bf16[64,768]{1,0:T(8,128)(2,1)S(1)}, u32[]{:S(2)}, u32[]{:S(2)}) collective-permute-start(bf16[64,768]{1,0:T(8,128)(2,1)S(1)} %get-tuple-element.213), channel_id=1, source_target_pairs={{0,16},{4,20},{8,24},{12,28},{16,0},{20,4},{24,8},{28,12},{1,17},{... | collective-permute-start | bytes 294920 | tf_op jit(solution)/shard_map/ppermute | solution.py:1117
  114.6 8.0 %collective-permute-start.17 = (bf16[64,768]{1,0:T(8,128)(2,1)S(1)}, bf16[64,768]{1,0:T(8,128)(2,1)S(1)}, u32[]{:S(2)}, u32[]{:S(2)}) collective-permute-start(bf16[64,768]{1,0:T(8,128)(2,1)S(1)} %get-tuple-element.214), channel_id=1, source_target_pairs={{0,24},{4,28},{8,16},{12,20},{16,8},{20,12},{24,0},{28,4},{1,25},{... | collective-permute-start | bytes 294920 | tf_op jit(solution)/shard_map/ppermute | solution.py:1117
  115.4 12.0 %collective-permute-start.19 = (bf16[160,768]{1,0:T(8,128)(2,1)S(1)}, bf16[160,768]{1,0:T(8,128)(2,1)S(1)}, u32[]{:S(2)}, u32[]{:S(2)}) collective-permute-start(bf16[160,768]{1,0:T(8,128)(2,1)S(1)} %get-tuple-element.219), channel_id=1, source_target_pairs={{0,2},{1,3},{2,0},{3,1},{4,6},{5,7},{6,4},{7,5},{8,10},{9,11},{10,... | collective-permute-start | bytes 737288 | tf_op jit(solution)/shard_map/ppermute | solution.py:1115
  123.0 22.8 %collective-permute-start.18 = (bf16[960,256]{1,0:T(8,128)(2,1)S(1)}, bf16[960,256]{1,0:T(8,128)(2,1)S(1)}, u32[]{:S(2)}, u32[]{:S(2)}) collective-permute-start(bf16[960,256]{1,0:T(8,128)(2,1)S(1)} %get-tuple-element.216), channel_id=1, source_target_pairs={{0,2},{1,3},{2,0},{3,1},{4,6},{5,7},{6,4},{7,5},{8,10},{9,11},{10,... | collective-permute-start | bytes 1474568 | tf_op jit(solution)/shard_map/ppermute | solution.py:1115
  124.8 18.5 %collective-permute-start.21 = (bf16[256,768]{1,0:T(8,128)(2,1)S(1)}, bf16[256,768]{1,0:T(8,128)(2,1)S(1)}, u32[]{:S(2)}, u32[]{:S(2)}) collective-permute-start(bf16[256,768]{1,0:T(8,128)(2,1)S(1)} %copy-done.40), channel_id=1, source_target_pairs={{0,4},{4,0},{8,12},{12,8},{16,20},{20,16},{24,28},{28,24},{1,5},{5... | collective-permute-start | bytes 1179656 | tf_op jit(solution)/shard_map/ppermute | solution.py:1117
  126.3 14.6 %collective-permute-start.22 = (bf16[192,768]{1,0:T(8,128)(2,1)S(1)}, bf16[192,768]{1,0:T(8,128)(2,1)S(1)}, u32[]{:S(2)}, u32[]{:S(2)}) collective-permute-start(bf16[192,768]{1,0:T(8,128)(2,1)S(1)} %get-tuple-element.223), channel_id=1, source_target_pairs={{0,4},{4,0},{8,12},{12,8},{16,20},{20,16},{24,28},{28,24},{1,5},{5... | collective-permute-start | bytes 884744 | tf_op jit(solution)/shard_map/ppermute | solution.py:1117
  126.8 43.0 %collective-permute-start.31 = (bf16[384,768]{1,0:T(8,128)(2,1)S(1)}, bf16[384,768]{1,0:T(8,128)(2,1)S(1)}, u32[]{:S(2)}, u32[]{:S(2)}) collective-permute-start(bf16[384,768]{1,0:T(8,128)(2,1)S(1)} %get-tuple-element.235), channel_id=1, source_target_pairs={{0,2},{1,3},{2,0},{3,1},{4,6},{5,7},{6,4},{7,5},{8,10},{9,11},{10,... | collective-permute-start | bytes 1769480 | tf_op jit(solution)/shard_map/ppermute | solution.py:1115
  127.4 7.1 %collective-permute-start.23 = (bf16[64,768]{1,0:T(8,128)(2,1)S(1)}, bf16[64,768]{1,0:T(8,128)(2,1)S(1)}, u32[]{:S(2)}, u32[]{:S(2)}) collective-permute-start(bf16[64,768]{1,0:T(8,128)(2,1)S(1)} %add.35.refs_4_.refs_0_), channel_id=1, source_target_pairs={{0,16},{4,20},{8,24},{12,28},{16,0},{20,4},{24,8},{28,12},{1,17},{... | collective-permute-start | bytes 294920 | tf_op jit(solution)/shard_map/ppermute | solution.py:1117
  134.5 9.8 %collective-permute-start.20 = (bf16[80,768]{1,0:T(8,128)(2,1)S(1)}, bf16[80,768]{1,0:T(8,128)(2,1)S(1)}, u32[]{:S(2)}, u32[]{:S(2)}) collective-permute-start(bf16[80,768]{1,0:T(8,128)(2,1)S(1)} %get-tuple-element.221), channel_id=1, source_target_pairs={{0,16},{4,20},{8,24},{12,28},{16,0},{20,4},{24,8},{28,12},{1,17},{... | collective-permute-start | bytes 368648 | tf_op jit(solution)/shard_map/ppermute | solution.py:1117
  136.5 10.9 %copy-start.20 = (f32[256,768]{1,0:T(8,128)S(1)}, f32[256,768]{1,0:T(8,128)}, u32[]{:S(2)}) copy-start(f32[256,768]{1,0:T(8,128)} %get-tuple-element.217.mid_t) | copy-start | bytes 2359300
  136.5 10.9 %copy-start.28 = (f32[2,192,128]{2,1,0:T(8,128)S(1)}, f32[2,192,128]{2,1,0:T(8,128)}, u32[]{:S(2)}) copy-start(f32[2,192,128]{2,1,0:T(8,128)} %get-tuple-element.218.mid_l) | copy-start | bytes 589828
  140.9 7.7 %collective-permute-start.26 = (bf16[128,768]{1,0:T(8,128)(2,1)S(1)}, bf16[128,768]{1,0:T(8,128)(2,1)S(1)}, u32[]{:S(2)}, u32[]{:S(2)}) collective-permute-start(bf16[128,768]{1,0:T(8,128)(2,1)S(1)} %join.10.refs_4_.refs_0_), channel_id=1, source_target_pairs={{0,8},{4,12},{8,0},{12,4},{16,24},{20,28},{24,16},{28,20},{1,9},{5... | collective-permute-start | bytes 589832 | tf_op jit(solution)/shard_map/ppermute | solution.py:1117
  143.4 12.7 %collective-permute-start.24 = (bf16[128,768]{1,0:T(8,128)(2,1)S(1)}, bf16[128,768]{1,0:T(8,128)(2,1)S(1)}, u32[]{:S(2)}, u32[]{:S(2)}) collective-permute-start(bf16[128,768]{1,0:T(8,128)(2,1)S(1)} %get-tuple-element.228), channel_id=1, source_target_pairs={{0,2},{1,3},{2,0},{3,1},{4,6},{5,7},{6,4},{7,5},{8,10},{9,11},{10,... | collective-permute-start | bytes 589832 | tf_op jit(solution)/shard_map/ppermute | solution.py:1115
  144.4 11.7 %collective-permute-start.25 = (bf16[96,768]{1,0:T(8,128)(2,1)S(1)}, bf16[96,768]{1,0:T(8,128)(2,1)S(1)}, u32[]{:S(2)}, u32[]{:S(2)}) collective-permute-start(bf16[96,768]{1,0:T(8,128)(2,1)S(1)} %get-tuple-element.229), channel_id=1, source_target_pairs={{0,16},{4,20},{8,24},{12,28},{16,0},{20,4},{24,8},{28,12},{1,17},{... | collective-permute-start | bytes 442376 | tf_op jit(solution)/shard_map/ppermute | solution.py:1117
  145.8 11.5 %collective-permute-start.28 = (bf16[80,768]{1,0:T(8,128)(2,1)S(1)}, bf16[80,768]{1,0:T(8,128)(2,1)S(1)}, u32[]{:S(2)}, u32[]{:S(2)}) collective-permute-start(bf16[80,768]{1,0:T(8,128)(2,1)S(1)} %add.40.after.refs_0_), channel_id=1, source_target_pairs={{0,16},{4,20},{8,24},{12,28},{16,0},{20,4},{24,8},{28,12},{1,17},{... | collective-permute-start | bytes 368648 | tf_op jit(solution)/shard_map/ppermute | solution.py:1117
  148.6 21.2 %copy-start.5 = (bf16[384,768]{1,0:T(8,128)(2,1)S(1)}, bf16[384,768]{1,0:T(8,128)(2,1)}, u32[]{:S(2)}) copy-start(bf16[384,768]{1,0:T(8,128)(2,1)} %copy-done.4) | copy-start | bytes 1769476
  157.4 17.0 %collective-permute-start.34 = (bf16[160,768]{1,0:T(8,128)(2,1)S(1)}, bf16[160,768]{1,0:T(8,128)(2,1)S(1)}, u32[]{:S(2)}, u32[]{:S(2)}) collective-permute-start(bf16[160,768]{1,0:T(8,128)(2,1)S(1)} %join.12.refs_4_.refs_0_), channel_id=1, source_target_pairs={{0,8},{4,12},{8,0},{12,4},{16,24},{20,28},{24,16},{28,20},{1,9},{5... | collective-permute-start | bytes 737288 | tf_op jit(solution)/shard_map/ppermute | solution.py:1117
  157.5 11.5 %collective-permute-start.27 = (bf16[64,768]{1,0:T(8,128)(2,1)S(1)}, bf16[64,768]{1,0:T(8,128)(2,1)S(1)}, u32[]{:S(2)}, u32[]{:S(2)}) collective-permute-start(bf16[64,768]{1,0:T(8,128)(2,1)S(1)} %get-tuple-element.232), channel_id=1, source_target_pairs={{0,8},{4,12},{8,0},{12,4},{16,24},{20,28},{24,16},{28,20},{1,9},{5... | collective-permute-start | bytes 294920 | tf_op jit(solution)/shard_map/ppermute | solution.py:1117
  159.5 11.9 %collective-permute-start.30 = (bf16[96,768]{1,0:T(8,128)(2,1)S(1)}, bf16[96,768]{1,0:T(8,128)(2,1)S(1)}, u32[]{:S(2)}, u32[]{:S(2)}) collective-permute-start(bf16[96,768]{1,0:T(8,128)(2,1)S(1)} %add.41.refs_4_.refs_0_), channel_id=1, source_target_pairs={{0,16},{4,20},{8,24},{12,28},{16,0},{20,4},{24,8},{28,12},{1,17},{... | collective-permute-start | bytes 442376 | tf_op jit(solution)/shard_map/ppermute | solution.py:1117
  169.0 5.3 %collective-permute-start.29 = (bf16[32,768]{1,0:T(8,128)(2,1)S(1)}, bf16[32,768]{1,0:T(8,128)(2,1)S(1)}, u32[]{:S(2)}, u32[]{:S(2)}) collective-permute-start(bf16[32,768]{1,0:T(8,128)(2,1)S(1)} %get-tuple-element.234), channel_id=1, source_target_pairs={{0,16},{4,20},{8,24},{12,28},{16,0},{20,4},{24,8},{28,12},{1,17},{... | collective-permute-start | bytes 147464 | tf_op jit(solution)/shard_map/ppermute | solution.py:1117
  170.0 9.9 %collective-permute-start.33 = (bf16[192,768]{1,0:T(8,128)(2,1)S(1)}, bf16[192,768]{1,0:T(8,128)(2,1)S(1)}, u32[]{:S(2)}, u32[]{:S(2)}) collective-permute-start(bf16[192,768]{1,0:T(8,128)(2,1)S(1)} %get-tuple-element.237), channel_id=1, source_target_pairs={{0,4},{4,0},{8,12},{12,8},{16,20},{20,16},{24,28},{28,24},{1,5},{5... | collective-permute-start | bytes 884744 | tf_op jit(solution)/shard_map/ppermute | solution.py:1117
  174.4 24.5 %collective-permute-start.42 = (bf16[320,768]{1,0:T(8,128)(2,1)S(1)}, bf16[320,768]{1,0:T(8,128)(2,1)S(1)}, u32[]{:S(2)}, u32[]{:S(2)}) collective-permute-start(bf16[320,768]{1,0:T(8,128)(2,1)S(1)} %join.14.refs_8_.refs_0_), channel_id=1, source_target_pairs={{0,4},{4,0},{8,12},{12,8},{16,20},{20,16},{24,28},{28,24},{1,5},{5... | collective-permute-start | bytes 1474568 | tf_op jit(solution)/shard_map/ppermute | solution.py:1117
  175.8 10.4 %collective-permute-start.36 = (bf16[192,768]{1,0:T(8,128)(2,1)S(1)}, bf16[192,768]{1,0:T(8,128)(2,1)S(1)}, u32[]{:S(2)}, u32[]{:S(2)}) collective-permute-start(bf16[192,768]{1,0:T(8,128)(2,1)S(1)} %join.13.refs_2_.refs_0_), channel_id=1, source_target_pairs={{0,8},{4,12},{8,0},{12,4},{16,24},{20,28},{24,16},{28,20},{1,9},{5... | collective-permute-start | bytes 884744 | tf_op jit(solution)/shard_map/ppermute | solution.py:1117
  175.8 23.0 %collective-permute-start.43 = (bf16[256,768]{1,0:T(8,128)(2,1)S(1)}, bf16[256,768]{1,0:T(8,128)(2,1)S(1)}, u32[]{:S(2)}, u32[]{:S(2)}) collective-permute-start(bf16[256,768]{1,0:T(8,128)(2,1)S(1)} %join.11.refs_2_), channel_id=1, source_target_pairs={{0,4},{4,0},{8,12},{12,8},{16,20},{20,16},{24,28},{28,24},{1,5},{5... | collective-permute-start | bytes 1179656 | tf_op jit(solution)/shard_map/ppermute | solution.py:1117
  176.5 5.3 %collective-permute-start.32 = (bf16[32,768]{1,0:T(8,128)(2,1)S(1)}, bf16[32,768]{1,0:T(8,128)(2,1)S(1)}, u32[]{:S(2)}, u32[]{:S(2)}) collective-permute-start(bf16[32,768]{1,0:T(8,128)(2,1)S(1)} %add.45.refs_2_.refs_0_), channel_id=1, source_target_pairs={{0,16},{4,20},{8,24},{12,28},{16,0},{20,4},{24,8},{28,12},{1,17},{... | collective-permute-start | bytes 147464 | tf_op jit(solution)/shard_map/ppermute | solution.py:1117
  181.8 10.2 %collective-permute-start.35 = (bf16[64,768]{1,0:T(8,128)(2,1)S(1)}, bf16[64,768]{1,0:T(8,128)(2,1)S(1)}, u32[]{:S(2)}, u32[]{:S(2)}) collective-permute-start(bf16[64,768]{1,0:T(8,128)(2,1)S(1)} %join.15.refs_2_.refs_0_), channel_id=1, source_target_pairs={{0,8},{4,12},{8,0},{12,4},{16,24},{20,28},{24,16},{28,20},{1,9},{5... | collective-permute-start | bytes 294920 | tf_op jit(solution)/shard_map/ppermute | solution.py:1117
  186.1 5.8 %collective-permute-start.38 = (bf16[48,768]{1,0:T(8,128)(2,1)S(1)}, bf16[48,768]{1,0:T(8,128)(2,1)S(1)}, u32[]{:S(2)}, u32[]{:S(2)}) collective-permute-start(bf16[48,768]{1,0:T(8,128)(2,1)S(1)} %get-tuple-element.239), channel_id=1, source_target_pairs={{0,8},{4,12},{8,0},{12,4},{16,24},{20,28},{24,16},{28,20},{1,9},{5... | collective-permute-start | bytes 221192 | tf_op jit(solution)/shard_map/ppermute | solution.py:1117
  186.2 6.5 %collective-permute-start.39 = (bf16[48,768]{1,0:T(8,128)(2,1)S(1)}, bf16[48,768]{1,0:T(8,128)(2,1)S(1)}, u32[]{:S(2)}, u32[]{:S(2)}) collective-permute-start(bf16[48,768]{1,0:T(8,128)(2,1)S(1)} %get-tuple-element.240), channel_id=1, source_target_pairs={{0,16},{4,20},{8,24},{12,28},{16,0},{20,4},{24,8},{28,12},{1,17},{... | collective-permute-start | bytes 221192 | tf_op jit(solution)/shard_map/ppermute | solution.py:1117
  192.0 6.2 %collective-permute-start.40 = (bf16[48,768]{1,0:T(8,128)(2,1)S(1)}, bf16[48,768]{1,0:T(8,128)(2,1)S(1)}, u32[]{:S(2)}, u32[]{:S(2)}) collective-permute-start(bf16[48,768]{1,0:T(8,128)(2,1)S(1)} %get-tuple-element.241), channel_id=1, source_target_pairs={{0,24},{4,28},{8,16},{12,20},{16,8},{20,12},{24,0},{28,4},{1,25},{... | collective-permute-start | bytes 221192 | tf_op jit(solution)/shard_map/ppermute | solution.py:1117
  192.0 19.5 %collective-permute-start.46 = (bf16[384,768]{1,0:T(8,128)(2,1)S(1)}, bf16[384,768]{1,0:T(8,128)(2,1)S(1)}, u32[]{:S(2)}, u32[]{:S(2)}) collective-permute-start(bf16[384,768]{1,0:T(8,128)(2,1)S(1)} %join.16.refs_2_.refs_0_), channel_id=1, source_target_pairs={{0,4},{4,0},{8,12},{12,8},{16,20},{20,16},{24,28},{28,24},{1,5},{5... | collective-permute-start | bytes 1769480 | tf_op jit(solution)/shard_map/ppermute | solution.py:1117
  198.2 5.3 %collective-permute-start.41 = (bf16[48,768]{1,0:T(8,128)(2,1)S(1)}, bf16[48,768]{1,0:T(8,128)(2,1)S(1)}, u32[]{:S(2)}, u32[]{:S(2)}) collective-permute-start(bf16[48,768]{1,0:T(8,128)(2,1)S(1)} %add.47.refs_4_.refs_0_), channel_id=1, source_target_pairs={{0,16},{4,20},{8,24},{12,28},{16,0},{20,4},{24,8},{28,12},{1,17},{... | collective-permute-start | bytes 221192 | tf_op jit(solution)/shard_map/ppermute | solution.py:1117
  203.5 5.2 %collective-permute-start.44 = (bf16[96,768]{1,0:T(8,128)(2,1)S(1)}, bf16[96,768]{1,0:T(8,128)(2,1)S(1)}, u32[]{:S(2)}, u32[]{:S(2)}) collective-permute-start(bf16[96,768]{1,0:T(8,128)(2,1)S(1)} %join.18.refs_0_.refs_2_), channel_id=1, source_target_pairs={{0,8},{4,12},{8,0},{12,4},{16,24},{20,28},{24,16},{28,20},{1,9},{5... | collective-permute-start | bytes 442376 | tf_op jit(solution)/shard_map/ppermute | solution.py:1117
  208.7 10.1 %collective-permute-start.45 = (bf16[192,768]{1,0:T(8,128)(2,1)S(1)}, bf16[192,768]{1,0:T(8,128)(2,1)S(1)}, u32[]{:S(2)}, u32[]{:S(2)}) collective-permute-start(bf16[192,768]{1,0:T(8,128)(2,1)S(1)} %join.19.refs_2_), channel_id=1, source_target_pairs={{0,4},{4,0},{8,12},{12,8},{16,20},{20,16},{24,28},{28,24},{1,5},{5... | collective-permute-start | bytes 884744 | tf_op jit(solution)/shard_map/ppermute | solution.py:1117
  209.2 9.6 %collective-permute-start.37 = (bf16[128,768]{1,0:T(8,128)(2,1)S(1)}, bf16[128,768]{1,0:T(8,128)(2,1)S(1)}, u32[]{:S(2)}, u32[]{:S(2)}) collective-permute-start(bf16[128,768]{1,0:T(8,128)(2,1)S(1)} %join.17.refs_4_.refs_0_), channel_id=1, source_target_pairs={{0,4},{4,0},{8,12},{12,8},{16,20},{20,16},{24,28},{28,24},{1,5},{5... | collective-permute-start | bytes 589832 | tf_op jit(solution)/shard_map/ppermute | solution.py:1117
  (24 other events, 57.0 us)

commit v5 on v4

--- a/solution.py
+++ b/solution.py
@@ -946,7 +946,7 @@
             pltpu.VMEM((4, DT + DL, tokens), BF16),
             pltpu.SemaphoreType.DMA((9,)),
         ],
-        compiler_params=pltpu.CompilerParams(vmem_limit_bytes=LIMIT),
+        compiler_params=pltpu.CompilerParams(vmem_limit_bytes=22 * MIB),
         cost_estimate=COST,
         name="input_back",
     )(joined_t, joined_l, query_t, query_l, wt, wl, after[0])
@@ -1151,7 +1151,7 @@
 SPLIT_S = ((768, "y1x2B"), )
 SPLIT_E = ((576, "1xy2B"), (576, "xyzB"), )
 SPLIT_P = ((256, "xy12B"), (384, "yxzB"), )
-ORDER = ('B', 'NE', 'S0', 'E1', 'E0', 'C', 'GP', 'E1', 'S0', 'E0', 'P0', 'P1', 'D', 'E1', 'S0', 'E0', 'GX', 'E1', 'X0', 'E0', 'E1', 'S0', 'P0', 'E0', 'FX', 'E1', 'S0', 'P0', 'E0', 'P0', 'P1', 'S0', 'P0', 'E0', 'P1', 'P0', 'S0', 'P0', 'P1', 'FE', 'P1', 'P1', 'FS', 'FP')
+ORDER = ('B', 'NE', 'S0', 'E1', 'E0', 'C', 'GP', 'E1', 'S0', 'E0', 'P0', 'P1', 'D', 'E1', 'S0', 'E0', 'GX', 'E1', 'X0', 'E0', 'E1', 'S0', 'P0', 'E0', 'FX', 'E1', 'S0', 'P0', 'E0', 'P0', 'P1', 'S0', 'P0', 'E0', 'P1', 'P0', 'S0', 'P0', 'P1', 'FE', 'HP0', 'P1', 'P1', 'FS', 'FP')
 
 
 def local(
@@ -1195,6 +1195,7 @@
     growths = {
         "B": tuple(reversed(extra)) + ((Z2,), (Z1,), (X,)),
         "D": tuple(reversed(extra)) + ((Z1, Z2), (X,)),
+        "F": tuple(reversed(extra)) + ((Z2,), (X,), (Z1,)),
     }
     subs = {
         name: sub_chunks(count, [(share, hops_of(text[:-1], extra), growths[text[-1]]) for share, text in split], dp_size)
@@ -1287,6 +1288,12 @@
 
         return call
 
+    def arrive(name, after):
+        while name in calls:
+            after = advance(name, after)
+        halves[name] = list(gate_call(halves[name], after))
+        return halves[name][1], ANY
+
     def inputs_add(after):
         own, onward = add_call(values["inputs"], 2, after)
         values.update(onward=(own, send(onward, (Y,), 1)))
@@ -1317,6 +1324,7 @@
         "NE": gate("E", False),
         "NP": gate("P", False),
         "NX": functools.partial(inputs_gate, gated=False),
+        "HP0": functools.partial(arrive, "P0"),
         "X0": inputs_add,
         "FX": inputs_end,
         "FS": end("S", shrink_store, "shrink_out", [(DT // 4, FT)]),

time: 221 us -> 214 us (0.968)
  starting transfers between devices: 54 us -> 59.7 us
  waiting for transfers between devices: 75.5 us -> 71 us
  local copies, waits for them, and re-layouts: 8.73 us -> 4.36 us
  Pallas kernels: 80.6 us -> 77.4 us
    ppermute x32, waiting for transfers between devices: 60.8 us -> 55.1 us  [sent(): lax.ppermute(array, 'dp', [(at, at ^ other) for at in range(dp_size)])]
    ppermute x32, starting transfers between devices: 42 us -> 47.7 us  [sent(): lax.ppermute(array, 'dp', [(at, at ^ other) for at in range(dp_size)])]
    unnamed x82 -> x64, local copies, waits for them, and re-layouts: 8.73 us -> 4.36 us
    pallas_call x24, Pallas kernels: 8.76 us -> 6.38 us  [add_call(): pl.pallas_call(functools.partial(add_kernel, len(sources), parts), grid=(...]
  transfers between devices with their start and end apart: 47 -> 47, of which waited for: 21 -> 22; matrix products, arithmetic and copies ran while one was open for 0% -> 0% of each run, Pallas kernels for 25% -> 24%
where the time goes in v5:
time: 214 us
  Pallas kernels  77.4 us (36%)
  waiting for transfers between devices  71 us (33%)
  starting transfers between devices  59.7 us (28%)
  local copies, waits for them, and re-layouts  4.36 us (2%)
    ppermute x32, waiting for transfers between devices, sent(): lax.ppermute(array, 'dp', [(at, at ^ other) for at in range(dp_size)])  55.1 us
    ppermute x32, starting transfers between devices, sent(): lax.ppermute(array, 'dp', [(at, at ^ other) for at in range(dp_size)])  47.7 us
    pallas_call x1, Pallas kernels, forward_call(): pl.pallas_call(functools.partial(forward_kernel, packs, rows, dp_size, su...  22.3 us
    pallas_call x1, Pallas kernels, attention_call(): pl.pallas_call(functools.partial(attention_kernel, packs, rows, dp_size,...  18 us
    ppermute x15, waiting for transfers between devices, sent(): lax.ppermute(array, 'seq', [(at, at ^ across) for at in range(seq_size)])  16 us
    pallas_call x1, Pallas kernels, middle_call(): pl.pallas_call(functools.partial(middle_kernel, dp_size, subs), out_shape...  14.5 us
    ppermute x15, starting transfers between devices, sent(): lax.ppermute(array, 'seq', [(at, at ^ across) for at in range(seq_size)])  12 us
    pallas_call x1, Pallas kernels, input_call(): pl.pallas_call(functools.partial(input_kernel, packs, rows), out_shape=(s...  7.38 us
  transfers between devices with their start and end apart: 47, of which 22 were waited for; matrix products, arithmetic and copies ran while one was open for 0% of the time, Pallas kernels for 24%

profile of v5, /device:TPU:0, one launch (start us, length us, event | category | flops | bytes accessed | tf_op | source)
XLA Modules:
  0.0 213.8 jit_solution(3130172293903355385)
XLA Ops:
  0.7 2.2 %prepare.1 = (bf16[2,128,1024]{2,1,0:T(8,128)(2,1)}, bf16[192,768]{1,0:T(8,128)(2,1)}, bf16[1,3072]{1,0:T(2,128)(2,1)}, bf16[1,768]{1,0:T(2,128)(2,1)}) custom-call(bf16[2,128,768]{2,1,0:T(8,128)(2,1)} %text_rows.1, bf16[2,192,128]{2,1,0:T(8,128)(2,1)} %bitcast.22, s32[2,128]{1,0:T(2,128)} %segments.1, bf16[192,576]{1,0:T(8,128)(2,1)} %project.1, ...), custom_call_target="tpu_custom_call" | custom-call | flops 1 | bytes 1 | tf_op jit(solution)/shard_map/prepare/pallas_call | solution.py:206
  2.8 3.0 %collective-permute-start.1 = (bf16[2,128,1024]{2,1,0:T(8,128)(2,1)}, bf16[2,128,1024]{2,1,0:T(8,128)(2,1)S(1)}, u32[]{:S(2)}, u32[]{:S(2)}) collective-permute-start(bf16[2,128,1024]{2,1,0:T(8,128)(2,1)} %get-tuple-element.140.x0), channel_id=1, source_target_pairs={{0,2},{1,3},{2,0},{3,1},{4,6},{5,7},{6,4},{7,5},{8,10},{9,11},{10,... | collective-permute-start | bytes 1572872 | tf_op jit(solution)/shard_map/ppermute | solution.py:1115
  5.8 12.1 %collective-permute-done.1.x2 = bf16[2,128,1024]{2,1,0:T(8,128)(2,1)S(1)} collective-permute-done((bf16[2,128,1024]{2,1,0:T(8,128)(2,1)}, bf16[2,128,1024]{2,1,0:T(8,128)(2,1)S(1)}, u32[]{:S(2)}, u32[]{:S(2)}) %collective-permute-start.1) | collective-permute-done | bytes 524320 | tf_op jit(solution)/shard_map/ppermute | solution.py:1115
  18.0 1.9 collective-permute-done.2.x3
  19.9 0.8 copy-done.10
  20.7 22.3 %forward.1 = (bf16[256,768]{1,0:T(8,128)(2,1)}, bf16[2,192,128]{2,1,0:T(8,128)(2,1)}, bf16[256,768]{1,0:T(8,128)(2,1)}, bf16[256,256]{1,0:T(8,128)(2,1)}, bf16[1...) custom-call(bf16[2,128,1024]{2,1,0:T(8,128)(2,1)} %get-tuple-element, ...), custom_call_target="tpu_custom_call" | custom-call | flops 1 | bytes 1 | tf_op jit(solution)/shard_map/forward/pallas_call | solution.py:508
  43.2 14.5 %middle.1 = (f32[256,768]{1,0:T(8,128)}, f32[2,192,128]{2,1,0:T(8,128)}, bf16[256,768]{1,0:T(8,128)(2,1)}, bf16[256,256]{1,0:T(8,128)(2,1)}, f32[8,768]{1,0:T(8,...) custom-call(bf16[256,768]{1,0:T(8,128)(2,1)} %get-tuple-element.153., ...), custom_call_target="tpu_custom_call" | custom-call | flops 1 | bytes 1 | tf_op jit(solution)/shard_map/middle/pallas_call | solution.py:676
  58.3 0.7 copy-done.26
  59.0 2.7 %add.24 = (bf16[768,768]{1,0:T(8,128)(2,1)S(1)}, bf16[768,768]{1,0:T(8,128)(2,1)S(1)}) custom-call(bf16[1536,768]{1,0:T(8,128)(2,1)S(1)} %copy-done.1, bf16[1536,768]{1,0:T(8,128)(2,1)S(1)} %copy-done.1, bf16[1536,768]{1,0:T(8,128)(2,1)} %collective-permute-done.5.refs_2_.refs_3_, bf16[1536,768]{1,0:T(8,128)(2,1)} %collective-permute-done.5.refs_2_.refs_3_, ...), custom_call_target="tpu_custom_call" | custom-call | flops 1 | bytes 1 | tf_op jit(solution)/shard_map/add/pallas_call | solution.py:1060
  61.8 1.8 collective-permute-start.9
  64.7 1.0 copy-done.2
  66.4 1.9 collective-permute-start.8
  68.3 1.5 collective-permute-start.10
  70.0 18.0 %attention_back.1 = (bf16[1536,1024]{1,0:T(8,128)(2,1)S(1)}, bf16[512,1024]{1,0:T(8,128)(2,1)S(1)}, bf16[768,256]{1,0:T(8,128)(2,1)S(1)}, bf16[256,256]{1,0:T(8,...) custom-call(bf16[2,128,1024]{2,1,0:T(8,128)(2,1)S(1)} %copy-done.5, ...), custom_call_target="tpu_custom_call" | custom-call | flops 1 | bytes 1 | tf_op jit(solution)/shard_map/attention_back/pallas_call | solution.py:886
  88.8 1.3 collective-permute-done.9.refs_2_.refs_3_
  90.4 1.9 collective-permute-start.12
  92.6 1.6 collective-permute-start.11
  94.1 1.5 collective-permute-start.13
  96.2 1.6 copy-done
  97.9 7.4 %input_back.1 = (bf16[2,960,256]{2,1,0:T(8,128)(2,1)S(1)}, bf16[2,960,256]{2,1,0:T(8,128)(2,1)S(1)}, f32[8,128]{1,0:T(8,128)S(1)}) custom-call(bf16[1536,1024]{1,0:T(8,128)(2,1)S(1)} %get-tuple-element.183.joined_in, bf16[512,1024]{1,0:T(8,128)(2,1)S(1)} %get-tuple-element.184.joined_l, bf16[768,256]{1,0:T(8,128)(2,1)S(1)} %get-tuple-element.185.query_t, ...), custom_call_target="tpu_custom_call" | custom-call | flops 1 | bytes 1 | tf_op jit(solution)/shard_map/input_back/pallas_call | solution.py:937
  105.8 1.7 collective-permute-start.15
  107.5 2.6 %collective-permute-start.16 = (bf16[64,768]{1,0:T(8,128)(2,1)S(1)}, bf16[64,768]{1,0:T(8,128)(2,1)S(1)}, u32[]{:S(2)}, u32[]{:S(2)}) collective-permute-start(bf16[64,768]{1,0:T(8,128)(2,1)S(1)} %get-tuple-element.215), channel_id=1, source_target_pairs={{0,16},{4,20},{8,24},{12,28},{16,0},{20,4},{24,8},{28,12},{1,17},{... | collective-permute-start | bytes 294920 | tf_op jit(solution)/shard_map/ppermute | solution.py:1117
  110.2 1.6 collective-permute-start.19
  111.8 6.4 %collective-permute-done.16.refs_2_ = bf16[64,768]{1,0:T(8,128)(2,1)S(1)} collective-permute-done((bf16[64,768]{1,0:T(8,128)(2,1)S(1)}, bf16[64,768]{1,0:T(8,128)(2,1)S(1)}, u32[]{:S(2)}, u32[]{:S(2)}) %collective-permute-start.16) | collective-permute-done | bytes 98336 | tf_op jit(solution)/shard_map/ppermute | solution.py:1117
  118.6 1.6 collective-permute-start.18
  120.2 1.5 collective-permute-start.21
  122.8 3.0 %collective-permute-start.23 = (bf16[64,768]{1,0:T(8,128)(2,1)S(1)}, bf16[64,768]{1,0:T(8,128)(2,1)S(1)}, u32[]{:S(2)}, u32[]{:S(2)}) collective-permute-start(bf16[64,768]{1,0:T(8,128)(2,1)S(1)} %add.35.refs_4_.refs_0_), channel_id=1, source_target_pairs={{0,16},{4,20},{8,24},{12,28},{16,0},{20,4},{24,8},{28,12},{1,17},{... | collective-permute-start | bytes 294920 | tf_op jit(solution)/shard_map/ppermute | solution.py:1117
  125.8 2.5 %collective-permute-done.23.refs_1_ = bf16[64,768]{1,0:T(8,128)(2,1)S(1)} collective-permute-done((bf16[64,768]{1,0:T(8,128)(2,1)S(1)}, bf16[64,768]{1,0:T(8,128)(2,1)S(1)}, u32[]{:S(2)}, u32[]{:S(2)}) %collective-permute-start.23) | collective-permute-done | bytes 98336 | tf_op jit(solution)/shard_map/ppermute | solution.py:1117
  128.3 3.0 %collective-permute-start.20 = (bf16[80,768]{1,0:T(8,128)(2,1)S(1)}, bf16[80,768]{1,0:T(8,128)(2,1)S(1)}, u32[]{:S(2)}, u32[]{:S(2)}) collective-permute-start(bf16[80,768]{1,0:T(8,128)(2,1)S(1)} %get-tuple-element.223), channel_id=1, source_target_pairs={{0,16},{4,20},{8,24},{12,28},{16,0},{20,4},{24,8},{28,12},{1,17},{... | collective-permute-start | bytes 368648 | tf_op jit(solution)/shard_map/ppermute | solution.py:1117
  131.4 4.7 %collective-permute-done.22.refs_2_.refs_3_ = bf16[192,768]{1,0:T(8,128)(2,1)S(1)} collective-permute-done((bf16[192,768]{1,0:T(8,128)(2,1)S(1)}, bf16[192,768]{1,0:T(8,128)(2,1)S(1)}, u32[]{:S(2)}, u32[]{:S(2)}) %collective-permute-start.22) | collective-permute-done | bytes 294944 | tf_op jit(solution)/shard_map/ppermute | solution.py:1117
  136.0 2.5 %collective-permute-start.26 = (bf16[128,768]{1,0:T(8,128)(2,1)S(1)}, bf16[128,768]{1,0:T(8,128)(2,1)S(1)}, u32[]{:S(2)}, u32[]{:S(2)}) collective-permute-start(bf16[128,768]{1,0:T(8,128)(2,1)S(1)} %join.10.refs_4_.refs_0_), channel_id=1, source_target_pairs={{0,8},{4,12},{8,0},{12,4},{16,24},{20,28},{24,16},{28,20},{1,9},{5... | collective-permute-start | bytes 589832 | tf_op jit(solution)/shard_map/ppermute | solution.py:1117
  139.3 1.1 collective-permute-start.25
  140.4 1.9 collective-permute-start.28
  142.3 1.2 sensitivity.1
  143.5 1.1 collective-permute-done.26.refs_1_
  144.6 6.1 %collective-permute-done.25.refs_1_ = bf16[96,768]{1,0:T(8,128)(2,1)S(1)} collective-permute-done((bf16[96,768]{1,0:T(8,128)(2,1)S(1)}, bf16[96,768]{1,0:T(8,128)(2,1)S(1)}, u32[]{:S(2)}, u32[]{:S(2)}) %collective-permute-start.25) | collective-permute-done | bytes 147488 | tf_op jit(solution)/shard_map/ppermute | solution.py:1117
  150.8 1.2 collective-permute-done.28.refs_1_
  152.1 2.0 collective-permute-start.27
  154.1 1.1 collective-permute-start.30
  155.2 8.1 %collective-permute-done.27.refs_2_.refs_3_ = bf16[64,768]{1,0:T(8,128)(2,1)S(1)} collective-permute-done((bf16[64,768]{1,0:T(8,128)(2,1)S(1)}, bf16[64,768]{1,0:T(8,128)(2,1)S(1)}, u32[]{:S(2)}, u32[]{:S(2)}) %collective-permute-start.27) | collective-permute-done | bytes 98336 | tf_op jit(solution)/shard_map/ppermute | solution.py:1117
  163.4 1.5 collective-permute-start.33
  165.0 1.1 collective-permute-start.29
  166.1 2.5 %collective-permute-start.36 = (bf16[192,768]{1,0:T(8,128)(2,1)S(1)}, bf16[192,768]{1,0:T(8,128)(2,1)S(1)}, u32[]{:S(2)}, u32[]{:S(2)}) collective-permute-start(bf16[192,768]{1,0:T(8,128)(2,1)S(1)} %join.13.refs_2_.refs_0_), channel_id=1, source_target_pairs={{0,8},{4,12},{8,0},{12,4},{16,24},{20,28},{24,16},{28,20},{1,9},{5... | collective-permute-start | bytes 884744 | tf_op jit(solution)/shard_map/ppermute | solution.py:1117
  168.7 1.6 collective-permute-done.29.refs_1_
  171.0 1.5 collective-permute-start.39
  172.5 1.3 collective-permute-start.32
  173.9 4.6 %collective-permute-done.32.refs_1_ = bf16[32,768]{1,0:T(8,128)(2,1)S(1)} collective-permute-done((bf16[32,768]{1,0:T(8,128)(2,1)S(1)}, bf16[32,768]{1,0:T(8,128)(2,1)S(1)}, u32[]{:S(2)}, u32[]{:S(2)}) %collective-permute-start.32) | collective-permute-done | bytes 49184 | tf_op jit(solution)/shard_map/ppermute | solution.py:1117
  178.8 1.8 collective-permute-start.40
  180.5 1.9 collective-permute-start.41
  182.5 0.6 collective-permute-done.35.refs_1_
  183.1 0.6 collective-permute-start.37
  183.9 3.5 %collective-permute-start.42 = (bf16[48,768]{1,0:T(8,128)(2,1)S(1)}, bf16[48,768]{1,0:T(8,128)(2,1)S(1)}, u32[]{:S(2)}, u32[]{:S(2)}) collective-permute-start(bf16[48,768]{1,0:T(8,128)(2,1)S(1)} %get-tuple-element.243), channel_id=1, source_target_pairs={{0,24},{4,28},{8,16},{12,20},{16,8},{20,12},{24,0},{28,4},{1,25},{... | collective-permute-start | bytes 221192 | tf_op jit(solution)/shard_map/ppermute | solution.py:1117
  187.4 0.6 collective-permute-done.41.refs_2_
  188.6 1.5 collective-permute-done.42.refs_3_
  190.1 1.1 collective-permute-start.43
  191.2 1.8 collective-permute-done.39.refs_3_
  193.0 2.0 expand_out.1
  195.1 2.2 %collective-permute-done.37.refs_1_ = bf16[128,768]{1,0:T(8,128)(2,1)S(1)} collective-permute-done((bf16[128,768]{1,0:T(8,128)(2,1)S(1)}, bf16[128,768]{1,0:T(8,128)(2,1)S(1)}, u32[]{:S(2)}, u32[]{:S(2)}) %collective-permute-start.37) | collective-permute-done | bytes 196640 | tf_op jit(solution)/shard_map/ppermute | solution.py:1117
  197.2 0.8 collective-permute-start.44
  198.1 4.4 %collective-permute-done.44.refs_1_ = bf16[96,768]{1,0:T(8,128)(2,1)S(1)} collective-permute-done((bf16[96,768]{1,0:T(8,128)(2,1)S(1)}, bf16[96,768]{1,0:T(8,128)(2,1)S(1)}, u32[]{:S(2)}, u32[]{:S(2)}) %collective-permute-start.44) | collective-permute-done | bytes 147488 | tf_op jit(solution)/shard_map/ppermute | solution.py:1117
  203.1 6.1 %collective-permute-done.46.refs_1_ = bf16[384,768]{1,0:T(8,128)(2,1)S(1)} collective-permute-done((bf16[384,768]{1,0:T(8,128)(2,1)S(1)}, bf16[384,768]{1,0:T(8,128)(2,1)S(1)}, u32[]{:S(2)}, u32[]{:S(2)}) %collective-permute-start.46) | collective-permute-done | bytes 589856 | tf_op jit(solution)/shard_map/ppermute | solution.py:1117
  209.2 1.7 shrink_out.1
  210.9 1.4 collective-permute-done.45.refs_3_
  212.3 1.5 project_out.1
  (140 shorter events, 10.2 us)
Async XLA Ops:
  2.8 15.1 %collective-permute-start.1 = (bf16[2,128,1024]{2,1,0:T(8,128)(2,1)}, bf16[2,128,1024]{2,1,0:T(8,128)(2,1)S(1)}, u32[]{:S(2)}, u32[]{:S(2)}) collective-permute-start(bf16[2,128,1024]{2,1,0:T(8,128)(2,1)} %get-tuple-element.140.x0), channel_id=1, source_target_pairs={{0,2},{1,3},{2,0},{3,1},{4,6},{5,7},{6,4},{7,5},{8,10},{9,11},{10,... | collective-permute-start | bytes 1572872 | tf_op jit(solution)/shard_map/ppermute | solution.py:1115
  5.8 12.1 %collective-permute-start = (bf16[2,128,1024]{2,1,0:T(8,128)(2,1)}, bf16[2,128,1024]{2,1,0:T(8,128)(2,1)S(1)}, u32[]{:S(2)}, u32[]{:S(2)}) collective-permute-start(bf16[2,128,1024]{2,1,0:T(8,128)(2,1)} %get-tuple-element.140.x0), channel_id=1, source_target_pairs={{0,1},{1,0},{2,3},{3,2},{4,5},{5,4},{6,7},{7,6},{8,9},{9,8},{10,11... | collective-permute-start | bytes 1572872 | tf_op jit(solution)/shard_map/ppermute | solution.py:1115
  17.9 1.9 collective-permute-start.2
  43.0 15.3 %collective-permute-start.5 = (bf16[1536,768]{1,0:T(8,128)(2,1)}, bf16[1536,768]{1,0:T(8,128)(2,1)}, u32[]{:S(2)}, u32[]{:S(2)}) collective-permute-start(bf16[1536,768]{1,0:T(8,128)(2,1)} %get-tuple-element.179), channel_id=1, source_target_pairs={{0,1},{1,0},{2,3},{3,2},{4,5},{5,4},{6,7},{7,6},{8,9},{9,8},{10,11... | collective-permute-start | bytes 7077896 | tf_op jit(solution)/shard_map/ppermute | solution.py:1115
  43.2 15.1 %copy-start.1 = (bf16[1536,768]{1,0:T(8,128)(2,1)S(1)}, bf16[1536,768]{1,0:T(8,128)(2,1)}, u32[]{:S(2)}) copy-start(bf16[1536,768]{1,0:T(8,128)(2,1)} %get-tuple-element.178.refs_0_.refs_1_) | copy-start | bytes 7077892
  57.7 7.0 %collective-permute-start.3 = (bf16[1280,768]{1,0:T(8,128)(2,1)}, bf16[1280,768]{1,0:T(8,128)(2,1)S(1)}, u32[]{:S(2)}, u32[]{:S(2)}) collective-permute-start(bf16[1280,768]{1,0:T(8,128)(2,1)} %get-tuple-element.175), channel_id=1, source_target_pairs={{0,1},{1,0},{2,3},{3,2},{4,5},{5,4},{6,7},{7,6},{8,9},{9,8},{10,11... | collective-permute-start | bytes 5898248 | tf_op jit(solution)/shard_map/ppermute | solution.py:1115
  58.1 6.1 %collective-permute-start.4 = (bf16[1024,768]{1,0:T(8,128)(2,1)}, bf16[1024,768]{1,0:T(8,128)(2,1)S(1)}, u32[]{:S(2)}, u32[]{:S(2)}) collective-permute-start(bf16[1024,768]{1,0:T(8,128)(2,1)} %get-tuple-element.177), channel_id=1, source_target_pairs={{0,1},{1,0},{2,3},{3,2},{4,5},{5,4},{6,7},{7,6},{8,9},{9,8},{10,11... | collective-permute-start | bytes 4718600 | tf_op jit(solution)/shard_map/ppermute | solution.py:1115
  59.0 5.2 %copy-start.3 = (bf16[1024,768]{1,0:T(8,128)(2,1)S(1)}, bf16[1024,768]{1,0:T(8,128)(2,1)}, u32[]{:S(2)}) copy-start(bf16[1024,768]{1,0:T(8,128)(2,1)} %get-tuple-element.176.refs_0_.refs_1_) | copy-start | bytes 4718596
  61.8 28.3 %collective-permute-start.9 = (bf16[768,768]{1,0:T(8,128)(2,1)S(1)}, bf16[768,768]{1,0:T(8,128)(2,1)S(1)}, u32[]{:S(2)}, u32[]{:S(2)}) collective-permute-start(bf16[768,768]{1,0:T(8,128)(2,1)S(1)} %get-tuple-element.196), channel_id=1, source_target_pairs={{0,2},{1,3},{2,0},{3,1},{4,6},{5,7},{6,4},{7,5},{8,10},{9,11},{10,... | collective-permute-start | bytes 3538952 | tf_op jit(solution)/shard_map/ppermute | solution.py:1115
  64.2 5.6 %copy-start.14 = (bf16[1024,768]{1,0:T(8,128)(2,1)S(1)}, bf16[1024,768]{1,0:T(8,128)(2,1)}, u32[]{:S(2)}) copy-start(bf16[1024,768]{1,0:T(8,128)(2,1)} %get-tuple-element.148.vt_in) | copy-start | bytes 4718596
  64.2 5.6 %copy-start.20 = (bf16[256,768]{1,0:T(8,128)(2,1)S(1)}, bf16[256,768]{1,0:T(8,128)(2,1)}, u32[]{:S(2)}) copy-start(bf16[256,768]{1,0:T(8,128)(2,1)} %get-tuple-element.151.q_t) | copy-start | bytes 1179652
  64.2 5.6 %copy-start.21 = (bf16[256,768]{1,0:T(8,128)(2,1)S(1)}, bf16[256,768]{1,0:T(8,128)(2,1)}, u32[]{:S(2)}) copy-start(bf16[256,768]{1,0:T(8,128)(2,1)} %get-tuple-element.167.dctx_t) | copy-start | bytes 1179652
  64.2 5.6 %copy-start.27 = (f32[8,768]{1,0:T(8,128)S(1)}, f32[8,768]{1,0:T(8,128)}, u32[]{:S(2)}) copy-start(f32[8,768]{1,0:T(8,128)} %get-tuple-element.170.refs_4_.sm_t) | copy-start | bytes 73732
  64.3 5.6 %copy-start.28 = (f32[1,3072]{1,0:T(1,128)S(1)}, f32[1,3072]{1,0:T(1,128)}, u32[]{:S(2)}) copy-start(f32[1,3072]{1,0:T(1,128)} %get-tuple-element.172.so_t) | copy-start | bytes 36868
  64.3 5.6 %copy-start.29 = (f32[8,192]{1,0:T(8,128)S(1)}, f32[8,192]{1,0:T(8,128)}, u32[]{:S(2)}) copy-start(f32[8,192]{1,0:T(8,128)} %get-tuple-element.169.sf_l) | copy-start | bytes 18436
  64.3 5.6 %copy-start.30 = (f32[8,192]{1,0:T(8,128)S(1)}, f32[8,192]{1,0:T(8,128)}, u32[]{:S(2)}) copy-start(f32[8,192]{1,0:T(8,128)} %get-tuple-element.171.sm_l) | copy-start | bytes 18436
  65.8 4.1 %copy-start.11 = (bf16[2,128,1024]{2,1,0:T(8,128)(2,1)S(1)}, bf16[2,128,1024]{2,1,0:T(8,128)(2,1)}, u32[]{:S(2)}) copy-start(bf16[2,128,1024]{2,1,0:T(8,128)(2,1)} %copy-done.10) | copy-start | bytes 1572868
  65.8 4.1 %copy-start.12 = (bf16[256,768]{1,0:T(8,128)(2,1)S(1)}, bf16[256,768]{1,0:T(8,128)(2,1)}, u32[]{:S(2)}) copy-start(bf16[256,768]{1,0:T(8,128)(2,1)} %get-tuple-element.164.ctx_t_in.ctx_t) | copy-start | bytes 1179652
  65.8 4.1 %copy-start.13 = (bf16[1024,768]{1,0:T(8,128)(2,1)S(1)}, bf16[1024,768]{1,0:T(8,128)(2,1)}, u32[]{:S(2)}) copy-start(bf16[1024,768]{1,0:T(8,128)(2,1)} %get-tuple-element.146.kt_in) | copy-start | bytes 4718596
  65.8 4.1 %copy-start.17 = (bf16[256,256]{1,0:T(8,128)(2,1)S(1)}, bf16[256,256]{1,0:T(8,128)(2,1)}, u32[]{:S(2)}) copy-start(bf16[256,256]{1,0:T(8,128)(2,1)} %get-tuple-element.165.ctx_l) | copy-start | bytes 393220
  65.8 4.1 %copy-start.18 = (bf16[1024,256]{1,0:T(8,128)(2,1)S(1)}, bf16[1024,256]{1,0:T(8,128)(2,1)}, u32[]{:S(2)}) copy-start(bf16[1024,256]{1,0:T(8,128)(2,1)} %get-tuple-element.147.kl_in) | copy-start | bytes 1572868
  65.8 4.1 %copy-start.19 = (bf16[1024,256]{1,0:T(8,128)(2,1)S(1)}, bf16[1024,256]{1,0:T(8,128)(2,1)}, u32[]{:S(2)}) copy-start(bf16[1024,256]{1,0:T(8,128)(2,1)} %get-tuple-element.149.vl_in) | copy-start | bytes 1572868
  66.4 25.9 %collective-permute-start.8 = (bf16[640,768]{1,0:T(8,128)(2,1)S(1)}, bf16[640,768]{1,0:T(8,128)(2,1)S(1)}, u32[]{:S(2)}, u32[]{:S(2)}) collective-permute-start(bf16[640,768]{1,0:T(8,128)(2,1)S(1)} %get-tuple-element.195), channel_id=1, source_target_pairs={{0,8},{4,12},{8,0},{12,4},{16,24},{20,28},{24,16},{28,20},{1,9},{5... | collective-permute-start | bytes 2949128 | tf_op jit(solution)/shard_map/ppermute | solution.py:1117
  68.3 20.2 %collective-permute-start.10 = (bf16[512,768]{1,0:T(8,128)(2,1)S(1)}, bf16[512,768]{1,0:T(8,128)(2,1)S(1)}, u32[]{:S(2)}, u32[]{:S(2)}) collective-permute-start(bf16[512,768]{1,0:T(8,128)(2,1)S(1)} %get-tuple-element.197), channel_id=1, source_target_pairs={{0,4},{4,0},{8,12},{12,8},{16,20},{20,16},{24,28},{28,24},{1,5},{5... | collective-permute-start | bytes 2359304 | tf_op jit(solution)/shard_map/ppermute | solution.py:1117
  88.0 7.9 %collective-permute-start.6 = (bf16[768,768]{1,0:T(8,128)(2,1)S(1)}, bf16[768,768]{1,0:T(8,128)(2,1)S(1)}, u32[]{:S(2)}, u32[]{:S(2)}) collective-permute-start(bf16[768,768]{1,0:T(8,128)(2,1)S(1)} %get-tuple-element.192), channel_id=1, source_target_pairs={{0,1},{1,0},{2,3},{3,2},{4,5},{5,4},{6,7},{7,6},{8,9},{9,8},{10,11... | collective-permute-start | bytes 3538952 | tf_op jit(solution)/shard_map/ppermute | solution.py:1115
  88.0 7.6 %collective-permute-start.7 = (bf16[512,768]{1,0:T(8,128)(2,1)S(1)}, bf16[512,768]{1,0:T(8,128)(2,1)S(1)}, u32[]{:S(2)}, u32[]{:S(2)}) collective-permute-start(bf16[512,768]{1,0:T(8,128)(2,1)S(1)} %get-tuple-element.194), channel_id=1, source_target_pairs={{0,1},{1,0},{2,3},{3,2},{4,5},{5,4},{6,7},{7,6},{8,9},{9,8},{10,11... | collective-permute-start | bytes 2359304 | tf_op jit(solution)/shard_map/ppermute | solution.py:1115
  90.4 15.0 %collective-permute-start.12 = (bf16[384,768]{1,0:T(8,128)(2,1)S(1)}, bf16[384,768]{1,0:T(8,128)(2,1)S(1)}, u32[]{:S(2)}, u32[]{:S(2)}) collective-permute-start(bf16[384,768]{1,0:T(8,128)(2,1)S(1)} %get-tuple-element.206), channel_id=1, source_target_pairs={{0,8},{4,12},{8,0},{12,4},{16,24},{20,28},{24,16},{28,20},{1,9},{5... | collective-permute-start | bytes 1769480 | tf_op jit(solution)/shard_map/ppermute | solution.py:1117
  92.6 13.0 %collective-permute-start.11 = (bf16[320,768]{1,0:T(8,128)(2,1)S(1)}, bf16[320,768]{1,0:T(8,128)(2,1)S(1)}, u32[]{:S(2)}, u32[]{:S(2)}) collective-permute-start(bf16[320,768]{1,0:T(8,128)(2,1)S(1)} %get-tuple-element.205), channel_id=1, source_target_pairs={{0,4},{4,0},{8,12},{12,8},{16,20},{20,16},{24,28},{28,24},{1,5},{5... | collective-permute-start | bytes 1474568 | tf_op jit(solution)/shard_map/ppermute | solution.py:1117
  94.1 11.2 %collective-permute-start.13 = (bf16[256,768]{1,0:T(8,128)(2,1)S(1)}, bf16[256,768]{1,0:T(8,128)(2,1)S(1)}, u32[]{:S(2)}, u32[]{:S(2)}) collective-permute-start(bf16[256,768]{1,0:T(8,128)(2,1)S(1)} %get-tuple-element.207), channel_id=1, source_target_pairs={{0,2},{1,3},{2,0},{3,1},{4,6},{5,7},{6,4},{7,5},{8,10},{9,11},{10,... | collective-permute-start | bytes 1179656 | tf_op jit(solution)/shard_map/ppermute | solution.py:1115
  105.7 12.6 %collective-permute-start.14 = (bf16[2,960,256]{2,1,0:T(8,128)(2,1)S(1)}, bf16[2,960,256]{2,1,0:T(8,128)(2,1)S(1)}, u32[]{:S(2)}, u32[]{:S(2)}) collective-permute-start(bf16[2,960,256]{2,1,0:T(8,128)(2,1)S(1)} %get-tuple-element.213), channel_id=1, source_target_pairs={{0,1},{1,0},{2,3},{3,2},{4,5},{5,4},{6,7},{7,6},{8,9},{9,8},{10,11... | collective-permute-start | bytes 2949128 | tf_op jit(solution)/shard_map/ppermute | solution.py:1115
  105.8 6.1 %collective-permute-start.15 = (bf16[64,768]{1,0:T(8,128)(2,1)S(1)}, bf16[64,768]{1,0:T(8,128)(2,1)S(1)}, u32[]{:S(2)}, u32[]{:S(2)}) collective-permute-start(bf16[64,768]{1,0:T(8,128)(2,1)S(1)} %get-tuple-element.214), channel_id=1, source_target_pairs={{0,8},{4,12},{8,0},{12,4},{16,24},{20,28},{24,16},{28,20},{1,9},{5... | collective-permute-start | bytes 294920 | tf_op jit(solution)/shard_map/ppermute | solution.py:1117
  107.5 10.8 %collective-permute-start.16 = (bf16[64,768]{1,0:T(8,128)(2,1)S(1)}, bf16[64,768]{1,0:T(8,128)(2,1)S(1)}, u32[]{:S(2)}, u32[]{:S(2)}) collective-permute-start(bf16[64,768]{1,0:T(8,128)(2,1)S(1)} %get-tuple-element.215), channel_id=1, source_target_pairs={{0,16},{4,20},{8,24},{12,28},{16,0},{20,4},{24,8},{28,12},{1,17},{... | collective-permute-start | bytes 294920 | tf_op jit(solution)/shard_map/ppermute | solution.py:1117
  110.1 8.2 %collective-permute-start.17 = (bf16[64,768]{1,0:T(8,128)(2,1)S(1)}, bf16[64,768]{1,0:T(8,128)(2,1)S(1)}, u32[]{:S(2)}, u32[]{:S(2)}) collective-permute-start(bf16[64,768]{1,0:T(8,128)(2,1)S(1)} %get-tuple-element.216), channel_id=1, source_target_pairs={{0,24},{4,28},{8,16},{12,20},{16,8},{20,12},{24,0},{28,4},{1,25},{... | collective-permute-start | bytes 294920 | tf_op jit(solution)/shard_map/ppermute | solution.py:1117
  110.2 12.5 %collective-permute-start.19 = (bf16[160,768]{1,0:T(8,128)(2,1)S(1)}, bf16[160,768]{1,0:T(8,128)(2,1)S(1)}, u32[]{:S(2)}, u32[]{:S(2)}) collective-permute-start(bf16[160,768]{1,0:T(8,128)(2,1)S(1)} %get-tuple-element.221), channel_id=1, source_target_pairs={{0,2},{1,3},{2,0},{3,1},{4,6},{5,7},{6,4},{7,5},{8,10},{9,11},{10,... | collective-permute-start | bytes 737288 | tf_op jit(solution)/shard_map/ppermute | solution.py:1115
  118.6 21.7 %collective-permute-start.18 = (bf16[960,256]{1,0:T(8,128)(2,1)S(1)}, bf16[960,256]{1,0:T(8,128)(2,1)S(1)}, u32[]{:S(2)}, u32[]{:S(2)}) collective-permute-start(bf16[960,256]{1,0:T(8,128)(2,1)S(1)} %get-tuple-element.218), channel_id=1, source_target_pairs={{0,2},{1,3},{2,0},{3,1},{4,6},{5,7},{6,4},{7,5},{8,10},{9,11},{10,... | collective-permute-start | bytes 1474568 | tf_op jit(solution)/shard_map/ppermute | solution.py:1115
  120.2 18.4 %collective-permute-start.21 = (bf16[256,768]{1,0:T(8,128)(2,1)S(1)}, bf16[256,768]{1,0:T(8,128)(2,1)S(1)}, u32[]{:S(2)}, u32[]{:S(2)}) collective-permute-start(bf16[256,768]{1,0:T(8,128)(2,1)S(1)} %get-tuple-element.224), channel_id=1, source_target_pairs={{0,4},{4,0},{8,12},{12,8},{16,20},{20,16},{24,28},{28,24},{1,5},{5... | collective-permute-start | bytes 1179656 | tf_op jit(solution)/shard_map/ppermute | solution.py:1117
  121.7 14.3 %collective-permute-start.22 = (bf16[192,768]{1,0:T(8,128)(2,1)S(1)}, bf16[192,768]{1,0:T(8,128)(2,1)S(1)}, u32[]{:S(2)}, u32[]{:S(2)}) collective-permute-start(bf16[192,768]{1,0:T(8,128)(2,1)S(1)} %get-tuple-element.225), channel_id=1, source_target_pairs={{0,4},{4,0},{8,12},{12,8},{16,20},{20,16},{24,28},{28,24},{1,5},{5... | collective-permute-start | bytes 884744 | tf_op jit(solution)/shard_map/ppermute | solution.py:1117
  122.2 41.0 %collective-permute-start.31 = (bf16[384,768]{1,0:T(8,128)(2,1)S(1)}, bf16[384,768]{1,0:T(8,128)(2,1)S(1)}, u32[]{:S(2)}, u32[]{:S(2)}) collective-permute-start(bf16[384,768]{1,0:T(8,128)(2,1)S(1)} %get-tuple-element.237), channel_id=1, source_target_pairs={{0,2},{1,3},{2,0},{3,1},{4,6},{5,7},{6,4},{7,5},{8,10},{9,11},{10,... | collective-permute-start | bytes 1769480 | tf_op jit(solution)/shard_map/ppermute | solution.py:1115
  122.8 5.5 %collective-permute-start.23 = (bf16[64,768]{1,0:T(8,128)(2,1)S(1)}, bf16[64,768]{1,0:T(8,128)(2,1)S(1)}, u32[]{:S(2)}, u32[]{:S(2)}) collective-permute-start(bf16[64,768]{1,0:T(8,128)(2,1)S(1)} %add.35.refs_4_.refs_0_), channel_id=1, source_target_pairs={{0,16},{4,20},{8,24},{12,28},{16,0},{20,4},{24,8},{28,12},{1,17},{... | collective-permute-start | bytes 294920 | tf_op jit(solution)/shard_map/ppermute | solution.py:1117
  128.3 11.0 %collective-permute-start.20 = (bf16[80,768]{1,0:T(8,128)(2,1)S(1)}, bf16[80,768]{1,0:T(8,128)(2,1)S(1)}, u32[]{:S(2)}, u32[]{:S(2)}) collective-permute-start(bf16[80,768]{1,0:T(8,128)(2,1)S(1)} %get-tuple-element.223), channel_id=1, source_target_pairs={{0,16},{4,20},{8,24},{12,28},{16,0},{20,4},{24,8},{28,12},{1,17},{... | collective-permute-start | bytes 368648 | tf_op jit(solution)/shard_map/ppermute | solution.py:1117
  131.3 11.0 %copy-start.16 = (f32[256,768]{1,0:T(8,128)S(1)}, f32[256,768]{1,0:T(8,128)}, u32[]{:S(2)}) copy-start(f32[256,768]{1,0:T(8,128)} %get-tuple-element.219.mid_t) | copy-start | bytes 2359300
  131.4 11.0 %copy-start.22 = (f32[2,192,128]{2,1,0:T(8,128)S(1)}, f32[2,192,128]{2,1,0:T(8,128)}, u32[]{:S(2)}) copy-start(f32[2,192,128]{2,1,0:T(8,128)} %get-tuple-element.220.mid_l) | copy-start | bytes 589828
  136.0 8.5 %collective-permute-start.26 = (bf16[128,768]{1,0:T(8,128)(2,1)S(1)}, bf16[128,768]{1,0:T(8,128)(2,1)S(1)}, u32[]{:S(2)}, u32[]{:S(2)}) collective-permute-start(bf16[128,768]{1,0:T(8,128)(2,1)S(1)} %join.10.refs_4_.refs_0_), channel_id=1, source_target_pairs={{0,8},{4,12},{8,0},{12,4},{16,24},{20,28},{24,16},{28,20},{1,9},{5... | collective-permute-start | bytes 589832 | tf_op jit(solution)/shard_map/ppermute | solution.py:1117
  138.7 12.0 %collective-permute-start.24 = (bf16[128,768]{1,0:T(8,128)(2,1)S(1)}, bf16[128,768]{1,0:T(8,128)(2,1)S(1)}, u32[]{:S(2)}, u32[]{:S(2)}) collective-permute-start(bf16[128,768]{1,0:T(8,128)(2,1)S(1)} %get-tuple-element.230), channel_id=1, source_target_pairs={{0,2},{1,3},{2,0},{3,1},{4,6},{5,7},{6,4},{7,5},{8,10},{9,11},{10,... | collective-permute-start | bytes 589832 | tf_op jit(solution)/shard_map/ppermute | solution.py:1115
  139.3 11.4 %collective-permute-start.25 = (bf16[96,768]{1,0:T(8,128)(2,1)S(1)}, bf16[96,768]{1,0:T(8,128)(2,1)S(1)}, u32[]{:S(2)}, u32[]{:S(2)}) collective-permute-start(bf16[96,768]{1,0:T(8,128)(2,1)S(1)} %get-tuple-element.231), channel_id=1, source_target_pairs={{0,16},{4,20},{8,24},{12,28},{16,0},{20,4},{24,8},{28,12},{1,17},{... | collective-permute-start | bytes 442376 | tf_op jit(solution)/shard_map/ppermute | solution.py:1117
  140.4 11.6 %collective-permute-start.28 = (bf16[80,768]{1,0:T(8,128)(2,1)S(1)}, bf16[80,768]{1,0:T(8,128)(2,1)S(1)}, u32[]{:S(2)}, u32[]{:S(2)}) collective-permute-start(bf16[80,768]{1,0:T(8,128)(2,1)S(1)} %add.40.after.refs_0_), channel_id=1, source_target_pairs={{0,16},{4,20},{8,24},{12,28},{16,0},{20,4},{24,8},{28,12},{1,17},{... | collective-permute-start | bytes 368648 | tf_op jit(solution)/shard_map/ppermute | solution.py:1117
  152.0 18.3 %collective-permute-start.34 = (bf16[160,768]{1,0:T(8,128)(2,1)S(1)}, bf16[160,768]{1,0:T(8,128)(2,1)S(1)}, u32[]{:S(2)}, u32[]{:S(2)}) collective-permute-start(bf16[160,768]{1,0:T(8,128)(2,1)S(1)} %join.12.refs_4_.refs_0_), channel_id=1, source_target_pairs={{0,8},{4,12},{8,0},{12,4},{16,24},{20,28},{24,16},{28,20},{1,9},{5... | collective-permute-start | bytes 737288 | tf_op jit(solution)/shard_map/ppermute | solution.py:1117
  152.1 11.2 %collective-permute-start.27 = (bf16[64,768]{1,0:T(8,128)(2,1)S(1)}, bf16[64,768]{1,0:T(8,128)(2,1)S(1)}, u32[]{:S(2)}, u32[]{:S(2)}) collective-permute-start(bf16[64,768]{1,0:T(8,128)(2,1)S(1)} %get-tuple-element.234), channel_id=1, source_target_pairs={{0,8},{4,12},{8,0},{12,4},{16,24},{20,28},{24,16},{28,20},{1,9},{5... | collective-permute-start | bytes 294920 | tf_op jit(solution)/shard_map/ppermute | solution.py:1117
  154.1 12.0 %collective-permute-start.30 = (bf16[96,768]{1,0:T(8,128)(2,1)S(1)}, bf16[96,768]{1,0:T(8,128)(2,1)S(1)}, u32[]{:S(2)}, u32[]{:S(2)}) collective-permute-start(bf16[96,768]{1,0:T(8,128)(2,1)S(1)} %add.41.refs_4_.refs_0_), channel_id=1, source_target_pairs={{0,16},{4,20},{8,24},{12,28},{16,0},{20,4},{24,8},{28,12},{1,17},{... | collective-permute-start | bytes 442376 | tf_op jit(solution)/shard_map/ppermute | solution.py:1117
  163.4 10.4 %collective-permute-start.33 = (bf16[192,768]{1,0:T(8,128)(2,1)S(1)}, bf16[192,768]{1,0:T(8,128)(2,1)S(1)}, u32[]{:S(2)}, u32[]{:S(2)}) collective-permute-start(bf16[192,768]{1,0:T(8,128)(2,1)S(1)} %get-tuple-element.239), channel_id=1, source_target_pairs={{0,4},{4,0},{8,12},{12,8},{16,20},{20,16},{24,28},{28,24},{1,5},{5... | collective-permute-start | bytes 884744 | tf_op jit(solution)/shard_map/ppermute | solution.py:1117
  165.0 5.3 %collective-permute-start.29 = (bf16[32,768]{1,0:T(8,128)(2,1)S(1)}, bf16[32,768]{1,0:T(8,128)(2,1)S(1)}, u32[]{:S(2)}, u32[]{:S(2)}) collective-permute-start(bf16[32,768]{1,0:T(8,128)(2,1)S(1)} %get-tuple-element.236), channel_id=1, source_target_pairs={{0,16},{4,20},{8,24},{12,28},{16,0},{20,4},{24,8},{28,12},{1,17},{... | collective-permute-start | bytes 147464 | tf_op jit(solution)/shard_map/ppermute | solution.py:1117
  166.1 14.4 %collective-permute-start.36 = (bf16[192,768]{1,0:T(8,128)(2,1)S(1)}, bf16[192,768]{1,0:T(8,128)(2,1)S(1)}, u32[]{:S(2)}, u32[]{:S(2)}) collective-permute-start(bf16[192,768]{1,0:T(8,128)(2,1)S(1)} %join.13.refs_2_.refs_0_), channel_id=1, source_target_pairs={{0,8},{4,12},{8,0},{12,4},{16,24},{20,28},{24,16},{28,20},{1,9},{5... | collective-permute-start | bytes 884744 | tf_op jit(solution)/shard_map/ppermute | solution.py:1117
  170.4 22.7 %collective-permute-start.38 = (bf16[320,768]{1,0:T(8,128)(2,1)S(1)}, bf16[320,768]{1,0:T(8,128)(2,1)S(1)}, u32[]{:S(2)}, u32[]{:S(2)}) collective-permute-start(bf16[320,768]{1,0:T(8,128)(2,1)S(1)} %join.14.refs_8_.refs_0_), channel_id=1, source_target_pairs={{0,4},{4,0},{8,12},{12,8},{16,20},{20,16},{24,28},{28,24},{1,5},{5... | collective-permute-start | bytes 1474568 | tf_op jit(solution)/shard_map/ppermute | solution.py:1117
  171.0 22.0 %collective-permute-start.39 = (bf16[256,768]{1,0:T(8,128)(2,1)S(1)}, bf16[256,768]{1,0:T(8,128)(2,1)S(1)}, u32[]{:S(2)}, u32[]{:S(2)}) collective-permute-start(bf16[256,768]{1,0:T(8,128)(2,1)S(1)} %join.11.refs_2_), channel_id=1, source_target_pairs={{0,4},{4,0},{8,12},{12,8},{16,20},{20,16},{24,28},{28,24},{1,5},{5... | collective-permute-start | bytes 1179656 | tf_op jit(solution)/shard_map/ppermute | solution.py:1117
  172.5 6.0 %collective-permute-start.32 = (bf16[32,768]{1,0:T(8,128)(2,1)S(1)}, bf16[32,768]{1,0:T(8,128)(2,1)S(1)}, u32[]{:S(2)}, u32[]{:S(2)}) collective-permute-start(bf16[32,768]{1,0:T(8,128)(2,1)S(1)} %add.45.refs_2_.refs_0_), channel_id=1, source_target_pairs={{0,16},{4,20},{8,24},{12,28},{16,0},{20,4},{24,8},{28,12},{1,17},{... | collective-permute-start | bytes 147464 | tf_op jit(solution)/shard_map/ppermute | solution.py:1117
  178.4 4.7 %collective-permute-start.35 = (bf16[64,768]{1,0:T(8,128)(2,1)S(1)}, bf16[64,768]{1,0:T(8,128)(2,1)S(1)}, u32[]{:S(2)}, u32[]{:S(2)}) collective-permute-start(bf16[64,768]{1,0:T(8,128)(2,1)S(1)} %join.15.refs_2_.refs_0_), channel_id=1, source_target_pairs={{0,8},{4,12},{8,0},{12,4},{16,24},{20,28},{24,16},{28,20},{1,9},{5... | collective-permute-start | bytes 294920 | tf_op jit(solution)/shard_map/ppermute | solution.py:1117
  178.8 5.2 %collective-permute-start.40 = (bf16[48,768]{1,0:T(8,128)(2,1)S(1)}, bf16[48,768]{1,0:T(8,128)(2,1)S(1)}, u32[]{:S(2)}, u32[]{:S(2)}) collective-permute-start(bf16[48,768]{1,0:T(8,128)(2,1)S(1)} %get-tuple-element.241), channel_id=1, source_target_pairs={{0,8},{4,12},{8,0},{12,4},{16,24},{20,28},{24,16},{28,20},{1,9},{5... | collective-permute-start | bytes 221192 | tf_op jit(solution)/shard_map/ppermute | solution.py:1117
  180.5 7.5 %collective-permute-start.41 = (bf16[48,768]{1,0:T(8,128)(2,1)S(1)}, bf16[48,768]{1,0:T(8,128)(2,1)S(1)}, u32[]{:S(2)}, u32[]{:S(2)}) collective-permute-start(bf16[48,768]{1,0:T(8,128)(2,1)S(1)} %get-tuple-element.242), channel_id=1, source_target_pairs={{0,16},{4,20},{8,24},{12,28},{16,0},{20,4},{24,8},{28,12},{1,17},{... | collective-permute-start | bytes 221192 | tf_op jit(solution)/shard_map/ppermute | solution.py:1117
  183.1 14.1 %collective-permute-start.37 = (bf16[128,768]{1,0:T(8,128)(2,1)S(1)}, bf16[128,768]{1,0:T(8,128)(2,1)S(1)}, u32[]{:S(2)}, u32[]{:S(2)}) collective-permute-start(bf16[128,768]{1,0:T(8,128)(2,1)S(1)} %join.17.refs_4_.refs_0_), channel_id=1, source_target_pairs={{0,4},{4,0},{8,12},{12,8},{16,20},{20,16},{24,28},{28,24},{1,5},{5... | collective-permute-start | bytes 589832 | tf_op jit(solution)/shard_map/ppermute | solution.py:1117
  183.9 6.2 %collective-permute-start.42 = (bf16[48,768]{1,0:T(8,128)(2,1)S(1)}, bf16[48,768]{1,0:T(8,128)(2,1)S(1)}, u32[]{:S(2)}, u32[]{:S(2)}) collective-permute-start(bf16[48,768]{1,0:T(8,128)(2,1)S(1)} %get-tuple-element.243), channel_id=1, source_target_pairs={{0,24},{4,28},{8,16},{12,20},{16,8},{20,12},{24,0},{28,4},{1,25},{... | collective-permute-start | bytes 221192 | tf_op jit(solution)/shard_map/ppermute | solution.py:1117
  188.0 21.2 %collective-permute-start.46 = (bf16[384,768]{1,0:T(8,128)(2,1)S(1)}, bf16[384,768]{1,0:T(8,128)(2,1)S(1)}, u32[]{:S(2)}, u32[]{:S(2)}) collective-permute-start(bf16[384,768]{1,0:T(8,128)(2,1)S(1)} %join.16.refs_2_.refs_0_), channel_id=1, source_target_pairs={{0,4},{4,0},{8,12},{12,8},{16,20},{20,16},{24,28},{28,24},{1,5},{5... | collective-permute-start | bytes 1769480 | tf_op jit(solution)/shard_map/ppermute | solution.py:1117
  190.1 7.1 %collective-permute-start.43 = (bf16[48,768]{1,0:T(8,128)(2,1)S(1)}, bf16[48,768]{1,0:T(8,128)(2,1)S(1)}, u32[]{:S(2)}, u32[]{:S(2)}) collective-permute-start(bf16[48,768]{1,0:T(8,128)(2,1)S(1)} %add.47.refs_4_.refs_0_), channel_id=1, source_target_pairs={{0,16},{4,20},{8,24},{12,28},{16,0},{20,4},{24,8},{28,12},{1,17},{... | collective-permute-start | bytes 221192 | tf_op jit(solution)/shard_map/ppermute | solution.py:1117
  197.2 5.2 %collective-permute-start.44 = (bf16[96,768]{1,0:T(8,128)(2,1)S(1)}, bf16[96,768]{1,0:T(8,128)(2,1)S(1)}, u32[]{:S(2)}, u32[]{:S(2)}) collective-permute-start(bf16[96,768]{1,0:T(8,128)(2,1)S(1)} %join.18.refs_0_.refs_2_), channel_id=1, source_target_pairs={{0,8},{4,12},{8,0},{12,4},{16,24},{20,28},{24,16},{28,20},{1,9},{5... | collective-permute-start | bytes 442376 | tf_op jit(solution)/shard_map/ppermute | solution.py:1117
  202.5 9.9 %collective-permute-start.45 = (bf16[192,768]{1,0:T(8,128)(2,1)S(1)}, bf16[192,768]{1,0:T(8,128)(2,1)S(1)}, u32[]{:S(2)}, u32[]{:S(2)}) collective-permute-start(bf16[192,768]{1,0:T(8,128)(2,1)S(1)} %join.19.refs_2_), channel_id=1, source_target_pairs={{0,4},{4,0},{8,12},{12,8},{16,20},{20,16},{24,28},{28,24},{1,5},{5... | collective-permute-start | bytes 884744 | tf_op jit(solution)/shard_map/ppermute | solution.py:1117
  (15 other events, 43.7 us)
